TPU v7x, 256 devices: a whole 4x4x8 slice. The times are simulated.
256 devices in a mesh: mode: 8 (over x, core), elem: 32 (over z, y).
Axes of the slice: x: 4, y: 4, z: 8, core: 2. Of those that a mesh axis runs over, the one named last changes fastest.
Arguments:
- forcing: float32 [128, 81, 4096], P('mode', None, 'elem'), may hold values from -300 to 300
- metric: float32 [4, 81, 4096], P(None, None, 'elem'), as said below
- edge_map: int32 [4096, 32], P('elem'), may hold values from 0 to 2112, as said below
- shared_rows: int32 [12288], P('elem'), may hold values from 0 to 2112, as said below
- partner_masks: int32 [12288], P('elem'), may hold values from 1 to 16, as said below
- penalty: float32 [67616], P('elem'), may hold values from 50 to 500
Outputs:
- pressure: float32 [128, 81, 4096], P('mode', None, 'elem')
Inputs may be any that keep to these rules, and one draw needn't show every extreme that they name: `edge_map`: entries index skeleton nodes of the element's own device; an element's 32 entries are distinct, and every skeleton node of a device is named by some element of it. `shared_rows`: each device's 384 slots name distinct skeleton nodes on the perimeter of that device's patch of elements. `partner_masks`: every entry has exactly one bit set. Along each device's slots the pattern is constant over four runs in order, of lengths 8 * 8 + 1, 65, 127 and 127. The partner device of a slot holds the same pattern at that slot. `metric`: at every node the first, second and fourth components are positive and the third's magnitude is at most half the geometric mean of the first two.
All inputs are finite; a program needn't handle non-finite values.
Results may differ from a plain program's by a relative error of at most 0.0003.
Values sent between devices are 32-bit elements; how exact they have to be, the bound alone decides.
No kernel may reach another device: no remote copies, remote signals or barrier semaphores. Data moves between devices by JAX's collectives and lax.ppermute only.
A program may use at most 64 MiB of HBM per device.

v0:
```python
import math

import jax
import jax.numpy as jnp
import numpy as np
from jax import lax
from jax.sharding import PartitionSpec as P

ORDER = 8
ITERS = 2


plane_spacing = 0.25


def partner(array, axis, bit):
    return lax.ppermute(array, axis, [(i, i ^ 1 << bit) for i in range(lax.axis_size(axis))])


def legendre_table(points, poly_order):
    table = np.zeros((points.shape[0], poly_order + 1))
    table[:, 0] = 1.0
    table[:, 1] = points
    for degree in range(2, poly_order + 1):
        table[:, degree] = (
            (2 * degree - 1) * points * table[:, degree - 1] - (degree - 1) * table[:, degree - 2]
        ) / degree
    return table


def lobatto_derivative(poly_order):
    node_count = poly_order + 1
    points = np.cos(np.pi * np.arange(node_count) / poly_order)
    for newton_step in range(100):
        table = legendre_table(points, poly_order)
        points = points - (points * table[:, poly_order] - table[:, poly_order - 1]) / (
            node_count * table[:, poly_order]
        )
    points = np.sort(points)
    top_values = legendre_table(points, poly_order)[:, poly_order]
    identity = np.eye(node_count)
    differ = points[:, None] - points[None, :] + identity
    matrix = top_values[:, None] / (top_values[None, :] * differ)
    matrix = matrix * (1.0 - identity)
    matrix[0, 0] = -poly_order * node_count / 4.0
    matrix[poly_order, poly_order] = poly_order * node_count / 4.0
    return matrix


def fourier_tables(planes):
    positions = jnp.arange(planes, dtype=jnp.int32)
    wavenumber = positions // 2
    phases = (wavenumber[:, None] * positions[None, :] % planes).astype(jnp.float32) * (
        2.0 * math.pi / planes
    )
    cosine = jnp.cos(phases)
    sine_table = jnp.sin(phases)
    is_even = (positions % 2 == 0)[:, None]
    nyquist = (positions == 1)[:, None]
    alternate = (1 - 2 * (positions % 2)).astype(jnp.float32)[None, :]
    forward = jnp.where(nyquist, alternate, jnp.where(is_even, cosine, -sine_table)) / planes
    backward = jnp.where(is_even, 2.0 * cosine, -2.0 * sine_table)
    backward = jnp.where(nyquist, alternate, backward)
    backward = jnp.where((positions == 0)[:, None], 1.0, backward)
    return (forward, backward.T)


def helmholtz_shift(rows_global, planes):
    wavenumber = (rows_global // 2).astype(jnp.float32)
    spanwise = wavenumber * (2.0 * math.pi / (planes * plane_spacing))
    spanwise = jnp.where(rows_global == 1, math.pi / plane_spacing, spanwise)
    return spanwise * spanwise


def cycle_of(values_grid):
    last_node = values_grid.shape[-2] - 1
    return jnp.concatenate(
        [
            values_grid[..., :, 0, :],
            values_grid[..., :, last_node, :],
            values_grid[..., 0, 1:last_node, :],
            values_grid[..., last_node, 1:last_node, :],
        ],
        axis=-2,
    )


def element_of(interior, boundary):
    node_count = interior.shape[-2] + 2
    side_bottom = boundary[..., 0:node_count, :]
    side_top = boundary[..., node_count : 2 * node_count, :]
    side_left = boundary[..., 2 * node_count : 3 * node_count - 2, :]
    side_right = boundary[..., 3 * node_count - 2 :, :]
    middle = jnp.concatenate(
        [side_left[..., None, :, :], interior, side_right[..., None, :, :]], axis=-3
    )
    return jnp.concatenate(
        [side_bottom[..., :, None, :], middle, side_top[..., :, None, :]], axis=-2
    )


def element_apply(values_grid, metric, shift_row, derivative):
    grad_first = jnp.einsum(
        "ik,...kje->...ije", derivative, values_grid, precision=lax.Precision.HIGHEST
    )
    grad_second = jnp.einsum(
        "jk,...ike->...ije", derivative, values_grid, precision=lax.Precision.HIGHEST
    )
    flux_first = metric[0] * grad_first + metric[2] * grad_second
    flux_second = metric[2] * grad_first + metric[1] * grad_second
    result = jnp.einsum(
        "ki,...kje->...ije", derivative, flux_first, precision=lax.Precision.HIGHEST
    )
    result = result + jnp.einsum(
        "kj,...ike->...ije", derivative, flux_second, precision=lax.Precision.HIGHEST
    )
    return result + shift_row * metric[3] * values_grid


def element_diagonal(metric, derivative):
    squared = derivative * derivative
    term_first = jnp.einsum(
        "ki,...kje->...ije", squared, metric[0], precision=lax.Precision.HIGHEST
    )
    term_second = jnp.einsum(
        "kj,...ike->...ije", squared, metric[1], precision=lax.Precision.HIGHEST
    )
    corner = jnp.diagonal(derivative)
    cross_term = 2.0 * (corner[:, None] * corner[None, :])[:, :, None] * metric[2]
    return term_first + term_second + cross_term


def body(forcing, metric, edge_map, shared_rows, partner_masks, penalty):
    derivative = jnp.asarray(lobatto_derivative(ORDER), jnp.float32)
    nodes_side = ORDER + 1
    local_rows = forcing.shape[0]
    elements = forcing.shape[2]
    planes = local_rows * lax.axis_size("mode")
    forward, backward = fourier_tables(planes)
    geometry = metric.reshape(4, nodes_side, nodes_side, elements)
    node_map = edge_map.T
    skeleton_count = penalty.shape[0]
    weights = jnp.ones((skeleton_count,), jnp.float32).at[shared_rows].set(0.5)
    rows_global = lax.axis_index("mode") * local_rows + jnp.arange(local_rows, dtype=jnp.int32)
    shifts = helmholtz_shift(rows_global, planes)[:, None, None, None]
    sections = lax.axis_size("elem").bit_length() - 1

    def share_rows(skeleton):
        slot_values = skeleton[:, shared_rows]
        for bit_level in range(sections):
            arrived = partner(slot_values, "elem", bit_level)
            moving = jnp.bitwise_and(jnp.right_shift(partner_masks, bit_level), 1) == 1
            slot_values = jnp.where(moving[None, :], arrived, slot_values)
        return skeleton.at[:, shared_rows].add(slot_values)

    def scatter_cycle(cycle_values):
        return (
            jnp.zeros((cycle_values.shape[0], skeleton_count), jnp.float32)
            .at[:, node_map]
            .add(cycle_values)
        )

    def assemble(values_grid, addition):
        return (
            values_grid[:, 1:ORDER, 1:ORDER, :],
            share_rows(scatter_cycle(cycle_of(values_grid)) + addition),
        )

    def local_product(left_pair, right_pair):
        return jnp.sum(left_pair[0] * right_pair[0], axis=(1, 2, 3)) + jnp.sum(
            left_pair[1] * right_pair[1] * weights[None, :], axis=1
        )

    def update_pair(scale, base_pair, other_pair):
        return (
            base_pair[0] + scale[:, None, None, None] * other_pair[0],
            base_pair[1] + scale[:, None] * other_pair[1],
        )

    def precond_sum(residual, precond):
        return lax.psum(local_product(residual, precond), "elem")

    gathered = lax.all_to_all(forcing, "mode", split_axis=2, concat_axis=0, tiled=True)
    mixed_rows = jnp.dot(
        forward, gathered.reshape(planes, -1), precision=lax.Precision.HIGHEST
    ).reshape(gathered.shape)
    coefficients = lax.all_to_all(mixed_rows, "mode", split_axis=0, concat_axis=2, tiled=True)
    stacked = jnp.stack([element_diagonal(geometry, derivative), geometry[3]])
    diag_parts = assemble(stacked, jnp.stack([penalty, jnp.zeros_like(penalty)]))
    diag_interior = diag_parts[0][0][None] + shifts * diag_parts[0][1][None]
    diag_skeleton = diag_parts[1][0][None] + shifts[:, :, 0, 0] * diag_parts[1][1][None]
    right_side = assemble(coefficients.reshape(local_rows, nodes_side, nodes_side, elements), 0.0)
    residual = right_side
    precond = (residual[0] / diag_interior, residual[1] / diag_skeleton)
    solution = (jnp.zeros_like(right_side[0]), jnp.zeros_like(right_side[1]))
    search = precond
    current = precond_sum(residual, precond)
    for iteration in range(ITERS):
        operate_skeleton = search[1]
        operate_values_grid = element_of(search[0], operate_skeleton[:, node_map])
        result = element_apply(operate_values_grid, geometry, shifts, derivative)
        applied = assemble(result, penalty[None, :] * operate_skeleton)
        energy = lax.psum(local_product(search, applied), "elem")
        step_size = current / energy
        solution = update_pair(step_size, solution, search)
        residual = update_pair(-step_size, residual, applied)
        if iteration + 1 < ITERS:
            precond = (residual[0] / diag_interior, residual[1] / diag_skeleton)
            following = precond_sum(residual, precond)
            search = update_pair(following / current, precond, search)
            current = following
    final_values = element_of(solution[0], solution[1][:, node_map]).reshape(forcing.shape)
    gathered = lax.all_to_all(final_values, "mode", split_axis=2, concat_axis=0, tiled=True)
    physical = jnp.dot(
        backward, gathered.reshape(planes, -1), precision=lax.Precision.HIGHEST
    ).reshape(gathered.shape)
    return lax.all_to_all(physical, "mode", split_axis=0, concat_axis=2, tiled=True)


def solution(mesh):
    placed = (
        P("mode", None, "elem"),
        P(None, None, "elem"),
        P("elem", None),
        P("elem"),
        P("elem"),
        P("elem"),
    )
    return jax.shard_map(
        body, mesh=mesh, in_specs=placed, out_specs=P("mode", None, "elem"), check_vma=False
    )
```

profile of v0, /device:TPU:1, one launch (start us, length us, event | category | flops | bytes accessed | tf_op | source)
XLA Modules:
  0.0 648.0 jit_solution(17544494463612637682)
XLA Ops:
  2.6 6.8 %all-to-all-start = ((f32[16,81,128]{1,0,2:T(8,128)}), f32[16,81,128]{1,0,2:T(8,128)S(1)}, u32[]{:S(2)}, u32[]{:S(2)}) async-start(f32[16,81,128]{1,0,2:T(8,128)} %copy.305), calls=%async_computation | async-start | bytes 2097152 | tf_op jit(solution)/shard_map/all_to_all | solution.py:183
  14.2 23.0 %scatter_fusion = f32[2,2113]{0,1:T(8,128)S(1)} fusion(f32[2,2113]{0,1:T(8,128)S(1)} %stack.14, s32[4096]{0:T(1024)S(1)} %fusion.89, f32[4096,2]{1,0:T(8,128)} %bitcast.237), kind=kCustom, calls=%fused_computation.10 | custom fusion | flops 8192 | bytes 114688 | tf_op jit(solution)/shard_map/scatter-add | solution.py:160
  58.4 5.4 collective-permute-done.6
  80.7 22.9 %scatter_custom_fusion = f32[16,2113]{0,1:T(8,128)S(1)} fusion(s32[4096]{0:T(1024)} %copy-done.19, f32[4096,16]{1,0:T(8,128)} %bitcast.238, f32[]{:T(128)} %constant.107.clone.1), kind=kCustom, calls=%fused_computation.63 | custom fusion | flops 65536 | bytes 135744 | tf_op jit(solution)/shard_map/scatter-add | solution.py:160
  117.1 6.7 %collective-permute-start.9 = (f32[2,384]{0,1:T(8,128)S(1)}, f32[2,384]{0,1:T(8,128)S(1)}, u32[]{:S(2)}, u32[]{:S(2)}) collective-permute-start(f32[2,384]{0,1:T(8,128)S(1)} %broadcast_select_fusion.3), channel_id=1, source_target_pairs={{0,16},{1,17},{2,18},{3,19},{4,20},{5,21},{6,22},{7,23},{8,24},{9,... | collective-permute-start | bytes 9224 | tf_op jit(solution)/shard_map/ppermute | solution.py:17
  125.0 6.0 collective-permute-done.9
  138.5 8.3 %collective-permute-done.3 = f32[16,384]{0,1:T(8,128)S(1)} collective-permute-done((f32[16,384]{0,1:T(8,128)S(1)}, f32[16,384]{0,1:T(8,128)S(1)}, u32[]{:S(2)}, u32[]{:S(2)}) %collective-permute-start.3) | collective-permute-done | bytes 24608 | tf_op jit(solution)/shard_map/ppermute | solution.py:17
  147.2 12.0 %collective-permute-done.4 = f32[16,384]{0,1:T(8,128)S(1)} collective-permute-done((f32[16,384]{0,1:T(8,128)S(1)}, f32[16,384]{0,1:T(8,128)S(1)}, u32[]{:S(2)}, u32[]{:S(2)}) %collective-permute-start.4) | collective-permute-done | bytes 24608 | tf_op jit(solution)/shard_map/ppermute | solution.py:17
  164.2 14.2 %gather_fusion.3 = f32[4096,16]{1,0:T(8,128)} fusion(f32[16,2113]{0,1:T(8,128)S(1)} %copy.330, s32[4096]{0:T(1024)S(1)} %broadcast_clamp_fusion), kind=kCustom, calls=%fused_computation.3 | custom fusion | bytes 540672 | tf_op jit(solution)/shard_map/gather | solution.py:200
  192.8 23.2 %scatter_fusion.1 = f32[16,2113]{0,1:T(8,128)S(1)} fusion(f32[16,2113]{0,1:T(8,128)S(1)} %copy.349, s32[4096]{0:T(1024)S(1)} %copy-done.20, f32[4096,16]{1,0:T(8,128)} %bitcast.232), kind=kCustom, calls=%fused_computation.13 | custom fusion | flops 65536 | bytes 802816 | tf_op jit(solution)/shard_map/scatter-add | solution.py:160
  233.8 5.7 collective-permute-start.13
  252.4 7.6 %collective-permute-done.14 = f32[16,384]{0,1:T(8,128)} collective-permute-done((f32[16,384]{0,1:T(8,128)S(1)}, f32[16,384]{0,1:T(8,128)}, u32[]{:S(2)}, u32[]{:S(2)}) %collective-permute-start.14) | collective-permute-done | bytes 24608 | tf_op jit(solution)/shard_map/ppermute | solution.py:17
  264.1 64.1 %all-reduce.1 = (f32[16]{0:T(128)S(1)}, f32[16]{0:T(128)S(1)}) all-reduce(f32[16]{0:T(128)S(1)} %add.204, f32[16]{0:T(128)S(1)} %add.209), channel_id=1, replica_groups=mesh['mode'=8,'elem'=32] {'elem'}, use_global_device_ids=true, to_apply=%region_7.8 | all-reduce | flops 32 | bytes 256 | tf_op jit(solution)/shard_map/psum | solution.py:181
  328.8 56.3 %psum.30 = f32[16]{0:T(128)S(1)} all-reduce(f32[16]{0:T(128)S(1)} %add.212), channel_id=1, replica_groups=mesh['mode'=8,'elem'=32] {'elem'}, use_global_device_ids=true, to_apply=%region_15.16 | all-reduce | flops 16 | bytes 128 | tf_op jit(solution)/shard_map/psum | solution.py:181
  386.0 14.2 %gather_fusion.5 = f32[4096,16]{1,0:T(8,128)} fusion(f32[16,2113]{0,1:T(8,128)S(1)} %copy.354, s32[4096]{0:T(1024)S(1)} %copy-done.18), kind=kCustom, calls=%fused_computation.5 | custom fusion | bytes 540672 | tf_op jit(solution)/shard_map/gather | solution.py:200
  412.7 23.0 %scatter_fusion.2 = f32[16,2113]{0,1:T(8,128)S(1)} fusion(f32[16,2113]{0,1:T(8,128)S(1)} %copy.368, s32[4096]{0:T(1024)S(1)} %copy-done.21, f32[4096,16]{1,0:T(8,128)} %bitcast.231), kind=kCustom, calls=%fused_computation.15 | custom fusion | flops 65536 | bytes 802816 | tf_op jit(solution)/shard_map/scatter-add | solution.py:160
  442.0 6.0 collective-permute-done.16
  453.2 7.2 %collective-permute-done.18 = f32[16,384]{0,1:T(8,128)S(1)} collective-permute-done((f32[16,384]{0,1:T(8,128)S(1)}, f32[16,384]{0,1:T(8,128)S(1)}, u32[]{:S(2)}, u32[]{:S(2)}) %collective-permute-start.18) | collective-permute-done | bytes 24608 | tf_op jit(solution)/shard_map/ppermute | solution.py:17
  464.9 6.3 collective-permute-done.19
  474.9 58.4 %psum.31 = f32[16]{0:T(128)S(1)} all-reduce(f32[16]{0:T(128)S(1)} %add.219), channel_id=1, replica_groups=mesh['mode'=8,'elem'=32] {'elem'}, use_global_device_ids=true, to_apply=%region_20.21 | all-reduce | flops 16 | bytes 128 | tf_op jit(solution)/shard_map/psum | solution.py:203
  533.8 14.2 %gather_fusion.7 = f32[4096,16]{1,0:T(8,128)} fusion(f32[16,2113]{0,1:T(8,128)S(1)} %copy.371, s32[4096]{0:T(1024)S(1)} %copy-done.18), kind=kCustom, calls=%fused_computation.7 | custom fusion | bytes 540672 | tf_op jit(solution)/shard_map/gather | solution.py:212
  552.6 50.3 %all-to-all-start.2 = ((f32[16,81,128]{1,0,2:T(8,128)}), f32[16,81,128]{1,0,2:T(8,128)S(1)}, u32[]{:S(2)}, u32[]{:S(2)}) async-start(f32[16,81,128]{1,0,2:T(8,128)} %copy.377), calls=%async_computation.2 | async-start | bytes 2097152 | tf_op jit(solution)/shard_map/all_to_all | solution.py:213
  602.9 15.1 %all-to-all-done.2 = f32[16,81,128]{1,0,2:T(8,128)S(1)} async-done(((f32[16,81,128]{1,0,2:T(8,128)}), f32[16,81,128]{1,0,2:T(8,128)S(1)}, u32[]{:S(2)}, u32[]{:S(2)}) %all-to-all-start.2) | async-done | bytes 663584 | tf_op jit(solution)/shard_map/all_to_all | solution.py:213
  627.8 18.4 %all_to_all.63 = f32[128,81,16]{1,2,0:T(8,128)S(1)} all-to-all(f32[128,81,16]{1,2,0:T(8,128)S(1)} %copy.381), channel_id=1, replica_groups=mesh['mode'=8,'elem'=32] {'mode'}, dimensions={0} | all-to-all | bytes 1327104 | tf_op jit(solution)/shard_map/all_to_all | solution.py:217
  (308 shorter events, 170.8 us)
Async XLA Ops:
  2.6 37.0 %all-to-all-start = ((f32[16,81,128]{1,0,2:T(8,128)}), f32[16,81,128]{1,0,2:T(8,128)S(1)}, u32[]{:S(2)}, u32[]{:S(2)}) async-start(f32[16,81,128]{1,0,2:T(8,128)} %copy.305), calls=%async_computation | async-start | bytes 2097152 | tf_op jit(solution)/shard_map/all_to_all | solution.py:183
  38.4 17.1 %collective-permute-start.5 = (f32[2,384]{0,1:T(8,128)S(1)}, f32[2,384]{0,1:T(8,128)S(1)}, u32[]{:S(2)}, u32[]{:S(2)}) collective-permute-start(f32[2,384]{0,1:T(8,128)S(1)} %bitcast.254), channel_id=1, source_target_pairs={{0,1},{1,0},{2,3},{3,2},{4,5},{5,4},{6,7},{7,6},{8,9},{9,8},{10,11... | collective-permute-start | bytes 9224 | tf_op jit(solution)/shard_map/ppermute | solution.py:17
  50.3 20.3 %all-to-all-start.1 = ((f32[128,81,16]{1,2,0:T(8,128)}), f32[128,81,16]{1,2,0:T(8,128)S(1)}, u32[]{:S(2)}, u32[]{:S(2)}) async-start(f32[128,81,16]{1,2,0:T(8,128)} %copy.309), calls=%async_computation.1 | async-start | bytes 2097152 | tf_op jit(solution)/shard_map/all_to_all | solution.py:187
  55.6 8.1 %collective-permute-start.6 = (f32[2,384]{0,1:T(8,128)S(1)}, f32[2,384]{0,1:T(8,128)S(1)}, u32[]{:S(2)}, u32[]{:S(2)}) collective-permute-start(f32[2,384]{0,1:T(8,128)S(1)} %broadcast_select_fusion), channel_id=1, source_target_pairs={{0,2},{1,3},{2,0},{3,1},{4,6},{5,7},{6,4},{7,5},{8,10},{9,11},{10,... | collective-permute-start | bytes 9224 | tf_op jit(solution)/shard_map/ppermute | solution.py:17
  63.9 42.1 %collective-permute-start.7 = (f32[2,384]{0,1:T(8,128)S(1)}, f32[2,384]{0,1:T(8,128)S(1)}, u32[]{:S(2)}, u32[]{:S(2)}) collective-permute-start(f32[2,384]{0,1:T(8,128)S(1)} %broadcast_select_fusion.1), channel_id=1, source_target_pairs={{0,4},{1,5},{2,6},{3,7},{4,0},{5,1},{6,2},{7,3},{8,12},{9,13},{10,... | collective-permute-start | bytes 9224 | tf_op jit(solution)/shard_map/ppermute | solution.py:17
  104.8 5.6 collective-permute-start
  106.1 10.9 %collective-permute-start.8 = (f32[2,384]{0,1:T(8,128)S(1)}, f32[2,384]{0,1:T(8,128)S(1)}, u32[]{:S(2)}, u32[]{:S(2)}) collective-permute-start(f32[2,384]{0,1:T(8,128)S(1)} %broadcast_select_fusion.2), channel_id=1, source_target_pairs={{0,8},{1,9},{2,10},{3,11},{4,12},{5,13},{6,14},{7,15},{8,0},{9,1},... | collective-permute-start | bytes 9224 | tf_op jit(solution)/shard_map/ppermute | solution.py:17
  110.5 13.3 %collective-permute-start.1 = (f32[16,384]{0,1:T(8,128)S(1)}, f32[16,384]{0,1:T(8,128)S(1)}, u32[]{:S(2)}, u32[]{:S(2)}) collective-permute-start(f32[16,384]{0,1:T(8,128)S(1)} %broadcast_select_fusion.6), channel_id=1, source_target_pairs={{0,2},{1,3},{2,0},{3,1},{4,6},{5,7},{6,4},{7,5},{8,10},{9,11},{10,... | collective-permute-start | bytes 73736 | tf_op jit(solution)/shard_map/ppermute | solution.py:17
  117.1 13.9 %collective-permute-start.9 = (f32[2,384]{0,1:T(8,128)S(1)}, f32[2,384]{0,1:T(8,128)S(1)}, u32[]{:S(2)}, u32[]{:S(2)}) collective-permute-start(f32[2,384]{0,1:T(8,128)S(1)} %broadcast_select_fusion.3), channel_id=1, source_target_pairs={{0,16},{1,17},{2,18},{3,19},{4,20},{5,21},{6,22},{7,23},{8,24},{9,... | collective-permute-start | bytes 9224 | tf_op jit(solution)/shard_map/ppermute | solution.py:17
  124.0 11.3 %collective-permute-start.2 = (f32[16,384]{0,1:T(8,128)S(1)}, f32[16,384]{0,1:T(8,128)S(1)}, u32[]{:S(2)}, u32[]{:S(2)}) collective-permute-start(f32[16,384]{0,1:T(8,128)S(1)} %broadcast_select_fusion.9), channel_id=1, source_target_pairs={{0,4},{1,5},{2,6},{3,7},{4,0},{5,1},{6,2},{7,3},{8,12},{9,13},{10,... | collective-permute-start | bytes 73736 | tf_op jit(solution)/shard_map/ppermute | solution.py:17
  135.4 11.3 %collective-permute-start.3 = (f32[16,384]{0,1:T(8,128)S(1)}, f32[16,384]{0,1:T(8,128)S(1)}, u32[]{:S(2)}, u32[]{:S(2)}) collective-permute-start(f32[16,384]{0,1:T(8,128)S(1)} %broadcast_select_fusion.12), channel_id=1, source_target_pairs={{0,8},{1,9},{2,10},{3,11},{4,12},{5,13},{6,14},{7,15},{8,0},{9,1},... | collective-permute-start | bytes 73736 | tf_op jit(solution)/shard_map/ppermute | solution.py:17
  146.9 12.3 %collective-permute-start.4 = (f32[16,384]{0,1:T(8,128)S(1)}, f32[16,384]{0,1:T(8,128)S(1)}, u32[]{:S(2)}, u32[]{:S(2)}) collective-permute-start(f32[16,384]{0,1:T(8,128)S(1)} %broadcast_select_fusion.15), channel_id=1, source_target_pairs={{0,16},{1,17},{2,18},{3,19},{4,20},{5,21},{6,22},{7,23},{8,24},{9,... | collective-permute-start | bytes 73736 | tf_op jit(solution)/shard_map/ppermute | solution.py:17
  217.2 4.6 collective-permute-start.10
  221.9 7.0 %collective-permute-start.11 = (f32[16,384]{0,1:T(8,128)S(1)}, f32[16,384]{0,1:T(8,128)S(1)}, u32[]{:S(2)}, u32[]{:S(2)}) collective-permute-start(f32[16,384]{0,1:T(8,128)S(1)} %broadcast_select_fusion.5), channel_id=1, source_target_pairs={{0,2},{1,3},{2,0},{3,1},{4,6},{5,7},{6,4},{7,5},{8,10},{9,11},{10,... | collective-permute-start | bytes 73736 | tf_op jit(solution)/shard_map/ppermute | solution.py:17
  229.1 4.6 collective-permute-start.12
  233.8 14.1 %collective-permute-start.13 = (f32[16,384]{0,1:T(8,128)S(1)}, f32[16,384]{0,1:T(8,128)}, u32[]{:S(2)}, u32[]{:S(2)}) collective-permute-start(f32[16,384]{0,1:T(8,128)S(1)} %broadcast_select_fusion.11), channel_id=1, source_target_pairs={{0,8},{1,9},{2,10},{3,11},{4,12},{5,13},{6,14},{7,15},{8,0},{9,1},... | collective-permute-start | bytes 73736 | tf_op jit(solution)/shard_map/ppermute | solution.py:17
  249.0 11.0 %collective-permute-start.14 = (f32[16,384]{0,1:T(8,128)S(1)}, f32[16,384]{0,1:T(8,128)}, u32[]{:S(2)}, u32[]{:S(2)}) collective-permute-start(f32[16,384]{0,1:T(8,128)S(1)} %broadcast_select_fusion.14), channel_id=1, source_target_pairs={{0,16},{1,17},{2,18},{3,19},{4,20},{5,21},{6,22},{7,23},{8,24},{9,... | collective-permute-start | bytes 73736 | tf_op jit(solution)/shard_map/ppermute | solution.py:17
  263.4 121.7 %copy-start.26 = (f32[2113]{0:T(1024)S(1)}, f32[2113]{0:T(1024)}, u32[]{:S(2)}) copy-start(f32[2113]{0:T(1024)} %param.12) | copy-start | bytes 25360
  436.9 4.8 collective-permute-start.15
  441.9 6.1 collective-permute-start.16
  448.1 4.9 collective-permute-start.17
  453.1 7.3 %collective-permute-start.18 = (f32[16,384]{0,1:T(8,128)S(1)}, f32[16,384]{0,1:T(8,128)S(1)}, u32[]{:S(2)}, u32[]{:S(2)}) collective-permute-start(f32[16,384]{0,1:T(8,128)S(1)} %broadcast_select_fusion.10), channel_id=1, source_target_pairs={{0,8},{1,9},{2,10},{3,11},{4,12},{5,13},{6,14},{7,15},{8,0},{9,1},... | collective-permute-start | bytes 73736 | tf_op jit(solution)/shard_map/ppermute | solution.py:17
  460.6 10.6 %collective-permute-start.19 = (f32[16,384]{0,1:T(8,128)S(1)}, f32[16,384]{0,1:T(8,128)S(1)}, u32[]{:S(2)}, u32[]{:S(2)}) collective-permute-start(f32[16,384]{0,1:T(8,128)S(1)} %broadcast_select_fusion.13), channel_id=1, source_target_pairs={{0,16},{1,17},{2,18},{3,19},{4,20},{5,21},{6,22},{7,23},{8,24},{9,... | collective-permute-start | bytes 73736 | tf_op jit(solution)/shard_map/ppermute | solution.py:17
  552.6 65.4 %all-to-all-start.2 = ((f32[16,81,128]{1,0,2:T(8,128)}), f32[16,81,128]{1,0,2:T(8,128)S(1)}, u32[]{:S(2)}, u32[]{:S(2)}) async-start(f32[16,81,128]{1,0,2:T(8,128)} %copy.377), calls=%async_computation.2 | async-start | bytes 2097152 | tf_op jit(solution)/shard_map/all_to_all | solution.py:213
  (63 other events, 1454.2 us)
where the time goes:
time: 656 us; the launch traced here: 648 us
  blocking collectives  197 us (30%)
  other arithmetic  115 us (18%)
  waiting for transfers between devices  110 us (17%)
  local copies, waits for them, and re-layouts  107 us (16%)
  starting transfers between devices  101 us (15%)
  matrix products  15.4 us (2%)
    psum x2, blocking collectives, precond_sum(): return lax.psum(local_product(residual, precond), 'elem')  120 us
    scatter-add x4, other arithmetic, scatter_cycle(): return jnp.zeros((cycle_values.shape[0], skeleton_count), jnp.float32).at...  92.1 us
    ppermute x20, waiting for transfers between devices, partner(): lax.ppermute(array, axis, [(i, i ^ 1 << bit) for i in range(lax.axis_size...  90.5 us
    psum x1, blocking collectives, body(): energy = lax.psum(local_product(search, applied), 'elem')  58.4 us
    all_to_all x1, starting transfers between devices, body(): lax.all_to_all(final_values, 'mode', split_axis=2, concat_axis=0, tiled=T...  50.3 us
    ppermute x20, starting transfers between devices, partner(): lax.ppermute(array, axis, [(i, i ^ 1 << bit) for i in range(lax.axis_size...  38.5 us
    gather x4, local copies, waits for them, and re-layouts, body(): operate_values_grid = element_of(search[0], operate_skeleton[:, node_map])  32.8 us
    all_to_all x1, blocking collectives, body(): lax.all_to_all(physical, 'mode', split_axis=0, concat_axis=2, tiled=True)  18.4 us
  transfers between devices with their start and end apart: 23, of which 19 were waited for; matrix products, arithmetic and copies ran while one was open for 13% of the time, Pallas kernels for 0%

commit v1 on v0

v1 whole, which is shorter than its diff:
```python
import math

import jax
import jax.numpy as jnp
import numpy as np
from jax import lax
from jax.experimental import pallas as pl
from jax.experimental.pallas import tpu as pltpu
from jax.sharding import PartitionSpec as P

ORDER = 8
SIDE = ORDER + 1
NODES = SIDE * SIDE
CYCLE = 32
INNER = (ORDER - 1) ** 2
ROWS = 16
LANES = 128
PLANES = 128
MODES = 8
ELEMS_AXIS = 32
SKEL = 2113
LOW = 256
HIGH = 9
TILES = 2 * HIGH
SLOTS = 384
SLOT_TILES = SLOTS // LANES
BLOCK = 9
PACKED = MODES * BLOCK
SCALARS = 5
SPACING = 0.25
F32 = jnp.float32
BF16 = jnp.bfloat16
HIGHEST = lax.Precision.HIGHEST
VMEM_LIMIT = 56 * 1024 * 1024


def legendre_table(points, poly_order):
    table = np.zeros((points.shape[0], poly_order + 1))
    table[:, 0] = 1.0
    table[:, 1] = points
    for degree in range(2, poly_order + 1):
        table[:, degree] = (
            (2 * degree - 1) * points * table[:, degree - 1] - (degree - 1) * table[:, degree - 2]
        ) / degree
    return table


def lobatto_derivative(poly_order):
    node_count = poly_order + 1
    points = np.cos(np.pi * np.arange(node_count) / poly_order)
    for newton_step in range(100):
        table = legendre_table(points, poly_order)
        points = points - (points * table[:, poly_order] - table[:, poly_order - 1]) / (
            node_count * table[:, poly_order]
        )
    points = np.sort(points)
    top_values = legendre_table(points, poly_order)[:, poly_order]
    identity = np.eye(node_count)
    differ = points[:, None] - points[None, :] + identity
    matrix = top_values[:, None] / (top_values[None, :] * differ)
    matrix = matrix * (1.0 - identity)
    matrix[0, 0] = -poly_order * node_count / 4.0
    matrix[poly_order, poly_order] = poly_order * node_count / 4.0
    return matrix


def fourier_tables():
    positions = np.arange(PLANES)
    phases = ((positions // 2)[:, None] * positions[None, :] % PLANES) * (2.0 * np.pi / PLANES)
    cosine, sine = np.cos(phases), np.sin(phases)
    even = (positions % 2 == 0)[:, None]
    nyquist = (positions == 1)[:, None]
    alternate = (1.0 - 2.0 * (positions % 2))[None, :]
    forward = np.where(nyquist, alternate, np.where(even, cosine, -sine)) / PLANES
    backward = np.where(nyquist, alternate, np.where(even, 2.0 * cosine, -2.0 * sine))
    backward = np.where((positions == 0)[:, None], 1.0, backward)
    return forward.astype(np.float32), backward.T.astype(np.float32)


DERIVATIVE = lobatto_derivative(ORDER).astype(np.float32)
CYCLE_NODES = (
    [i * SIDE for i in range(SIDE)]
    + [i * SIDE + ORDER for i in range(SIDE)]
    + [j for j in range(1, ORDER)]
    + [ORDER * SIDE + j for j in range(1, ORDER)]
)
INNER_NODES = [i * SIDE + j for i in range(1, ORDER) for j in range(1, ORDER)]


def diagonal_tables():
    squared = (DERIVATIVE * DERIVATIVE).astype(np.float64)
    first = np.kron(squared.T, np.eye(SIDE))
    second = np.kron(np.eye(SIDE), squared.T)
    corner = np.diagonal(DERIVATIVE)
    cross = 2.0 * np.outer(corner, corner).reshape(NODES, 1)
    cross = np.broadcast_to(cross, (NODES, LANES))
    return np.concatenate([first, second], axis=1).astype(np.float32), cross.astype(np.float32)


def helmholtz_shift(rows_global):
    wavenumber = (rows_global // 2).astype(F32)
    spanwise = wavenumber * (2.0 * math.pi / (PLANES * SPACING))
    spanwise = jnp.where(rows_global == 1, math.pi / SPACING, spanwise)
    return spanwise * spanwise


def row_block(index):
    return slice(index * ROWS, (index + 1) * ROWS)


def lane_block(index):
    return slice(index * LANES, (index + 1) * LANES)


def pieces(value):
    top = value.astype(BF16).astype(F32)
    return top, value - top


def one_hot_columns(low_columns):
    lanes = lax.broadcasted_iota(jnp.int32, (low_columns.shape[0], LOW), 1)
    return jnp.where(low_columns == lanes, 1.0, 0.0).astype(BF16)


def one_hot_rows(low_rows):
    sublanes = lax.broadcasted_iota(jnp.int32, (LOW, low_rows.shape[1]), 0)
    return jnp.where(low_rows == sublanes, 1.0, 0.0).astype(BF16)


def masked_store(value, high_row, left_ref, column):
    top, rest = pieces(value)
    for high in range(HIGH):
        here = high_row == high
        left_ref[row_block(high), lane_block(column)] = jnp.where(here, top, 0.0).astype(BF16)
        left_ref[row_block(HIGH + high), lane_block(column)] = jnp.where(here, rest, 0.0).astype(BF16)


def scatter_sum(left, right):
    both = jnp.dot(left, right, preferred_element_type=F32)
    return both[: HIGH * ROWS] + both[HIGH * ROWS :]


def scatter_cycle(load, edge, edge_rows, left_ref, right_ref):
    low = jnp.bitwise_and(edge, LOW - 1)
    high_rows = jnp.right_shift(edge_rows, 8)
    for slot in range(CYCLE):
        right_ref[lane_block(slot), :] = one_hot_columns(low[:, slot : slot + 1])
        masked_store(load(slot), high_rows[slot : slot + 1, :], left_ref, slot)
    return scatter_sum(left_ref[...], right_ref[...])


def scatter_slots(load, shared, shared_rows, left_ref, right_ref):
    low = jnp.bitwise_and(shared, LOW - 1)
    high_rows = jnp.right_shift(shared_rows, 8)
    for tile in range(SLOT_TILES):
        right_ref[lane_block(tile), :] = one_hot_columns(low[:, tile : tile + 1])
        masked_store(load(tile), high_rows[tile : tile + 1, :], left_ref, tile)
    return scatter_sum(left_ref[:, :SLOTS], right_ref[:SLOTS, :])


def stack_pieces(skeleton):
    top, rest = pieces(skeleton)
    return jnp.concatenate([top.astype(BF16), rest.astype(BF16)], axis=0)


def gather_tile(stacked, rows):
    low = jnp.bitwise_and(rows, LOW - 1)
    high = jnp.right_shift(rows, 8)
    found = jnp.dot(stacked, one_hot_rows(low), preferred_element_type=F32)
    total = None
    for index in range(HIGH):
        part = found[row_block(index), :] + found[row_block(HIGH + index), :]
        part = jnp.where(high == index, part, 0.0)
        total = part if total is None else total + part
    return total


def gather_cycle(skeleton, edge_rows, store):
    stacked = stack_pieces(skeleton)
    for pair in range(CYCLE // 2):
        rows = jnp.concatenate(
            [edge_rows[2 * pair : 2 * pair + 1, :], edge_rows[2 * pair + 1 : 2 * pair + 2, :]], axis=1
        )
        total = gather_tile(stacked, rows)
        store(2 * pair, total[:, :LANES])
        store(2 * pair + 1, total[:, LANES:])


def gather_slots(skeleton, shared_rows):
    stacked = stack_pieces(skeleton)
    return [gather_tile(stacked, shared_rows[tile : tile + 1, :]) for tile in range(SLOT_TILES)]


def read_skeleton(packed_ref):
    return jnp.concatenate(
        [
            jnp.concatenate([packed_ref[INNER + 2 * high], packed_ref[INNER + 2 * high + 1]], axis=1)
            for high in range(HIGH)
        ],
        axis=0,
    )


def write_skeleton(packed_ref, skeleton):
    for high in range(HIGH):
        packed_ref[INNER + 2 * high] = skeleton[row_block(high), :LANES]
        packed_ref[INNER + 2 * high + 1] = skeleton[row_block(high), LANES:]


def clear_tail(packed_ref):
    for index in range(INNER + TILES, PACKED):
        packed_ref[index] = jnp.zeros((ROWS, LANES), F32)


def fold(value):
    return value[:, :LANES] + value[:, LANES:]


def per_tile(penalty_ref):
    return jnp.concatenate(
        [jnp.broadcast_to(penalty_ref[high : high + 1, :], (ROWS, LOW)) for high in range(HIGH)], axis=0
    )


def skeleton_sum(product):
    total = None
    for high in range(HIGH):
        part = fold(product[row_block(high), :])
        total = part if total is None else total + part
    return total


def pack_kernel(forcing_ref, edge_ref, out_ref, left_ref, right_ref):
    edge = edge_ref[...]
    edge_rows = edge.T
    for index, node in enumerate(INNER_NODES):
        out_ref[index] = forcing_ref[:, node, :]
    skeleton = scatter_cycle(
        lambda slot: forcing_ref[:, CYCLE_NODES[slot], :], edge, edge_rows, left_ref, right_ref
    )
    write_skeleton(out_ref, skeleton)
    clear_tail(out_ref)


def transform_kernel(matrix_ref, in_ref, out_ref):
    matrix = matrix_ref[...]
    for index in range(BLOCK):
        block = in_ref[:, index].reshape(PLANES, LANES)
        mixed = jnp.dot(matrix, block, precision=HIGHEST, preferred_element_type=F32)
        out_ref[:, index] = mixed.reshape(MODES, ROWS, LANES)


def diagonal_kernel(
    metric_ref, table_ref, cross_ref, edge_ref, penalty_ref, shared_ref, inner_ref, skeleton_ref, slots_ref,
    cells_ref, left_ref, right_ref,
):
    both = jnp.concatenate([metric_ref[0], metric_ref[1]], axis=0)
    terms = jnp.dot(table_ref[...], both, precision=HIGHEST, preferred_element_type=F32)
    cells_ref[0] = terms + cross_ref[...] * metric_ref[2]
    cells_ref[1] = metric_ref[3]
    for index, node in enumerate(INNER_NODES):
        inner_ref[0, index : index + 1, :] = cells_ref[0, node : node + 1, :]
        inner_ref[1, index : index + 1, :] = cells_ref[1, node : node + 1, :]
    edge = edge_ref[...]
    edge_rows = edge.T
    sublanes = lax.broadcasted_iota(jnp.int32, (ROWS, LANES), 0)

    def load(slot):
        node = CYCLE_NODES[slot]
        laplace = jnp.broadcast_to(cells_ref[0, node : node + 1, :], (ROWS, LANES))
        mass = jnp.broadcast_to(cells_ref[1, node : node + 1, :], (ROWS, LANES))
        return jnp.where(sublanes == 0, laplace, jnp.where(sublanes == 1, mass, 0.0))

    skeleton = scatter_cycle(load, edge, edge_rows, left_ref, right_ref)
    wide = lax.broadcasted_iota(jnp.int32, (HIGH * ROWS, LOW), 0)
    skeleton = skeleton + jnp.where(jnp.bitwise_and(wide, ROWS - 1) == 0, per_tile(penalty_ref), 0.0)
    skeleton_ref[...] = skeleton
    for tile, value in enumerate(gather_slots(skeleton, shared_ref[...])):
        slots_ref[tile] = value[:8]


def slots_kernel(packed_ref, shared_ref, extra_ref, out_ref):
    for tile, value in enumerate(gather_slots(read_skeleton(packed_ref), shared_ref[...])):
        out_ref[tile, :ROWS, :] = value
        out_ref[tile, ROWS:, :] = extra_ref[tile]


def select_arrived(masks, tile, arrived):
    chosen = arrived[0]
    row = masks[tile : tile + 1, :]
    for level in range(1, len(arrived)):
        moving = jnp.bitwise_and(jnp.right_shift(row, level), 1) == 1
        chosen = jnp.where(moving, arrived[level], chosen)
    return chosen


def derivative_line(values, transposed):
    results = []
    for out in range(SIDE):
        total = None
        for k in range(SIDE):
            weight = float(DERIVATIVE[k, out] if transposed else DERIVATIVE[out, k])
            if weight == 0.0:
                continue
            part = weight * values[k]
            total = part if total is None else total + part
        results.append(total)
    return results


def gradients(cells_ref, first_ref, metric_ref, rows, visit):
    for j in range(SIDE):
        line = derivative_line([cells_ref[k * SIDE + j, rows, :] for k in range(SIDE)], False)
        for i in range(SIDE):
            first_ref[i * SIDE + j] = line[i]
    for i in range(SIDE):
        line = derivative_line([cells_ref[i * SIDE + k, rows, :] for k in range(SIDE)], False)
        seconds = []
        for j in range(SIDE):
            node = i * SIDE + j
            m0, m1, m2 = [metric_ref[c, node : node + 1, :] for c in range(3)]
            g1, g2 = first_ref[node], line[j]
            p1 = m0 * g1 + m2 * g2
            p2 = m2 * g1 + m1 * g2
            visit(node, g1, g2, p1, p2)
            seconds.append(p2)
        yield i, seconds


def apply_operator(cells_ref, result_ref, first_ref, energy_ref, metric_ref, shift_ref):
    @pl.loop(0, 2)
    def half(part):
        rows = pl.ds(pl.multiple_of(part * 8, 8), 8)
        shift = shift_ref[rows, :]

        def visit(node, g1, g2, p1, p2):
            first_ref[node] = p1

        for i, seconds in gradients(cells_ref, first_ref, metric_ref, rows, visit):
            line = derivative_line(seconds, True)
            for j in range(SIDE):
                node = i * SIDE + j
                mass = shift * metric_ref[3, node : node + 1, :]
                result_ref[node, rows, :] = line[j] + mass * cells_ref[node, rows, :]
        energy = jnp.zeros((8, LANES), F32)
        for j in range(SIDE):
            line = derivative_line([first_ref[k * SIDE + j] for k in range(SIDE)], True)
            for i in range(SIDE):
                node = i * SIDE + j
                value = result_ref[node, rows, :] + line[i]
                result_ref[node, rows, :] = value
                energy = energy + value * cells_ref[node, rows, :]
        energy_ref[rows, :] = energy


def apply_energy(cells_ref, first_ref, energy_ref, metric_ref, shift_ref):
    @pl.loop(0, 2)
    def half(part):
        rows = pl.ds(pl.multiple_of(part * 8, 8), 8)
        shift = shift_ref[rows, :]
        sums = [jnp.zeros((8, LANES), F32)]

        def visit(node, g1, g2, p1, p2):
            value = cells_ref[node, rows, :]
            mass = shift * metric_ref[3, node : node + 1, :]
            sums[0] = sums[0] + (g1 * p1 + g2 * p2 + mass * value * value)

        for i, seconds in gradients(cells_ref, first_ref, metric_ref, rows, visit):
            pass
        energy_ref[rows, :] = sums[0]


def first_kernel(
    packed_ref, a0, a1, a2, a3, a4, masks_ref, shared_ref, shared_columns_ref, edge_ref, metric_ref, inner_ref,
    diagonal_ref, penalty_ref, shift_ref, search_ref, applied_ref, inverse_ref, slots_ref, sums_ref,
    left_ref, right_ref, cells_ref, result_ref, first_ref, energy_ref,
):
    arrived_refs = [a0, a1, a2, a3, a4]
    masks = masks_ref[...]
    shared_rows = shared_ref[...]
    shared_columns = shared_columns_ref[...]
    shift = shift_ref[...]

    def load_right(tile):
        return select_arrived(masks, tile, [ref[tile, :ROWS, :] for ref in arrived_refs])

    def load_extra(tile):
        chosen = select_arrived(masks, tile, [ref[tile, ROWS:, :] for ref in arrived_refs])
        return jnp.concatenate([chosen, jnp.zeros_like(chosen)], axis=0)

    local = read_skeleton(packed_ref)
    right_side = local + scatter_slots(load_right, shared_columns, shared_rows, left_ref, right_ref)
    diagonal = diagonal_ref[...] + scatter_slots(
        load_extra, shared_columns, shared_rows, left_ref, right_ref
    )
    parts = []
    for high in range(HIGH):
        block = diagonal[row_block(high), :]
        wide_shift = jnp.concatenate([shift, shift], axis=1)
        parts.append(block[0:1, :] + wide_shift * block[1:2, :])
    inverse = 1.0 / jnp.concatenate(parts, axis=0)
    search = right_side * inverse
    write_skeleton(search_ref, search)
    write_skeleton(inverse_ref, inverse)
    clear_tail(search_ref)
    start = skeleton_sum(local * search)
    for index, node in enumerate(INNER_NODES):
        value = packed_ref[index]
        inverted = 1.0 / (inner_ref[0, index : index + 1, :] + shift * inner_ref[1, index : index + 1, :])
        scaled = value * inverted
        inverse_ref[index] = inverted
        search_ref[index] = scaled
        cells_ref[node] = scaled
        start = start + value * scaled

    def store(slot, value):
        cells_ref[CYCLE_NODES[slot]] = value

    edge = edge_ref[...]
    edge_rows = edge.T
    gather_cycle(search, edge_rows, store)
    apply_operator(cells_ref, result_ref, first_ref, energy_ref, metric_ref, shift_ref)
    for index, node in enumerate(INNER_NODES):
        applied_ref[index] = result_ref[node]
    weighted = per_tile(penalty_ref) * search
    applied = weighted + scatter_cycle(
        lambda slot: result_ref[CYCLE_NODES[slot]], edge, edge_rows, left_ref, right_ref
    )
    write_skeleton(applied_ref, applied)
    for tile, value in enumerate(gather_slots(applied, shared_rows)):
        slots_ref[tile] = value
    sums_ref[0] = energy_ref[...] + skeleton_sum(weighted * search)
    sums_ref[1] = start


def second_kernel(
    packed_ref, search_ref, applied_ref, inverse_ref, sums_ref, a0, a1, a2, a3, a4, masks_ref, shared_ref,
    shared_columns_ref, edge_ref, metric_ref, penalty_ref, shift_ref, change_ref, message_ref,
    left_ref, right_ref, cells_ref, first_ref, energy_ref,
):
    arrived_refs = [a0, a1, a2, a3, a4]
    masks = masks_ref[...]

    def load(tile):
        return select_arrived(masks, tile, [ref[tile] for ref in arrived_refs])

    local = read_skeleton(applied_ref)
    search = read_skeleton(search_ref)
    full = local + scatter_slots(load, shared_columns_ref[...], shared_ref[...], left_ref, right_ref)
    change = full * read_skeleton(inverse_ref) - search
    write_skeleton(change_ref, change)
    clear_tail(change_ref)
    crossed = skeleton_sum(local * change)
    sourced = skeleton_sum(read_skeleton(packed_ref) * change)
    for index, node in enumerate(INNER_NODES):
        value = applied_ref[index]
        moved = value * inverse_ref[index] - search_ref[index]
        change_ref[index] = moved
        cells_ref[node] = moved
        crossed = crossed + value * moved
        sourced = sourced + packed_ref[index] * moved

    def store(slot, value):
        cells_ref[CYCLE_NODES[slot]] = value

    gather_cycle(change, edge_ref[...].T, store)
    apply_energy(cells_ref, first_ref, energy_ref, metric_ref, shift_ref)
    energy = energy_ref[...] + skeleton_sum(per_tile(penalty_ref) * change * change)
    sublanes = lax.broadcasted_iota(jnp.int32, (ROWS, LANES), 0)
    lanes = lax.broadcasted_iota(jnp.int32, (ROWS, LANES), 1)
    spread = jnp.zeros((ROWS, LANES), F32)
    for index, value in enumerate([sums_ref[0], crossed, energy, sums_ref[1], sourced]):
        column = jnp.sum(value, axis=1, keepdims=True)
        spread = jnp.where(lanes == sublanes + index * ROWS, column, spread)
    message = jnp.sum(spread, axis=0, keepdims=True)
    message_ref[...] = jnp.broadcast_to(message, message_ref.shape)


def combine_kernel(matrix_ref, scalars_ref, search_ref, change_ref, out_ref, block_ref):
    sublanes = lax.broadcasted_iota(jnp.int32, (ROWS, LANES), 0)
    lanes = lax.broadcasted_iota(jnp.int32, (ROWS, LANES), 1)
    for mode in range(MODES):
        total = jnp.sum(scalars_ref[mode], axis=0, keepdims=True)
        g00, g01, g11, h0, h1 = [
            jnp.sum(jnp.where(lanes == sublanes + index * ROWS, total, 0.0), axis=1, keepdims=True)
            for index in range(SCALARS)
        ]
        ratio = g01 / g00
        pivot = g11 - ratio * g01
        second = jnp.where(pivot > 0.0, (h1 - ratio * h0) / pivot, 0.0)
        first = h0 / g00 - ratio * second
        for index in range(BLOCK):
            block_ref[index, row_block(mode), :] = (
                first * search_ref[mode, index] + second * change_ref[mode, index]
            )
    matrix = matrix_ref[...]
    for index in range(BLOCK):
        mixed = jnp.dot(matrix, block_ref[index], precision=HIGHEST, preferred_element_type=F32)
        out_ref[:, index] = mixed.reshape(MODES, ROWS, LANES)


def unpack_kernel(packed_ref, edge_ref, out_ref):
    for index, node in enumerate(INNER_NODES):
        out_ref[:, node, :] = packed_ref[index]

    def store(slot, value):
        out_ref[:, CYCLE_NODES[slot], :] = value

    gather_cycle(read_skeleton(packed_ref), edge_ref[...].T, store)


def call(kernel, out_shapes, scratch, *operands):
    return pl.pallas_call(
        kernel,
        out_shape=out_shapes,
        scratch_shapes=scratch,
        compiler_params=pltpu.CompilerParams(vmem_limit_bytes=VMEM_LIMIT),
    )(*operands)


def shape(*dims):
    return jax.ShapeDtypeStruct(dims, F32)


def swap_blocks(packed):
    blocks = packed.reshape(MODES, BLOCK, ROWS, LANES)
    return lax.all_to_all(blocks, "mode", split_axis=0, concat_axis=0, tiled=True)


def exchange(slots):
    count = lax.axis_size("elem")
    return [
        lax.ppermute(slots, "elem", [(i, i ^ 1 << level) for i in range(count)])
        for level in range(count.bit_length() - 1)
    ]


def body(forcing, metric, edge_map, shared_rows, partner_masks, penalty):
    forward, backward = [jnp.asarray(table) for table in fourier_tables()]
    table, cross = [jnp.asarray(part) for part in diagonal_tables()]
    rows_global = lax.axis_index("mode") * ROWS + jnp.arange(ROWS, dtype=jnp.int32)
    shift = jnp.broadcast_to(helmholtz_shift(rows_global)[:, None], (ROWS, LANES))
    shared = shared_rows.reshape(SLOT_TILES, LANES)
    shared_columns = shared.T
    masks = partner_masks.reshape(SLOT_TILES, LANES)
    penalties = jnp.pad(penalty, (0, HIGH * LOW - SKEL), constant_values=1.0).reshape(HIGH, LOW)
    left = pltpu.VMEM((2 * HIGH * ROWS, CYCLE * LANES), BF16)
    right = pltpu.VMEM((CYCLE * LANES, LOW), BF16)
    left_slots = pltpu.VMEM((2 * HIGH * ROWS, SLOTS), BF16)
    right_slots = pltpu.VMEM((SLOTS, LOW), BF16)
    cells = pltpu.VMEM((NODES, ROWS, LANES), F32)
    first = pltpu.VMEM((NODES, 8, LANES), F32)
    energy = pltpu.VMEM((ROWS, LANES), F32)

    packed = call(pack_kernel, shape(PACKED, ROWS, LANES), [left, right], forcing, edge_map)
    gathered = swap_blocks(packed)
    inner, diagonal, extra = call(
        diagonal_kernel,
        [shape(2, INNER, LANES), shape(HIGH * ROWS, LOW), shape(SLOT_TILES, 8, LANES)],
        [pltpu.VMEM((2, NODES, LANES), F32), left, right],
        metric, table, cross, edge_map, penalties, shared,
    )
    mixed = call(transform_kernel, shape(MODES, BLOCK, ROWS, LANES), [], forward, gathered)
    source = swap_blocks(mixed).reshape(PACKED, ROWS, LANES)
    slots = call(slots_kernel, shape(SLOT_TILES, ROWS + 8, LANES), [], source, shared, extra)
    search, applied, inverse, slots, sums = call(
        first_kernel,
        [
            shape(PACKED, ROWS, LANES), shape(INNER + TILES, ROWS, LANES), shape(INNER + TILES, ROWS, LANES),
            shape(SLOT_TILES, ROWS, LANES), shape(2, ROWS, LANES),
        ],
        [left, right, cells, cells, first, energy],
        source, *exchange(slots), masks, shared, shared_columns, edge_map, metric, inner, diagonal, penalties, shift,
    )
    search_blocks = swap_blocks(search)
    change, message = call(
        second_kernel,
        [shape(PACKED, ROWS, LANES), shape(MODES * ELEMS_AXIS, LANES)],
        [left_slots, right_slots, cells, first, energy],
        source, search, applied, inverse, sums, *exchange(slots), masks, shared, shared_columns, edge_map, metric,
        penalties, shift,
    )
    change_blocks = swap_blocks(change)
    scalars = lax.all_to_all(message, ("mode", "elem"), split_axis=0, concat_axis=0, tiled=True)
    mixed = call(
        combine_kernel, shape(MODES, BLOCK, ROWS, LANES), [pltpu.VMEM((BLOCK, PLANES, LANES), F32)],
        backward, scalars.reshape(MODES, ELEMS_AXIS, LANES), search_blocks, change_blocks,
    )
    result = swap_blocks(mixed).reshape(PACKED, ROWS, LANES)
    return call(unpack_kernel, shape(ROWS, NODES, LANES), [], result, edge_map)


def solution(mesh):
    placed = (
        P("mode", None, "elem"),
        P(None, None, "elem"),
        P("elem", None),
        P("elem"),
        P("elem"),
        P("elem"),
    )
    return jax.shard_map(
        body, mesh=mesh, in_specs=placed, out_specs=P("mode", None, "elem"), check_vma=False
    )
```

time: 656 us -> 164 us (0.25); the launches traced: 648 us -> 163 us
  other arithmetic: 115 us -> 0.01 us
  blocking collectives: 197 us -> 90 us
  waiting for transfers between devices: 110 us -> 9.16 us
  local copies, waits for them, and re-layouts: 107 us -> 9.83 us
  starting transfers between devices: 101 us -> 22.8 us
  Pallas kernels: 0 us -> 31 us
  matrix products: 15.4 us -> 0 us
    psum x3 -> x0, blocking collectives: 179 us -> none  [the longest x2 120 us: precond_sum(): return lax.psum(local_product(residual, precond), 'elem')]
    scatter-add x8 -> x0, other arithmetic: 106 us -> none  [the longest x4 92.1 us: scatter_cycle(): return jnp.zeros((cycle_values.shape[0], skeleton_count), jnp.float32).at...]
    ppermute x20 -> x10, waiting for transfers between devices: 90.5 us -> 3.76 us  [exchange(): lax.ppermute(slots, 'elem', [(i, i ^ 1 << level) for i in range(count)])]
    all_to_all x1 -> x5, blocking collectives: 18.4 us -> 90 us  [the longest x4 61.7 us: swap_blocks(): lax.all_to_all(blocks, 'mode', split_axis=0, concat_axis=0, tiled=True)]
    all_to_all x3 -> x1, starting transfers between devices: 62.4 us -> 4.32 us  [swap_blocks(): lax.all_to_all(blocks, 'mode', split_axis=0, concat_axis=0, tiled=True)]
    gather x11 -> x0, local copies, waits for them, and re-layouts: 54.4 us -> none  [the longest x4 32.8 us: body(): operate_values_grid = element_of(search[0], operate_skeleton[:, node_map])]
    pallas_call x0 -> x8, Pallas kernels: none -> 31 us  [call(): pl.pallas_call(kernel, out_shape=out_shapes, scratch_shapes=scratch, comp...]
    ppermute x20 -> x10, starting transfers between devices: 38.5 us -> 18.5 us  [exchange(): lax.ppermute(slots, 'elem', [(i, i ^ 1 << level) for i in range(count)])]
  transfers between devices with their start and end apart: 23 -> 11, of which waited for: 19 -> 3; matrix products, arithmetic and copies ran while one was open for 13% -> 1% of each run, Pallas kernels for 0% -> 2%
where the time goes in v1:
time: 164 us; the launch traced here: 163 us
  blocking collectives  90 us (55%)
  Pallas kernels  31 us (19%)
  starting transfers between devices  22.8 us (14%)
  local copies, waits for them, and re-layouts  9.83 us (6%)
  waiting for transfers between devices  9.16 us (6%)
    all_to_all x4, blocking collectives, swap_blocks(): lax.all_to_all(blocks, 'mode', split_axis=0, concat_axis=0, tiled=True)  61.7 us
    pallas_call x8, Pallas kernels, call(): pl.pallas_call(kernel, out_shape=out_shapes, scratch_shapes=scratch, comp...  31 us
    all_to_all x1, blocking collectives, body(): lax.all_to_all(message, ('mode', 'elem'), split_axis=0, concat_axis=0, ti...  28.3 us
    ppermute x10, starting transfers between devices, exchange(): lax.ppermute(slots, 'elem', [(i, i ^ 1 << level) for i in range(count)])  18.5 us
    unnamed x35, local copies, waits for them, and re-layouts  5.76 us
    all_to_all x1, waiting for transfers between devices, swap_blocks(): lax.all_to_all(blocks, 'mode', split_axis=0, concat_axis=0, tiled=True)  5.4 us
    all_to_all x1, starting transfers between devices, swap_blocks(): lax.all_to_all(blocks, 'mode', split_axis=0, concat_axis=0, tiled=True)  4.32 us
    ppermute x10, waiting for transfers between devices, exchange(): lax.ppermute(slots, 'elem', [(i, i ^ 1 << level) for i in range(count)])  3.76 us
  transfers between devices with their start and end apart: 11, of which 3 were waited for; matrix products, arithmetic and copies ran while one was open for 1% of the time, Pallas kernels for 2%

profile of v1, /device:TPU:1, one launch (start us, length us, event | category | flops | bytes accessed | tf_op | source)
XLA Modules:
  0.0 163.0 jit_solution(7098906097400739173)
XLA Ops:
  1.4 2.2 %copy.36.forcing_ref = f32[16,81,128]{2,1,0:T(8,128)} copy(f32[16,81,128]{2,0,1:T(8,128)} %param.10) | data formatting | bytes 1327104 | tf_op args[0]
  3.6 4.0 %shard_map.100 = f32[72,16,128]{2,1,0:T(8,128)} custom-call(f32[16,81,128]{2,1,0:T(8,128)} %copy.36.forcing_ref, s32[128,32]{1,0:T(8,128)} %copy.37.edge_ref), custom_call_target="tpu_custom_call" | custom-call | tf_op jit(solution)/shard_map/pallas_call | solution.py:513
  7.6 17.8 %all_to_all.34.in_ref = f32[8,9,16,128]{3,2,1,0:T(8,128)} all-to-all(f32[8,9,16,128]{3,2,1,0:T(8,128)} %bitcast.17), channel_id=1, replica_groups=mesh['mode'=8,'elem'=32] {'mode'}, dimensions={0} | all-to-all | bytes 1179648 | tf_op jit(solution)/shard_map/all_to_all | solution.py:527
  25.3 2.5 %shard_map.101 = f32[8,9,16,128]{3,2,1,0:T(8,128)} custom-call(f32[128,128]{1,0:T(8,128)} %constant.37.clone.matrix_ref, f32[8,9,16,128]{3,2,1,0:T(8,128)} %all_to_all.34.in_ref), custom_call_target="tpu_custom_call" | custom-call | tf_op jit(solution)/shard_map/pallas_call | solution.py:513
  27.9 4.3 %all-to-all-start.1 = ((f32[8,9,16,128]{3,2,1,0:T(8,128)}), f32[8,9,16,128]{3,2,1,0:T(8,128)S(1)}, u32[]{:S(2)}, u32[]{:S(2)}) async-start(f32[8,9,16,128]{3,2,1,0:T(8,128)} %shard_map.101), calls=%async_computation.1 | async-start | bytes 1179648 | tf_op jit(solution)/shard_map/all_to_all | solution.py:527
  33.5 3.5 %shard_map.102 = (f32[2,49,128]{2,1,0:T(8,128)}, f32[144,256]{1,0:T(8,128)}, f32[3,8,128]{2,1,0:T(8,128)}) custom-call(f32[4,81,128]{2,1,0:T(8,128)} %copy.38.metric_ref, f32[81,162]{1,0:T(8,128)} %constant.39.clone.table_ref, f32[81,128]{1,0:T(8,128)} %constant.40.clone.cross_ref, s32[128,32]{1,0:T(8,128)} %copy.37.edge_ref, f32[9,256]{1,0:T(8,128)} %reshape.57.penalty_ref, ...), custom_call_target="tpu_custom_call" | custom-call | tf_op jit(solution)/shard_map/pallas_call | solution.py:513
  37.0 5.4 %all-to-all-done.1 = f32[8,9,16,128]{3,2,1,0:T(8,128)S(1)} async-done(((f32[8,9,16,128]{3,2,1,0:T(8,128)}), f32[8,9,16,128]{3,2,1,0:T(8,128)S(1)}, u32[]{:S(2)}, u32[]{:S(2)}) %all-to-all-start.1) | async-done | bytes 589856 | tf_op jit(solution)/shard_map/all_to_all | solution.py:527
  43.2 2.0 %shard_map.103 = f32[3,24,128]{2,1,0:T(8,128)} custom-call(f32[72,16,128]{2,1,0:T(8,128)} %bitcast.12, s32[3,128]{1,0:T(4,128)} %bitcast.24, f32[3,8,128]{2,1,0:T(8,128)} %get-tuple-element.15.extra_ref), custom_call_target="tpu_custom_call" | custom-call | tf_op jit(solution)/shard_map/pallas_call | solution.py:513
  45.2 2.4 %collective-permute-start.1 = (f32[3,24,128]{2,1,0:T(8,128)}, f32[3,24,128]{2,1,0:T(8,128)S(1)}, u32[]{:S(2)}, u32[]{:S(2)}) collective-permute-start(f32[3,24,128]{2,1,0:T(8,128)} %shard_map.103), channel_id=1, source_target_pairs={{0,2},{1,3},{2,0},{3,1},{4,6},{5,7},{6,4},{7,5},{8,10},{9,11},{10,... | collective-permute-start | bytes 110600 | tf_op jit(solution)/shard_map/ppermute | solution.py:533
  47.6 1.6 %collective-permute-start.2 = (f32[3,24,128]{2,1,0:T(8,128)}, f32[3,24,128]{2,1,0:T(8,128)S(1)}, u32[]{:S(2)}, u32[]{:S(2)}) collective-permute-start(f32[3,24,128]{2,1,0:T(8,128)} %shard_map.103), channel_id=1, source_target_pairs={{0,4},{1,5},{2,6},{3,7},{4,0},{5,1},{6,2},{7,3},{8,12},{9,13},{10,... | collective-permute-start | bytes 110600 | tf_op jit(solution)/shard_map/ppermute | solution.py:533
  49.3 3.0 %collective-permute-start.3 = (f32[3,24,128]{2,1,0:T(8,128)}, f32[3,24,128]{2,1,0:T(8,128)S(1)}, u32[]{:S(2)}, u32[]{:S(2)}) collective-permute-start(f32[3,24,128]{2,1,0:T(8,128)} %shard_map.103), channel_id=1, source_target_pairs={{0,8},{1,9},{2,10},{3,11},{4,12},{5,13},{6,14},{7,15},{8,0},{9,1},... | collective-permute-start | bytes 110600 | tf_op jit(solution)/shard_map/ppermute | solution.py:533
  52.3 4.2 %collective-permute-start.4 = (f32[3,24,128]{2,1,0:T(8,128)}, f32[3,24,128]{2,1,0:T(8,128)S(1)}, u32[]{:S(2)}, u32[]{:S(2)}) collective-permute-start(f32[3,24,128]{2,1,0:T(8,128)} %shard_map.103), channel_id=1, source_target_pairs={{0,16},{1,17},{2,18},{3,19},{4,20},{5,21},{6,22},{7,23},{8,24},{9,... | collective-permute-start | bytes 110600 | tf_op jit(solution)/shard_map/ppermute | solution.py:533
  57.3 1.9 %collective-permute-done.4.a4 = f32[3,24,128]{2,1,0:T(8,128)S(1)} collective-permute-done((f32[3,24,128]{2,1,0:T(8,128)}, f32[3,24,128]{2,1,0:T(8,128)S(1)}, u32[]{:S(2)}, u32[]{:S(2)}) %collective-permute-start.4) | collective-permute-done | bytes 36896 | tf_op jit(solution)/shard_map/ppermute | solution.py:533
  59.9 7.6 %shard_map.104 = (f32[72,16,128]{2,1,0:T(8,128)}, f32[67,16,128]{2,1,0:T(8,128)}, f32[67,16,128]{2,1,0:T(8,128)}, f32[3,16,128]{2,1,0:T(8,128)}, f32[2,16,128]{2,1,0:T(8,128)}) custom-call(f32[72,16,128]{2,1,0:T(8,128)} %bitcast.13, f32[3,24,128]{2,1,0:T(8,128)} %copy-done.5, f32[3,24,128]{2,1,0:T(8,128)} %copy-done.6, f32[3,24,128]{2,1,0:T(8,128)} %copy-done.7, ...), custom_call_target="tpu_custom_call" | custom-call | tf_op jit(solution)/shard_map/pallas_call | solution.py:513
  69.8 4.9 %collective-permute-start.9 = (f32[3,16,128]{2,1,0:T(8,128)}, f32[3,16,128]{2,1,0:T(8,128)S(1)}, u32[]{:S(2)}, u32[]{:S(2)}) collective-permute-start(f32[3,16,128]{2,1,0:T(8,128)} %get-tuple-element.22), channel_id=1, source_target_pairs={{0,16},{1,17},{2,18},{3,19},{4,20},{5,21},{6,22},{7,23},{8,24},{9,... | collective-permute-start | bytes 73736 | tf_op jit(solution)/shard_map/ppermute | solution.py:533
  74.8 1.8 %collective-permute-done.9.a4 = f32[3,16,128]{2,1,0:T(8,128)S(1)} collective-permute-done((f32[3,16,128]{2,1,0:T(8,128)}, f32[3,16,128]{2,1,0:T(8,128)S(1)}, u32[]{:S(2)}, u32[]{:S(2)}) %collective-permute-start.9) | collective-permute-done | bytes 24608 | tf_op jit(solution)/shard_map/ppermute | solution.py:533
  77.2 5.1 %shard_map.105 = (f32[72,16,128]{2,1,0:T(8,128)}, f32[256,128]{1,0:T(8,128)}) custom-call(f32[72,16,128]{2,1,0:T(8,128)} %bitcast.14, f32[72,16,128]{2,1,0:T(8,128)} %get-tuple-element.18.search_ref, f32[67,16,128]{2,1,0:T(8,128)} %get-tuple-element.19.applied_ref, f32[67,16,128]{2,1,0:T(8,128)} %get-tuple-element.20.inverse_ref, ...), custom_call_target="tpu_custom_call" | custom-call | tf_op jit(solution)/shard_map/pallas_call | solution.py:513
  82.3 28.3 %all_to_all.35 = f32[256,1,128]{2,1,0:T(1,128)} all-to-all(f32[256,1,128]{2,1,0:T(1,128)} %bitcast.22), channel_id=1, replica_groups=mesh['mode'=8,'elem'=32] {'mode','elem'}, dimensions={0} | all-to-all | bytes 262144 | tf_op jit(solution)/shard_map/all_to_all | solution.py:584
  110.6 14.5 %all_to_all.36.search_ref = f32[8,9,16,128]{3,2,1,0:T(8,128)} all-to-all(f32[8,9,16,128]{3,2,1,0:T(8,128)S(1)} %bitcast.15), channel_id=1, replica_groups=mesh['mode'=8,'elem'=32] {'mode'}, dimensions={0} | all-to-all | bytes 1179648 | tf_op jit(solution)/shard_map/all_to_all | solution.py:527
  125.1 14.2 %all_to_all.37.change_ref = f32[8,9,16,128]{3,2,1,0:T(8,128)} all-to-all(f32[8,9,16,128]{3,2,1,0:T(8,128)S(1)} %bitcast.20), channel_id=1, replica_groups=mesh['mode'=8,'elem'=32] {'mode'}, dimensions={0} | all-to-all | bytes 1179648 | tf_op jit(solution)/shard_map/all_to_all | solution.py:527
  139.3 3.0 %shard_map.106 = f32[8,9,16,128]{3,2,1,0:T(8,128)} custom-call(f32[128,128]{1,0:T(8,128)} %constant.38.clone.matrix_ref, f32[8,32,128]{2,1,0:T(8,128)} %bitcast.21, f32[8,9,16,128]{3,2,1,0:T(8,128)} %all_to_all.36.search_ref, f32[8,9,16,128]{3,2,1,0:T(8,128)} %all_to_all.37.change_ref), custom_call_target="tpu_custom_call" | custom-call | tf_op jit(solution)/shard_map/pallas_call | solution.py:513
  142.3 15.3 %all_to_all.38 = f32[8,9,16,128]{3,2,1,0:T(8,128)} all-to-all(f32[8,9,16,128]{3,2,1,0:T(8,128)} %shard_map.106), channel_id=1, replica_groups=mesh['mode'=8,'elem'=32] {'mode'}, dimensions={0} | all-to-all | bytes 1179648 | tf_op jit(solution)/shard_map/all_to_all | solution.py:527
  157.5 3.4 %shard_map.107 = f32[16,81,128]{2,1,0:T(8,128)} custom-call(f32[72,16,128]{2,1,0:T(8,128)} %bitcast.16, s32[128,32]{1,0:T(8,128)} %copy.37.edge_ref), custom_call_target="tpu_custom_call" | custom-call | tf_op jit(solution)/shard_map/pallas_call | solution.py:513
  160.9 2.1 %copy.47 = f32[16,81,128]{2,0,1:T(8,128)} copy(f32[16,81,128]{2,1,0:T(8,128)} %shard_map.107) | data formatting | bytes 1327104 | tf_op jit(solution)/shard_map/pallas_call | solution.py:513
  (52 shorter events, 8.0 us)
Async XLA Ops:
  27.9 4.3 %copy-start.3 = (f32[4,81,128]{2,0,1:T(4,128)S(1)}, f32[4,81,128]{2,0,1:T(4,128)}, u32[]{:S(2)}) copy-start(f32[4,81,128]{2,0,1:T(4,128)} %param.11) | copy-start | bytes 497668
  27.9 14.5 %all-to-all-start.1 = ((f32[8,9,16,128]{3,2,1,0:T(8,128)}), f32[8,9,16,128]{3,2,1,0:T(8,128)S(1)}, u32[]{:S(2)}, u32[]{:S(2)}) async-start(f32[8,9,16,128]{3,2,1,0:T(8,128)} %shard_map.101), calls=%async_computation.1 | async-start | bytes 1179648 | tf_op jit(solution)/shard_map/all_to_all | solution.py:527
  42.4 0.8 copy-start
  43.2 13.3 %copy-start.4 = (s32[384]{0:T(512)S(1)}, s32[384]{0:T(512)}, u32[]{:S(2)}) copy-start(s32[384]{0:T(512)} %param.13) | copy-start | bytes 4612
  45.2 12.0 %collective-permute-start = (f32[3,24,128]{2,1,0:T(8,128)}, f32[3,24,128]{2,1,0:T(8,128)S(1)}, u32[]{:S(2)}, u32[]{:S(2)}) collective-permute-start(f32[3,24,128]{2,1,0:T(8,128)} %shard_map.103), channel_id=1, source_target_pairs={{0,1},{1,0},{2,3},{3,2},{4,5},{5,4},{6,7},{7,6},{8,9},{9,8},{10,11... | collective-permute-start | bytes 110600 | tf_op jit(solution)/shard_map/ppermute | solution.py:533
  45.2 12.0 %collective-permute-start.1 = (f32[3,24,128]{2,1,0:T(8,128)}, f32[3,24,128]{2,1,0:T(8,128)S(1)}, u32[]{:S(2)}, u32[]{:S(2)}) collective-permute-start(f32[3,24,128]{2,1,0:T(8,128)} %shard_map.103), channel_id=1, source_target_pairs={{0,2},{1,3},{2,0},{3,1},{4,6},{5,7},{6,4},{7,5},{8,10},{9,11},{10,... | collective-permute-start | bytes 110600 | tf_op jit(solution)/shard_map/ppermute | solution.py:533
  47.6 9.6 %collective-permute-start.2 = (f32[3,24,128]{2,1,0:T(8,128)}, f32[3,24,128]{2,1,0:T(8,128)S(1)}, u32[]{:S(2)}, u32[]{:S(2)}) collective-permute-start(f32[3,24,128]{2,1,0:T(8,128)} %shard_map.103), channel_id=1, source_target_pairs={{0,4},{1,5},{2,6},{3,7},{4,0},{5,1},{6,2},{7,3},{8,12},{9,13},{10,... | collective-permute-start | bytes 110600 | tf_op jit(solution)/shard_map/ppermute | solution.py:533
  49.3 8.0 %collective-permute-start.3 = (f32[3,24,128]{2,1,0:T(8,128)}, f32[3,24,128]{2,1,0:T(8,128)S(1)}, u32[]{:S(2)}, u32[]{:S(2)}) collective-permute-start(f32[3,24,128]{2,1,0:T(8,128)} %shard_map.103), channel_id=1, source_target_pairs={{0,8},{1,9},{2,10},{3,11},{4,12},{5,13},{6,14},{7,15},{8,0},{9,1},... | collective-permute-start | bytes 110600 | tf_op jit(solution)/shard_map/ppermute | solution.py:533
  52.3 7.0 %collective-permute-start.4 = (f32[3,24,128]{2,1,0:T(8,128)}, f32[3,24,128]{2,1,0:T(8,128)S(1)}, u32[]{:S(2)}, u32[]{:S(2)}) collective-permute-start(f32[3,24,128]{2,1,0:T(8,128)} %shard_map.103), channel_id=1, source_target_pairs={{0,16},{1,17},{2,18},{3,19},{4,20},{5,21},{6,22},{7,23},{8,24},{9,... | collective-permute-start | bytes 110600 | tf_op jit(solution)/shard_map/ppermute | solution.py:533
  57.2 2.6 %copy-start.5 = (f32[3,24,128]{2,1,0:T(8,128)}, f32[3,24,128]{2,1,0:T(8,128)S(1)}, u32[]{:S(2)}) copy-start(f32[3,24,128]{2,1,0:T(8,128)S(1)} %collective-permute-done.a0) | copy-start | bytes 110596
  57.2 2.6 %copy-start.6 = (f32[3,24,128]{2,1,0:T(8,128)}, f32[3,24,128]{2,1,0:T(8,128)S(1)}, u32[]{:S(2)}) copy-start(f32[3,24,128]{2,1,0:T(8,128)S(1)} %collective-permute-done.1.a1) | copy-start | bytes 110596
  57.3 2.6 %copy-start.7 = (f32[3,24,128]{2,1,0:T(8,128)}, f32[3,24,128]{2,1,0:T(8,128)S(1)}, u32[]{:S(2)}) copy-start(f32[3,24,128]{2,1,0:T(8,128)S(1)} %collective-permute-done.2.a2) | copy-start | bytes 110596
  57.3 2.6 %copy-start.8 = (f32[3,24,128]{2,1,0:T(8,128)}, f32[3,24,128]{2,1,0:T(8,128)S(1)}, u32[]{:S(2)}) copy-start(f32[3,24,128]{2,1,0:T(8,128)S(1)} %collective-permute-done.3.a3) | copy-start | bytes 110596
  67.5 7.3 %collective-permute-start.5 = (f32[3,16,128]{2,1,0:T(8,128)}, f32[3,16,128]{2,1,0:T(8,128)S(1)}, u32[]{:S(2)}, u32[]{:S(2)}) collective-permute-start(f32[3,16,128]{2,1,0:T(8,128)} %get-tuple-element.22), channel_id=1, source_target_pairs={{0,1},{1,0},{2,3},{3,2},{4,5},{5,4},{6,7},{7,6},{8,9},{9,8},{10,11... | collective-permute-start | bytes 73736 | tf_op jit(solution)/shard_map/ppermute | solution.py:533
  67.5 7.3 %collective-permute-start.6 = (f32[3,16,128]{2,1,0:T(8,128)}, f32[3,16,128]{2,1,0:T(8,128)S(1)}, u32[]{:S(2)}, u32[]{:S(2)}) collective-permute-start(f32[3,16,128]{2,1,0:T(8,128)} %get-tuple-element.22), channel_id=1, source_target_pairs={{0,2},{1,3},{2,0},{3,1},{4,6},{5,7},{6,4},{7,5},{8,10},{9,11},{10,... | collective-permute-start | bytes 73736 | tf_op jit(solution)/shard_map/ppermute | solution.py:533
  68.6 6.2 %collective-permute-start.7 = (f32[3,16,128]{2,1,0:T(8,128)}, f32[3,16,128]{2,1,0:T(8,128)S(1)}, u32[]{:S(2)}, u32[]{:S(2)}) collective-permute-start(f32[3,16,128]{2,1,0:T(8,128)} %get-tuple-element.22), channel_id=1, source_target_pairs={{0,4},{1,5},{2,6},{3,7},{4,0},{5,1},{6,2},{7,3},{8,12},{9,13},{10,... | collective-permute-start | bytes 73736 | tf_op jit(solution)/shard_map/ppermute | solution.py:533
  69.6 5.1 %collective-permute-start.8 = (f32[3,16,128]{2,1,0:T(8,128)}, f32[3,16,128]{2,1,0:T(8,128)S(1)}, u32[]{:S(2)}, u32[]{:S(2)}) collective-permute-start(f32[3,16,128]{2,1,0:T(8,128)} %get-tuple-element.22), channel_id=1, source_target_pairs={{0,8},{1,9},{2,10},{3,11},{4,12},{5,13},{6,14},{7,15},{8,0},{9,1},... | collective-permute-start | bytes 73736 | tf_op jit(solution)/shard_map/ppermute | solution.py:533
  69.8 6.8 %collective-permute-start.9 = (f32[3,16,128]{2,1,0:T(8,128)}, f32[3,16,128]{2,1,0:T(8,128)S(1)}, u32[]{:S(2)}, u32[]{:S(2)}) collective-permute-start(f32[3,16,128]{2,1,0:T(8,128)} %get-tuple-element.22), channel_id=1, source_target_pairs={{0,16},{1,17},{2,18},{3,19},{4,20},{5,21},{6,22},{7,23},{8,24},{9,... | collective-permute-start | bytes 73736 | tf_op jit(solution)/shard_map/ppermute | solution.py:533
  74.7 1.9 %copy-start.10 = (f32[3,16,128]{2,1,0:T(8,128)}, f32[3,16,128]{2,1,0:T(8,128)S(1)}, u32[]{:S(2)}) copy-start(f32[3,16,128]{2,1,0:T(8,128)S(1)} %collective-permute-done.5.a0) | copy-start | bytes 73732
  74.7 1.9 %copy-start.11 = (f32[3,16,128]{2,1,0:T(8,128)}, f32[3,16,128]{2,1,0:T(8,128)S(1)}, u32[]{:S(2)}) copy-start(f32[3,16,128]{2,1,0:T(8,128)S(1)} %collective-permute-done.6.a1) | copy-start | bytes 73732
  74.8 1.9 %copy-start.12 = (f32[3,16,128]{2,1,0:T(8,128)}, f32[3,16,128]{2,1,0:T(8,128)S(1)}, u32[]{:S(2)}) copy-start(f32[3,16,128]{2,1,0:T(8,128)S(1)} %collective-permute-done.7.a2) | copy-start | bytes 73732
  74.8 1.8 %copy-start.13 = (f32[3,16,128]{2,1,0:T(8,128)}, f32[3,16,128]{2,1,0:T(8,128)S(1)}, u32[]{:S(2)}) copy-start(f32[3,16,128]{2,1,0:T(8,128)S(1)} %collective-permute-done.8.a3) | copy-start | bytes 73732
  77.2 33.4 %copy-start.1 = (f32[72,16,128]{2,1,0:T(8,128)S(1)}, f32[72,16,128]{2,1,0:T(8,128)}, u32[]{:S(2)}) copy-start(f32[72,16,128]{2,1,0:T(8,128)} %get-tuple-element.18.search_ref) | copy-start | bytes 1769476
  110.6 14.5 %copy-start.2 = (f32[72,16,128]{2,1,0:T(8,128)S(1)}, f32[72,16,128]{2,1,0:T(8,128)}, u32[]{:S(2)}) copy-start(f32[72,16,128]{2,1,0:T(8,128)} %get-tuple-element.24) | copy-start | bytes 1769476
  (3 other events, 2.0 us)

commit v2 on v1

v2 whole, which is shorter than its diff:
```python
import math

import jax
import jax.numpy as jnp
import numpy as np
from jax import lax
from jax.experimental import pallas as pl
from jax.experimental.pallas import tpu as pltpu
from jax.sharding import PartitionSpec as P

ORDER = 8
SIDE = ORDER + 1
NODES = SIDE * SIDE
CYCLE = 32
INNER = (ORDER - 1) ** 2
ROWS = 16
LANES = 128
PLANES = 128
MODES = 8
ELEMS_AXIS = 32
SKEL = 2113
LOW = 256
HIGH = 9
TILES = 2 * HIGH
SLOTS = 384
SLOT_TILES = SLOTS // LANES
BLOCK = 9
SHARE = BLOCK + SLOT_TILES
GROUP = 7
TAIL = 4
SCALARS = 5
SPACING = 0.25
F32 = jnp.float32
BF16 = jnp.bfloat16
HIGHEST = lax.Precision.HIGHEST
VMEM_LIMIT = 32 * 1024 * 1024


def legendre_table(points, poly_order):
    table = np.zeros((points.shape[0], poly_order + 1))
    table[:, 0] = 1.0
    table[:, 1] = points
    for degree in range(2, poly_order + 1):
        table[:, degree] = (
            (2 * degree - 1) * points * table[:, degree - 1] - (degree - 1) * table[:, degree - 2]
        ) / degree
    return table


def lobatto_derivative(poly_order):
    node_count = poly_order + 1
    points = np.cos(np.pi * np.arange(node_count) / poly_order)
    for newton_step in range(100):
        table = legendre_table(points, poly_order)
        points = points - (points * table[:, poly_order] - table[:, poly_order - 1]) / (
            node_count * table[:, poly_order]
        )
    points = np.sort(points)
    top_values = legendre_table(points, poly_order)[:, poly_order]
    identity = np.eye(node_count)
    differ = points[:, None] - points[None, :] + identity
    matrix = top_values[:, None] / (top_values[None, :] * differ)
    matrix = matrix * (1.0 - identity)
    matrix[0, 0] = -poly_order * node_count / 4.0
    matrix[poly_order, poly_order] = poly_order * node_count / 4.0
    return matrix


def fourier_tables():
    positions = np.arange(PLANES)
    phases = ((positions // 2)[:, None] * positions[None, :] % PLANES) * (2.0 * np.pi / PLANES)
    cosine, sine = np.cos(phases), np.sin(phases)
    even = (positions % 2 == 0)[:, None]
    nyquist = (positions == 1)[:, None]
    alternate = (1.0 - 2.0 * (positions % 2))[None, :]
    forward = np.where(nyquist, alternate, np.where(even, cosine, -sine)) / PLANES
    backward = np.where(nyquist, alternate, np.where(even, 2.0 * cosine, -2.0 * sine))
    backward = np.where((positions == 0)[:, None], 1.0, backward)
    return forward.astype(np.float32), backward.T.astype(np.float32)


DERIVATIVE = lobatto_derivative(ORDER).astype(np.float32)
CYCLE_NODES = (
    [i * SIDE for i in range(SIDE)]
    + [i * SIDE + ORDER for i in range(SIDE)]
    + [j for j in range(1, ORDER)]
    + [ORDER * SIDE + j for j in range(1, ORDER)]
)
INNER_NODES = [i * SIDE + j for i in range(1, ORDER) for j in range(1, ORDER)]


def diagonal_tables():
    squared = (DERIVATIVE * DERIVATIVE).astype(np.float64)
    first = np.kron(squared.T, np.eye(SIDE))
    second = np.kron(np.eye(SIDE), squared.T)
    corner = np.diagonal(DERIVATIVE)
    cross = 2.0 * np.outer(corner, corner).reshape(NODES, 1)
    cross = np.broadcast_to(cross, (NODES, LANES))
    return np.concatenate([first, second], axis=1).astype(np.float32), cross.astype(np.float32)


def helmholtz_shift(rows_global):
    wavenumber = (rows_global // 2).astype(F32)
    spanwise = wavenumber * (2.0 * math.pi / (PLANES * SPACING))
    spanwise = jnp.where(rows_global == 1, math.pi / SPACING, spanwise)
    return spanwise * spanwise


def row_block(index):
    return slice(index * ROWS, (index + 1) * ROWS)


def lane_block(index):
    return slice(index * LANES, (index + 1) * LANES)


def pieces(value):
    top = value.astype(BF16).astype(F32)
    return top, value - top


def one_hot_columns(low_columns):
    lanes = lax.broadcasted_iota(jnp.int32, (low_columns.shape[0], LOW), 1)
    return jnp.where(low_columns == lanes, 1.0, 0.0).astype(BF16)


def one_hot_rows(low_rows):
    sublanes = lax.broadcasted_iota(jnp.int32, (LOW, low_rows.shape[1]), 0)
    return jnp.where(low_rows == sublanes, 1.0, 0.0).astype(BF16)


def masked_store(value, high_row, left_ref, column):
    top, rest = pieces(value)
    for high in range(HIGH):
        here = high_row == high
        left_ref[row_block(high), lane_block(column)] = jnp.where(here, top, 0.0).astype(BF16)
        left_ref[row_block(HIGH + high), lane_block(column)] = jnp.where(here, rest, 0.0).astype(BF16)


def scatter_sum(left, right):
    both = jnp.dot(left, right, preferred_element_type=F32)
    return both[: HIGH * ROWS] + both[HIGH * ROWS :]


def scatter_cycle(load, edge_rows, left_ref, right_ref):
    low = jnp.bitwise_and(edge_rows.T, LOW - 1)
    high_rows = jnp.right_shift(edge_rows, 8)
    for slot in range(CYCLE):
        right_ref[lane_block(slot), :] = one_hot_columns(low[:, slot : slot + 1])
        masked_store(load(slot), high_rows[slot : slot + 1, :], left_ref, slot)
    return scatter_sum(left_ref[...], right_ref[...])


def scatter_slots(load, shared_rows, left_ref, right):
    high_rows = jnp.right_shift(shared_rows, 8)
    for tile in range(SLOT_TILES):
        masked_store(load(tile), high_rows[tile : tile + 1, :], left_ref, tile)
    return scatter_sum(left_ref[:, :SLOTS], right)


def stack_pieces(skeleton):
    top, rest = pieces(skeleton)
    return jnp.concatenate([top.astype(BF16), rest.astype(BF16)], axis=0)


def gather_tile(stacked, rows):
    low = jnp.bitwise_and(rows, LOW - 1)
    high = jnp.right_shift(rows, 8)
    found = jnp.dot(stacked, one_hot_rows(low), preferred_element_type=F32)
    total = None
    for index in range(HIGH):
        part = found[row_block(index), :] + found[row_block(HIGH + index), :]
        part = jnp.where(high == index, part, 0.0)
        total = part if total is None else total + part
    return total


def gather_cycle(skeleton, edge_rows, store):
    stacked = stack_pieces(skeleton)
    for pair in range(CYCLE // 2):
        rows = jnp.concatenate(
            [edge_rows[2 * pair : 2 * pair + 1, :], edge_rows[2 * pair + 1 : 2 * pair + 2, :]], axis=1
        )
        total = gather_tile(stacked, rows)
        store(2 * pair, total[:, :LANES])
        store(2 * pair + 1, total[:, LANES:])


def gather_slots(skeleton, shared_rows):
    stacked = stack_pieces(skeleton)
    return [gather_tile(stacked, shared_rows[tile : tile + 1, :]) for tile in range(SLOT_TILES)]


def sent_place(index):
    return index // BLOCK, index % BLOCK


def tail_place(index):
    return min(index // 2, MODES - 1), index - 2 * min(index // 2, MODES - 1)


def result_place(index):
    block, row = tail_place(index)
    return block, row + GROUP if row < 2 else row - 2


def read_skeleton(load):
    return jnp.concatenate(
        [jnp.concatenate([load(2 * high), load(2 * high + 1)], axis=1) for high in range(HIGH)], axis=0
    )


def write_skeleton(skeleton, store):
    for high in range(HIGH):
        store(2 * high, skeleton[row_block(high), :LANES])
        store(2 * high + 1, skeleton[row_block(high), LANES:])


def write_place(ref, place):
    def store(index, value):
        block, row = place(index)
        ref[block, row] = value

    return store


def fold(value):
    return value[:, :LANES] + value[:, LANES:]


def per_tile(penalty_ref):
    return jnp.concatenate(
        [jnp.broadcast_to(penalty_ref[high : high + 1, :], (ROWS, LOW)) for high in range(HIGH)], axis=0
    )


def skeleton_sum(product):
    total = None
    for high in range(HIGH):
        part = fold(product[row_block(high), :])
        total = part if total is None else total + part
    return total


def select_arrived(masks, tile, arrived):
    chosen = arrived[0]
    row = masks[tile : tile + 1, :]
    for level in range(1, len(arrived)):
        moving = jnp.bitwise_and(jnp.right_shift(row, level), 1) == 1
        chosen = jnp.where(moving, arrived[level], chosen)
    return chosen


def derivative_line(values, transposed):
    results = []
    for out in range(SIDE):
        total = None
        for k in range(SIDE):
            weight = float(DERIVATIVE[k, out] if transposed else DERIVATIVE[out, k])
            if weight == 0.0:
                continue
            part = weight * values[k]
            total = part if total is None else total + part
        results.append(total)
    return results


def gradients(cells_ref, first_ref, metric_ref, rows, visit):
    for j in range(SIDE):
        line = derivative_line([cells_ref[k * SIDE + j, rows, :] for k in range(SIDE)], False)
        for i in range(SIDE):
            first_ref[i * SIDE + j] = line[i]
    for i in range(SIDE):
        line = derivative_line([cells_ref[i * SIDE + k, rows, :] for k in range(SIDE)], False)
        seconds = []
        for j in range(SIDE):
            node = i * SIDE + j
            m0, m1, m2 = [metric_ref[c, node : node + 1, :] for c in range(3)]
            g1, g2 = first_ref[node], line[j]
            p1 = m0 * g1 + m2 * g2
            p2 = m2 * g1 + m1 * g2
            visit(node, g1, g2, p1, p2)
            seconds.append(p2)
        yield i, seconds


def apply_operator(cells_ref, result_ref, first_ref, energy_ref, metric_ref, shift_ref):
    @pl.loop(0, 2)
    def half(part):
        rows = pl.ds(pl.multiple_of(part * 8, 8), 8)
        shift = shift_ref[rows, :]

        def visit(node, g1, g2, p1, p2):
            first_ref[node] = p1

        for i, seconds in gradients(cells_ref, first_ref, metric_ref, rows, visit):
            line = derivative_line(seconds, True)
            for j in range(SIDE):
                node = i * SIDE + j
                mass = shift * metric_ref[3, node : node + 1, :]
                result_ref[node, rows, :] = line[j] + mass * cells_ref[node, rows, :]
        energy = jnp.zeros((8, LANES), F32)
        for j in range(SIDE):
            line = derivative_line([first_ref[k * SIDE + j] for k in range(SIDE)], True)
            for i in range(SIDE):
                node = i * SIDE + j
                value = result_ref[node, rows, :] + line[i]
                result_ref[node, rows, :] = value
                energy = energy + value * cells_ref[node, rows, :]
        energy_ref[rows, :] = energy


def apply_energy(cells_ref, first_ref, energy_ref, metric_ref, shift_ref):
    @pl.loop(0, 2)
    def half(part):
        rows = pl.ds(pl.multiple_of(part * 8, 8), 8)
        shift = shift_ref[rows, :]
        sums = [jnp.zeros((8, LANES), F32)]

        def visit(node, g1, g2, p1, p2):
            value = cells_ref[node, rows, :]
            mass = shift * metric_ref[3, node : node + 1, :]
            sums[0] = sums[0] + (g1 * p1 + g2 * p2 + mass * value * value)

        for i, seconds in gradients(cells_ref, first_ref, metric_ref, rows, visit):
            pass
        energy_ref[rows, :] = sums[0]


def pack_kernel(forcing_ref, edge_ref, shared_ref, out_ref, slots_ref, left_ref, right_ref):
    store = write_place(out_ref, sent_place)
    for index, node in enumerate(INNER_NODES):
        store(index, forcing_ref[node])
    for index in range(INNER + TILES, MODES * BLOCK):
        store(index, jnp.zeros((ROWS, LANES), F32))
    skeleton = scatter_cycle(lambda slot: forcing_ref[CYCLE_NODES[slot]], edge_ref[...], left_ref, right_ref)
    write_skeleton(skeleton, lambda index, value: store(INNER + index, value))
    for tile, value in enumerate(gather_slots(skeleton, shared_ref[...])):
        slots_ref[tile] = value


def diagonal_kernel(
    metric_ref, table_ref, cross_ref, edge_ref, penalty_ref, shared_ref, columns_ref, slots_ref,
    inner_ref, skeleton_ref, message_ref, right_slots_ref, cells_ref, left_ref, right_ref,
):
    both = jnp.concatenate([metric_ref[0], metric_ref[1]], axis=0)
    terms = jnp.dot(table_ref[...], both, precision=HIGHEST, preferred_element_type=F32)
    cells_ref[0] = terms + cross_ref[...] * metric_ref[2]
    cells_ref[1] = metric_ref[3]
    for index, node in enumerate(INNER_NODES):
        inner_ref[0, index : index + 1, :] = cells_ref[0, node : node + 1, :]
        inner_ref[1, index : index + 1, :] = cells_ref[1, node : node + 1, :]
    sublanes = lax.broadcasted_iota(jnp.int32, (ROWS, LANES), 0)

    def load(slot):
        node = CYCLE_NODES[slot]
        laplace = jnp.broadcast_to(cells_ref[0, node : node + 1, :], (ROWS, LANES))
        mass = jnp.broadcast_to(cells_ref[1, node : node + 1, :], (ROWS, LANES))
        return jnp.where(sublanes == 0, laplace, jnp.where(sublanes == 1, mass, 0.0))

    skeleton = scatter_cycle(load, edge_ref[...], left_ref, right_ref)
    wide = lax.broadcasted_iota(jnp.int32, (HIGH * ROWS, LOW), 0)
    skeleton = skeleton + jnp.where(jnp.bitwise_and(wide, ROWS - 1) == 0, per_tile(penalty_ref), 0.0)
    skeleton_ref[...] = skeleton
    low = jnp.bitwise_and(columns_ref[...], LOW - 1)
    for tile, value in enumerate(gather_slots(skeleton, shared_ref[...])):
        message_ref[tile, :ROWS, :] = slots_ref[tile]
        message_ref[tile, ROWS:, :] = value[:8]
        right_slots_ref[lane_block(tile), :] = one_hot_columns(low[:, tile : tile + 1])


def transform_kernel(matrix_ref, share_ref, in_ref, a0, a1, a2, a3, a4, masks_ref, out_ref, extra_ref):
    matrix = matrix_ref[...]
    arrived_refs = [a0, a1, a2, a3, a4]
    masks = masks_ref[...]
    for index in range(BLOCK):
        block = in_ref[:, index].reshape(PLANES, LANES)
        mixed = jnp.dot(matrix, block, precision=HIGHEST, preferred_element_type=F32)
        out_ref[:, index] = mixed.reshape(MODES, ROWS, LANES)
    share = share_ref[...]
    for tile in range(SLOT_TILES):
        chosen = select_arrived(masks, tile, [ref[tile] for ref in arrived_refs])
        mixed = jnp.dot(share, chosen[:ROWS], precision=HIGHEST, preferred_element_type=F32)
        out_ref[:, BLOCK + tile] = mixed.reshape(MODES, ROWS, LANES)
        extra_ref[tile] = chosen[ROWS:]


def first_kernel(
    source_ref, extra_ref, shared_ref, right_slots_ref, edge_ref, metric_ref, inner_ref, diagonal_ref,
    penalty_ref, shift_ref, pairs_ref, kept_ref, slots_ref, sums_ref,
    left_ref, right_ref, cells_ref, result_ref, first_ref, energy_ref,
):
    shared_rows = shared_ref[...]
    right_slots = right_slots_ref[...]
    shift = shift_ref[...]
    edge_rows = edge_ref[...]

    def load_right(tile):
        total = source_ref[0, BLOCK + tile]
        for mode in range(1, MODES):
            total = total + source_ref[mode, BLOCK + tile]
        return total

    def load_extra(tile):
        return jnp.concatenate([extra_ref[tile], jnp.zeros((8, LANES), F32)], axis=0)

    def source(index):
        block, row = sent_place(index)
        return source_ref[block, row]

    local = read_skeleton(lambda index: source(INNER + index))
    right_side = local + scatter_slots(load_right, shared_rows, left_ref, right_slots)
    diagonal = diagonal_ref[...] + scatter_slots(load_extra, shared_rows, left_ref, right_slots)
    wide_shift = jnp.concatenate([shift, shift], axis=1)
    parts = []
    for high in range(HIGH):
        block = diagonal[row_block(high), :]
        parts.append(block[0:1, :] + wide_shift * block[1:2, :])
    inverse = 1.0 / jnp.concatenate(parts, axis=0)
    search = right_side * inverse
    kept_ref[0] = local
    kept_ref[1] = inverse
    kept_ref[2] = search
    start = skeleton_sum(local * search)
    for index, node in enumerate(INNER_NODES):
        value = source(index)
        inverted = 1.0 / (inner_ref[0, index : index + 1, :] + shift * inner_ref[1, index : index + 1, :])
        scaled = value * inverted
        pairs_ref[index // GROUP, index % GROUP] = scaled
        pairs_ref[index // GROUP, GROUP + index % GROUP] = inverted
        cells_ref[node] = scaled
        start = start + value * scaled

    def store(slot, value):
        cells_ref[CYCLE_NODES[slot]] = value

    gather_cycle(search, edge_rows, store)
    apply_operator(cells_ref, result_ref, first_ref, energy_ref, metric_ref, shift_ref)
    weighted = per_tile(penalty_ref) * search
    applied = weighted + scatter_cycle(
        lambda slot: result_ref[CYCLE_NODES[slot]], edge_rows, left_ref, right_ref
    )
    kept_ref[3] = applied
    for tile, value in enumerate(gather_slots(applied, shared_rows)):
        slots_ref[tile] = value
    crossed = jnp.zeros((ROWS, LANES), F32)
    sourced = jnp.zeros((ROWS, LANES), F32)
    for index, node in enumerate(INNER_NODES):
        value = result_ref[node]
        moved = value * pairs_ref[index // GROUP, GROUP + index % GROUP] - cells_ref[node]
        pairs_ref[index // GROUP, GROUP + index % GROUP] = moved
        crossed = crossed + value * moved
        sourced = sourced + source(index) * moved
    for row in range(2 * GROUP):
        pairs_ref[MODES - 1, row] = jnp.zeros((ROWS, LANES), F32)
    sums_ref[0] = energy_ref[...] + skeleton_sum(weighted * search)
    sums_ref[1] = crossed
    sums_ref[2] = start
    sums_ref[3] = sourced


def second_kernel(
    pairs_ref, kept_ref, sums_ref, a0, a1, a2, a3, a4, masks_ref, shared_ref, right_slots_ref, edge_ref,
    metric_ref, penalty_ref, shift_ref, change_ref, message_ref, left_ref, cells_ref, first_ref, energy_ref,
):
    arrived_refs = [a0, a1, a2, a3, a4]
    masks = masks_ref[...]

    def load(tile):
        return select_arrived(masks, tile, [ref[tile] for ref in arrived_refs])

    local, inverse, search, applied = [kept_ref[index] for index in range(4)]
    full = applied + scatter_slots(load, shared_ref[...], left_ref, right_slots_ref[...])
    change = full * inverse - search
    change_ref[...] = change
    crossed = sums_ref[1] + skeleton_sum(applied * change)
    sourced = sums_ref[3] + skeleton_sum(local * change)
    for index, node in enumerate(INNER_NODES):
        cells_ref[node] = pairs_ref[index // GROUP, GROUP + index % GROUP]

    def store(slot, value):
        cells_ref[CYCLE_NODES[slot]] = value

    gather_cycle(change, edge_ref[...], store)
    apply_energy(cells_ref, first_ref, energy_ref, metric_ref, shift_ref)
    energy = energy_ref[...] + skeleton_sum(per_tile(penalty_ref) * change * change)
    sublanes = lax.broadcasted_iota(jnp.int32, (ROWS, LANES), 0)
    lanes = lax.broadcasted_iota(jnp.int32, (ROWS, LANES), 1)
    spread = jnp.zeros((ROWS, LANES), F32)
    for index, value in enumerate([sums_ref[0], crossed, energy, sums_ref[2], sourced]):
        column = jnp.sum(value, axis=1, keepdims=True)
        spread = jnp.where(lanes == sublanes + index * ROWS, column, spread)
    message = jnp.sum(spread, axis=0, keepdims=True)
    message_ref[...] = jnp.broadcast_to(message, message_ref.shape)


def scale_kernel(scalars_ref, kept_ref, change_ref, out_ref):
    sublanes = lax.broadcasted_iota(jnp.int32, (ROWS, LANES), 0)
    lanes = lax.broadcasted_iota(jnp.int32, (ROWS, LANES), 1)
    total = jnp.sum(scalars_ref[...], axis=0, keepdims=True)
    g00, g01, g11, h0, h1 = [
        jnp.sum(jnp.where(lanes == sublanes + index * ROWS, total, 0.0), axis=1, keepdims=True)
        for index in range(SCALARS)
    ]
    ratio = g01 / g00
    pivot = g11 - ratio * g01
    second = jnp.where(pivot > 0.0, (h1 - ratio * h0) / pivot, 0.0)
    first = h0 / g00 - ratio * second
    for mode in range(MODES - 1):
        out_ref[mode, 2] = jnp.where(lanes < LANES // 2, first, second)
        out_ref[mode, 3] = jnp.zeros((ROWS, LANES), F32)
    for high in range(HIGH):
        value = first * kept_ref[2, row_block(high), :] + second * change_ref[row_block(high), :]
        for part in range(2):
            block, row = tail_place(2 * high + part)
            out_ref[block, row] = value[:, lane_block(part)]


def combine_kernel(matrix_ref, last_ref, tail_ref, pairs_ref, out_ref, block_ref):
    last = last_ref[...]
    for mode in range(MODES):
        first = tail_ref[mode, 2, :, 0:1]
        second = tail_ref[mode, 2, :, LANES // 2 : LANES // 2 + 1]
        for index in range(GROUP):
            value = first * pairs_ref[mode, index] + second * pairs_ref[mode, GROUP + index]
            if index < 2:
                value = value + last * tail_ref[mode, 2 + index]
            block_ref[index, row_block(mode), :] = value
        for index in range(2):
            block_ref[GROUP + index, row_block(mode), :] = tail_ref[mode, index]
    matrix = matrix_ref[...]
    for index in range(BLOCK):
        mixed = jnp.dot(matrix, block_ref[index], precision=HIGHEST, preferred_element_type=F32)
        out_ref[:, index] = mixed.reshape(MODES, ROWS, LANES)


def unpack_kernel(packed_ref, edge_ref, out_ref):
    for index, node in enumerate(INNER_NODES):
        out_ref[node] = packed_ref[index // GROUP, index % GROUP]

    def load(index):
        block, row = result_place(index)
        return packed_ref[block, row]

    def store(slot, value):
        out_ref[CYCLE_NODES[slot]] = value

    gather_cycle(read_skeleton(load), edge_ref[...], store)


def call(kernel, out_shapes, scratch, *operands):
    return pl.pallas_call(
        kernel,
        out_shape=out_shapes,
        scratch_shapes=scratch,
        compiler_params=pltpu.CompilerParams(vmem_limit_bytes=VMEM_LIMIT),
    )(*operands)


def shape(*dims):
    return jax.ShapeDtypeStruct(dims, F32)


def swap_blocks(blocks, axis="mode"):
    return lax.all_to_all(blocks, axis, split_axis=0, concat_axis=0, tiled=True)


def exchange(slots):
    count = lax.axis_size("elem")
    return [
        lax.ppermute(slots, "elem", [(i, i ^ 1 << level) for i in range(count)])
        for level in range(count.bit_length() - 1)
    ]


def body(forcing, metric, edge_map, shared_rows, partner_masks, penalty):
    forward, backward = [jnp.asarray(table) for table in fourier_tables()]
    table, cross = [jnp.asarray(part) for part in diagonal_tables()]
    mode = lax.axis_index("mode")
    rows_global = mode * ROWS + jnp.arange(ROWS, dtype=jnp.int32)
    shift = jnp.broadcast_to(helmholtz_shift(rows_global)[:, None], (ROWS, LANES))
    last = jnp.broadcast_to(jnp.where(mode == MODES - 1, 1.0, 0.0), (ROWS, LANES)).astype(F32)
    share = lax.dynamic_slice(forward, (0, mode * ROWS), (PLANES, ROWS))
    edge_rows = edge_map.T
    shared = shared_rows.reshape(SLOT_TILES, LANES)
    masks = partner_masks.reshape(SLOT_TILES, LANES)
    penalties = jnp.pad(penalty, (0, HIGH * LOW - SKEL), constant_values=1.0).reshape(HIGH, LOW)
    left = pltpu.VMEM((2 * HIGH * ROWS, CYCLE * LANES), BF16)
    right = pltpu.VMEM((CYCLE * LANES, LOW), BF16)
    left_slots = pltpu.VMEM((2 * HIGH * ROWS, SLOTS), BF16)
    cells = pltpu.VMEM((NODES, ROWS, LANES), F32)
    first = pltpu.VMEM((NODES, 8, LANES), F32)
    energy = pltpu.VMEM((ROWS, LANES), F32)
    wide = (HIGH * ROWS, LOW)

    packed, slots = call(
        pack_kernel, [shape(MODES, BLOCK, ROWS, LANES), shape(SLOT_TILES, ROWS, LANES)], [left, right],
        forcing.transpose(1, 0, 2), edge_rows, shared,
    )
    gathered = swap_blocks(packed)
    inner, diagonal, message, right_slots = call(
        diagonal_kernel,
        [
            shape(2, INNER, LANES), shape(*wide), shape(SLOT_TILES, ROWS + 8, LANES),
            jax.ShapeDtypeStruct((SLOTS, LOW), BF16),
        ],
        [pltpu.VMEM((2, NODES, LANES), F32), left, right],
        metric, table, cross, edge_rows, penalties, shared, shared.T, slots,
    )
    mixed, extra = call(
        transform_kernel, [shape(MODES, SHARE, ROWS, LANES), shape(SLOT_TILES, 8, LANES)], [],
        forward, share, gathered, *exchange(message), masks,
    )
    source = swap_blocks(mixed)
    pairs, kept, slots, sums = call(
        first_kernel,
        [
            shape(MODES, 2 * GROUP, ROWS, LANES), shape(4, *wide), shape(SLOT_TILES, ROWS, LANES),
            shape(4, ROWS, LANES),
        ],
        [left, right, cells, cells, first, energy],
        source, extra, shared, right_slots, edge_rows, metric, inner, diagonal, penalties, shift,
    )
    pair_blocks = swap_blocks(pairs)
    change, message = call(
        second_kernel,
        [shape(*wide), shape(ELEMS_AXIS, LANES)],
        [left_slots, cells, first, energy],
        pairs, kept, sums, *exchange(slots), masks, shared, right_slots, edge_rows, metric, penalties, shift,
    )
    message, pair_blocks = lax.optimization_barrier((message, pair_blocks))
    scalars = swap_blocks(message, "elem")
    tail = call(scale_kernel, shape(MODES, TAIL, ROWS, LANES), [], scalars, kept, change)
    mixed = call(
        combine_kernel, shape(MODES, BLOCK, ROWS, LANES), [pltpu.VMEM((BLOCK, PLANES, LANES), F32)],
        backward, last, swap_blocks(tail), pair_blocks,
    )
    result = call(unpack_kernel, shape(NODES, ROWS, LANES), [], swap_blocks(mixed), edge_rows)
    return result.transpose(1, 0, 2)


def solution(mesh):
    placed = (
        P("mode", None, "elem"),
        P(None, None, "elem"),
        P("elem", None),
        P("elem"),
        P("elem"),
        P("elem"),
    )
    return jax.shard_map(
        body, mesh=mesh, in_specs=placed, out_specs=P("mode", None, "elem"), check_vma=False
    )
```

time: 164 us -> 124 us (0.76)
  blocking collectives: 90 us -> 30.1 us
  starting transfers between devices: 22.8 us -> 45.7 us
  waiting for transfers between devices: 9.16 us -> 24.3 us
  Pallas kernels: 31 us -> 19.3 us
  local copies, waits for them, and re-layouts: 9.83 us -> 4.23 us
    all_to_all x5 -> x2, blocking collectives: 90 us -> 30.1 us  [swap_blocks(): return lax.all_to_all(blocks, axis, split_axis=0, concat_axis=0, tiled=True)]
    all_to_all x1 -> x4, starting transfers between devices: 4.32 us -> 26.5 us  [swap_blocks(): return lax.all_to_all(blocks, axis, split_axis=0, concat_axis=0, tiled=True)]
    all_to_all x1 -> x4, waiting for transfers between devices: 5.4 us -> 19.8 us  [swap_blocks(): return lax.all_to_all(blocks, axis, split_axis=0, concat_axis=0, tiled=True)]
    pallas_call x8, Pallas kernels: 31 us -> 19.3 us  [call(): pl.pallas_call(kernel, out_shape=out_shapes, scratch_shapes=scratch, comp...]
    pallas_call x1 -> x0, local copies, waits for them, and re-layouts: 2.08 us -> none  [call(): pl.pallas_call(kernel, out_shape=out_shapes, scratch_shapes=scratch, comp...]
    unnamed x35 -> x23, local copies, waits for them, and re-layouts: 5.76 us -> 3.96 us
  transfers between devices with their start and end apart: 11 -> 14, of which waited for: 3 -> 5; matrix products, arithmetic and copies ran while one was open for 1% -> 0% of each run, Pallas kernels for 2% -> 4%
where the time goes in v2:
time: 124 us
  starting transfers between devices  45.7 us (37%)
  blocking collectives  30.1 us (24%)
  waiting for transfers between devices  24.3 us (20%)
  Pallas kernels  19.3 us (16%)
  local copies, waits for them, and re-layouts  4.23 us (3%)
    all_to_all x2, blocking collectives, swap_blocks(): return lax.all_to_all(blocks, axis, split_axis=0, concat_axis=0, tiled=True)  30.1 us
    all_to_all x4, starting transfers between devices, swap_blocks(): return lax.all_to_all(blocks, axis, split_axis=0, concat_axis=0, tiled=True)  26.5 us
    all_to_all x4, waiting for transfers between devices, swap_blocks(): return lax.all_to_all(blocks, axis, split_axis=0, concat_axis=0, tiled=True)  19.8 us
    pallas_call x8, Pallas kernels, call(): pl.pallas_call(kernel, out_shape=out_shapes, scratch_shapes=scratch, comp...  19.3 us
    ppermute x10, starting transfers between devices, exchange(): lax.ppermute(slots, 'elem', [(i, i ^ 1 << level) for i in range(count)])  19.2 us
    ppermute x10, waiting for transfers between devices, exchange(): lax.ppermute(slots, 'elem', [(i, i ^ 1 << level) for i in range(count)])  4.45 us
    unnamed x23, local copies, waits for them, and re-layouts  3.96 us
  transfers between devices with their start and end apart: 14, of which 5 were waited for; matrix products, arithmetic and copies ran while one was open for 0% of the time, Pallas kernels for 4%

profile of v2, /device:TPU:1, one launch (start us, length us, event | category | flops | bytes accessed | tf_op | source)
XLA Modules:
  0.0 123.7 jit_solution(5005507847590836571)
XLA Ops:
  0.7 1.1 copy-done
  2.5 2.3 %shard_map.100 = (f32[8,9,16,128]{3,2,1,0:T(8,128)}, f32[3,16,128]{2,1,0:T(8,128)S(1)}) custom-call(f32[81,16,128]{2,1,0:T(8,128)S(1)} %bitcast.11, s32[32,128]{1,0:T(8,128)S(1)} %bitcast.12, s32[3,128]{1,0:T(4,128)S(1)} %bitcast.18), custom_call_target="tpu_custom_call" | custom-call | tf_op jit(solution)/shard_map/pallas_call | solution.py:552
  4.8 6.8 %all-to-all-start = ((f32[8,9,16,128]{3,2,1,0:T(8,128)}), f32[8,9,16,128]{3,2,1,0:T(8,128)S(1)}, u32[]{:S(2)}, u32[]{:S(2)}) async-start(f32[8,9,16,128]{3,2,1,0:T(8,128)} %get-tuple-element.21), calls=%async_computation | async-start | bytes 1179648 | tf_op jit(solution)/shard_map/all_to_all | solution.py:565
  13.2 1.8 %shard_map.101 = (f32[2,49,128]{2,1,0:T(8,128)S(1)}, f32[144,256]{1,0:T(8,128)S(1)}, f32[3,24,128]{2,1,0:T(8,128)S(1)}, bf16[384,256]{1,0:T(8,128)(2,1)S(1)}) custom-call(f32[4,81,128]{2,1,0:T(8,128)S(1)} %copy.15.metric_ref, f32[81,162]{1,0:T(8,128)S(1)} %copy-done.4, f32[81,128]{1,0:T(8,128)S(1)} %copy-done.7, s32[32,128]{1,0:T(8,128)S(1)} %bitcast.13, ...), custom_call_target="tpu_custom_call" | custom-call | tf_op jit(solution)/shard_map/pallas_call | solution.py:552
  15.6 2.6 %collective-permute-start.1 = (f32[3,24,128]{2,1,0:T(8,128)S(1)}, f32[3,24,128]{2,1,0:T(8,128)S(1)}, u32[]{:S(2)}, u32[]{:S(2)}) collective-permute-start(f32[3,24,128]{2,1,0:T(8,128)S(1)} %get-tuple-element.23), channel_id=1, source_target_pairs={{0,2},{1,3},{2,0},{3,1},{4,6},{5,7},{6,4},{7,5},{8,10},{9,11},{10,... | collective-permute-start | bytes 110600 | tf_op jit(solution)/shard_map/ppermute | solution.py:571
  18.2 1.6 %collective-permute-start.2 = (f32[3,24,128]{2,1,0:T(8,128)S(1)}, f32[3,24,128]{2,1,0:T(8,128)S(1)}, u32[]{:S(2)}, u32[]{:S(2)}) collective-permute-start(f32[3,24,128]{2,1,0:T(8,128)S(1)} %get-tuple-element.23), channel_id=1, source_target_pairs={{0,4},{1,5},{2,6},{3,7},{4,0},{5,1},{6,2},{7,3},{8,12},{9,13},{10,... | collective-permute-start | bytes 110600 | tf_op jit(solution)/shard_map/ppermute | solution.py:571
  19.8 3.0 %collective-permute-start.3 = (f32[3,24,128]{2,1,0:T(8,128)S(1)}, f32[3,24,128]{2,1,0:T(8,128)S(1)}, u32[]{:S(2)}, u32[]{:S(2)}) collective-permute-start(f32[3,24,128]{2,1,0:T(8,128)S(1)} %get-tuple-element.23), channel_id=1, source_target_pairs={{0,8},{1,9},{2,10},{3,11},{4,12},{5,13},{6,14},{7,15},{8,0},{9,1},... | collective-permute-start | bytes 110600 | tf_op jit(solution)/shard_map/ppermute | solution.py:571
  22.8 4.2 %collective-permute-start.4 = (f32[3,24,128]{2,1,0:T(8,128)S(1)}, f32[3,24,128]{2,1,0:T(8,128)S(1)}, u32[]{:S(2)}, u32[]{:S(2)}) collective-permute-start(f32[3,24,128]{2,1,0:T(8,128)S(1)} %get-tuple-element.23), channel_id=1, source_target_pairs={{0,16},{1,17},{2,18},{3,19},{4,20},{5,21},{6,22},{7,23},{8,24},{9,... | collective-permute-start | bytes 110600 | tf_op jit(solution)/shard_map/ppermute | solution.py:571
  27.2 2.7 %collective-permute-done.4.a4 = f32[3,24,128]{2,1,0:T(8,128)S(1)} collective-permute-done((f32[3,24,128]{2,1,0:T(8,128)S(1)}, f32[3,24,128]{2,1,0:T(8,128)S(1)}, u32[]{:S(2)}, u32[]{:S(2)}) %collective-permute-start.4) | collective-permute-done | bytes 36896 | tf_op jit(solution)/shard_map/ppermute | solution.py:571
  29.9 1.7 %shard_map.102 = (f32[8,12,16,128]{3,2,1,0:T(8,128)}, f32[3,8,128]{2,1,0:T(8,128)S(1)}) custom-call(f32[128,128]{1,0:T(8,128)S(1)} %copy-done.3, f32[128,16]{1,0:T(8,128)S(1)} %constant_dynamic-slice_fusion.share_ref, f32[8,9,16,128]{3,2,1,0:T(8,128)S(1)} %all-to-all-done.in_ref, f32[3,24,128]{2,1,0:T(8,128)S(1)} %collective-permute-done.a0, ...), custom_call_target="tpu_custom_call" | custom-call | tf_op jit(solution)/shard_map/pallas_call | solution.py:552
  31.6 6.7 %all-to-all-start.1 = ((f32[8,12,16,128]{3,2,1,0:T(8,128)}), f32[8,12,16,128]{3,2,1,0:T(8,128)S(1)}, u32[]{:S(2)}, u32[]{:S(2)}) async-start(f32[8,12,16,128]{3,2,1,0:T(8,128)} %get-tuple-element.24), calls=%async_computation.1 | async-start | bytes 1572864 | tf_op jit(solution)/shard_map/all_to_all | solution.py:565
  38.3 12.3 %all-to-all-done.1.source_ref = f32[8,12,16,128]{3,2,1,0:T(8,128)S(1)} async-done(((f32[8,12,16,128]{3,2,1,0:T(8,128)}), f32[8,12,16,128]{3,2,1,0:T(8,128)S(1)}, u32[]{:S(2)}, u32[]{:S(2)}) %all-to-all-start.1) | async-done | bytes 786464 | tf_op jit(solution)/shard_map/all_to_all | solution.py:565
  50.7 6.1 %shard_map.103 = (f32[8,14,16,128]{3,2,1,0:T(8,128)}, f32[4,144,256]{2,1,0:T(8,128)S(1)}, f32[3,16,128]{2,1,0:T(8,128)S(1)}, f32[4,16,128]{2,1,0:T(8,128)S(1)}) custom-call(f32[8,12,16,128]{3,2,1,0:T(8,128)S(1)} %all-to-all-done.1.source_ref, f32[3,8,128]{2,1,0:T(8,128)S(1)} %get-tuple-element.25.extra_ref, s32[3,128]{1,0:T(4,128)S(1)} %bitcast.21, ...), custom_call_target="tpu_custom_call" | custom-call | tf_op jit(solution)/shard_map/pallas_call | solution.py:552
  56.8 4.3 %all-to-all-start.2 = ((f32[8,14,16,128]{3,2,1,0:T(8,128)}), f32[8,14,16,128]{3,2,1,0:T(8,128)S(1)}, u32[]{:S(2)}, u32[]{:S(2)}) async-start(f32[8,14,16,128]{3,2,1,0:T(8,128)} %get-tuple-element.29.pairs_ref), calls=%async_computation.2 | async-start | bytes 1835008 | tf_op jit(solution)/shard_map/all_to_all | solution.py:565
  61.1 1.1 collective-permute-start.6
  63.1 5.3 %collective-permute-start.9 = (f32[3,16,128]{2,1,0:T(8,128)S(1)}, f32[3,16,128]{2,1,0:T(8,128)S(1)}, u32[]{:S(2)}, u32[]{:S(2)}) collective-permute-start(f32[3,16,128]{2,1,0:T(8,128)S(1)} %get-tuple-element.32), channel_id=1, source_target_pairs={{0,16},{1,17},{2,18},{3,19},{4,20},{5,21},{6,22},{7,23},{8,24},{9,... | collective-permute-start | bytes 73736 | tf_op jit(solution)/shard_map/ppermute | solution.py:571
  68.4 1.7 %collective-permute-done.9.a4 = f32[3,16,128]{2,1,0:T(8,128)S(1)} collective-permute-done((f32[3,16,128]{2,1,0:T(8,128)S(1)}, f32[3,16,128]{2,1,0:T(8,128)S(1)}, u32[]{:S(2)}, u32[]{:S(2)}) %collective-permute-start.9) | collective-permute-done | bytes 24608 | tf_op jit(solution)/shard_map/ppermute | solution.py:571
  70.1 3.7 %shard_map.104 = (f32[144,256]{1,0:T(8,128)S(1)}, f32[32,128]{1,0:T(8,128)S(1)}) custom-call(f32[8,14,16,128]{3,2,1,0:T(8,128)} %get-tuple-element.29.pairs_ref, f32[4,144,256]{2,1,0:T(8,128)S(1)} %get-tuple-element.30.kept_ref, f32[4,16,128]{2,1,0:T(8,128)S(1)} %get-tuple-element.31.sums_ref, f32[3,16,128]{2,1,0:T(8,128)S(1)} %collective-permute-done.5.a0, ...), custom_call_target="tpu_custom_call" | custom-call | tf_op jit(solution)/shard_map/pallas_call | solution.py:552
  73.8 1.0 all-to-all-done.2.pairs_ref
  74.8 16.3 %all_to_all.36 = f32[32,1,128]{2,1,0:T(1,128)S(1)} all-to-all(f32[32,1,128]{2,1,0:T(1,128)S(1)} %bitcast.23), channel_id=1, replica_groups=mesh['mode'=8,'elem'=32] {'elem'}, dimensions={0} | all-to-all | bytes 32768 | tf_op jit(solution)/shard_map/all_to_all | solution.py:565
  92.0 8.7 %all-to-all-start.4 = ((f32[8,4,16,128]{3,2,1,0:T(8,128)}), f32[8,4,16,128]{3,2,1,0:T(8,128)S(1)}, u32[]{:S(2)}, u32[]{:S(2)}) async-start(f32[8,4,16,128]{3,2,1,0:T(8,128)} %shard_map.105), calls=%async_computation.4 | async-start | bytes 524288 | tf_op jit(solution)/shard_map/all_to_all | solution.py:565
  100.6 6.5 %all-to-all-done.4.tail_ref = f32[8,4,16,128]{3,2,1,0:T(8,128)S(1)} async-done(((f32[8,4,16,128]{3,2,1,0:T(8,128)}), f32[8,4,16,128]{3,2,1,0:T(8,128)S(1)}, u32[]{:S(2)}, u32[]{:S(2)}) %all-to-all-start.4) | async-done | bytes 262176 | tf_op jit(solution)/shard_map/all_to_all | solution.py:565
  107.9 13.8 %all_to_all.37.packed_ref = f32[8,9,16,128]{3,2,1,0:T(8,128)S(1)} all-to-all(f32[8,9,16,128]{3,2,1,0:T(8,128)S(1)} %shard_map.106), channel_id=1, replica_groups=mesh['mode'=8,'elem'=32] {'mode'}, dimensions={0} | all-to-all | bytes 1179648 | tf_op jit(solution)/shard_map/all_to_all | solution.py:565
  121.7 2.0 %shard_map.107 = f32[81,16,128]{2,1,0:T(8,128)} custom-call(f32[8,9,16,128]{3,2,1,0:T(8,128)S(1)} %all_to_all.37.packed_ref, s32[32,128]{1,0:T(8,128)S(1)} %bitcast.16), custom_call_target="tpu_custom_call" | custom-call | tf_op jit(solution)/shard_map/pallas_call | solution.py:552
  (44 shorter events, 6.1 us)
Async XLA Ops:
  0.7 1.1 copy-start
  1.8 0.7 copy-start.1
  4.8 6.8 %copy-start.9 = (f32[4,81,128]{2,0,1:T(4,128)S(1)}, f32[4,81,128]{2,0,1:T(4,128)}, u32[]{:S(2)}) copy-start(f32[4,81,128]{2,0,1:T(4,128)} %param.11) | copy-start | bytes 497668
  4.8 25.1 %all-to-all-start = ((f32[8,9,16,128]{3,2,1,0:T(8,128)}), f32[8,9,16,128]{3,2,1,0:T(8,128)S(1)}, u32[]{:S(2)}, u32[]{:S(2)}) async-start(f32[8,9,16,128]{3,2,1,0:T(8,128)} %get-tuple-element.21), calls=%async_computation | async-start | bytes 1179648 | tf_op jit(solution)/shard_map/all_to_all | solution.py:565
  11.6 0.7 copy-start.10
  11.6 0.8 copy-start.7
  12.3 0.9 copy-start.4
  12.3 0.9 copy-start.2
  13.2 13.8 %copy-start.3 = (f32[128,128]{1,0:T(8,128)S(1)}, f32[128,128]{1,0:T(8,128)}, u32[]{:S(2)}) copy-start(f32[128,128]{1,0:T(8,128)} %constant.44.clone.matrix_ref) | copy-start | bytes 196612
  15.1 12.1 %collective-permute-start = (f32[3,24,128]{2,1,0:T(8,128)S(1)}, f32[3,24,128]{2,1,0:T(8,128)S(1)}, u32[]{:S(2)}, u32[]{:S(2)}) collective-permute-start(f32[3,24,128]{2,1,0:T(8,128)S(1)} %get-tuple-element.23), channel_id=1, source_target_pairs={{0,1},{1,0},{2,3},{3,2},{4,5},{5,4},{6,7},{7,6},{8,9},{9,8},{10,11... | collective-permute-start | bytes 110600 | tf_op jit(solution)/shard_map/ppermute | solution.py:571
  15.6 11.6 %collective-permute-start.1 = (f32[3,24,128]{2,1,0:T(8,128)S(1)}, f32[3,24,128]{2,1,0:T(8,128)S(1)}, u32[]{:S(2)}, u32[]{:S(2)}) collective-permute-start(f32[3,24,128]{2,1,0:T(8,128)S(1)} %get-tuple-element.23), channel_id=1, source_target_pairs={{0,2},{1,3},{2,0},{3,1},{4,6},{5,7},{6,4},{7,5},{8,10},{9,11},{10,... | collective-permute-start | bytes 110600 | tf_op jit(solution)/shard_map/ppermute | solution.py:571
  18.2 9.0 %collective-permute-start.2 = (f32[3,24,128]{2,1,0:T(8,128)S(1)}, f32[3,24,128]{2,1,0:T(8,128)S(1)}, u32[]{:S(2)}, u32[]{:S(2)}) collective-permute-start(f32[3,24,128]{2,1,0:T(8,128)S(1)} %get-tuple-element.23), channel_id=1, source_target_pairs={{0,4},{1,5},{2,6},{3,7},{4,0},{5,1},{6,2},{7,3},{8,12},{9,13},{10,... | collective-permute-start | bytes 110600 | tf_op jit(solution)/shard_map/ppermute | solution.py:571
  19.8 7.3 %collective-permute-start.3 = (f32[3,24,128]{2,1,0:T(8,128)S(1)}, f32[3,24,128]{2,1,0:T(8,128)S(1)}, u32[]{:S(2)}, u32[]{:S(2)}) collective-permute-start(f32[3,24,128]{2,1,0:T(8,128)S(1)} %get-tuple-element.23), channel_id=1, source_target_pairs={{0,8},{1,9},{2,10},{3,11},{4,12},{5,13},{6,14},{7,15},{8,0},{9,1},... | collective-permute-start | bytes 110600 | tf_op jit(solution)/shard_map/ppermute | solution.py:571
  22.8 7.0 %collective-permute-start.4 = (f32[3,24,128]{2,1,0:T(8,128)S(1)}, f32[3,24,128]{2,1,0:T(8,128)S(1)}, u32[]{:S(2)}, u32[]{:S(2)}) collective-permute-start(f32[3,24,128]{2,1,0:T(8,128)S(1)} %get-tuple-element.23), channel_id=1, source_target_pairs={{0,16},{1,17},{2,18},{3,19},{4,20},{5,21},{6,22},{7,23},{8,24},{9,... | collective-permute-start | bytes 110600 | tf_op jit(solution)/shard_map/ppermute | solution.py:571
  27.0 2.8 %copy-start.8 = (s32[384]{0:T(512)S(1)}, s32[384]{0:T(512)}, u32[]{:S(2)}) copy-start(s32[384]{0:T(512)} %param.14) | copy-start | bytes 4612
  31.6 19.0 %all-to-all-start.1 = ((f32[8,12,16,128]{3,2,1,0:T(8,128)}), f32[8,12,16,128]{3,2,1,0:T(8,128)S(1)}, u32[]{:S(2)}, u32[]{:S(2)}) async-start(f32[8,12,16,128]{3,2,1,0:T(8,128)} %get-tuple-element.24), calls=%async_computation.1 | async-start | bytes 1572864 | tf_op jit(solution)/shard_map/all_to_all | solution.py:565
  56.8 18.0 %all-to-all-start.2 = ((f32[8,14,16,128]{3,2,1,0:T(8,128)}), f32[8,14,16,128]{3,2,1,0:T(8,128)S(1)}, u32[]{:S(2)}, u32[]{:S(2)}) async-start(f32[8,14,16,128]{3,2,1,0:T(8,128)} %get-tuple-element.29.pairs_ref), calls=%async_computation.2 | async-start | bytes 1835008 | tf_op jit(solution)/shard_map/all_to_all | solution.py:565
  61.1 7.2 %collective-permute-start.5 = (f32[3,16,128]{2,1,0:T(8,128)S(1)}, f32[3,16,128]{2,1,0:T(8,128)S(1)}, u32[]{:S(2)}, u32[]{:S(2)}) collective-permute-start(f32[3,16,128]{2,1,0:T(8,128)S(1)} %get-tuple-element.32), channel_id=1, source_target_pairs={{0,1},{1,0},{2,3},{3,2},{4,5},{5,4},{6,7},{7,6},{8,9},{9,8},{10,11... | collective-permute-start | bytes 73736 | tf_op jit(solution)/shard_map/ppermute | solution.py:571
  61.1 7.2 %collective-permute-start.6 = (f32[3,16,128]{2,1,0:T(8,128)S(1)}, f32[3,16,128]{2,1,0:T(8,128)S(1)}, u32[]{:S(2)}, u32[]{:S(2)}) collective-permute-start(f32[3,16,128]{2,1,0:T(8,128)S(1)} %get-tuple-element.32), channel_id=1, source_target_pairs={{0,2},{1,3},{2,0},{3,1},{4,6},{5,7},{6,4},{7,5},{8,10},{9,11},{10,... | collective-permute-start | bytes 73736 | tf_op jit(solution)/shard_map/ppermute | solution.py:571
  62.2 6.1 %collective-permute-start.7 = (f32[3,16,128]{2,1,0:T(8,128)S(1)}, f32[3,16,128]{2,1,0:T(8,128)S(1)}, u32[]{:S(2)}, u32[]{:S(2)}) collective-permute-start(f32[3,16,128]{2,1,0:T(8,128)S(1)} %get-tuple-element.32), channel_id=1, source_target_pairs={{0,4},{1,5},{2,6},{3,7},{4,0},{5,1},{6,2},{7,3},{8,12},{9,13},{10,... | collective-permute-start | bytes 73736 | tf_op jit(solution)/shard_map/ppermute | solution.py:571
  62.4 6.0 %collective-permute-start.8 = (f32[3,16,128]{2,1,0:T(8,128)S(1)}, f32[3,16,128]{2,1,0:T(8,128)S(1)}, u32[]{:S(2)}, u32[]{:S(2)}) collective-permute-start(f32[3,16,128]{2,1,0:T(8,128)S(1)} %get-tuple-element.32), channel_id=1, source_target_pairs={{0,8},{1,9},{2,10},{3,11},{4,12},{5,13},{6,14},{7,15},{8,0},{9,1},... | collective-permute-start | bytes 73736 | tf_op jit(solution)/shard_map/ppermute | solution.py:571
  63.1 7.0 %collective-permute-start.9 = (f32[3,16,128]{2,1,0:T(8,128)S(1)}, f32[3,16,128]{2,1,0:T(8,128)S(1)}, u32[]{:S(2)}, u32[]{:S(2)}) collective-permute-start(f32[3,16,128]{2,1,0:T(8,128)S(1)} %get-tuple-element.32), channel_id=1, source_target_pairs={{0,16},{1,17},{2,18},{3,19},{4,20},{5,21},{6,22},{7,23},{8,24},{9,... | collective-permute-start | bytes 73736 | tf_op jit(solution)/shard_map/ppermute | solution.py:571
  92.0 15.2 %copy-start.5 = (f32[128,128]{1,0:T(8,128)S(1)}, f32[128,128]{1,0:T(8,128)}, u32[]{:S(2)}) copy-start(f32[128,128]{1,0:T(8,128)} %constant.45.clone.matrix_ref) | copy-start | bytes 196612
  92.0 15.2 %all-to-all-start.4 = ((f32[8,4,16,128]{3,2,1,0:T(8,128)}), f32[8,4,16,128]{3,2,1,0:T(8,128)S(1)}, u32[]{:S(2)}, u32[]{:S(2)}) async-start(f32[8,4,16,128]{3,2,1,0:T(8,128)} %shard_map.105), calls=%async_computation.4 | async-start | bytes 524288 | tf_op jit(solution)/shard_map/all_to_all | solution.py:565
  (1 other events, 0.7 us)

commit v3 on v2

v3 whole, which is shorter than its diff:
```python
import functools
import math

import jax
import jax.numpy as jnp
import numpy as np
from jax import lax
from jax.experimental import pallas as pl
from jax.experimental.pallas import tpu as pltpu
from jax.sharding import PartitionSpec as P

ORDER = 8
SIDE = ORDER + 1
NODES = SIDE * SIDE
CYCLE = 32
INNER = (ORDER - 1) ** 2
ROWS = 16
LANES = 128
PLANES = 128
MODES = 8
ELEMS_AXIS = 32
SKEL = 2113
LOW = 256
HIGH = 9
TILES = 2 * HIGH
SLOTS = 384
SLOT_TILES = SLOTS // LANES
BLOCK = 9
SHARE = BLOCK + SLOT_TILES
SCALARS = 5
STEP_ORDER = [4, 5, 7, 2, 6, 3, 1]
SPACING = 0.25
F32 = jnp.float32
BF16 = jnp.bfloat16
HIGHEST = lax.Precision.HIGHEST
VMEM_LIMIT = 32 * 1024 * 1024
FIRST_LIMIT = 56 * 1024 * 1024


def legendre_table(points, poly_order):
    table = np.zeros((points.shape[0], poly_order + 1))
    table[:, 0] = 1.0
    table[:, 1] = points
    for degree in range(2, poly_order + 1):
        table[:, degree] = (
            (2 * degree - 1) * points * table[:, degree - 1] - (degree - 1) * table[:, degree - 2]
        ) / degree
    return table


def lobatto_derivative(poly_order):
    node_count = poly_order + 1
    points = np.cos(np.pi * np.arange(node_count) / poly_order)
    for newton_step in range(100):
        table = legendre_table(points, poly_order)
        points = points - (points * table[:, poly_order] - table[:, poly_order - 1]) / (
            node_count * table[:, poly_order]
        )
    points = np.sort(points)
    top_values = legendre_table(points, poly_order)[:, poly_order]
    identity = np.eye(node_count)
    differ = points[:, None] - points[None, :] + identity
    matrix = top_values[:, None] / (top_values[None, :] * differ)
    matrix = matrix * (1.0 - identity)
    matrix[0, 0] = -poly_order * node_count / 4.0
    matrix[poly_order, poly_order] = poly_order * node_count / 4.0
    return matrix


def fourier_tables():
    positions = np.arange(PLANES)
    phases = ((positions // 2)[:, None] * positions[None, :] % PLANES) * (2.0 * np.pi / PLANES)
    cosine, sine = np.cos(phases), np.sin(phases)
    even = (positions % 2 == 0)[:, None]
    nyquist = (positions == 1)[:, None]
    alternate = (1.0 - 2.0 * (positions % 2))[None, :]
    forward = np.where(nyquist, alternate, np.where(even, cosine, -sine)) / PLANES
    backward = np.where(nyquist, alternate, np.where(even, 2.0 * cosine, -2.0 * sine))
    backward = np.where((positions == 0)[:, None], 1.0, backward)
    return forward.astype(np.float32), backward.T.astype(np.float32)


DERIVATIVE64 = lobatto_derivative(ORDER)
DERIVATIVE = DERIVATIVE64.astype(np.float32)
CYCLE_NODES = (
    [i * SIDE for i in range(SIDE)]
    + [i * SIDE + ORDER for i in range(SIDE)]
    + [j for j in range(1, ORDER)]
    + [ORDER * SIDE + j for j in range(1, ORDER)]
)
INNER_NODES = [i * SIDE + j for i in range(1, ORDER) for j in range(1, ORDER)]


def diagonal_tables():
    squared = (DERIVATIVE * DERIVATIVE).astype(np.float64)
    first = np.kron(squared.T, np.eye(SIDE))
    second = np.kron(np.eye(SIDE), squared.T)
    corner = np.diagonal(DERIVATIVE)
    cross = 2.0 * np.outer(corner, corner).reshape(NODES, 1)
    cross = np.broadcast_to(cross, (NODES, LANES))
    return np.concatenate([first, second], axis=1).astype(np.float32), cross.astype(np.float32)


def helmholtz_shift():
    rows_global = lax.axis_index("mode") * ROWS + lax.broadcasted_iota(jnp.int32, (ROWS, LANES), 0)
    wavenumber = jnp.right_shift(rows_global, 1).astype(F32)
    spanwise = wavenumber * (2.0 * math.pi / (PLANES * SPACING))
    spanwise = jnp.where(rows_global == 1, math.pi / SPACING, spanwise)
    return spanwise * spanwise


def row_block(index):
    return slice(index * ROWS, (index + 1) * ROWS)


def lane_block(index):
    return slice(index * LANES, (index + 1) * LANES)


def pieces(value):
    top = value.astype(BF16).astype(F32)
    return top, value - top


def one_hot_rows(low_rows):
    sublanes = lax.broadcasted_iota(jnp.int32, (LOW, low_rows.shape[1]), 0)
    return jnp.where(low_rows == sublanes, 1.0, 0.0).astype(BF16)


def masked_store(value, high_row, left_ref, column):
    top, rest = pieces(value)
    for high in range(HIGH):
        here = high_row == high
        left_ref[row_block(high), lane_block(column)] = jnp.where(here, top, 0.0).astype(BF16)
        left_ref[row_block(HIGH + high), lane_block(column)] = jnp.where(here, rest, 0.0).astype(BF16)


def scatter_sum(left, selectors):
    contract = (((1,), (1,)), ((), ()))
    both = lax.dot_general(left, selectors, contract, preferred_element_type=F32)
    return both[: HIGH * ROWS] + both[HIGH * ROWS :]


def one_hot_cycle(edge_rows, selectors_ref):
    low = jnp.bitwise_and(edge_rows, LOW - 1)
    for slot in range(CYCLE):
        selectors_ref[:, lane_block(slot)] = one_hot_rows(low[slot : slot + 1, :])


def scatter_cycle(load, edge_rows, left_ref, selectors_ref):
    high_rows = jnp.right_shift(edge_rows, 8)
    for slot in range(CYCLE):
        masked_store(load(slot), high_rows[slot : slot + 1, :], left_ref, slot)
    return scatter_sum(left_ref[...], selectors_ref[...])


def slot_selectors(shared_rows):
    low = jnp.bitwise_and(shared_rows, LOW - 1)
    return jnp.concatenate(
        [one_hot_rows(low[tile : tile + 1, :]) for tile in range(SLOT_TILES)], axis=1
    )


def four_pieces(first, second):
    sublanes = lax.broadcasted_iota(jnp.int32, (ROWS, first.shape[1]), 0)
    first_top, first_rest = pieces(first)
    second_top, second_rest = pieces(second)
    rest = jnp.where(sublanes == 2, first_rest, jnp.where(sublanes == 3, second_rest, 0.0))
    return jnp.where(sublanes == 0, first_top, jnp.where(sublanes == 1, second_top, rest))


def masked_store_four(value, high_row, left_ref, column):
    for high in range(HIGH):
        part = jnp.where(high_row == high, value, 0.0).astype(BF16)
        left_ref[row_block(high), lane_block(column)] = part


def two_rows(total, high):
    base = high * ROWS
    first = total[base : base + 1, :] + total[base + 2 : base + 3, :]
    second = total[base + 1 : base + 2, :] + total[base + 3 : base + 4, :]
    return first, second


def scatter_slots(load, shared_rows, left_ref, right):
    high_rows = jnp.right_shift(shared_rows, 8)
    for tile in range(SLOT_TILES):
        masked_store(load(tile), high_rows[tile : tile + 1, :], left_ref, tile)
    return scatter_sum(left_ref[:, :SLOTS], right)


def stack_pieces(skeleton):
    top, rest = pieces(skeleton)
    return jnp.concatenate([top.astype(BF16), rest.astype(BF16)], axis=0)


def gather_tile(stacked, rows, keep=None):
    low = jnp.bitwise_and(rows, LOW - 1)
    high = jnp.right_shift(rows, 8)
    selector = one_hot_rows(low)
    if keep is not None:
        keep(selector)
    found = jnp.dot(stacked, selector, preferred_element_type=F32)
    total = None
    for index in range(HIGH):
        part = found[row_block(index), :] + found[row_block(HIGH + index), :]
        part = jnp.where(high == index, part, 0.0)
        total = part if total is None else total + part
    return total


def keep_columns(selectors_ref, column, selector):
    selectors_ref[:, column * LANES : (column + 2) * LANES] = selector


def gather_cycle(skeleton, edge_rows, store, selectors_ref=None):
    stacked = stack_pieces(skeleton)
    for pair in range(CYCLE // 2):
        rows = jnp.concatenate(
            [edge_rows[2 * pair : 2 * pair + 1, :], edge_rows[2 * pair + 1 : 2 * pair + 2, :]], axis=1
        )
        keep = None
        if selectors_ref is not None:
            keep = functools.partial(keep_columns, selectors_ref, 2 * pair)
        total = gather_tile(stacked, rows, keep)
        store(2 * pair, total[:, :LANES])
        store(2 * pair + 1, total[:, LANES:])


def gather_slots(skeleton, shared_rows):
    stacked = stack_pieces(skeleton)
    return [gather_tile(stacked, shared_rows[tile : tile + 1, :]) for tile in range(SLOT_TILES)]


def sent_place(index):
    return index // BLOCK, index % BLOCK


def read_skeleton(load):
    return jnp.concatenate(
        [jnp.concatenate([load(2 * high), load(2 * high + 1)], axis=1) for high in range(HIGH)], axis=0
    )


def write_skeleton(skeleton, store):
    for high in range(HIGH):
        store(2 * high, skeleton[row_block(high), :LANES])
        store(2 * high + 1, skeleton[row_block(high), LANES:])


def write_place(ref, place):
    def store(index, value):
        block, row = place(index)
        ref[block, row] = value

    return store


def fold(value):
    return value[:, :LANES] + value[:, LANES:]


def per_tile(penalty_ref):
    return jnp.concatenate(
        [jnp.broadcast_to(penalty_ref[high : high + 1, :], (ROWS, LOW)) for high in range(HIGH)], axis=0
    )


def skeleton_sum(product):
    total = None
    for high in range(HIGH):
        part = fold(product[row_block(high), :])
        total = part if total is None else total + part
    return total


def select_arrived(masks, tile, arrived):
    chosen = arrived[0]
    row = masks[tile : tile + 1, :]
    for level in range(1, len(arrived)):
        moving = jnp.bitwise_and(jnp.right_shift(row, level), 1) == 1
        chosen = jnp.where(moving, arrived[level], chosen)
    return chosen


def weighted_sum(weights, values):
    total = None
    for weight, value in zip(weights, values):
        if weight == 0.0:
            continue
        part = float(weight) * value
        total = part if total is None else total + part
    return total


def derivative_line(values, transposed):
    matrix = DERIVATIVE64.T if transposed else DERIVATIVE64
    half = SIDE // 2
    evens = [values[k] + values[ORDER - k] for k in range(half)] + [values[half]]
    odds = [values[k] - values[ORDER - k] for k in range(half)]
    results = [None] * SIDE
    for out in range(half):
        near, far = matrix[out, :half], matrix[out, :half:-1]
        even = weighted_sum(np.float32(np.append(0.5 * (near + far), matrix[out, half])), evens)
        odd = weighted_sum(np.float32(0.5 * (near - far)), odds)
        results[out] = odd + even
        results[ORDER - out] = odd - even
    results[half] = weighted_sum(np.float32(matrix[half, :half]), odds)
    return results


def gradients(cells_ref, first_ref, metric_ref, rows, visit):
    for j in range(SIDE):
        line = derivative_line([cells_ref[k * SIDE + j, rows, :] for k in range(SIDE)], False)
        for i in range(SIDE):
            first_ref[i * SIDE + j] = line[i]
    for i in range(SIDE):
        line = derivative_line([cells_ref[i * SIDE + k, rows, :] for k in range(SIDE)], False)
        seconds = []
        for j in range(SIDE):
            node = i * SIDE + j
            m0, m1, m2 = [metric_ref[node, c : c + 1, :] for c in range(3)]
            g1, g2 = first_ref[node], line[j]
            p1 = m0 * g1 + m2 * g2
            p2 = m2 * g1 + m1 * g2
            visit(node, g1, g2, p1, p2)
            seconds.append(p2)
        yield i, seconds


def apply_operator(cells_ref, result_ref, first_ref, energy_ref, metric_ref, shift_ref):
    @pl.loop(0, 2)
    def half(part):
        rows = pl.ds(pl.multiple_of(part * 8, 8), 8)
        shift = shift_ref[rows, :]

        def visit(node, g1, g2, p1, p2):
            first_ref[node] = p1

        for i, seconds in gradients(cells_ref, first_ref, metric_ref, rows, visit):
            line = derivative_line(seconds, True)
            for j in range(SIDE):
                node = i * SIDE + j
                mass = shift * metric_ref[node, 3:4, :]
                result_ref[node, rows, :] = line[j] + mass * cells_ref[node, rows, :]
        energy = jnp.zeros((8, LANES), F32)
        for j in range(SIDE):
            line = derivative_line([first_ref[k * SIDE + j] for k in range(SIDE)], True)
            for i in range(SIDE):
                node = i * SIDE + j
                value = result_ref[node, rows, :] + line[i]
                result_ref[node, rows, :] = value
                energy = energy + value * cells_ref[node, rows, :]
        energy_ref[rows, :] = energy


def apply_energy(cells_ref, first_ref, energy_ref, metric_ref, shift_ref):
    @pl.loop(0, 2)
    def half(part):
        rows = pl.ds(pl.multiple_of(part * 8, 8), 8)
        shift = shift_ref[rows, :]
        sums = [jnp.zeros((8, LANES), F32)]

        def visit(node, g1, g2, p1, p2):
            value = cells_ref[node, rows, :]
            mass = shift * metric_ref[node, 3:4, :]
            sums[0] = sums[0] + (g1 * p1 + g2 * p2 + mass * value * value)

        for i, seconds in gradients(cells_ref, first_ref, metric_ref, rows, visit):
            pass
        energy_ref[rows, :] = sums[0]


def diagonal_slots(
    metric_ref, table_ref, cross_ref, penalty_ref, edge_rows, shared_rows, right_ref,
    inner_ref, skeleton_ref, padded_ref, cells_ref, left_ref,
):
    both = jnp.concatenate([metric_ref[:, 0, :], metric_ref[:, 1, :]], axis=0)
    terms = jnp.dot(table_ref[...], both, precision=HIGHEST, preferred_element_type=F32)
    cells_ref[0] = terms + cross_ref[...] * metric_ref[:, 2, :]
    cells_ref[1] = metric_ref[:, 3, :]
    padded_ref[...] = jnp.ones((HIGH, LOW), F32)
    for high in range(HIGH):
        count = min(LOW, SKEL - high * LOW)
        line = penalty_ref[pl.ds(high * LOW, count)]
        padded_ref[high : high + 1, :count] = line.reshape(1, count)
    for index, node in enumerate(INNER_NODES):
        inner_ref[0, index : index + 1, :] = cells_ref[0, node : node + 1, :]
        inner_ref[1, index : index + 1, :] = cells_ref[1, node : node + 1, :]
    high_rows = jnp.right_shift(edge_rows, 8)
    for slot in range(CYCLE):
        node = CYCLE_NODES[slot]
        value = four_pieces(cells_ref[0, node : node + 1, :], cells_ref[1, node : node + 1, :])
        masked_store_four(value, high_rows[slot : slot + 1, :], left_ref, slot)
    contract = (((1,), (1,)), ((), ()))
    total = lax.dot_general(
        left_ref[: HIGH * ROWS, :], right_ref[...], contract, preferred_element_type=F32
    )
    stacked = []
    for high in range(HIGH):
        laplace, mass = two_rows(total, high)
        laplace = laplace + padded_ref[high : high + 1, :]
        skeleton_ref[0, high : high + 1, :] = laplace
        skeleton_ref[1, high : high + 1, :] = mass
        stacked.append(four_pieces(laplace, mass).astype(BF16))
    stacked = jnp.concatenate(stacked, axis=0)
    results = []
    for tile in range(SLOT_TILES):
        rows = shared_rows[tile : tile + 1, :]
        low = jnp.bitwise_and(rows, LOW - 1)
        high_row = jnp.right_shift(rows, 8)
        found = jnp.dot(stacked, one_hot_rows(low), preferred_element_type=F32)
        value = jnp.zeros((ROWS, LANES), F32)
        for high in range(HIGH):
            value = value + jnp.where(high_row == high, found[row_block(high), :], 0.0)
        results.append(two_rows(value, 0))
    return results


def pack_kernel(
    forcing_hbm, edge_hbm, shared_hbm, metric_hbm, penalty_hbm, table_hbm, cross_hbm,
    out_hbm, message_hbm, inner_hbm, skeleton_hbm, padded_hbm,
    forcing_ref, edge_ref, shared_ref, metric_ref, penalty_ref, table_ref, cross_ref,
    packed_ref, message_ref, inner_ref, skeleton_ref, padded_ref,
    cells_ref, left_ref, right_ref, in_semaphores, out_semaphores,
):
    ins = [
        pltpu.make_async_copy(source, target, in_semaphores.at[index])
        for index, (source, target) in enumerate(
            [
                (edge_hbm, edge_ref), (shared_hbm, shared_ref), (forcing_hbm, forcing_ref),
                (metric_hbm, metric_ref), (table_hbm, table_ref), (cross_hbm, cross_ref),
                (penalty_hbm, penalty_ref),
            ]
        )
    ]
    for copy in ins:
        copy.start()
    outs = []

    def send(source, target):
        copy = pltpu.make_async_copy(source, target, out_semaphores.at[len(outs)])
        copy.start()
        outs.append(copy)

    width = ORDER - 1
    for index in range(TILES, MODES * BLOCK - INNER):
        packed_ref[index] = jnp.zeros((ROWS, LANES), F32)
    ins[0].wait()
    edge_rows = edge_ref[...]
    one_hot_cycle(edge_rows, right_ref)
    ins[1].wait()
    shared_rows = shared_ref[...]
    ins[2].wait()
    for line in range(width):
        send(forcing_ref.at[pl.ds((line + 1) * SIDE + 1, width)], out_hbm.at[pl.ds(line * width, width)])
    for copy in ins[3:]:
        copy.wait()
    pairs = diagonal_slots(
        metric_ref, table_ref, cross_ref, penalty_ref, edge_rows, shared_rows, right_ref,
        inner_ref, skeleton_ref, padded_ref, cells_ref, left_ref,
    )
    send(inner_ref, inner_hbm)
    send(skeleton_ref, skeleton_hbm)
    send(padded_ref, padded_hbm)
    skeleton = scatter_cycle(lambda slot: forcing_ref[CYCLE_NODES[slot]], edge_rows, left_ref, right_ref)

    def store(index, value):
        packed_ref[index] = value

    write_skeleton(skeleton, store)
    send(packed_ref, out_hbm.at[pl.ds(INNER, MODES * BLOCK - INNER)])
    for tile, value in enumerate(gather_slots(skeleton, shared_rows)):
        laplace, mass = pairs[tile]
        message_ref[tile, :ROWS, :] = value
        message_ref[tile, ROWS:, :] = jnp.zeros((8, LANES), F32)
        message_ref[tile, ROWS : ROWS + 1, :] = laplace
        message_ref[tile, ROWS + 1 : ROWS + 2, :] = mass
    send(message_ref, message_hbm)
    for copy in outs:
        copy.wait()


def place(index):
    return pl.ds(pl.multiple_of(index * ROWS, ROWS), ROWS)


def relative_rows(matrix_ref, mode):
    parts = [matrix_ref[place(jnp.bitwise_xor(mode, step)), :] for step in range(MODES)]
    return jnp.concatenate(parts, axis=0)


def transform_kernel(
    matrix_ref, in_ref, a0, a1, a2, a3, a4, masks_ref, o0, o1, o2, o3, o4, o5, o6, o7, extra_ref, slots_ref
):
    mode = lax.axis_index("mode")
    outs = [o0, o1, o2, o3, o4, o5, o6, o7]
    matrix = relative_rows(matrix_ref, mode)
    slots_ref[...] = jnp.zeros(slots_ref.shape, F32)
    arrived_refs = [a0, a1, a2, a3, a4]
    masks = masks_ref[...]
    for index in range(BLOCK):
        block = in_ref[:, index].reshape(PLANES, LANES)
        mixed = jnp.dot(matrix, block, precision=HIGHEST, preferred_element_type=F32)
        for step, out_ref in enumerate(outs):
            out_ref[index] = mixed[row_block(step), :]
    for tile in range(SLOT_TILES):
        chosen = select_arrived(masks, tile, [ref[tile] for ref in arrived_refs])
        slots_ref[tile, place(mode), :] = chosen[:ROWS]
        mixed = jnp.dot(matrix, slots_ref[tile], precision=HIGHEST, preferred_element_type=F32)
        for step, out_ref in enumerate(outs):
            out_ref[BLOCK + tile] = mixed[row_block(step), :]
        extra_ref[tile] = chosen[ROWS:]


def first_kernel(
    i4, i5, i7, i2, i6, i3, i1, i0, extra_ref, shared_ref, edge_ref, metric_ref,
    inner_ref, diagonal_ref, penalty_ref, search_ref, change_ref, kept_ref, slots_ref, sums_ref,
    left_ref, right_ref, source_ref, cells_ref, result_ref, first_ref, energy_ref, shift_ref,
):
    mode = lax.axis_index("mode")
    ins = [i0, i1, i2, i3, i4, i5, i6, i7]
    for step, in_ref in enumerate(ins):
        source_ref[jnp.bitwise_xor(mode, step)] = in_ref[:BLOCK]
    shared_rows = shared_ref[...]
    right_slots = slot_selectors(shared_rows)
    shift = helmholtz_shift()
    shift_ref[...] = shift
    edge_rows = edge_ref[...]

    def load_right(tile):
        total = ins[0][BLOCK + tile]
        for in_ref in ins[1:]:
            total = total + in_ref[BLOCK + tile]
        return total

    def source(index):
        block, row = sent_place(index)
        return source_ref[block, row]

    high_rows = jnp.right_shift(shared_rows, 8)
    for tile in range(SLOT_TILES):
        value = four_pieces(extra_ref[tile, 0:1, :], extra_ref[tile, 1:2, :])
        masked_store_four(value, high_rows[tile : tile + 1, :], left_ref, tile)
    contract = (((1,), (1,)), ((), ()))
    added = lax.dot_general(
        left_ref[: HIGH * ROWS, :SLOTS], right_slots, contract, preferred_element_type=F32
    )
    wide_shift = jnp.concatenate([shift, shift], axis=1)
    parts = []
    for high in range(HIGH):
        laplace, mass = two_rows(added, high)
        laplace = laplace + diagonal_ref[0, high : high + 1, :]
        mass = mass + diagonal_ref[1, high : high + 1, :]
        parts.append(1.0 / (laplace + wide_shift * mass))
    inverse = jnp.concatenate(parts, axis=0)
    local = read_skeleton(lambda index: source(INNER + index))
    right_side = local + scatter_slots(load_right, shared_rows, left_ref, right_slots)
    search = right_side * inverse
    kept_ref[0] = local
    kept_ref[1] = inverse
    kept_ref[2] = search
    start = skeleton_sum(local * search)
    for index, node in enumerate(INNER_NODES):
        value = source(index)
        inverted = 1.0 / (inner_ref[0, index : index + 1, :] + shift * inner_ref[1, index : index + 1, :])
        scaled = value * inverted
        search_ref[index] = scaled
        change_ref[index] = inverted
        cells_ref[node] = scaled
        start = start + value * scaled

    def store(slot, value):
        cells_ref[CYCLE_NODES[slot]] = value

    gather_cycle(search, edge_rows, store, right_ref)
    apply_operator(cells_ref, result_ref, first_ref, energy_ref, metric_ref, shift_ref)
    weighted = per_tile(penalty_ref) * search
    applied = weighted + scatter_cycle(
        lambda slot: result_ref[CYCLE_NODES[slot]], edge_rows, left_ref, right_ref
    )
    kept_ref[3] = applied
    for tile, value in enumerate(gather_slots(applied, shared_rows)):
        slots_ref[tile] = value
    crossed = jnp.zeros((ROWS, LANES), F32)
    sourced = jnp.zeros((ROWS, LANES), F32)
    for index, node in enumerate(INNER_NODES):
        value = result_ref[node]
        moved = value * change_ref[index] - cells_ref[node]
        change_ref[index] = moved
        crossed = crossed + value * moved
        sourced = sourced + source(index) * moved
    sums_ref[0] = energy_ref[...] + skeleton_sum(weighted * search)
    sums_ref[1] = crossed
    sums_ref[2] = start
    sums_ref[3] = sourced


def second_kernel(
    moved_ref, kept_ref, sums_ref, a0, a1, a2, a3, a4, masks_ref, shared_ref, edge_ref,
    metric_ref, penalty_ref, change_ref, message_ref, left_ref, cells_ref, first_ref, energy_ref, shift_ref,
):
    arrived_refs = [a0, a1, a2, a3, a4]
    masks = masks_ref[...]
    shared_rows = shared_ref[...]
    shift_ref[...] = helmholtz_shift()

    def load(tile):
        return select_arrived(masks, tile, [ref[tile] for ref in arrived_refs])

    local, inverse, search, applied = [kept_ref[index] for index in range(4)]
    full = applied + scatter_slots(load, shared_rows, left_ref, slot_selectors(shared_rows))
    change = full * inverse - search
    change_ref[...] = change
    crossed = sums_ref[1] + skeleton_sum(applied * change)
    sourced = sums_ref[3] + skeleton_sum(local * change)
    for index, node in enumerate(INNER_NODES):
        cells_ref[node] = moved_ref[index]

    def store(slot, value):
        cells_ref[CYCLE_NODES[slot]] = value

    gather_cycle(change, edge_ref[...], store)
    apply_energy(cells_ref, first_ref, energy_ref, metric_ref, shift_ref)
    energy = energy_ref[...] + skeleton_sum(per_tile(penalty_ref) * change * change)
    sublanes = lax.broadcasted_iota(jnp.int32, (ROWS, LANES), 0)
    lanes = lax.broadcasted_iota(jnp.int32, (ROWS, LANES), 1)
    spread = jnp.zeros((ROWS, LANES), F32)
    for index, value in enumerate([sums_ref[0], crossed, energy, sums_ref[2], sourced]):
        column = jnp.sum(value, axis=1, keepdims=True)
        spread = jnp.where(lanes == sublanes + index * ROWS, column, spread)
    message = jnp.sum(spread, axis=0, keepdims=True)
    message_ref[...] = jnp.broadcast_to(message, message_ref.shape)


def scale_kernel(
    scalars_ref, inner_ref, moved_ref, kept_ref, change_ref, o0, o1, o2, o3, o4, o5, o6, o7, packed_ref
):
    sublanes = lax.broadcasted_iota(jnp.int32, (ROWS, LANES), 0)
    lanes = lax.broadcasted_iota(jnp.int32, (ROWS, LANES), 1)
    total = jnp.sum(scalars_ref[...], axis=0, keepdims=True)
    g00, g01, g11, h0, h1 = [
        jnp.sum(jnp.where(lanes == sublanes + index * ROWS, total, 0.0), axis=1, keepdims=True)
        for index in range(SCALARS)
    ]
    ratio = g01 / g00
    pivot = g11 - ratio * g01
    second = jnp.where(pivot > 0.0, (h1 - ratio * h0) / pivot, 0.0)
    first = jnp.broadcast_to(h0 / g00 - ratio * second, (ROWS, LANES))
    second = jnp.broadcast_to(second, (ROWS, LANES))
    store = write_place(packed_ref, sent_place)
    for index in range(INNER):
        store(index, first * inner_ref[index] + second * moved_ref[index])
    for high in range(HIGH):
        for part in range(2):
            place = (row_block(high), lane_block(part))
            value = first * kept_ref[(2,) + place] + second * change_ref[place]
            store(INNER + 2 * high + part, value)
    for index in range(INNER + TILES, MODES * BLOCK):
        store(index, jnp.zeros((ROWS, LANES), F32))
    mode = lax.axis_index("mode")
    for step, out_ref in enumerate([o0, o1, o2, o3, o4, o5, o6, o7]):
        out_ref[...] = packed_ref[jnp.bitwise_xor(mode, step)]


def combine_kernel(
    matrix_ref, i4, i5, i7, i2, i6, i3, i1, i0, o0, o1, o2, o3, o4, o5, o6, o7, block_ref
):
    mode = lax.axis_index("mode")
    for step, in_ref in enumerate([i0, i1, i2, i3, i4, i5, i6, i7]):
        block_ref[:, place(jnp.bitwise_xor(mode, step)), :] = in_ref[...]
    matrix = relative_rows(matrix_ref, mode)
    for index in range(BLOCK):
        mixed = jnp.dot(matrix, block_ref[index], precision=HIGHEST, preferred_element_type=F32)
        for step, out_ref in enumerate([o0, o1, o2, o3, o4, o5, o6, o7]):
            out_ref[index] = mixed[row_block(step), :]


def unpack_kernel(i4, i5, i7, i2, i6, i3, i1, i0, edge_ref, out_ref, packed_ref):
    mode = lax.axis_index("mode")
    for step, in_ref in enumerate([i0, i1, i2, i3, i4, i5, i6, i7]):
        packed_ref[jnp.bitwise_xor(mode, step)] = in_ref[...]

    def load(index):
        block, row = sent_place(index)
        return packed_ref[block, row]

    for index, node in enumerate(INNER_NODES):
        out_ref[node] = load(index)

    def store(slot, value):
        out_ref[CYCLE_NODES[slot]] = value

    gather_cycle(read_skeleton(lambda index: load(INNER + index)), edge_ref[...], store)


def call(kernel, out_shapes, scratch, *operands, limit=VMEM_LIMIT, **options):
    return pl.pallas_call(
        kernel,
        out_shape=out_shapes,
        scratch_shapes=scratch,
        compiler_params=pltpu.CompilerParams(vmem_limit_bytes=limit),
        **options,
    )(*operands)


def shape(*dims, dtype=F32):
    return jax.ShapeDtypeStruct(dims, dtype)


def swap_blocks(blocks, axis):
    return lax.all_to_all(blocks, axis, split_axis=0, concat_axis=0, tiled=True)


def permute(value, axis, flip):
    return lax.ppermute(value, axis, [(i, i ^ flip) for i in range(lax.axis_size(axis))])


def swap_steps(blocks):
    return [permute(blocks[step], "mode", step) for step in STEP_ORDER] + [blocks[0]]


def exchange(slots):
    levels = lax.axis_size("elem").bit_length() - 1
    return [permute(slots, "elem", 1 << level) for level in range(levels)]


def body(forcing, metric, edge_map, shared_rows, partner_masks, penalty):
    forward, backward = [jnp.asarray(part) for part in fourier_tables()]
    table, cross = [jnp.asarray(part) for part in diagonal_tables()]
    metric = metric.transpose(1, 0, 2)
    edge_rows = edge_map.T
    shared = shared_rows.reshape(SLOT_TILES, LANES)
    masks = partner_masks.reshape(SLOT_TILES, LANES)
    left = pltpu.VMEM((2 * HIGH * ROWS, CYCLE * LANES), BF16)
    right = pltpu.VMEM((LOW, CYCLE * LANES), BF16)
    left_slots = pltpu.VMEM((2 * HIGH * ROWS, SLOTS), BF16)
    cells = pltpu.VMEM((NODES, ROWS, LANES), F32)
    first = pltpu.VMEM((NODES, 8, LANES), F32)
    energy = pltpu.VMEM((ROWS, LANES), F32)
    packing = pltpu.VMEM((MODES, BLOCK, ROWS, LANES), F32)
    wide = (HIGH * ROWS, LOW)
    blocks = [shape(BLOCK, ROWS, LANES)] * MODES

    hbm = pl.BlockSpec(memory_space=pltpu.HBM)
    packed_shapes = [
        shape(MODES * BLOCK, ROWS, LANES), shape(SLOT_TILES, ROWS + 8, LANES),
        shape(2, INNER, LANES), shape(2, HIGH, LOW), shape(HIGH, LOW),
    ]
    operands = [forcing.transpose(1, 0, 2), edge_rows, shared, metric, penalty, table, cross]
    packed, message, inner, diagonal, penalties = call(
        pack_kernel, packed_shapes,
        [pltpu.VMEM(operand.shape, operand.dtype) for operand in operands]
        + [pltpu.VMEM((MODES * BLOCK - INNER, ROWS, LANES), F32)]
        + [pltpu.VMEM(part.shape, part.dtype) for part in packed_shapes[1:]]
        + [
            pltpu.VMEM((2, NODES, LANES), F32), left, right,
            pltpu.SemaphoreType.DMA((len(operands),)), pltpu.SemaphoreType.DMA((ORDER + 4,)),
        ],
        *operands,
        in_specs=[hbm] * len(operands), out_specs=[hbm] * len(packed_shapes), limit=FIRST_LIMIT,
    )
    gathered = swap_blocks(packed.reshape(MODES, BLOCK, ROWS, LANES), "mode")
    *mixed, extra = call(
        transform_kernel, [shape(SHARE, ROWS, LANES)] * MODES + [shape(SLOT_TILES, 8, LANES)],
        [pltpu.VMEM((SLOT_TILES, PLANES, LANES), F32)], forward, gathered, *exchange(message), masks,
    )
    search, moved, kept, slots, sums = call(
        first_kernel,
        [
            shape(INNER, ROWS, LANES), shape(INNER, ROWS, LANES), shape(4, *wide),
            shape(SLOT_TILES, ROWS, LANES), shape(4, ROWS, LANES),
        ],
        [left, right, packing, cells, cells, first, energy, energy],
        *swap_steps(mixed), extra, shared, edge_rows, metric, inner, diagonal, penalties,
    )
    change, message = call(
        second_kernel,
        [shape(*wide), shape(ELEMS_AXIS, LANES)],
        [left_slots, cells, first, energy, energy],
        moved, kept, sums, *exchange(slots), masks, shared, edge_rows, metric, penalties,
    )
    scalars = swap_blocks(message, "elem")
    scaled = call(scale_kernel, blocks, [packing], scalars, search, moved, kept, change)
    mixed = call(
        combine_kernel, blocks, [pltpu.VMEM((BLOCK, PLANES, LANES), F32)], backward, *swap_steps(scaled)
    )
    result = call(unpack_kernel, shape(NODES, ROWS, LANES), [packing], *swap_steps(mixed), edge_rows)
    return result.transpose(1, 0, 2)


def solution(mesh):
    placed = (
        P("mode", None, "elem"),
        P(None, None, "elem"),
        P("elem", None),
        P("elem"),
        P("elem"),
        P("elem"),
    )
    return jax.shard_map(
        body, mesh=mesh, in_specs=placed, out_specs=P("mode", None, "elem"), check_vma=False
    )
```

time: 124 us -> 103 us (0.83)
  blocking collectives: 30.1 us -> 14.5 us
  starting transfers between devices: 45.7 us -> 55.2 us
  waiting for transfers between devices: 24.3 us -> 15.3 us
  local copies, waits for them, and re-layouts: 4.23 us -> 0.68 us
  Pallas kernels: 19.3 us -> 16.5 us
    ppermute x10 -> x31, starting transfers between devices: 19.2 us -> 48.4 us  [permute(): lax.ppermute(value, axis, [(i, i ^ flip) for i in range(lax.axis_size(axi...]
    all_to_all x4 -> x1, waiting for transfers between devices: 19.8 us -> 0.01 us  [swap_blocks(): return lax.all_to_all(blocks, axis, split_axis=0, concat_axis=0, tiled=True)]
    all_to_all x4 -> x1, starting transfers between devices: 26.5 us -> 6.82 us  [swap_blocks(): return lax.all_to_all(blocks, axis, split_axis=0, concat_axis=0, tiled=True)]
    all_to_all x2 -> x1, blocking collectives: 30.1 us -> 14.5 us  [swap_blocks(): return lax.all_to_all(blocks, axis, split_axis=0, concat_axis=0, tiled=True)]
    ppermute x10 -> x31, waiting for transfers between devices: 4.45 us -> 15.3 us  [permute(): lax.ppermute(value, axis, [(i, i ^ flip) for i in range(lax.axis_size(axi...]
    unnamed x23 -> x20, local copies, waits for them, and re-layouts: 3.96 us -> 0.68 us
    pallas_call x8 -> x7, Pallas kernels: 19.3 us -> 16.5 us  [call(): pl.pallas_call(kernel, out_shape=out_shapes, scratch_shapes=scratch, comp...]
  transfers between devices with their start and end apart: 14 -> 32, of which waited for: 5 -> 13; matrix products, arithmetic and copies ran while one was open for 0% -> 0% of each run, Pallas kernels for 4% -> 0%
where the time goes in v3:
time: 103 us; the launch traced here: 102 us
  starting transfers between devices  55.2 us (54%)
  Pallas kernels  16.5 us (16%)
  waiting for transfers between devices  15.3 us (15%)
  blocking collectives  14.5 us (14%)
    ppermute x31, starting transfers between devices, permute(): lax.ppermute(value, axis, [(i, i ^ flip) for i in range(lax.axis_size(axi...  48.4 us
    pallas_call x7, Pallas kernels, call(): pl.pallas_call(kernel, out_shape=out_shapes, scratch_shapes=scratch, comp...  16.5 us
    ppermute x31, waiting for transfers between devices, permute(): lax.ppermute(value, axis, [(i, i ^ flip) for i in range(lax.axis_size(axi...  15.3 us
    all_to_all x1, blocking collectives, swap_blocks(): return lax.all_to_all(blocks, axis, split_axis=0, concat_axis=0, tiled=True)  14.5 us
    all_to_all x1, starting transfers between devices, swap_blocks(): return lax.all_to_all(blocks, axis, split_axis=0, concat_axis=0, tiled=True)  6.82 us
  transfers between devices with their start and end apart: 32, of which 13 were waited for; matrix products, arithmetic and copies ran while one was open for 0% of the time, Pallas kernels for 0%

profile of v3, /device:TPU:1, one launch (start us, length us, event | category | flops | bytes accessed | tf_op | source)
XLA Modules:
  0.0 102.3 jit_solution(11365187777979639427)
XLA Ops:
  0.0 5.6 %shard_map.100 = (f32[72,16,128]{2,1,0:T(8,128)}, f32[3,24,128]{2,1,0:T(8,128)}, f32[2,49,128]{2,1,0:T(8,128)}, f32[2,9,256]{2,1,0:T(8,128)}, f32[9,256]{1,0:T(8,128)}) custom-call(f32[81,16,128]{2,1,0:T(8,128)} %bitcast.25, s32[32,128]{1,0:T(8,128)} %bitcast.14, s32[3,128]{1,0:T(4,128)} %bitcast.19, f32[81,4,128]{2,1,0:T(4,128)} %bitcast.11, ...), custom_call_target="tpu_custom_call" | custom-call | tf_op jit(solution)/shard_map/pallas_call | solution.py:698
  5.6 6.8 %all-to-all-start = ((f32[8,9,16,128]{3,2,1,0:T(8,128)}), f32[8,9,16,128]{3,2,1,0:T(8,128)S(1)}, u32[]{:S(2)}, u32[]{:S(2)}) async-start(f32[8,9,16,128]{3,2,1,0:T(8,128)} %bitcast.26), calls=%async_computation | async-start | bytes 1179648 | tf_op jit(solution)/shard_map/all_to_all | solution.py:712
  12.4 6.1 %collective-permute-start.4 = (f32[3,24,128]{2,1,0:T(8,128)S(1)}, f32[3,24,128]{2,1,0:T(8,128)S(1)}, u32[]{:S(2)}, u32[]{:S(2)}) collective-permute-start(f32[3,24,128]{2,1,0:T(8,128)S(1)} %copy-done.9), channel_id=1, source_target_pairs={{0,16},{1,17},{2,18},{3,19},{4,20},{5,21},{6,22},{7,23},{8,24},{9,... | collective-permute-start | bytes 110600 | tf_op jit(solution)/shard_map/ppermute | solution.py:716
  20.5 2.9 %collective-permute-start.1 = (f32[3,24,128]{2,1,0:T(8,128)S(1)}, f32[3,24,128]{2,1,0:T(8,128)S(1)}, u32[]{:S(2)}, u32[]{:S(2)}) collective-permute-start(f32[3,24,128]{2,1,0:T(8,128)S(1)} %copy-done.9), channel_id=1, source_target_pairs={{0,2},{1,3},{2,0},{3,1},{4,6},{5,7},{6,4},{7,5},{8,10},{9,11},{10,... | collective-permute-start | bytes 110600 | tf_op jit(solution)/shard_map/ppermute | solution.py:716
  24.8 1.6 %collective-permute-done.a0 = f32[3,24,128]{2,1,0:T(8,128)S(1)} collective-permute-done((f32[3,24,128]{2,1,0:T(8,128)S(1)}, f32[3,24,128]{2,1,0:T(8,128)S(1)}, u32[]{:S(2)}, u32[]{:S(2)}) %collective-permute-start) | collective-permute-done | bytes 36896 | tf_op jit(solution)/shard_map/ppermute | solution.py:716
  27.3 3.1 %collective-permute-start.5 = (f32[12,16,128]{2,1,0:T(8,128)S(1)}, f32[12,16,128]{2,1,0:T(8,128)S(1)}, u32[]{:S(2)}, u32[]{:S(2)}) collective-permute-start(f32[12,16,128]{2,1,0:T(8,128)S(1)} %get-tuple-element.44), channel_id=1, source_target_pairs={{0,128},{32,160},{64,192},{96,224},{128,0},{160,32},{192,64},{224,... | collective-permute-start | bytes 294920 | tf_op jit(solution)/shard_map/ppermute | solution.py:716
  30.4 2.3 %collective-permute-start.6 = (f32[12,16,128]{2,1,0:T(8,128)S(1)}, f32[12,16,128]{2,1,0:T(8,128)S(1)}, u32[]{:S(2)}, u32[]{:S(2)}) collective-permute-start(f32[12,16,128]{2,1,0:T(8,128)S(1)} %get-tuple-element.45), channel_id=1, source_target_pairs={{0,160},{32,128},{64,224},{96,192},{128,32},{160,0},{192,96},{224,... | collective-permute-start | bytes 294920 | tf_op jit(solution)/shard_map/ppermute | solution.py:716
  34.3 1.8 %collective-permute-start.9 = (f32[12,16,128]{2,1,0:T(8,128)S(1)}, f32[12,16,128]{2,1,0:T(8,128)S(1)}, u32[]{:S(2)}, u32[]{:S(2)}) collective-permute-start(f32[12,16,128]{2,1,0:T(8,128)S(1)} %get-tuple-element.48), channel_id=1, source_target_pairs={{0,192},{32,224},{64,128},{96,160},{128,64},{160,96},{192,0},{224,... | collective-permute-start | bytes 294920 | tf_op jit(solution)/shard_map/ppermute | solution.py:716
  36.1 1.5 %collective-permute-start.10 = (f32[12,16,128]{2,1,0:T(8,128)S(1)}, f32[12,16,128]{2,1,0:T(8,128)S(1)}, u32[]{:S(2)}, u32[]{:S(2)}) collective-permute-start(f32[12,16,128]{2,1,0:T(8,128)S(1)} %get-tuple-element.49), channel_id=1, source_target_pairs={{0,96},{32,64},{64,32},{96,0},{128,224},{160,192},{192,160},{224,1... | collective-permute-start | bytes 294920 | tf_op jit(solution)/shard_map/ppermute | solution.py:716
  40.0 1.4 %collective-permute-done.9.i6 = f32[12,16,128]{2,1,0:T(8,128)S(1)} collective-permute-done((f32[12,16,128]{2,1,0:T(8,128)S(1)}, f32[12,16,128]{2,1,0:T(8,128)S(1)}, u32[]{:S(2)}, u32[]{:S(2)}) %collective-permute-start.9) | collective-permute-done | bytes 98336 | tf_op jit(solution)/shard_map/ppermute | solution.py:716
  42.8 4.7 %shard_map.102 = (f32[49,16,128]{2,1,0:T(8,128)S(1)}, f32[49,16,128]{2,1,0:T(8,128)S(1)}, f32[4,144,256]{2,1,0:T(8,128)S(1)}, f32[3,16,128]{2,1,0:T(8,128)S(1)}, f32[4,16,128]{2,1,0:T(8,128)S(1)}) custom-call(f32[12,16,128]{2,1,0:T(8,128)S(1)} %collective-permute-done.5.i4, f32[12,16,128]{2,1,0:T(8,128)S(1)} %collective-permute-done.6.i5, ...), custom_call_target="tpu_custom_call" | custom-call | tf_op jit(solution)/shard_map/pallas_call | solution.py:698
  49.9 2.9 %collective-permute-start.13 = (f32[3,16,128]{2,1,0:T(8,128)S(1)}, f32[3,16,128]{2,1,0:T(8,128)S(1)}, u32[]{:S(2)}, u32[]{:S(2)}) collective-permute-start(f32[3,16,128]{2,1,0:T(8,128)S(1)} %get-tuple-element.59), channel_id=1, source_target_pairs={{0,2},{1,3},{2,0},{3,1},{4,6},{5,7},{6,4},{7,5},{8,10},{9,11},{10,... | collective-permute-start | bytes 73736 | tf_op jit(solution)/shard_map/ppermute | solution.py:716
  54.4 1.3 %collective-permute-done.12.a0 = f32[3,16,128]{2,1,0:T(8,128)S(1)} collective-permute-done((f32[3,16,128]{2,1,0:T(8,128)S(1)}, f32[3,16,128]{2,1,0:T(8,128)S(1)}, u32[]{:S(2)}, u32[]{:S(2)}) %collective-permute-start.12) | collective-permute-done | bytes 24608 | tf_op jit(solution)/shard_map/ppermute | solution.py:716
  55.8 2.3 %shard_map.103 = (f32[144,256]{1,0:T(8,128)S(1)}, f32[32,128]{1,0:T(8,128)S(1)}) custom-call(f32[49,16,128]{2,1,0:T(8,128)S(1)} %get-tuple-element.56.moved_ref, f32[4,144,256]{2,1,0:T(8,128)S(1)} %get-tuple-element.57.kept_ref, f32[4,16,128]{2,1,0:T(8,128)S(1)} %get-tuple-element.58.sums_ref, f32[3,16,128]{2,1,0:T(8,128)S(1)} %collective-permute-done.12.a0, ...), custom_call_target="tpu_custom_call" | custom-call | tf_op jit(solution)/shard_map/pallas_call | solution.py:698
  58.1 14.5 %all_to_all.16 = f32[32,1,128]{2,1,0:T(1,128)S(1)} all-to-all(f32[32,1,128]{2,1,0:T(1,128)S(1)} %bitcast.22), channel_id=1, replica_groups=mesh['mode'=8,'elem'=32] {'elem'}, dimensions={0} | all-to-all | bytes 32768 | tf_op jit(solution)/shard_map/all_to_all | solution.py:712
  72.9 2.0 %collective-permute-start.17 = (f32[9,16,128]{2,1,0:T(8,128)S(1)}, f32[9,16,128]{2,1,0:T(8,128)S(1)}, u32[]{:S(2)}, u32[]{:S(2)}) collective-permute-start(f32[9,16,128]{2,1,0:T(8,128)S(1)} %get-tuple-element.63), channel_id=1, source_target_pairs={{0,128},{32,160},{64,192},{96,224},{128,0},{160,32},{192,64},{224,... | collective-permute-start | bytes 221192 | tf_op jit(solution)/shard_map/ppermute | solution.py:716
  74.9 5.3 %collective-permute-start.18 = (f32[9,16,128]{2,1,0:T(8,128)S(1)}, f32[9,16,128]{2,1,0:T(8,128)S(1)}, u32[]{:S(2)}, u32[]{:S(2)}) collective-permute-start(f32[9,16,128]{2,1,0:T(8,128)S(1)} %get-tuple-element.64), channel_id=1, source_target_pairs={{0,160},{32,128},{64,224},{96,192},{128,32},{160,0},{192,96},{224,... | collective-permute-start | bytes 221192 | tf_op jit(solution)/shard_map/ppermute | solution.py:716
  81.4 1.3 %collective-permute-start.21 = (f32[9,16,128]{2,1,0:T(8,128)S(1)}, f32[9,16,128]{2,1,0:T(8,128)S(1)}, u32[]{:S(2)}, u32[]{:S(2)}) collective-permute-start(f32[9,16,128]{2,1,0:T(8,128)S(1)} %get-tuple-element.67), channel_id=1, source_target_pairs={{0,192},{32,224},{64,128},{96,160},{128,64},{160,96},{192,0},{224,... | collective-permute-start | bytes 221192 | tf_op jit(solution)/shard_map/ppermute | solution.py:716
  82.7 1.9 %collective-permute-start.22 = (f32[9,16,128]{2,1,0:T(8,128)S(1)}, f32[9,16,128]{2,1,0:T(8,128)S(1)}, u32[]{:S(2)}, u32[]{:S(2)}) collective-permute-start(f32[9,16,128]{2,1,0:T(8,128)S(1)} %get-tuple-element.68), channel_id=1, source_target_pairs={{0,96},{32,64},{64,32},{96,0},{128,224},{160,192},{192,160},{224,1... | collective-permute-start | bytes 221192 | tf_op jit(solution)/shard_map/ppermute | solution.py:716
  86.5 2.0 %collective-permute-done.22.i3 = f32[9,16,128]{2,1,0:T(8,128)S(1)} collective-permute-done((f32[9,16,128]{2,1,0:T(8,128)S(1)}, f32[9,16,128]{2,1,0:T(8,128)S(1)}, u32[]{:S(2)}, u32[]{:S(2)}) %collective-permute-start.22) | collective-permute-done | bytes 73760 | tf_op jit(solution)/shard_map/ppermute | solution.py:716
  90.1 2.7 %collective-permute-start.25 = (f32[9,16,128]{2,1,0:T(8,128)S(1)}, f32[9,16,128]{2,1,0:T(8,128)S(1)}, u32[]{:S(2)}, u32[]{:S(2)}) collective-permute-start(f32[9,16,128]{2,1,0:T(8,128)S(1)} %get-tuple-element.72), channel_id=1, source_target_pairs={{0,160},{32,128},{64,224},{96,192},{128,32},{160,0},{192,96},{224,... | collective-permute-start | bytes 221192 | tf_op jit(solution)/shard_map/ppermute | solution.py:716
  95.2 2.0 %collective-permute-start.29 = (f32[9,16,128]{2,1,0:T(8,128)S(1)}, f32[9,16,128]{2,1,0:T(8,128)S(1)}, u32[]{:S(2)}, u32[]{:S(2)}) collective-permute-start(f32[9,16,128]{2,1,0:T(8,128)S(1)} %get-tuple-element.76), channel_id=1, source_target_pairs={{0,96},{32,64},{64,32},{96,0},{128,224},{160,192},{192,160},{224,1... | collective-permute-start | bytes 221192 | tf_op jit(solution)/shard_map/ppermute | solution.py:716
  98.8 1.5 %collective-permute-done.29.i3 = f32[9,16,128]{2,1,0:T(8,128)S(1)} collective-permute-done((f32[9,16,128]{2,1,0:T(8,128)S(1)}, f32[9,16,128]{2,1,0:T(8,128)S(1)}, u32[]{:S(2)}, u32[]{:S(2)}) %collective-permute-start.29) | collective-permute-done | bytes 73760 | tf_op jit(solution)/shard_map/ppermute | solution.py:716
  100.3 2.1 %shard_map.106 = f32[81,16,128]{2,1,0:T(8,128)} custom-call(f32[9,16,128]{2,1,0:T(8,128)S(1)} %collective-permute-done.24.i4, f32[9,16,128]{2,1,0:T(8,128)S(1)} %collective-permute-done.25.i5, f32[9,16,128]{2,1,0:T(8,128)S(1)} %collective-permute-done.26.i7, f32[9,16,128]{2,1,0:T(8,128)S(1)} %collective-permute-done.27.i2, ...), custom_call_target="tpu_custom_call" | custom-call | tf_op jit(solution)/shard_map/pallas_call | solution.py:698
  (68 shorter events, 22.5 us)
Async XLA Ops:
  5.6 20.8 %all-to-all-start = ((f32[8,9,16,128]{3,2,1,0:T(8,128)}), f32[8,9,16,128]{3,2,1,0:T(8,128)S(1)}, u32[]{:S(2)}, u32[]{:S(2)}) async-start(f32[8,9,16,128]{3,2,1,0:T(8,128)} %bitcast.26), calls=%async_computation | async-start | bytes 1179648 | tf_op jit(solution)/shard_map/all_to_all | solution.py:712
  12.4 11.4 %collective-permute-start.4 = (f32[3,24,128]{2,1,0:T(8,128)S(1)}, f32[3,24,128]{2,1,0:T(8,128)S(1)}, u32[]{:S(2)}, u32[]{:S(2)}) collective-permute-start(f32[3,24,128]{2,1,0:T(8,128)S(1)} %copy-done.9), channel_id=1, source_target_pairs={{0,16},{1,17},{2,18},{3,19},{4,20},{5,21},{6,22},{7,23},{8,24},{9,... | collective-permute-start | bytes 110600 | tf_op jit(solution)/shard_map/ppermute | solution.py:716
  18.6 5.3 %collective-permute-start.3 = (f32[3,24,128]{2,1,0:T(8,128)S(1)}, f32[3,24,128]{2,1,0:T(8,128)S(1)}, u32[]{:S(2)}, u32[]{:S(2)}) collective-permute-start(f32[3,24,128]{2,1,0:T(8,128)S(1)} %copy-done.9), channel_id=1, source_target_pairs={{0,8},{1,9},{2,10},{3,11},{4,12},{5,13},{6,14},{7,15},{8,0},{9,1},... | collective-permute-start | bytes 110600 | tf_op jit(solution)/shard_map/ppermute | solution.py:716
  27.3 8.8 %collective-permute-start.5 = (f32[12,16,128]{2,1,0:T(8,128)S(1)}, f32[12,16,128]{2,1,0:T(8,128)S(1)}, u32[]{:S(2)}, u32[]{:S(2)}) collective-permute-start(f32[12,16,128]{2,1,0:T(8,128)S(1)} %get-tuple-element.44), channel_id=1, source_target_pairs={{0,128},{32,160},{64,192},{96,224},{128,0},{160,32},{192,64},{224,... | collective-permute-start | bytes 294920 | tf_op jit(solution)/shard_map/ppermute | solution.py:716
  30.4 7.2 %collective-permute-start.6 = (f32[12,16,128]{2,1,0:T(8,128)S(1)}, f32[12,16,128]{2,1,0:T(8,128)S(1)}, u32[]{:S(2)}, u32[]{:S(2)}) collective-permute-start(f32[12,16,128]{2,1,0:T(8,128)S(1)} %get-tuple-element.45), channel_id=1, source_target_pairs={{0,160},{32,128},{64,224},{96,192},{128,32},{160,0},{192,96},{224,... | collective-permute-start | bytes 294920 | tf_op jit(solution)/shard_map/ppermute | solution.py:716
  32.7 7.3 %collective-permute-start.7 = (f32[12,16,128]{2,1,0:T(8,128)S(1)}, f32[12,16,128]{2,1,0:T(8,128)S(1)}, u32[]{:S(2)}, u32[]{:S(2)}) collective-permute-start(f32[12,16,128]{2,1,0:T(8,128)S(1)} %get-tuple-element.46), channel_id=1, source_target_pairs={{0,224},{32,192},{64,160},{96,128},{128,96},{160,64},{192,32},{224... | collective-permute-start | bytes 294920 | tf_op jit(solution)/shard_map/ppermute | solution.py:716
  33.8 6.2 %collective-permute-start.8 = (f32[12,16,128]{2,1,0:T(8,128)S(1)}, f32[12,16,128]{2,1,0:T(8,128)S(1)}, u32[]{:S(2)}, u32[]{:S(2)}) collective-permute-start(f32[12,16,128]{2,1,0:T(8,128)S(1)} %get-tuple-element.47), channel_id=1, source_target_pairs={{0,64},{32,96},{64,0},{96,32},{128,192},{160,224},{192,128},{224,1... | collective-permute-start | bytes 294920 | tf_op jit(solution)/shard_map/ppermute | solution.py:716
  34.3 7.0 %collective-permute-start.9 = (f32[12,16,128]{2,1,0:T(8,128)S(1)}, f32[12,16,128]{2,1,0:T(8,128)S(1)}, u32[]{:S(2)}, u32[]{:S(2)}) collective-permute-start(f32[12,16,128]{2,1,0:T(8,128)S(1)} %get-tuple-element.48), channel_id=1, source_target_pairs={{0,192},{32,224},{64,128},{96,160},{128,64},{160,96},{192,0},{224,... | collective-permute-start | bytes 294920 | tf_op jit(solution)/shard_map/ppermute | solution.py:716
  36.1 5.9 %collective-permute-start.10 = (f32[12,16,128]{2,1,0:T(8,128)S(1)}, f32[12,16,128]{2,1,0:T(8,128)S(1)}, u32[]{:S(2)}, u32[]{:S(2)}) collective-permute-start(f32[12,16,128]{2,1,0:T(8,128)S(1)} %get-tuple-element.49), channel_id=1, source_target_pairs={{0,96},{32,64},{64,32},{96,0},{128,224},{160,192},{192,160},{224,1... | collective-permute-start | bytes 294920 | tf_op jit(solution)/shard_map/ppermute | solution.py:716
  47.5 6.9 %collective-permute-start.16 = (f32[3,16,128]{2,1,0:T(8,128)S(1)}, f32[3,16,128]{2,1,0:T(8,128)S(1)}, u32[]{:S(2)}, u32[]{:S(2)}) collective-permute-start(f32[3,16,128]{2,1,0:T(8,128)S(1)} %get-tuple-element.59), channel_id=1, source_target_pairs={{0,16},{1,17},{2,18},{3,19},{4,20},{5,21},{6,22},{7,23},{8,24},{9,... | collective-permute-start | bytes 73736 | tf_op jit(solution)/shard_map/ppermute | solution.py:716
  48.8 5.7 %collective-permute-start.15 = (f32[3,16,128]{2,1,0:T(8,128)S(1)}, f32[3,16,128]{2,1,0:T(8,128)S(1)}, u32[]{:S(2)}, u32[]{:S(2)}) collective-permute-start(f32[3,16,128]{2,1,0:T(8,128)S(1)} %get-tuple-element.59), channel_id=1, source_target_pairs={{0,8},{1,9},{2,10},{3,11},{4,12},{5,13},{6,14},{7,15},{8,0},{9,1},... | collective-permute-start | bytes 73736 | tf_op jit(solution)/shard_map/ppermute | solution.py:716
  49.1 5.3 %collective-permute-start.14 = (f32[3,16,128]{2,1,0:T(8,128)S(1)}, f32[3,16,128]{2,1,0:T(8,128)S(1)}, u32[]{:S(2)}, u32[]{:S(2)}) collective-permute-start(f32[3,16,128]{2,1,0:T(8,128)S(1)} %get-tuple-element.59), channel_id=1, source_target_pairs={{0,4},{1,5},{2,6},{3,7},{4,0},{5,1},{6,2},{7,3},{8,12},{9,13},{10,... | collective-permute-start | bytes 73736 | tf_op jit(solution)/shard_map/ppermute | solution.py:716
  49.9 4.6 %collective-permute-start.13 = (f32[3,16,128]{2,1,0:T(8,128)S(1)}, f32[3,16,128]{2,1,0:T(8,128)S(1)}, u32[]{:S(2)}, u32[]{:S(2)}) collective-permute-start(f32[3,16,128]{2,1,0:T(8,128)S(1)} %get-tuple-element.59), channel_id=1, source_target_pairs={{0,2},{1,3},{2,0},{3,1},{4,6},{5,7},{6,4},{7,5},{8,10},{9,11},{10,... | collective-permute-start | bytes 73736 | tf_op jit(solution)/shard_map/ppermute | solution.py:716
  72.9 9.8 %collective-permute-start.17 = (f32[9,16,128]{2,1,0:T(8,128)S(1)}, f32[9,16,128]{2,1,0:T(8,128)S(1)}, u32[]{:S(2)}, u32[]{:S(2)}) collective-permute-start(f32[9,16,128]{2,1,0:T(8,128)S(1)} %get-tuple-element.63), channel_id=1, source_target_pairs={{0,128},{32,160},{64,192},{96,224},{128,0},{160,32},{192,64},{224,... | collective-permute-start | bytes 221192 | tf_op jit(solution)/shard_map/ppermute | solution.py:716
  74.9 9.7 %collective-permute-start.18 = (f32[9,16,128]{2,1,0:T(8,128)S(1)}, f32[9,16,128]{2,1,0:T(8,128)S(1)}, u32[]{:S(2)}, u32[]{:S(2)}) collective-permute-start(f32[9,16,128]{2,1,0:T(8,128)S(1)} %get-tuple-element.64), channel_id=1, source_target_pairs={{0,160},{32,128},{64,224},{96,192},{128,32},{160,0},{192,96},{224,... | collective-permute-start | bytes 221192 | tf_op jit(solution)/shard_map/ppermute | solution.py:716
  80.2 5.8 %collective-permute-start.19 = (f32[9,16,128]{2,1,0:T(8,128)S(1)}, f32[9,16,128]{2,1,0:T(8,128)S(1)}, u32[]{:S(2)}, u32[]{:S(2)}) collective-permute-start(f32[9,16,128]{2,1,0:T(8,128)S(1)} %get-tuple-element.65), channel_id=1, source_target_pairs={{0,224},{32,192},{64,160},{96,128},{128,96},{160,64},{192,32},{224... | collective-permute-start | bytes 221192 | tf_op jit(solution)/shard_map/ppermute | solution.py:716
  80.8 5.2 %collective-permute-start.20 = (f32[9,16,128]{2,1,0:T(8,128)S(1)}, f32[9,16,128]{2,1,0:T(8,128)S(1)}, u32[]{:S(2)}, u32[]{:S(2)}) collective-permute-start(f32[9,16,128]{2,1,0:T(8,128)S(1)} %get-tuple-element.66), channel_id=1, source_target_pairs={{0,64},{32,96},{64,0},{96,32},{128,192},{160,224},{192,128},{224,1... | collective-permute-start | bytes 221192 | tf_op jit(solution)/shard_map/ppermute | solution.py:716
  81.4 5.1 %collective-permute-start.21 = (f32[9,16,128]{2,1,0:T(8,128)S(1)}, f32[9,16,128]{2,1,0:T(8,128)S(1)}, u32[]{:S(2)}, u32[]{:S(2)}) collective-permute-start(f32[9,16,128]{2,1,0:T(8,128)S(1)} %get-tuple-element.67), channel_id=1, source_target_pairs={{0,192},{32,224},{64,128},{96,160},{128,64},{160,96},{192,0},{224,... | collective-permute-start | bytes 221192 | tf_op jit(solution)/shard_map/ppermute | solution.py:716
  82.7 5.8 %collective-permute-start.22 = (f32[9,16,128]{2,1,0:T(8,128)S(1)}, f32[9,16,128]{2,1,0:T(8,128)S(1)}, u32[]{:S(2)}, u32[]{:S(2)}) collective-permute-start(f32[9,16,128]{2,1,0:T(8,128)S(1)} %get-tuple-element.68), channel_id=1, source_target_pairs={{0,96},{32,64},{64,32},{96,0},{128,224},{160,192},{192,160},{224,1... | collective-permute-start | bytes 221192 | tf_op jit(solution)/shard_map/ppermute | solution.py:716
  89.1 6.0 %collective-permute-start.24 = (f32[9,16,128]{2,1,0:T(8,128)S(1)}, f32[9,16,128]{2,1,0:T(8,128)S(1)}, u32[]{:S(2)}, u32[]{:S(2)}) collective-permute-start(f32[9,16,128]{2,1,0:T(8,128)S(1)} %get-tuple-element.71), channel_id=1, source_target_pairs={{0,128},{32,160},{64,192},{96,224},{128,0},{160,32},{192,64},{224,... | collective-permute-start | bytes 221192 | tf_op jit(solution)/shard_map/ppermute | solution.py:716
  90.1 7.1 %collective-permute-start.25 = (f32[9,16,128]{2,1,0:T(8,128)S(1)}, f32[9,16,128]{2,1,0:T(8,128)S(1)}, u32[]{:S(2)}, u32[]{:S(2)}) collective-permute-start(f32[9,16,128]{2,1,0:T(8,128)S(1)} %get-tuple-element.72), channel_id=1, source_target_pairs={{0,160},{32,128},{64,224},{96,192},{128,32},{160,0},{192,96},{224,... | collective-permute-start | bytes 221192 | tf_op jit(solution)/shard_map/ppermute | solution.py:716
  92.8 5.5 %collective-permute-start.26 = (f32[9,16,128]{2,1,0:T(8,128)S(1)}, f32[9,16,128]{2,1,0:T(8,128)S(1)}, u32[]{:S(2)}, u32[]{:S(2)}) collective-permute-start(f32[9,16,128]{2,1,0:T(8,128)S(1)} %get-tuple-element.73), channel_id=1, source_target_pairs={{0,224},{32,192},{64,160},{96,128},{128,96},{160,64},{192,32},{224... | collective-permute-start | bytes 221192 | tf_op jit(solution)/shard_map/ppermute | solution.py:716
  94.1 4.7 %collective-permute-start.28 = (f32[9,16,128]{2,1,0:T(8,128)S(1)}, f32[9,16,128]{2,1,0:T(8,128)S(1)}, u32[]{:S(2)}, u32[]{:S(2)}) collective-permute-start(f32[9,16,128]{2,1,0:T(8,128)S(1)} %get-tuple-element.75), channel_id=1, source_target_pairs={{0,192},{32,224},{64,128},{96,160},{128,64},{160,96},{192,0},{224,... | collective-permute-start | bytes 221192 | tf_op jit(solution)/shard_map/ppermute | solution.py:716
  95.2 5.1 %collective-permute-start.29 = (f32[9,16,128]{2,1,0:T(8,128)S(1)}, f32[9,16,128]{2,1,0:T(8,128)S(1)}, u32[]{:S(2)}, u32[]{:S(2)}) collective-permute-start(f32[9,16,128]{2,1,0:T(8,128)S(1)} %get-tuple-element.76), channel_id=1, source_target_pairs={{0,96},{32,64},{64,32},{96,0},{128,224},{160,192},{192,160},{224,1... | collective-permute-start | bytes 221192 | tf_op jit(solution)/shard_map/ppermute | solution.py:716
  (18 other events, 165.6 us)

commit v4 on v3

--- a/solution.py
+++ b/solution.py
@@ -29,6 +29,7 @@
 SHARE = BLOCK + SLOT_TILES
 SCALARS = 5
 STEP_ORDER = [4, 5, 7, 2, 6, 3, 1]
+LEVEL_ORDER = [0, 2, 1, 3, 4]
 SPACING = 0.25
 F32 = jnp.float32
 BF16 = jnp.bfloat16
@@ -135,9 +136,12 @@
         left_ref[row_block(HIGH + high), lane_block(column)] = jnp.where(here, rest, 0.0).astype(BF16)
 
 
+def contract_lanes(left, right):
+    return lax.dot_general(left, right, (((1,), (1,)), ((), ())), preferred_element_type=F32)
+
+
 def scatter_sum(left, selectors):
-    contract = (((1,), (1,)), ((), ()))
-    both = lax.dot_general(left, selectors, contract, preferred_element_type=F32)
+    both = contract_lanes(left, selectors)
     return both[: HIGH * ROWS] + both[HIGH * ROWS :]
 
 
@@ -309,13 +313,22 @@
     return results
 
 
-def gradients(cells_ref, first_ref, metric_ref, rows, visit):
+def grid_load(inner_ref, cycle_ref, rows):
+    def load(node):
+        if node in CYCLE_NODES:
+            return cycle_ref[CYCLE_NODES.index(node), rows, :]
+        return inner_ref[INNER_NODES.index(node), rows, :]
+
+    return load
+
+
+def gradients(load, first_ref, metric_ref, visit):
     for j in range(SIDE):
-        line = derivative_line([cells_ref[k * SIDE + j, rows, :] for k in range(SIDE)], False)
+        line = derivative_line([load(k * SIDE + j) for k in range(SIDE)], False)
         for i in range(SIDE):
             first_ref[i * SIDE + j] = line[i]
     for i in range(SIDE):
-        line = derivative_line([cells_ref[i * SIDE + k, rows, :] for k in range(SIDE)], False)
+        line = derivative_line([load(i * SIDE + k) for k in range(SIDE)], False)
         seconds = []
         for j in range(SIDE):
             node = i * SIDE + j
@@ -328,21 +341,22 @@
         yield i, seconds
 
 
-def apply_operator(cells_ref, result_ref, first_ref, energy_ref, metric_ref, shift_ref):
+def apply_operator(inner_ref, cycle_ref, result_ref, first_ref, energy_ref, metric_ref, shift_ref):
     @pl.loop(0, 2)
     def half(part):
         rows = pl.ds(pl.multiple_of(part * 8, 8), 8)
         shift = shift_ref[rows, :]
+        load = grid_load(inner_ref, cycle_ref, rows)
 
         def visit(node, g1, g2, p1, p2):
             first_ref[node] = p1
 
-        for i, seconds in gradients(cells_ref, first_ref, metric_ref, rows, visit):
+        for i, seconds in gradients(load, first_ref, metric_ref, visit):
             line = derivative_line(seconds, True)
             for j in range(SIDE):
                 node = i * SIDE + j
                 mass = shift * metric_ref[node, 3:4, :]
-                result_ref[node, rows, :] = line[j] + mass * cells_ref[node, rows, :]
+                result_ref[node, rows, :] = line[j] + mass * load(node)
         energy = jnp.zeros((8, LANES), F32)
         for j in range(SIDE):
             line = derivative_line([first_ref[k * SIDE + j] for k in range(SIDE)], True)
@@ -350,31 +364,29 @@
                 node = i * SIDE + j
                 value = result_ref[node, rows, :] + line[i]
                 result_ref[node, rows, :] = value
-                energy = energy + value * cells_ref[node, rows, :]
+                energy = energy + value * load(node)
         energy_ref[rows, :] = energy
 
 
-def apply_energy(cells_ref, first_ref, energy_ref, metric_ref, shift_ref):
+def apply_energy(inner_ref, cycle_ref, first_ref, energy_ref, metric_ref, shift_ref):
     @pl.loop(0, 2)
     def half(part):
         rows = pl.ds(pl.multiple_of(part * 8, 8), 8)
         shift = shift_ref[rows, :]
+        load = grid_load(inner_ref, cycle_ref, rows)
         sums = [jnp.zeros((8, LANES), F32)]
 
         def visit(node, g1, g2, p1, p2):
-            value = cells_ref[node, rows, :]
+            value = load(node)
             mass = shift * metric_ref[node, 3:4, :]
             sums[0] = sums[0] + (g1 * p1 + g2 * p2 + mass * value * value)
 
-        for i, seconds in gradients(cells_ref, first_ref, metric_ref, rows, visit):
+        for i, seconds in gradients(load, first_ref, metric_ref, visit):
             pass
         energy_ref[rows, :] = sums[0]
 
 
-def diagonal_slots(
-    metric_ref, table_ref, cross_ref, penalty_ref, edge_rows, shared_rows, right_ref,
-    inner_ref, skeleton_ref, padded_ref, cells_ref, left_ref,
-):
+def diagonal_cells(metric_ref, table_ref, cross_ref, penalty_ref, inner_ref, padded_ref, cells_ref):
     both = jnp.concatenate([metric_ref[:, 0, :], metric_ref[:, 1, :]], axis=0)
     terms = jnp.dot(table_ref[...], both, precision=HIGHEST, preferred_element_type=F32)
     cells_ref[0] = terms + cross_ref[...] * metric_ref[:, 2, :]
@@ -387,15 +399,9 @@
     for index, node in enumerate(INNER_NODES):
         inner_ref[0, index : index + 1, :] = cells_ref[0, node : node + 1, :]
         inner_ref[1, index : index + 1, :] = cells_ref[1, node : node + 1, :]
-    high_rows = jnp.right_shift(edge_rows, 8)
-    for slot in range(CYCLE):
-        node = CYCLE_NODES[slot]
-        value = four_pieces(cells_ref[0, node : node + 1, :], cells_ref[1, node : node + 1, :])
-        masked_store_four(value, high_rows[slot : slot + 1, :], left_ref, slot)
-    contract = (((1,), (1,)), ((), ()))
-    total = lax.dot_general(
-        left_ref[: HIGH * ROWS, :], right_ref[...], contract, preferred_element_type=F32
-    )
+
+
+def diagonal_slots(total, shared_rows, selectors, padded_ref, skeleton_ref):
     stacked = []
     for high in range(HIGH):
         laplace, mass = two_rows(total, high)
@@ -406,10 +412,8 @@
     stacked = jnp.concatenate(stacked, axis=0)
     results = []
     for tile in range(SLOT_TILES):
-        rows = shared_rows[tile : tile + 1, :]
-        low = jnp.bitwise_and(rows, LOW - 1)
-        high_row = jnp.right_shift(rows, 8)
-        found = jnp.dot(stacked, one_hot_rows(low), preferred_element_type=F32)
+        high_row = jnp.right_shift(shared_rows[tile : tile + 1, :], 8)
+        found = jnp.dot(stacked, selectors[:, lane_block(tile)], preferred_element_type=F32)
         value = jnp.zeros((ROWS, LANES), F32)
         for high in range(HIGH):
             value = value + jnp.where(high_row == high, found[row_block(high), :], 0.0)
@@ -418,19 +422,19 @@
 
 
 def pack_kernel(
-    forcing_hbm, edge_hbm, shared_hbm, metric_hbm, penalty_hbm, table_hbm, cross_hbm,
-    out_hbm, message_hbm, inner_hbm, skeleton_hbm, padded_hbm,
-    forcing_ref, edge_ref, shared_ref, metric_ref, penalty_ref, table_ref, cross_ref,
-    packed_ref, message_ref, inner_ref, skeleton_ref, padded_ref,
-    cells_ref, left_ref, right_ref, in_semaphores, out_semaphores,
+    forcing_hbm, edge_hbm, shared_hbm, masks_hbm, metric_hbm, penalty_hbm, table_hbm, cross_hbm,
+    out_hbm, message_hbm, inner_hbm, skeleton_hbm, padded_hbm, lists_hbm,
+    forcing_ref, edge_ref, shared_ref, masks_ref, metric_ref, penalty_ref, table_ref, cross_ref,
+    packed_ref, message_ref, inner_ref, skeleton_ref, padded_ref, lists_ref,
+    cells_ref, left_ref, selectors_ref, in_semaphores, out_semaphores,
 ):
     ins = [
         pltpu.make_async_copy(source, target, in_semaphores.at[index])
         for index, (source, target) in enumerate(
             [
-                (edge_hbm, edge_ref), (shared_hbm, shared_ref), (forcing_hbm, forcing_ref),
-                (metric_hbm, metric_ref), (table_hbm, table_ref), (cross_hbm, cross_ref),
-                (penalty_hbm, penalty_ref),
+                (edge_hbm, edge_ref), (metric_hbm, metric_ref), (table_hbm, table_ref), (cross_hbm, cross_ref),
+                (penalty_hbm, penalty_ref), (shared_hbm, shared_ref), (masks_hbm, masks_ref),
+                (forcing_hbm, forcing_ref),
             ]
         )
     ]
@@ -444,32 +448,43 @@
         outs.append(copy)
 
     width = ORDER - 1
+    base = 2 * HIGH * ROWS
     for index in range(TILES, MODES * BLOCK - INNER):
         packed_ref[index] = jnp.zeros((ROWS, LANES), F32)
     ins[0].wait()
     edge_rows = edge_ref[...]
-    one_hot_cycle(edge_rows, right_ref)
-    ins[1].wait()
+    one_hot_cycle(edge_rows, selectors_ref)
+    for copy in ins[1:7]:
+        copy.wait()
     shared_rows = shared_ref[...]
-    ins[2].wait()
+    lists_ref[:SLOT_TILES, :] = shared_rows
+    lists_ref[SLOT_TILES : 2 * SLOT_TILES, :] = masks_ref[...]
+    lists_ref[2 * SLOT_TILES :, :] = jnp.zeros((8 - 2 * SLOT_TILES, LANES), jnp.int32)
+    send(lists_ref, lists_hbm)
+    diagonal_cells(metric_ref, table_ref, cross_ref, penalty_ref, inner_ref, padded_ref, cells_ref)
+    send(inner_ref, inner_hbm)
+    send(padded_ref, padded_hbm)
+    ins[7].wait()
     for line in range(width):
         send(forcing_ref.at[pl.ds((line + 1) * SIDE + 1, width)], out_hbm.at[pl.ds(line * width, width)])
-    for copy in ins[3:]:
-        copy.wait()
-    pairs = diagonal_slots(
-        metric_ref, table_ref, cross_ref, penalty_ref, edge_rows, shared_rows, right_ref,
-        inner_ref, skeleton_ref, padded_ref, cells_ref, left_ref,
-    )
-    send(inner_ref, inner_hbm)
-    send(skeleton_ref, skeleton_hbm)
-    send(padded_ref, padded_hbm)
-    skeleton = scatter_cycle(lambda slot: forcing_ref[CYCLE_NODES[slot]], edge_rows, left_ref, right_ref)
+    high_rows = jnp.right_shift(edge_rows, 8)
+    for slot in range(CYCLE):
+        node = CYCLE_NODES[slot]
+        high_row = high_rows[slot : slot + 1, :]
+        masked_store(forcing_ref[node], high_row, left_ref, slot)
+        value = four_pieces(cells_ref[0, node : node + 1, :], cells_ref[1, node : node + 1, :])
+        masked_store_four(value, high_row, left_ref.at[pl.ds(base, HIGH * ROWS)], slot)
+    total = contract_lanes(left_ref[...], selectors_ref[...])
+    skeleton = total[: HIGH * ROWS] + total[HIGH * ROWS : base]
 
     def store(index, value):
         packed_ref[index] = value
 
     write_skeleton(skeleton, store)
     send(packed_ref, out_hbm.at[pl.ds(INNER, MODES * BLOCK - INNER)])
+    selectors = slot_selectors(shared_rows)
+    pairs = diagonal_slots(total[base:], shared_rows, selectors, padded_ref, skeleton_ref)
+    send(skeleton_ref, skeleton_hbm)
     for tile, value in enumerate(gather_slots(skeleton, shared_rows)):
         laplace, mass = pairs[tile]
         message_ref[tile, :ROWS, :] = value
@@ -491,14 +506,14 @@
 
 
 def transform_kernel(
-    matrix_ref, in_ref, a0, a1, a2, a3, a4, masks_ref, o0, o1, o2, o3, o4, o5, o6, o7, extra_ref, slots_ref
+    matrix_ref, in_ref, a0, a2, a1, a3, a4, lists_ref, o0, o1, o2, o3, o4, o5, o6, o7, extra_ref, slots_ref
 ):
     mode = lax.axis_index("mode")
     outs = [o0, o1, o2, o3, o4, o5, o6, o7]
     matrix = relative_rows(matrix_ref, mode)
     slots_ref[...] = jnp.zeros(slots_ref.shape, F32)
     arrived_refs = [a0, a1, a2, a3, a4]
-    masks = masks_ref[...]
+    masks = lists_ref[SLOT_TILES : 2 * SLOT_TILES, :]
     for index in range(BLOCK):
         block = in_ref[:, index].reshape(PLANES, LANES)
         mixed = jnp.dot(matrix, block, precision=HIGHEST, preferred_element_type=F32)
@@ -514,15 +529,15 @@
 
 
 def first_kernel(
-    i4, i5, i7, i2, i6, i3, i1, i0, extra_ref, shared_ref, edge_ref, metric_ref,
-    inner_ref, diagonal_ref, penalty_ref, search_ref, change_ref, kept_ref, slots_ref, sums_ref,
-    left_ref, right_ref, source_ref, cells_ref, result_ref, first_ref, energy_ref, shift_ref,
+    i4, i5, i7, i2, i6, i3, i1, i0, extra_ref, lists_ref, edge_ref, metric_ref,
+    inner_ref, diagonal_ref, penalty_ref, search_ref, inverse_ref, result_ref, source_ref, kept_ref, slots_ref,
+    sums_ref, left_ref, right_ref, cycle_ref, first_ref, energy_ref, shift_ref,
 ):
     mode = lax.axis_index("mode")
     ins = [i0, i1, i2, i3, i4, i5, i6, i7]
     for step, in_ref in enumerate(ins):
         source_ref[jnp.bitwise_xor(mode, step)] = in_ref[:BLOCK]
-    shared_rows = shared_ref[...]
+    shared_rows = lists_ref[:SLOT_TILES, :]
     right_slots = slot_selectors(shared_rows)
     shift = helmholtz_shift()
     shift_ref[...] = shift
@@ -542,10 +557,7 @@
     for tile in range(SLOT_TILES):
         value = four_pieces(extra_ref[tile, 0:1, :], extra_ref[tile, 1:2, :])
         masked_store_four(value, high_rows[tile : tile + 1, :], left_ref, tile)
-    contract = (((1,), (1,)), ((), ()))
-    added = lax.dot_general(
-        left_ref[: HIGH * ROWS, :SLOTS], right_slots, contract, preferred_element_type=F32
-    )
+    added = contract_lanes(left_ref[: HIGH * ROWS, :SLOTS], right_slots)
     wide_shift = jnp.concatenate([shift, shift], axis=1)
     parts = []
     for high in range(HIGH):
@@ -566,15 +578,14 @@
         inverted = 1.0 / (inner_ref[0, index : index + 1, :] + shift * inner_ref[1, index : index + 1, :])
         scaled = value * inverted
         search_ref[index] = scaled
-        change_ref[index] = inverted
-        cells_ref[node] = scaled
+        inverse_ref[index] = inverted
         start = start + value * scaled
 
     def store(slot, value):
-        cells_ref[CYCLE_NODES[slot]] = value
+        cycle_ref[slot] = value
 
     gather_cycle(search, edge_rows, store, right_ref)
-    apply_operator(cells_ref, result_ref, first_ref, energy_ref, metric_ref, shift_ref)
+    apply_operator(search_ref, cycle_ref, result_ref, first_ref, energy_ref, metric_ref, shift_ref)
     weighted = per_tile(penalty_ref) * search
     applied = weighted + scatter_cycle(
         lambda slot: result_ref[CYCLE_NODES[slot]], edge_rows, left_ref, right_ref
@@ -582,27 +593,30 @@
     kept_ref[3] = applied
     for tile, value in enumerate(gather_slots(applied, shared_rows)):
         slots_ref[tile] = value
+    sums_ref[0] = energy_ref[...] + skeleton_sum(weighted * search)
+    sums_ref[1] = start
+
+
+def change_kernel(search_ref, inverse_ref, result_ref, source_ref, moved_ref, sums_ref):
     crossed = jnp.zeros((ROWS, LANES), F32)
     sourced = jnp.zeros((ROWS, LANES), F32)
     for index, node in enumerate(INNER_NODES):
         value = result_ref[node]
-        moved = value * change_ref[index] - cells_ref[node]
-        change_ref[index] = moved
+        moved = value * inverse_ref[index] - search_ref[index]
+        moved_ref[index] = moved
         crossed = crossed + value * moved
-        sourced = sourced + source(index) * moved
-    sums_ref[0] = energy_ref[...] + skeleton_sum(weighted * search)
-    sums_ref[1] = crossed
-    sums_ref[2] = start
-    sums_ref[3] = sourced
+        sourced = sourced + source_ref[index // BLOCK, index % BLOCK] * moved
+    sums_ref[0] = crossed
+    sums_ref[1] = sourced
 
 
 def second_kernel(
-    moved_ref, kept_ref, sums_ref, a0, a1, a2, a3, a4, masks_ref, shared_ref, edge_ref,
-    metric_ref, penalty_ref, change_ref, message_ref, left_ref, cells_ref, first_ref, energy_ref, shift_ref,
+    moved_ref, kept_ref, sums_ref, moved_sums_ref, a0, a2, a1, a3, a4, lists_ref, edge_ref,
+    metric_ref, penalty_ref, change_ref, message_ref, left_ref, cycle_ref, first_ref, energy_ref, shift_ref,
 ):
     arrived_refs = [a0, a1, a2, a3, a4]
-    masks = masks_ref[...]
-    shared_rows = shared_ref[...]
+    masks = lists_ref[SLOT_TILES : 2 * SLOT_TILES, :]
+    shared_rows = lists_ref[:SLOT_TILES, :]
     shift_ref[...] = helmholtz_shift()
 
     def load(tile):
@@ -612,21 +626,19 @@
     full = applied + scatter_slots(load, shared_rows, left_ref, slot_selectors(shared_rows))
     change = full * inverse - search
     change_ref[...] = change
-    crossed = sums_ref[1] + skeleton_sum(applied * change)
-    sourced = sums_ref[3] + skeleton_sum(local * change)
-    for index, node in enumerate(INNER_NODES):
-        cells_ref[node] = moved_ref[index]
+    crossed = moved_sums_ref[0] + skeleton_sum(applied * change)
+    sourced = moved_sums_ref[1] + skeleton_sum(local * change)
 
     def store(slot, value):
-        cells_ref[CYCLE_NODES[slot]] = value
+        cycle_ref[slot] = value
 
     gather_cycle(change, edge_ref[...], store)
-    apply_energy(cells_ref, first_ref, energy_ref, metric_ref, shift_ref)
+    apply_energy(moved_ref, cycle_ref, first_ref, energy_ref, metric_ref, shift_ref)
     energy = energy_ref[...] + skeleton_sum(per_tile(penalty_ref) * change * change)
     sublanes = lax.broadcasted_iota(jnp.int32, (ROWS, LANES), 0)
     lanes = lax.broadcasted_iota(jnp.int32, (ROWS, LANES), 1)
     spread = jnp.zeros((ROWS, LANES), F32)
-    for index, value in enumerate([sums_ref[0], crossed, energy, sums_ref[2], sourced]):
+    for index, value in enumerate([sums_ref[0], crossed, energy, sums_ref[1], sourced]):
         column = jnp.sum(value, axis=1, keepdims=True)
         spread = jnp.where(lanes == sublanes + index * ROWS, column, spread)
     message = jnp.sum(spread, axis=0, keepdims=True)
@@ -676,7 +688,9 @@
             out_ref[index] = mixed[row_block(step), :]
 
 
-def unpack_kernel(i4, i5, i7, i2, i6, i3, i1, i0, edge_ref, out_ref, packed_ref):
+def unpack_kernel(
+    i4, i5, i7, i2, i6, i3, i1, i0, edge_ref, out_hbm, packed_ref, out_ref, semaphores
+):
     mode = lax.axis_index("mode")
     for step, in_ref in enumerate([i0, i1, i2, i3, i4, i5, i6, i7]):
         packed_ref[jnp.bitwise_xor(mode, step)] = in_ref[...]
@@ -687,11 +701,23 @@
 
     for index, node in enumerate(INNER_NODES):
         out_ref[node] = load(index)
+    spans = [(SIDE, (SIDE - 2) * SIDE), (0, SIDE), (ORDER * SIDE, SIDE)]
+    copies = [
+        pltpu.make_async_copy(out_ref.at[pl.ds(*span)], out_hbm.at[pl.ds(*span)], semaphores.at[index])
+        for index, span in enumerate(spans)
+    ]
 
     def store(slot, value):
         out_ref[CYCLE_NODES[slot]] = value
+        if slot == 2 * SIDE - 1:
+            copies[0].start()
+        if slot == CYCLE - 1:
+            copies[1].start()
+            copies[2].start()
 
     gather_cycle(read_skeleton(lambda index: load(INNER + index)), edge_ref[...], store)
+    for copy in copies:
+        copy.wait()
 
 
 def call(kernel, out_shapes, scratch, *operands, limit=VMEM_LIMIT, **options):
@@ -721,8 +747,7 @@
 
 
 def exchange(slots):
-    levels = lax.axis_size("elem").bit_length() - 1
-    return [permute(slots, "elem", 1 << level) for level in range(levels)]
+    return [permute(slots, "elem", 1 << level) for level in LEVEL_ORDER]
 
 
 def body(forcing, metric, edge_map, shared_rows, partner_masks, penalty):
@@ -735,7 +760,7 @@
     left = pltpu.VMEM((2 * HIGH * ROWS, CYCLE * LANES), BF16)
     right = pltpu.VMEM((LOW, CYCLE * LANES), BF16)
     left_slots = pltpu.VMEM((2 * HIGH * ROWS, SLOTS), BF16)
-    cells = pltpu.VMEM((NODES, ROWS, LANES), F32)
+    cycle = pltpu.VMEM((CYCLE, ROWS, LANES), F32)
     first = pltpu.VMEM((NODES, 8, LANES), F32)
     energy = pltpu.VMEM((ROWS, LANES), F32)
     packing = pltpu.VMEM((MODES, BLOCK, ROWS, LANES), F32)
@@ -745,17 +770,17 @@
     hbm = pl.BlockSpec(memory_space=pltpu.HBM)
     packed_shapes = [
         shape(MODES * BLOCK, ROWS, LANES), shape(SLOT_TILES, ROWS + 8, LANES),
-        shape(2, INNER, LANES), shape(2, HIGH, LOW), shape(HIGH, LOW),
+        shape(2, INNER, LANES), shape(2, HIGH, LOW), shape(HIGH, LOW), shape(8, LANES, dtype=jnp.int32),
     ]
-    operands = [forcing.transpose(1, 0, 2), edge_rows, shared, metric, penalty, table, cross]
-    packed, message, inner, diagonal, penalties = call(
+    operands = [forcing.transpose(1, 0, 2), edge_rows, shared, masks, metric, penalty, table, cross]
+    packed, message, inner, diagonal, penalties, lists = call(
         pack_kernel, packed_shapes,
         [pltpu.VMEM(operand.shape, operand.dtype) for operand in operands]
         + [pltpu.VMEM((MODES * BLOCK - INNER, ROWS, LANES), F32)]
         + [pltpu.VMEM(part.shape, part.dtype) for part in packed_shapes[1:]]
         + [
-            pltpu.VMEM((2, NODES, LANES), F32), left, right,
-            pltpu.SemaphoreType.DMA((len(operands),)), pltpu.SemaphoreType.DMA((ORDER + 4,)),
+            pltpu.VMEM((2, NODES, LANES), F32), pltpu.VMEM((3 * HIGH * ROWS, CYCLE * LANES), BF16), right,
+            pltpu.SemaphoreType.DMA((len(operands),)), pltpu.SemaphoreType.DMA((ORDER + 5,)),
         ],
         *operands,
         in_specs=[hbm] * len(operands), out_specs=[hbm] * len(packed_shapes), limit=FIRST_LIMIT,
@@ -763,29 +788,37 @@
     gathered = swap_blocks(packed.reshape(MODES, BLOCK, ROWS, LANES), "mode")
     *mixed, extra = call(
         transform_kernel, [shape(SHARE, ROWS, LANES)] * MODES + [shape(SLOT_TILES, 8, LANES)],
-        [pltpu.VMEM((SLOT_TILES, PLANES, LANES), F32)], forward, gathered, *exchange(message), masks,
-    )
-    search, moved, kept, slots, sums = call(
+        [pltpu.VMEM((SLOT_TILES, PLANES, LANES), F32)], forward, gathered, *exchange(message), lists,
+    )
+    inside = shape(INNER, ROWS, LANES)
+    search, inverse, applied, source, kept, slots, sums = call(
         first_kernel,
         [
-            shape(INNER, ROWS, LANES), shape(INNER, ROWS, LANES), shape(4, *wide),
-            shape(SLOT_TILES, ROWS, LANES), shape(4, ROWS, LANES),
+            inside, inside, shape(NODES, ROWS, LANES), shape(MODES, BLOCK, ROWS, LANES), shape(4, *wide),
+            shape(SLOT_TILES, ROWS, LANES), shape(2, ROWS, LANES),
         ],
-        [left, right, packing, cells, cells, first, energy, energy],
-        *swap_steps(mixed), extra, shared, edge_rows, metric, inner, diagonal, penalties,
+        [left, right, cycle, first, energy, energy],
+        *swap_steps(mixed), extra, lists, edge_rows, metric, inner, diagonal, penalties,
+    )
+    moved, moved_sums = call(
+        change_kernel, [inside, shape(2, ROWS, LANES)], [], search, inverse, applied, source
     )
     change, message = call(
         second_kernel,
         [shape(*wide), shape(ELEMS_AXIS, LANES)],
-        [left_slots, cells, first, energy, energy],
-        moved, kept, sums, *exchange(slots), masks, shared, edge_rows, metric, penalties,
+        [left_slots, cycle, first, energy, energy],
+        moved, kept, sums, moved_sums, *exchange(slots), lists, edge_rows, metric, penalties,
     )
     scalars = swap_blocks(message, "elem")
     scaled = call(scale_kernel, blocks, [packing], scalars, search, moved, kept, change)
     mixed = call(
         combine_kernel, blocks, [pltpu.VMEM((BLOCK, PLANES, LANES), F32)], backward, *swap_steps(scaled)
     )
-    result = call(unpack_kernel, shape(NODES, ROWS, LANES), [packing], *swap_steps(mixed), edge_rows)
+    result = call(
+        unpack_kernel, shape(NODES, ROWS, LANES),
+        [packing, pltpu.VMEM((NODES, ROWS, LANES), F32), pltpu.SemaphoreType.DMA((3,))],
+        *swap_steps(mixed), edge_rows, out_specs=hbm,
+    )
     return result.transpose(1, 0, 2)
 
 

time: 103 us -> 101 us (0.981)
  Pallas kernels: 16.5 us -> 15.1 us
    pallas_call x7 -> x8, Pallas kernels: 16.5 us -> 15.1 us  [call(): pl.pallas_call(kernel, out_shape=out_shapes, scratch_shapes=scratch, comp...]
  transfers between devices with their start and end apart: 32 -> 32, of which waited for: 13 -> 15; matrix products, arithmetic and copies ran while one was open for 0% -> 0% of each run, Pallas kernels for 0% -> 0%
where the time goes in v4:
time: 101 us; the launch traced here: 100 us
  starting transfers between devices  55.4 us (55%)
  Pallas kernels  15.1 us (15%)
  blocking collectives  14.8 us (15%)
  waiting for transfers between devices  14.6 us (14%)
    ppermute x31, starting transfers between devices, permute(): lax.ppermute(value, axis, [(i, i ^ flip) for i in range(lax.axis_size(axi...  48.5 us
    pallas_call x8, Pallas kernels, call(): pl.pallas_call(kernel, out_shape=out_shapes, scratch_shapes=scratch, comp...  15.1 us
    all_to_all x1, blocking collectives, swap_blocks(): return lax.all_to_all(blocks, axis, split_axis=0, concat_axis=0, tiled=True)  14.8 us
    ppermute x31, waiting for transfers between devices, permute(): lax.ppermute(value, axis, [(i, i ^ flip) for i in range(lax.axis_size(axi...  14.6 us
    all_to_all x1, starting transfers between devices, swap_blocks(): return lax.all_to_all(blocks, axis, split_axis=0, concat_axis=0, tiled=True)  6.82 us
  transfers between devices with their start and end apart: 32, of which 15 were waited for; matrix products, arithmetic and copies ran while one was open for 0% of the time, Pallas kernels for 0%

profile of v4, /device:TPU:1, one launch (start us, length us, event | category | flops | bytes accessed | tf_op | source)
XLA Modules:
  0.0 100.4 jit_solution(14408952547759459766)
XLA Ops:
  0.0 4.4 %shard_map.100 = (f32[72,16,128]{2,1,0:T(8,128)}, f32[3,24,128]{2,1,0:T(8,128)}, f32[2,49,128]{2,1,0:T(8,128)}, f32[2,9,256]{2,1,0:T(8,128)}, f32[9,256]{1,0:T(8,128)}, /*index=5*/s32[8,128]{1,0:T(8,128)}) custom-call(f32[81,16,128]{2,1,0:T(8,128)} %bitcast.20, s32[32,128]{1,0:T(8,128)} %bitcast.14, s32[3,128]{1,0:T(4,128)} %bitcast.22, s32[3,128]{1,0:T(4,128)} %bitcast.23, ...), custom_call_target="tpu_custom_call" | custom-call | tf_op jit(solution)/shard_map/pallas_call | solution.py:724
  4.5 6.8 %all-to-all-start = ((f32[8,9,16,128]{3,2,1,0:T(8,128)}), f32[8,9,16,128]{3,2,1,0:T(8,128)S(1)}, u32[]{:S(2)}, u32[]{:S(2)}) async-start(f32[8,9,16,128]{3,2,1,0:T(8,128)} %bitcast.21), calls=%async_computation | async-start | bytes 1179648 | tf_op jit(solution)/shard_map/all_to_all | solution.py:738
  11.3 6.0 %collective-permute-start.4 = (f32[3,24,128]{2,1,0:T(8,128)S(1)}, f32[3,24,128]{2,1,0:T(8,128)S(1)}, u32[]{:S(2)}, u32[]{:S(2)}) collective-permute-start(f32[3,24,128]{2,1,0:T(8,128)S(1)} %copy-done.8), channel_id=1, source_target_pairs={{0,16},{1,17},{2,18},{3,19},{4,20},{5,21},{6,22},{7,23},{8,24},{9,... | collective-permute-start | bytes 110600 | tf_op jit(solution)/shard_map/ppermute | solution.py:742
  18.5 2.9 %collective-permute-start.2 = (f32[3,24,128]{2,1,0:T(8,128)S(1)}, f32[3,24,128]{2,1,0:T(8,128)S(1)}, u32[]{:S(2)}, u32[]{:S(2)}) collective-permute-start(f32[3,24,128]{2,1,0:T(8,128)S(1)} %copy-done.8), channel_id=1, source_target_pairs={{0,2},{1,3},{2,0},{3,1},{4,6},{5,7},{6,4},{7,5},{8,10},{9,11},{10,... | collective-permute-start | bytes 110600 | tf_op jit(solution)/shard_map/ppermute | solution.py:742
  22.8 1.4 %collective-permute-done.1.a2 = f32[3,24,128]{2,1,0:T(8,128)S(1)} collective-permute-done((f32[3,24,128]{2,1,0:T(8,128)S(1)}, f32[3,24,128]{2,1,0:T(8,128)S(1)}, u32[]{:S(2)}, u32[]{:S(2)}) %collective-permute-start.1) | collective-permute-done | bytes 36896 | tf_op jit(solution)/shard_map/ppermute | solution.py:742
  25.9 3.0 %collective-permute-start.5 = (f32[12,16,128]{2,1,0:T(8,128)S(1)}, f32[12,16,128]{2,1,0:T(8,128)S(1)}, u32[]{:S(2)}, u32[]{:S(2)}) collective-permute-start(f32[12,16,128]{2,1,0:T(8,128)S(1)} %get-tuple-element.50), channel_id=1, source_target_pairs={{0,128},{32,160},{64,192},{96,224},{128,0},{160,32},{192,64},{224,... | collective-permute-start | bytes 294920 | tf_op jit(solution)/shard_map/ppermute | solution.py:742
  28.8 2.6 %collective-permute-start.6 = (f32[12,16,128]{2,1,0:T(8,128)S(1)}, f32[12,16,128]{2,1,0:T(8,128)S(1)}, u32[]{:S(2)}, u32[]{:S(2)}) collective-permute-start(f32[12,16,128]{2,1,0:T(8,128)S(1)} %get-tuple-element.51), channel_id=1, source_target_pairs={{0,160},{32,128},{64,224},{96,192},{128,32},{160,0},{192,96},{224,... | collective-permute-start | bytes 294920 | tf_op jit(solution)/shard_map/ppermute | solution.py:742
  33.1 1.8 %collective-permute-start.9 = (f32[12,16,128]{2,1,0:T(8,128)S(1)}, f32[12,16,128]{2,1,0:T(8,128)S(1)}, u32[]{:S(2)}, u32[]{:S(2)}) collective-permute-start(f32[12,16,128]{2,1,0:T(8,128)S(1)} %get-tuple-element.54), channel_id=1, source_target_pairs={{0,192},{32,224},{64,128},{96,160},{128,64},{160,96},{192,0},{224,... | collective-permute-start | bytes 294920 | tf_op jit(solution)/shard_map/ppermute | solution.py:742
  34.9 1.5 %collective-permute-start.10 = (f32[12,16,128]{2,1,0:T(8,128)S(1)}, f32[12,16,128]{2,1,0:T(8,128)S(1)}, u32[]{:S(2)}, u32[]{:S(2)}) collective-permute-start(f32[12,16,128]{2,1,0:T(8,128)S(1)} %get-tuple-element.55), channel_id=1, source_target_pairs={{0,96},{32,64},{64,32},{96,0},{128,224},{160,192},{192,160},{224,1... | collective-permute-start | bytes 294920 | tf_op jit(solution)/shard_map/ppermute | solution.py:742
  37.4 1.3 %collective-permute-done.7.i7 = f32[12,16,128]{2,1,0:T(8,128)S(1)} collective-permute-done((f32[12,16,128]{2,1,0:T(8,128)S(1)}, f32[12,16,128]{2,1,0:T(8,128)S(1)}, u32[]{:S(2)}, u32[]{:S(2)}) %collective-permute-start.7) | collective-permute-done | bytes 98336 | tf_op jit(solution)/shard_map/ppermute | solution.py:742
  38.7 1.4 %collective-permute-done.9.i6 = f32[12,16,128]{2,1,0:T(8,128)S(1)} collective-permute-done((f32[12,16,128]{2,1,0:T(8,128)S(1)}, f32[12,16,128]{2,1,0:T(8,128)S(1)}, u32[]{:S(2)}, u32[]{:S(2)}) %collective-permute-start.9) | collective-permute-done | bytes 98336 | tf_op jit(solution)/shard_map/ppermute | solution.py:742
  40.9 4.7 %shard_map.102 = (f32[49,16,128]{2,1,0:T(8,128)S(1)}, f32[49,16,128]{2,1,0:T(8,128)S(1)}, f32[81,16,128]{2,1,0:T(8,128)S(1)}, f32[8,9,16,128]{3,2,1,0:T(8,128)S(...) custom-call(f32[12,16,128]{2,1,0:T(8,128)S(1)} %collective-permute-done.5.i4, ...), custom_call_target="tpu_custom_call" | custom-call | tf_op jit(solution)/shard_map/pallas_call | solution.py:724
  47.3 2.9 %collective-permute-start.14 = (f32[3,16,128]{2,1,0:T(8,128)S(1)}, f32[3,16,128]{2,1,0:T(8,128)S(1)}, u32[]{:S(2)}, u32[]{:S(2)}) collective-permute-start(f32[3,16,128]{2,1,0:T(8,128)S(1)} %get-tuple-element.70), channel_id=1, source_target_pairs={{0,2},{1,3},{2,0},{3,1},{4,6},{5,7},{6,4},{7,5},{8,10},{9,11},{10,... | collective-permute-start | bytes 73736 | tf_op jit(solution)/shard_map/ppermute | solution.py:742
  53.6 2.3 %shard_map.104 = (f32[144,256]{1,0:T(8,128)S(1)}, f32[32,128]{1,0:T(8,128)S(1)}) custom-call(f32[49,16,128]{2,1,0:T(8,128)S(1)} %get-tuple-element.66.moved_ref, f32[4,144,256]{2,1,0:T(8,128)S(1)} %get-tuple-element.67.kept_ref, f32[2,16,128]{2,1,0:T(8,128)S(1)} %get-tuple-element.68.sums_ref, f32[2,16,128]{2,1,0:T(8,128)S(1)} %get-tuple-element.69.moved_sums_ref, ...), custom_call_target="tpu_custom_call" | custom-call | tf_op jit(solution)/shard_map/pallas_call | solution.py:724
  56.0 14.8 %all_to_all.16 = f32[32,1,128]{2,1,0:T(1,128)S(1)} all-to-all(f32[32,1,128]{2,1,0:T(1,128)S(1)} %bitcast.19), channel_id=1, replica_groups=mesh['mode'=8,'elem'=32] {'elem'}, dimensions={0} | all-to-all | bytes 32768 | tf_op jit(solution)/shard_map/all_to_all | solution.py:738
  71.0 2.3 %collective-permute-start.17 = (f32[9,16,128]{2,1,0:T(8,128)S(1)}, f32[9,16,128]{2,1,0:T(8,128)S(1)}, u32[]{:S(2)}, u32[]{:S(2)}) collective-permute-start(f32[9,16,128]{2,1,0:T(8,128)S(1)} %get-tuple-element.73), channel_id=1, source_target_pairs={{0,128},{32,160},{64,192},{96,224},{128,0},{160,32},{192,64},{224,... | collective-permute-start | bytes 221192 | tf_op jit(solution)/shard_map/ppermute | solution.py:742
  73.3 4.9 %collective-permute-start.18 = (f32[9,16,128]{2,1,0:T(8,128)S(1)}, f32[9,16,128]{2,1,0:T(8,128)S(1)}, u32[]{:S(2)}, u32[]{:S(2)}) collective-permute-start(f32[9,16,128]{2,1,0:T(8,128)S(1)} %get-tuple-element.74), channel_id=1, source_target_pairs={{0,160},{32,128},{64,224},{96,192},{128,32},{160,0},{192,96},{224,... | collective-permute-start | bytes 221192 | tf_op jit(solution)/shard_map/ppermute | solution.py:742
  79.4 1.3 %collective-permute-start.21 = (f32[9,16,128]{2,1,0:T(8,128)S(1)}, f32[9,16,128]{2,1,0:T(8,128)S(1)}, u32[]{:S(2)}, u32[]{:S(2)}) collective-permute-start(f32[9,16,128]{2,1,0:T(8,128)S(1)} %get-tuple-element.77), channel_id=1, source_target_pairs={{0,192},{32,224},{64,128},{96,160},{128,64},{160,96},{192,0},{224,... | collective-permute-start | bytes 221192 | tf_op jit(solution)/shard_map/ppermute | solution.py:742
  80.7 1.9 %collective-permute-start.22 = (f32[9,16,128]{2,1,0:T(8,128)S(1)}, f32[9,16,128]{2,1,0:T(8,128)S(1)}, u32[]{:S(2)}, u32[]{:S(2)}) collective-permute-start(f32[9,16,128]{2,1,0:T(8,128)S(1)} %get-tuple-element.78), channel_id=1, source_target_pairs={{0,96},{32,64},{64,32},{96,0},{128,224},{160,192},{192,160},{224,1... | collective-permute-start | bytes 221192 | tf_op jit(solution)/shard_map/ppermute | solution.py:742
  84.5 2.0 %collective-permute-done.22.i3 = f32[9,16,128]{2,1,0:T(8,128)S(1)} collective-permute-done((f32[9,16,128]{2,1,0:T(8,128)S(1)}, f32[9,16,128]{2,1,0:T(8,128)S(1)}, u32[]{:S(2)}, u32[]{:S(2)}) %collective-permute-start.22) | collective-permute-done | bytes 73760 | tf_op jit(solution)/shard_map/ppermute | solution.py:742
  88.2 2.7 %collective-permute-start.25 = (f32[9,16,128]{2,1,0:T(8,128)S(1)}, f32[9,16,128]{2,1,0:T(8,128)S(1)}, u32[]{:S(2)}, u32[]{:S(2)}) collective-permute-start(f32[9,16,128]{2,1,0:T(8,128)S(1)} %get-tuple-element.82), channel_id=1, source_target_pairs={{0,160},{32,128},{64,224},{96,192},{128,32},{160,0},{192,96},{224,... | collective-permute-start | bytes 221192 | tf_op jit(solution)/shard_map/ppermute | solution.py:742
  93.2 2.0 %collective-permute-start.29 = (f32[9,16,128]{2,1,0:T(8,128)S(1)}, f32[9,16,128]{2,1,0:T(8,128)S(1)}, u32[]{:S(2)}, u32[]{:S(2)}) collective-permute-start(f32[9,16,128]{2,1,0:T(8,128)S(1)} %get-tuple-element.86), channel_id=1, source_target_pairs={{0,96},{32,64},{64,32},{96,0},{128,224},{160,192},{192,160},{224,1... | collective-permute-start | bytes 221192 | tf_op jit(solution)/shard_map/ppermute | solution.py:742
  96.8 1.5 %collective-permute-done.29.i3 = f32[9,16,128]{2,1,0:T(8,128)S(1)} collective-permute-done((f32[9,16,128]{2,1,0:T(8,128)S(1)}, f32[9,16,128]{2,1,0:T(8,128)S(1)}, u32[]{:S(2)}, u32[]{:S(2)}) %collective-permute-start.29) | collective-permute-done | bytes 73760 | tf_op jit(solution)/shard_map/ppermute | solution.py:742
  98.3 1.9 %shard_map.107 = f32[81,16,128]{2,1,0:T(8,128)} custom-call(f32[9,16,128]{2,1,0:T(8,128)S(1)} %collective-permute-done.24.i4, f32[9,16,128]{2,1,0:T(8,128)S(1)} %collective-permute-done.25.i5, f32[9,16,128]{2,1,0:T(8,128)S(1)} %collective-permute-done.26.i7, f32[9,16,128]{2,1,0:T(8,128)S(1)} %collective-permute-done.27.i2, ...), custom_call_target="tpu_custom_call" | custom-call | tf_op jit(solution)/shard_map/pallas_call | solution.py:724
  (67 shorter events, 21.7 us)
Async XLA Ops:
  4.5 20.5 %all-to-all-start = ((f32[8,9,16,128]{3,2,1,0:T(8,128)}), f32[8,9,16,128]{3,2,1,0:T(8,128)S(1)}, u32[]{:S(2)}, u32[]{:S(2)}) async-start(f32[8,9,16,128]{3,2,1,0:T(8,128)} %bitcast.21), calls=%async_computation | async-start | bytes 1179648 | tf_op jit(solution)/shard_map/all_to_all | solution.py:738
  11.3 11.3 %collective-permute-start.4 = (f32[3,24,128]{2,1,0:T(8,128)S(1)}, f32[3,24,128]{2,1,0:T(8,128)S(1)}, u32[]{:S(2)}, u32[]{:S(2)}) collective-permute-start(f32[3,24,128]{2,1,0:T(8,128)S(1)} %copy-done.8), channel_id=1, source_target_pairs={{0,16},{1,17},{2,18},{3,19},{4,20},{5,21},{6,22},{7,23},{8,24},{9,... | collective-permute-start | bytes 110600 | tf_op jit(solution)/shard_map/ppermute | solution.py:742
  17.3 5.3 %collective-permute-start.3 = (f32[3,24,128]{2,1,0:T(8,128)S(1)}, f32[3,24,128]{2,1,0:T(8,128)S(1)}, u32[]{:S(2)}, u32[]{:S(2)}) collective-permute-start(f32[3,24,128]{2,1,0:T(8,128)S(1)} %copy-done.8), channel_id=1, source_target_pairs={{0,8},{1,9},{2,10},{3,11},{4,12},{5,13},{6,14},{7,15},{8,0},{9,1},... | collective-permute-start | bytes 110600 | tf_op jit(solution)/shard_map/ppermute | solution.py:742
  25.9 9.0 %collective-permute-start.5 = (f32[12,16,128]{2,1,0:T(8,128)S(1)}, f32[12,16,128]{2,1,0:T(8,128)S(1)}, u32[]{:S(2)}, u32[]{:S(2)}) collective-permute-start(f32[12,16,128]{2,1,0:T(8,128)S(1)} %get-tuple-element.50), channel_id=1, source_target_pairs={{0,128},{32,160},{64,192},{96,224},{128,0},{160,32},{192,64},{224,... | collective-permute-start | bytes 294920 | tf_op jit(solution)/shard_map/ppermute | solution.py:742
  28.8 7.5 %collective-permute-start.6 = (f32[12,16,128]{2,1,0:T(8,128)S(1)}, f32[12,16,128]{2,1,0:T(8,128)S(1)}, u32[]{:S(2)}, u32[]{:S(2)}) collective-permute-start(f32[12,16,128]{2,1,0:T(8,128)S(1)} %get-tuple-element.51), channel_id=1, source_target_pairs={{0,160},{32,128},{64,224},{96,192},{128,32},{160,0},{192,96},{224,... | collective-permute-start | bytes 294920 | tf_op jit(solution)/shard_map/ppermute | solution.py:742
  31.4 7.3 %collective-permute-start.7 = (f32[12,16,128]{2,1,0:T(8,128)S(1)}, f32[12,16,128]{2,1,0:T(8,128)S(1)}, u32[]{:S(2)}, u32[]{:S(2)}) collective-permute-start(f32[12,16,128]{2,1,0:T(8,128)S(1)} %get-tuple-element.52), channel_id=1, source_target_pairs={{0,224},{32,192},{64,160},{96,128},{128,96},{160,64},{192,32},{224... | collective-permute-start | bytes 294920 | tf_op jit(solution)/shard_map/ppermute | solution.py:742
  32.5 6.2 %collective-permute-start.8 = (f32[12,16,128]{2,1,0:T(8,128)S(1)}, f32[12,16,128]{2,1,0:T(8,128)S(1)}, u32[]{:S(2)}, u32[]{:S(2)}) collective-permute-start(f32[12,16,128]{2,1,0:T(8,128)S(1)} %get-tuple-element.53), channel_id=1, source_target_pairs={{0,64},{32,96},{64,0},{96,32},{128,192},{160,224},{192,128},{224,1... | collective-permute-start | bytes 294920 | tf_op jit(solution)/shard_map/ppermute | solution.py:742
  33.1 7.0 %collective-permute-start.9 = (f32[12,16,128]{2,1,0:T(8,128)S(1)}, f32[12,16,128]{2,1,0:T(8,128)S(1)}, u32[]{:S(2)}, u32[]{:S(2)}) collective-permute-start(f32[12,16,128]{2,1,0:T(8,128)S(1)} %get-tuple-element.54), channel_id=1, source_target_pairs={{0,192},{32,224},{64,128},{96,160},{128,64},{160,96},{192,0},{224,... | collective-permute-start | bytes 294920 | tf_op jit(solution)/shard_map/ppermute | solution.py:742
  34.9 5.9 %collective-permute-start.10 = (f32[12,16,128]{2,1,0:T(8,128)S(1)}, f32[12,16,128]{2,1,0:T(8,128)S(1)}, u32[]{:S(2)}, u32[]{:S(2)}) collective-permute-start(f32[12,16,128]{2,1,0:T(8,128)S(1)} %get-tuple-element.55), channel_id=1, source_target_pairs={{0,96},{32,64},{64,32},{96,0},{128,224},{160,192},{192,160},{224,1... | collective-permute-start | bytes 294920 | tf_op jit(solution)/shard_map/ppermute | solution.py:742
  36.3 4.5 %collective-permute-start.11 = (f32[12,16,128]{2,1,0:T(8,128)S(1)}, f32[12,16,128]{2,1,0:T(8,128)S(1)}, u32[]{:S(2)}, u32[]{:S(2)}) collective-permute-start(f32[12,16,128]{2,1,0:T(8,128)S(1)} %get-tuple-element.56), channel_id=1, source_target_pairs={{0,32},{32,0},{64,96},{96,64},{128,160},{160,128},{192,224},{224,1... | collective-permute-start | bytes 294920 | tf_op jit(solution)/shard_map/ppermute | solution.py:742
  45.6 6.8 %collective-permute-start.16 = (f32[3,16,128]{2,1,0:T(8,128)S(1)}, f32[3,16,128]{2,1,0:T(8,128)S(1)}, u32[]{:S(2)}, u32[]{:S(2)}) collective-permute-start(f32[3,16,128]{2,1,0:T(8,128)S(1)} %get-tuple-element.70), channel_id=1, source_target_pairs={{0,16},{1,17},{2,18},{3,19},{4,20},{5,21},{6,22},{7,23},{8,24},{9,... | collective-permute-start | bytes 73736 | tf_op jit(solution)/shard_map/ppermute | solution.py:742
  46.8 5.5 %collective-permute-start.15 = (f32[3,16,128]{2,1,0:T(8,128)S(1)}, f32[3,16,128]{2,1,0:T(8,128)S(1)}, u32[]{:S(2)}, u32[]{:S(2)}) collective-permute-start(f32[3,16,128]{2,1,0:T(8,128)S(1)} %get-tuple-element.70), channel_id=1, source_target_pairs={{0,8},{1,9},{2,10},{3,11},{4,12},{5,13},{6,14},{7,15},{8,0},{9,1},... | collective-permute-start | bytes 73736 | tf_op jit(solution)/shard_map/ppermute | solution.py:742
  47.3 5.0 %collective-permute-start.14 = (f32[3,16,128]{2,1,0:T(8,128)S(1)}, f32[3,16,128]{2,1,0:T(8,128)S(1)}, u32[]{:S(2)}, u32[]{:S(2)}) collective-permute-start(f32[3,16,128]{2,1,0:T(8,128)S(1)} %get-tuple-element.70), channel_id=1, source_target_pairs={{0,2},{1,3},{2,0},{3,1},{4,6},{5,7},{6,4},{7,5},{8,10},{9,11},{10,... | collective-permute-start | bytes 73736 | tf_op jit(solution)/shard_map/ppermute | solution.py:742
  71.0 9.7 %collective-permute-start.17 = (f32[9,16,128]{2,1,0:T(8,128)S(1)}, f32[9,16,128]{2,1,0:T(8,128)S(1)}, u32[]{:S(2)}, u32[]{:S(2)}) collective-permute-start(f32[9,16,128]{2,1,0:T(8,128)S(1)} %get-tuple-element.73), channel_id=1, source_target_pairs={{0,128},{32,160},{64,192},{96,224},{128,0},{160,32},{192,64},{224,... | collective-permute-start | bytes 221192 | tf_op jit(solution)/shard_map/ppermute | solution.py:742
  73.3 9.4 %collective-permute-start.18 = (f32[9,16,128]{2,1,0:T(8,128)S(1)}, f32[9,16,128]{2,1,0:T(8,128)S(1)}, u32[]{:S(2)}, u32[]{:S(2)}) collective-permute-start(f32[9,16,128]{2,1,0:T(8,128)S(1)} %get-tuple-element.74), channel_id=1, source_target_pairs={{0,160},{32,128},{64,224},{96,192},{128,32},{160,0},{192,96},{224,... | collective-permute-start | bytes 221192 | tf_op jit(solution)/shard_map/ppermute | solution.py:742
  78.2 5.8 %collective-permute-start.19 = (f32[9,16,128]{2,1,0:T(8,128)S(1)}, f32[9,16,128]{2,1,0:T(8,128)S(1)}, u32[]{:S(2)}, u32[]{:S(2)}) collective-permute-start(f32[9,16,128]{2,1,0:T(8,128)S(1)} %get-tuple-element.75), channel_id=1, source_target_pairs={{0,224},{32,192},{64,160},{96,128},{128,96},{160,64},{192,32},{224... | collective-permute-start | bytes 221192 | tf_op jit(solution)/shard_map/ppermute | solution.py:742
  78.8 5.2 %collective-permute-start.20 = (f32[9,16,128]{2,1,0:T(8,128)S(1)}, f32[9,16,128]{2,1,0:T(8,128)S(1)}, u32[]{:S(2)}, u32[]{:S(2)}) collective-permute-start(f32[9,16,128]{2,1,0:T(8,128)S(1)} %get-tuple-element.76), channel_id=1, source_target_pairs={{0,64},{32,96},{64,0},{96,32},{128,192},{160,224},{192,128},{224,1... | collective-permute-start | bytes 221192 | tf_op jit(solution)/shard_map/ppermute | solution.py:742
  79.4 5.1 %collective-permute-start.21 = (f32[9,16,128]{2,1,0:T(8,128)S(1)}, f32[9,16,128]{2,1,0:T(8,128)S(1)}, u32[]{:S(2)}, u32[]{:S(2)}) collective-permute-start(f32[9,16,128]{2,1,0:T(8,128)S(1)} %get-tuple-element.77), channel_id=1, source_target_pairs={{0,192},{32,224},{64,128},{96,160},{128,64},{160,96},{192,0},{224,... | collective-permute-start | bytes 221192 | tf_op jit(solution)/shard_map/ppermute | solution.py:742
  80.7 5.8 %collective-permute-start.22 = (f32[9,16,128]{2,1,0:T(8,128)S(1)}, f32[9,16,128]{2,1,0:T(8,128)S(1)}, u32[]{:S(2)}, u32[]{:S(2)}) collective-permute-start(f32[9,16,128]{2,1,0:T(8,128)S(1)} %get-tuple-element.78), channel_id=1, source_target_pairs={{0,96},{32,64},{64,32},{96,0},{128,224},{160,192},{192,160},{224,1... | collective-permute-start | bytes 221192 | tf_op jit(solution)/shard_map/ppermute | solution.py:742
  87.2 6.0 %collective-permute-start.24 = (f32[9,16,128]{2,1,0:T(8,128)S(1)}, f32[9,16,128]{2,1,0:T(8,128)S(1)}, u32[]{:S(2)}, u32[]{:S(2)}) collective-permute-start(f32[9,16,128]{2,1,0:T(8,128)S(1)} %get-tuple-element.81), channel_id=1, source_target_pairs={{0,128},{32,160},{64,192},{96,224},{128,0},{160,32},{192,64},{224,... | collective-permute-start | bytes 221192 | tf_op jit(solution)/shard_map/ppermute | solution.py:742
  88.2 7.0 %collective-permute-start.25 = (f32[9,16,128]{2,1,0:T(8,128)S(1)}, f32[9,16,128]{2,1,0:T(8,128)S(1)}, u32[]{:S(2)}, u32[]{:S(2)}) collective-permute-start(f32[9,16,128]{2,1,0:T(8,128)S(1)} %get-tuple-element.82), channel_id=1, source_target_pairs={{0,160},{32,128},{64,224},{96,192},{128,32},{160,0},{192,96},{224,... | collective-permute-start | bytes 221192 | tf_op jit(solution)/shard_map/ppermute | solution.py:742
  90.8 5.5 %collective-permute-start.26 = (f32[9,16,128]{2,1,0:T(8,128)S(1)}, f32[9,16,128]{2,1,0:T(8,128)S(1)}, u32[]{:S(2)}, u32[]{:S(2)}) collective-permute-start(f32[9,16,128]{2,1,0:T(8,128)S(1)} %get-tuple-element.83), channel_id=1, source_target_pairs={{0,224},{32,192},{64,160},{96,128},{128,96},{160,64},{192,32},{224... | collective-permute-start | bytes 221192 | tf_op jit(solution)/shard_map/ppermute | solution.py:742
  92.1 4.7 %collective-permute-start.28 = (f32[9,16,128]{2,1,0:T(8,128)S(1)}, f32[9,16,128]{2,1,0:T(8,128)S(1)}, u32[]{:S(2)}, u32[]{:S(2)}) collective-permute-start(f32[9,16,128]{2,1,0:T(8,128)S(1)} %get-tuple-element.85), channel_id=1, source_target_pairs={{0,192},{32,224},{64,128},{96,160},{128,64},{160,96},{192,0},{224,... | collective-permute-start | bytes 221192 | tf_op jit(solution)/shard_map/ppermute | solution.py:742
  93.2 5.1 %collective-permute-start.29 = (f32[9,16,128]{2,1,0:T(8,128)S(1)}, f32[9,16,128]{2,1,0:T(8,128)S(1)}, u32[]{:S(2)}, u32[]{:S(2)}) collective-permute-start(f32[9,16,128]{2,1,0:T(8,128)S(1)} %get-tuple-element.86), channel_id=1, source_target_pairs={{0,96},{32,64},{64,32},{96,0},{128,224},{160,192},{192,160},{224,1... | collective-permute-start | bytes 221192 | tf_op jit(solution)/shard_map/ppermute | solution.py:742
  (17 other events, 168.7 us)

commit v5 on v4

--- a/solution.py
+++ b/solution.py
@@ -23,6 +23,7 @@
 LOW = 256
 HIGH = 9
 TILES = 2 * HIGH
+QUADS = -(-HIGH // 4)
 SLOTS = 384
 SLOT_TILES = SLOTS // LANES
 BLOCK = 9
@@ -124,16 +125,18 @@
 
 
 def one_hot_rows(low_rows):
-    sublanes = lax.broadcasted_iota(jnp.int32, (LOW, low_rows.shape[1]), 0)
-    return jnp.where(low_rows == sublanes, 1.0, 0.0).astype(BF16)
+    sublanes = lax.broadcasted_iota(jnp.int32, (LOW, low_rows.shape[1]), 0).astype(BF16)
+    wanted = jnp.broadcast_to(low_rows.astype(BF16), sublanes.shape)
+    return jnp.where(wanted == sublanes, BF16(1.0), BF16(0.0))
 
 
 def masked_store(value, high_row, left_ref, column):
-    top, rest = pieces(value)
+    top, rest = [part.astype(BF16) for part in pieces(value)]
+    wanted = jnp.broadcast_to(high_row.astype(BF16), value.shape)
     for high in range(HIGH):
-        here = high_row == high
-        left_ref[row_block(high), lane_block(column)] = jnp.where(here, top, 0.0).astype(BF16)
-        left_ref[row_block(HIGH + high), lane_block(column)] = jnp.where(here, rest, 0.0).astype(BF16)
+        here = wanted == BF16(high)
+        left_ref[row_block(high), lane_block(column)] = jnp.where(here, top, BF16(0.0))
+        left_ref[row_block(HIGH + high), lane_block(column)] = jnp.where(here, rest, BF16(0.0))
 
 
 def contract_lanes(left, right):
@@ -166,21 +169,25 @@
 
 
 def four_pieces(first, second):
-    sublanes = lax.broadcasted_iota(jnp.int32, (ROWS, first.shape[1]), 0)
+    sublanes = jnp.bitwise_and(lax.broadcasted_iota(jnp.int32, (ROWS, first.shape[1]), 0), 3)
     first_top, first_rest = pieces(first)
     second_top, second_rest = pieces(second)
-    rest = jnp.where(sublanes == 2, first_rest, jnp.where(sublanes == 3, second_rest, 0.0))
-    return jnp.where(sublanes == 0, first_top, jnp.where(sublanes == 1, second_top, rest))
+    tops = jnp.where(sublanes == 0, first_top, second_top)
+    rests = jnp.where(sublanes == 2, first_rest, second_rest)
+    return jnp.where(sublanes < 2, tops, rests)
 
 
 def masked_store_four(value, high_row, left_ref, column):
-    for high in range(HIGH):
-        part = jnp.where(high_row == high, value, 0.0).astype(BF16)
-        left_ref[row_block(high), lane_block(column)] = part
+    packed = value.astype(BF16)
+    quarter = jnp.right_shift(lax.broadcasted_iota(jnp.int32, value.shape, 0), 2).astype(BF16)
+    wanted = jnp.broadcast_to(high_row.astype(BF16), value.shape) - quarter
+    for block in range(QUADS):
+        here = wanted == BF16(4 * block)
+        left_ref[row_block(block), lane_block(column)] = jnp.where(here, packed, BF16(0.0))
 
 
 def two_rows(total, high):
-    base = high * ROWS
+    base = 4 * high
     first = total[base : base + 1, :] + total[base + 2 : base + 3, :]
     second = total[base + 1 : base + 2, :] + total[base + 3 : base + 4, :]
     return first, second
@@ -473,7 +480,7 @@
         high_row = high_rows[slot : slot + 1, :]
         masked_store(forcing_ref[node], high_row, left_ref, slot)
         value = four_pieces(cells_ref[0, node : node + 1, :], cells_ref[1, node : node + 1, :])
-        masked_store_four(value, high_row, left_ref.at[pl.ds(base, HIGH * ROWS)], slot)
+        masked_store_four(value, high_row, left_ref.at[pl.ds(base, QUADS * ROWS)], slot)
     total = contract_lanes(left_ref[...], selectors_ref[...])
     skeleton = total[: HIGH * ROWS] + total[HIGH * ROWS : base]
 
@@ -557,7 +564,7 @@
     for tile in range(SLOT_TILES):
         value = four_pieces(extra_ref[tile, 0:1, :], extra_ref[tile, 1:2, :])
         masked_store_four(value, high_rows[tile : tile + 1, :], left_ref, tile)
-    added = contract_lanes(left_ref[: HIGH * ROWS, :SLOTS], right_slots)
+    added = contract_lanes(left_ref[: QUADS * ROWS, :SLOTS], right_slots)
     wide_shift = jnp.concatenate([shift, shift], axis=1)
     parts = []
     for high in range(HIGH):
@@ -597,27 +604,38 @@
     sums_ref[1] = start
 
 
-def change_kernel(search_ref, inverse_ref, result_ref, source_ref, moved_ref, sums_ref):
+def change_kernel(search_ref, inverse_ref, result_ref, source_ref, kept_ref, moved_ref, sums_ref, both_ref):
     crossed = jnp.zeros((ROWS, LANES), F32)
     sourced = jnp.zeros((ROWS, LANES), F32)
     for index, node in enumerate(INNER_NODES):
+        block, row = sent_place(index)
         value = result_ref[node]
-        moved = value * inverse_ref[index] - search_ref[index]
+        search = search_ref[index]
+        moved = value * inverse_ref[index] - search
         moved_ref[index] = moved
+        both_ref[block, row] = search
+        both_ref[block, BLOCK + row] = moved
         crossed = crossed + value * moved
-        sourced = sourced + source_ref[index // BLOCK, index % BLOCK] * moved
+        sourced = sourced + source_ref[block, row] * moved
+    for high in range(HIGH):
+        for part in range(2):
+            block, row = sent_place(INNER + 2 * high + part)
+            both_ref[block, row] = kept_ref[2, row_block(high), lane_block(part)]
+    for index in range(INNER + TILES, MODES * BLOCK):
+        block, row = sent_place(index)
+        both_ref[block, row] = jnp.zeros((ROWS, LANES), F32)
+        both_ref[block, BLOCK + row] = jnp.zeros((ROWS, LANES), F32)
     sums_ref[0] = crossed
     sums_ref[1] = sourced
 
 
 def second_kernel(
-    moved_ref, kept_ref, sums_ref, moved_sums_ref, a0, a2, a1, a3, a4, lists_ref, edge_ref,
-    metric_ref, penalty_ref, change_ref, message_ref, left_ref, cycle_ref, first_ref, energy_ref, shift_ref,
+    kept_ref, moved_sums_ref, filled_ref, a0, a2, a1, a3, a4, lists_ref,
+    change_ref, sums_ref, both_ref, o0, o1, o2, o3, o4, o5, o6, o7, left_ref,
 ):
     arrived_refs = [a0, a1, a2, a3, a4]
     masks = lists_ref[SLOT_TILES : 2 * SLOT_TILES, :]
     shared_rows = lists_ref[:SLOT_TILES, :]
-    shift_ref[...] = helmholtz_shift()
 
     def load(tile):
         return select_arrived(masks, tile, [ref[tile] for ref in arrived_refs])
@@ -625,9 +643,24 @@
     local, inverse, search, applied = [kept_ref[index] for index in range(4)]
     full = applied + scatter_slots(load, shared_rows, left_ref, slot_selectors(shared_rows))
     change = full * inverse - search
+    for high in range(HIGH):
+        for part in range(2):
+            block, row = sent_place(INNER + 2 * high + part)
+            both_ref[block, BLOCK + row] = change[row_block(high), lane_block(part)]
+    mode = lax.axis_index("mode")
+    for step, out_ref in enumerate([o0, o1, o2, o3, o4, o5, o6, o7]):
+        out_ref[...] = both_ref[jnp.bitwise_xor(mode, step)]
     change_ref[...] = change
-    crossed = moved_sums_ref[0] + skeleton_sum(applied * change)
-    sourced = moved_sums_ref[1] + skeleton_sum(local * change)
+    sums_ref[0] = moved_sums_ref[0] + skeleton_sum(applied * change)
+    sums_ref[1] = moved_sums_ref[1] + skeleton_sum(local * change)
+
+
+def energy_kernel(
+    moved_ref, change_ref, sums_ref, changed_sums_ref, edge_ref, metric_ref, penalty_ref, message_ref,
+    cycle_ref, first_ref, energy_ref, shift_ref,
+):
+    shift_ref[...] = helmholtz_shift()
+    change = change_ref[...]
 
     def store(slot, value):
         cycle_ref[slot] = value
@@ -638,49 +671,32 @@
     sublanes = lax.broadcasted_iota(jnp.int32, (ROWS, LANES), 0)
     lanes = lax.broadcasted_iota(jnp.int32, (ROWS, LANES), 1)
     spread = jnp.zeros((ROWS, LANES), F32)
-    for index, value in enumerate([sums_ref[0], crossed, energy, sums_ref[1], sourced]):
+    for index, value in enumerate([sums_ref[0], changed_sums_ref[0], energy, sums_ref[1], changed_sums_ref[1]]):
         column = jnp.sum(value, axis=1, keepdims=True)
         spread = jnp.where(lanes == sublanes + index * ROWS, column, spread)
     message = jnp.sum(spread, axis=0, keepdims=True)
     message_ref[...] = jnp.broadcast_to(message, message_ref.shape)
 
 
-def scale_kernel(
-    scalars_ref, inner_ref, moved_ref, kept_ref, change_ref, o0, o1, o2, o3, o4, o5, o6, o7, packed_ref
+def combine_kernel(
+    matrix_ref, scalars_ref, i4, i5, i7, i2, i6, i3, i1, i0, o0, o1, o2, o3, o4, o5, o6, o7, block_ref
 ):
+    mode = lax.axis_index("mode")
     sublanes = lax.broadcasted_iota(jnp.int32, (ROWS, LANES), 0)
     lanes = lax.broadcasted_iota(jnp.int32, (ROWS, LANES), 1)
-    total = jnp.sum(scalars_ref[...], axis=0, keepdims=True)
-    g00, g01, g11, h0, h1 = [
-        jnp.sum(jnp.where(lanes == sublanes + index * ROWS, total, 0.0), axis=1, keepdims=True)
-        for index in range(SCALARS)
-    ]
-    ratio = g01 / g00
-    pivot = g11 - ratio * g01
-    second = jnp.where(pivot > 0.0, (h1 - ratio * h0) / pivot, 0.0)
-    first = jnp.broadcast_to(h0 / g00 - ratio * second, (ROWS, LANES))
-    second = jnp.broadcast_to(second, (ROWS, LANES))
-    store = write_place(packed_ref, sent_place)
-    for index in range(INNER):
-        store(index, first * inner_ref[index] + second * moved_ref[index])
-    for high in range(HIGH):
-        for part in range(2):
-            place = (row_block(high), lane_block(part))
-            value = first * kept_ref[(2,) + place] + second * change_ref[place]
-            store(INNER + 2 * high + part, value)
-    for index in range(INNER + TILES, MODES * BLOCK):
-        store(index, jnp.zeros((ROWS, LANES), F32))
-    mode = lax.axis_index("mode")
-    for step, out_ref in enumerate([o0, o1, o2, o3, o4, o5, o6, o7]):
-        out_ref[...] = packed_ref[jnp.bitwise_xor(mode, step)]
-
-
-def combine_kernel(
-    matrix_ref, i4, i5, i7, i2, i6, i3, i1, i0, o0, o1, o2, o3, o4, o5, o6, o7, block_ref
-):
-    mode = lax.axis_index("mode")
     for step, in_ref in enumerate([i0, i1, i2, i3, i4, i5, i6, i7]):
-        block_ref[:, place(jnp.bitwise_xor(mode, step)), :] = in_ref[...]
+        origin = jnp.bitwise_xor(mode, step)
+        total = jnp.sum(scalars_ref[origin], axis=0, keepdims=True)
+        g00, g01, g11, h0, h1 = [
+            jnp.sum(jnp.where(lanes == sublanes + index * ROWS, total, 0.0), axis=1, keepdims=True)
+            for index in range(SCALARS)
+        ]
+        ratio = g01 / g00
+        pivot = g11 - ratio * g01
+        second = jnp.where(pivot > 0.0, (h1 - ratio * h0) / pivot, 0.0)
+        first = h0 / g00 - ratio * second
+        for index in range(BLOCK):
+            block_ref[index, place(origin), :] = first * in_ref[index] + second * in_ref[BLOCK + index]
     matrix = relative_rows(matrix_ref, mode)
     for index in range(BLOCK):
         mixed = jnp.dot(matrix, block_ref[index], precision=HIGHEST, preferred_element_type=F32)
@@ -779,7 +795,7 @@
         + [pltpu.VMEM((MODES * BLOCK - INNER, ROWS, LANES), F32)]
         + [pltpu.VMEM(part.shape, part.dtype) for part in packed_shapes[1:]]
         + [
-            pltpu.VMEM((2, NODES, LANES), F32), pltpu.VMEM((3 * HIGH * ROWS, CYCLE * LANES), BF16), right,
+            pltpu.VMEM((2, NODES, LANES), F32), pltpu.VMEM(((2 * HIGH + QUADS) * ROWS, CYCLE * LANES), BF16), right,
             pltpu.SemaphoreType.DMA((len(operands),)), pltpu.SemaphoreType.DMA((ORDER + 5,)),
         ],
         *operands,
@@ -800,19 +816,24 @@
         [left, right, cycle, first, energy, energy],
         *swap_steps(mixed), extra, lists, edge_rows, metric, inner, diagonal, penalties,
     )
-    moved, moved_sums = call(
-        change_kernel, [inside, shape(2, ROWS, LANES)], [], search, inverse, applied, source
-    )
-    change, message = call(
+    pair = shape(MODES, 2 * BLOCK, ROWS, LANES)
+    moved, moved_sums, filled = call(
+        change_kernel, [inside, shape(2, ROWS, LANES), pair], [], search, inverse, applied, source, kept
+    )
+    change, changed_sums, both, *pairs = call(
         second_kernel,
-        [shape(*wide), shape(ELEMS_AXIS, LANES)],
-        [left_slots, cycle, first, energy, energy],
-        moved, kept, sums, moved_sums, *exchange(slots), lists, edge_rows, metric, penalties,
-    )
-    scalars = swap_blocks(message, "elem")
-    scaled = call(scale_kernel, blocks, [packing], scalars, search, moved, kept, change)
+        [shape(*wide), shape(2, ROWS, LANES), pair] + [shape(2 * BLOCK, ROWS, LANES)] * MODES,
+        [left_slots],
+        kept, moved_sums, filled, *exchange(slots), lists,
+        input_output_aliases={2: 2},
+    )
+    message = call(
+        energy_kernel, shape(MODES * ELEMS_AXIS, LANES), [cycle, first, energy, energy],
+        moved, change, sums, changed_sums, edge_rows, metric, penalties,
+    )
+    scalars = swap_blocks(message, ("mode", "elem")).reshape(MODES, ELEMS_AXIS, LANES)
     mixed = call(
-        combine_kernel, blocks, [pltpu.VMEM((BLOCK, PLANES, LANES), F32)], backward, *swap_steps(scaled)
+        combine_kernel, blocks, [pltpu.VMEM((BLOCK, PLANES, LANES), F32)], backward, scalars, *swap_steps(pairs)
     )
     result = call(
         unpack_kernel, shape(NODES, ROWS, LANES),

time: 101 us -> 97.5 us (0.965)
  blocking collectives: 14.8 us -> 0 us
  starting transfers between devices: 55.4 us -> 64.7 us
  waiting for transfers between devices: 14.6 us -> 17.7 us
    all_to_all x1 -> x0, blocking collectives: 14.8 us -> none  [swap_blocks(): return lax.all_to_all(blocks, axis, split_axis=0, concat_axis=0, tiled=True)]
    all_to_all x1 -> x2, starting transfers between devices: 6.82 us -> 15.8 us  [swap_blocks(): return lax.all_to_all(blocks, axis, split_axis=0, concat_axis=0, tiled=True)]
    ppermute x31, waiting for transfers between devices: 14.6 us -> 17.7 us  [permute(): lax.ppermute(value, axis, [(i, i ^ flip) for i in range(lax.axis_size(axi...]
  transfers between devices with their start and end apart: 32 -> 33, of which waited for: 15 -> 16; matrix products, arithmetic and copies ran while one was open for 0% -> 0% of each run, Pallas kernels for 0% -> 3%
where the time goes in v5:
time: 97.5 us; the launch traced here: 97.3 us
  starting transfers between devices  64.7 us (66%)
  waiting for transfers between devices  17.7 us (18%)
  Pallas kernels  14.6 us (15%)
    ppermute x31, starting transfers between devices, permute(): lax.ppermute(value, axis, [(i, i ^ flip) for i in range(lax.axis_size(axi...  48.9 us
    ppermute x31, waiting for transfers between devices, permute(): lax.ppermute(value, axis, [(i, i ^ flip) for i in range(lax.axis_size(axi...  17.7 us
    all_to_all x2, starting transfers between devices, swap_blocks(): return lax.all_to_all(blocks, axis, split_axis=0, concat_axis=0, tiled=True)  15.8 us
    pallas_call x8, Pallas kernels, call(): pl.pallas_call(kernel, out_shape=out_shapes, scratch_shapes=scratch, comp...  14.6 us
  transfers between devices with their start and end apart: 33, of which 16 were waited for; matrix products, arithmetic and copies ran while one was open for 0% of the time, Pallas kernels for 3%

profile of v5, /device:TPU:1, one launch (start us, length us, event | category | flops | bytes accessed | tf_op | source)
XLA Modules:
  0.0 97.3 jit_solution(6485204088126856282)
XLA Ops:
  0.0 4.1 %shard_map.100 = (f32[72,16,128]{2,1,0:T(8,128)}, f32[3,24,128]{2,1,0:T(8,128)}, f32[2,49,128]{2,1,0:T(8,128)}, f32[2,9,256]{2,1,0:T(8,128)}, f32[9,256]{1,0:T(8,128)}, /*index=5*/s32[8,128]{1,0:T(8,128)}) custom-call(f32[81,16,128]{2,1,0:T(8,128)} %bitcast.19, s32[32,128]{1,0:T(8,128)} %bitcast.15, s32[3,128]{1,0:T(4,128)} %bitcast.21, s32[3,128]{1,0:T(4,128)} %bitcast.22, ...), custom_call_target="tpu_custom_call" | custom-call | tf_op jit(solution)/shard_map/pallas_call | solution.py:740
  4.2 6.8 %all-to-all-start = ((f32[8,9,16,128]{3,2,1,0:T(8,128)}), f32[8,9,16,128]{3,2,1,0:T(8,128)S(1)}, u32[]{:S(2)}, u32[]{:S(2)}) async-start(f32[8,9,16,128]{3,2,1,0:T(8,128)} %bitcast.20), calls=%async_computation | async-start | bytes 1179648 | tf_op jit(solution)/shard_map/all_to_all | solution.py:754
  11.0 6.0 %collective-permute-start.4 = (f32[3,24,128]{2,1,0:T(8,128)S(1)}, f32[3,24,128]{2,1,0:T(8,128)S(1)}, u32[]{:S(2)}, u32[]{:S(2)}) collective-permute-start(f32[3,24,128]{2,1,0:T(8,128)S(1)} %copy-done.8), channel_id=1, source_target_pairs={{0,16},{1,17},{2,18},{3,19},{4,20},{5,21},{6,22},{7,23},{8,24},{9,... | collective-permute-start | bytes 110600 | tf_op jit(solution)/shard_map/ppermute | solution.py:758
  18.3 2.9 %collective-permute-start.2 = (f32[3,24,128]{2,1,0:T(8,128)S(1)}, f32[3,24,128]{2,1,0:T(8,128)S(1)}, u32[]{:S(2)}, u32[]{:S(2)}) collective-permute-start(f32[3,24,128]{2,1,0:T(8,128)S(1)} %copy-done.8), channel_id=1, source_target_pairs={{0,2},{1,3},{2,0},{3,1},{4,6},{5,7},{6,4},{7,5},{8,10},{9,11},{10,... | collective-permute-start | bytes 110600 | tf_op jit(solution)/shard_map/ppermute | solution.py:758
  22.6 1.4 %collective-permute-done.1.a2 = f32[3,24,128]{2,1,0:T(8,128)S(1)} collective-permute-done((f32[3,24,128]{2,1,0:T(8,128)S(1)}, f32[3,24,128]{2,1,0:T(8,128)S(1)}, u32[]{:S(2)}, u32[]{:S(2)}) %collective-permute-start.1) | collective-permute-done | bytes 36896 | tf_op jit(solution)/shard_map/ppermute | solution.py:758
  25.6 3.0 %collective-permute-start.5 = (f32[12,16,128]{2,1,0:T(8,128)S(1)}, f32[12,16,128]{2,1,0:T(8,128)S(1)}, u32[]{:S(2)}, u32[]{:S(2)}) collective-permute-start(f32[12,16,128]{2,1,0:T(8,128)S(1)} %get-tuple-element.51), channel_id=1, source_target_pairs={{0,128},{32,160},{64,192},{96,224},{128,0},{160,32},{192,64},{224,... | collective-permute-start | bytes 294920 | tf_op jit(solution)/shard_map/ppermute | solution.py:758
  28.5 2.6 %collective-permute-start.6 = (f32[12,16,128]{2,1,0:T(8,128)S(1)}, f32[12,16,128]{2,1,0:T(8,128)S(1)}, u32[]{:S(2)}, u32[]{:S(2)}) collective-permute-start(f32[12,16,128]{2,1,0:T(8,128)S(1)} %get-tuple-element.52), channel_id=1, source_target_pairs={{0,160},{32,128},{64,224},{96,192},{128,32},{160,0},{192,96},{224,... | collective-permute-start | bytes 294920 | tf_op jit(solution)/shard_map/ppermute | solution.py:758
  32.8 1.8 %collective-permute-start.9 = (f32[12,16,128]{2,1,0:T(8,128)S(1)}, f32[12,16,128]{2,1,0:T(8,128)S(1)}, u32[]{:S(2)}, u32[]{:S(2)}) collective-permute-start(f32[12,16,128]{2,1,0:T(8,128)S(1)} %get-tuple-element.55), channel_id=1, source_target_pairs={{0,192},{32,224},{64,128},{96,160},{128,64},{160,96},{192,0},{224,... | collective-permute-start | bytes 294920 | tf_op jit(solution)/shard_map/ppermute | solution.py:758
  34.6 1.5 %collective-permute-start.10 = (f32[12,16,128]{2,1,0:T(8,128)S(1)}, f32[12,16,128]{2,1,0:T(8,128)S(1)}, u32[]{:S(2)}, u32[]{:S(2)}) collective-permute-start(f32[12,16,128]{2,1,0:T(8,128)S(1)} %get-tuple-element.56), channel_id=1, source_target_pairs={{0,96},{32,64},{64,32},{96,0},{128,224},{160,192},{192,160},{224,1... | collective-permute-start | bytes 294920 | tf_op jit(solution)/shard_map/ppermute | solution.py:758
  38.4 1.4 %collective-permute-done.9.i6 = f32[12,16,128]{2,1,0:T(8,128)S(1)} collective-permute-done((f32[12,16,128]{2,1,0:T(8,128)S(1)}, f32[12,16,128]{2,1,0:T(8,128)S(1)}, u32[]{:S(2)}, u32[]{:S(2)}) %collective-permute-start.9) | collective-permute-done | bytes 98336 | tf_op jit(solution)/shard_map/ppermute | solution.py:758
  40.6 4.4 %shard_map.102 = (f32[49,16,128]{2,1,0:T(8,128)S(1)}, f32[49,16,128]{2,1,0:T(8,128)S(1)}, f32[81,16,128]{2,1,0:T(8,128)S(1)}, f32[8,9,16,128]{3,2,1,0:T(8,128)S(...) custom-call(f32[12,16,128]{2,1,0:T(8,128)S(1)} %collective-permute-done.5.i4, ...), custom_call_target="tpu_custom_call" | custom-call | tf_op jit(solution)/shard_map/pallas_call | solution.py:740
  46.8 2.9 %collective-permute-start.14 = (f32[3,16,128]{2,1,0:T(8,128)S(1)}, f32[3,16,128]{2,1,0:T(8,128)S(1)}, u32[]{:S(2)}, u32[]{:S(2)}) collective-permute-start(f32[3,16,128]{2,1,0:T(8,128)S(1)} %get-tuple-element.71), channel_id=1, source_target_pairs={{0,2},{1,3},{2,0},{3,1},{4,6},{5,7},{6,4},{7,5},{8,10},{9,11},{10,... | collective-permute-start | bytes 73736 | tf_op jit(solution)/shard_map/ppermute | solution.py:758
  54.8 4.6 %collective-permute-start.18 = (f32[18,16,128]{2,1,0:T(8,128)S(1)}, f32[18,16,128]{2,1,0:T(8,128)S(1)}, u32[]{:S(2)}, u32[]{:S(2)}) collective-permute-start(f32[18,16,128]{2,1,0:T(8,128)S(1)} %get-tuple-element.76), channel_id=1, source_target_pairs={{0,160},{32,128},{64,224},{96,192},{128,32},{160,0},{192,96},{224,... | collective-permute-start | bytes 442376 | tf_op jit(solution)/shard_map/ppermute | solution.py:758
  59.4 2.3 %shard_map.105 = f32[256,128]{1,0:T(8,128)} custom-call(f32[49,16,128]{2,1,0:T(8,128)S(1)} %get-tuple-element.68.moved_ref, f32[144,256]{1,0:T(8,128)S(1)} %get-tuple-element.72.change_ref, f32[2,16,128]{2,1,0:T(8,128)S(1)} %get-tuple-element.73.sums_ref, f32[2,16,128]{2,1,0:T(8,128)S(1)} %get-tuple-element.74.changed_sums_ref, s32[32,128]{1,0:T(8,128)S(1)} %bitcast.17, ...), custom_call_target="tpu_custom_call" | custom-call | tf_op jit(solution)/shard_map/pallas_call | solution.py:740
  61.7 8.9 %all-to-all-start.1 = ((f32[256,1,128]{2,1,0:T(1,128)}), f32[256,1,128]{2,1,0:T(1,128)S(1)}, u32[]{:S(2)}, u32[]{:S(2)}) async-start(f32[256,1,128]{2,1,0:T(1,128)} %bitcast.7), calls=%async_computation.1 | async-start | bytes 262144 | tf_op jit(solution)/shard_map/all_to_all | solution.py:754
  70.7 2.9 %collective-permute-start.19 = (f32[18,16,128]{2,1,0:T(8,128)S(1)}, f32[18,16,128]{2,1,0:T(8,128)S(1)}, u32[]{:S(2)}, u32[]{:S(2)}) collective-permute-start(f32[18,16,128]{2,1,0:T(8,128)S(1)} %get-tuple-element.77), channel_id=1, source_target_pairs={{0,224},{32,192},{64,160},{96,128},{128,96},{160,64},{192,32},{224... | collective-permute-start | bytes 442376 | tf_op jit(solution)/shard_map/ppermute | solution.py:758
  73.6 1.9 %collective-permute-start.21 = (f32[18,16,128]{2,1,0:T(8,128)S(1)}, f32[18,16,128]{2,1,0:T(8,128)S(1)}, u32[]{:S(2)}, u32[]{:S(2)}) collective-permute-start(f32[18,16,128]{2,1,0:T(8,128)S(1)} %get-tuple-element.79), channel_id=1, source_target_pairs={{0,192},{32,224},{64,128},{96,160},{128,64},{160,96},{192,0},{224,... | collective-permute-start | bytes 442376 | tf_op jit(solution)/shard_map/ppermute | solution.py:758
  77.6 2.1 %collective-permute-done.20.i2 = f32[18,16,128]{2,1,0:T(8,128)S(1)} collective-permute-done((f32[18,16,128]{2,1,0:T(8,128)S(1)}, f32[18,16,128]{2,1,0:T(8,128)S(1)}, u32[]{:S(2)}, u32[]{:S(2)}) %collective-permute-start.20) | collective-permute-done | bytes 147488 | tf_op jit(solution)/shard_map/ppermute | solution.py:758
  79.7 3.0 %collective-permute-done.21.i6 = f32[18,16,128]{2,1,0:T(8,128)S(1)} collective-permute-done((f32[18,16,128]{2,1,0:T(8,128)S(1)}, f32[18,16,128]{2,1,0:T(8,128)S(1)}, u32[]{:S(2)}, u32[]{:S(2)}) %collective-permute-start.21) | collective-permute-done | bytes 147488 | tf_op jit(solution)/shard_map/ppermute | solution.py:758
  85.4 2.7 %collective-permute-start.25 = (f32[9,16,128]{2,1,0:T(8,128)S(1)}, f32[9,16,128]{2,1,0:T(8,128)S(1)}, u32[]{:S(2)}, u32[]{:S(2)}) collective-permute-start(f32[9,16,128]{2,1,0:T(8,128)S(1)} %get-tuple-element.84), channel_id=1, source_target_pairs={{0,160},{32,128},{64,224},{96,192},{128,32},{160,0},{192,96},{224,... | collective-permute-start | bytes 221192 | tf_op jit(solution)/shard_map/ppermute | solution.py:758
  88.7 1.6 %collective-permute-start.28 = (f32[9,16,128]{2,1,0:T(8,128)S(1)}, f32[9,16,128]{2,1,0:T(8,128)S(1)}, u32[]{:S(2)}, u32[]{:S(2)}) collective-permute-start(f32[9,16,128]{2,1,0:T(8,128)S(1)} %get-tuple-element.87), channel_id=1, source_target_pairs={{0,192},{32,224},{64,128},{96,160},{128,64},{160,96},{192,0},{224,... | collective-permute-start | bytes 221192 | tf_op jit(solution)/shard_map/ppermute | solution.py:758
  90.3 2.3 %collective-permute-start.29 = (f32[9,16,128]{2,1,0:T(8,128)S(1)}, f32[9,16,128]{2,1,0:T(8,128)S(1)}, u32[]{:S(2)}, u32[]{:S(2)}) collective-permute-start(f32[9,16,128]{2,1,0:T(8,128)S(1)} %get-tuple-element.88), channel_id=1, source_target_pairs={{0,96},{32,64},{64,32},{96,0},{128,224},{160,192},{192,160},{224,1... | collective-permute-start | bytes 221192 | tf_op jit(solution)/shard_map/ppermute | solution.py:758
  92.6 1.4 %collective-permute-done.26.i7 = f32[9,16,128]{2,1,0:T(8,128)S(1)} collective-permute-done((f32[9,16,128]{2,1,0:T(8,128)S(1)}, f32[9,16,128]{2,1,0:T(8,128)S(1)}, u32[]{:S(2)}, u32[]{:S(2)}) %collective-permute-start.26) | collective-permute-done | bytes 73760 | tf_op jit(solution)/shard_map/ppermute | solution.py:758
  95.7 1.5 %shard_map.107 = f32[81,16,128]{2,1,0:T(8,128)} custom-call(f32[9,16,128]{2,1,0:T(8,128)S(1)} %collective-permute-done.24.i4, f32[9,16,128]{2,1,0:T(8,128)S(1)} %collective-permute-done.25.i5, f32[9,16,128]{2,1,0:T(8,128)S(1)} %collective-permute-done.26.i7, f32[9,16,128]{2,1,0:T(8,128)S(1)} %collective-permute-done.27.i2, ...), custom_call_target="tpu_custom_call" | custom-call | tf_op jit(solution)/shard_map/pallas_call | solution.py:740
  (68 shorter events, 22.8 us)
Async XLA Ops:
  4.2 20.5 %all-to-all-start = ((f32[8,9,16,128]{3,2,1,0:T(8,128)}), f32[8,9,16,128]{3,2,1,0:T(8,128)S(1)}, u32[]{:S(2)}, u32[]{:S(2)}) async-start(f32[8,9,16,128]{3,2,1,0:T(8,128)} %bitcast.20), calls=%async_computation | async-start | bytes 1179648 | tf_op jit(solution)/shard_map/all_to_all | solution.py:754
  11.0 11.3 %collective-permute-start.4 = (f32[3,24,128]{2,1,0:T(8,128)S(1)}, f32[3,24,128]{2,1,0:T(8,128)S(1)}, u32[]{:S(2)}, u32[]{:S(2)}) collective-permute-start(f32[3,24,128]{2,1,0:T(8,128)S(1)} %copy-done.8), channel_id=1, source_target_pairs={{0,16},{1,17},{2,18},{3,19},{4,20},{5,21},{6,22},{7,23},{8,24},{9,... | collective-permute-start | bytes 110600 | tf_op jit(solution)/shard_map/ppermute | solution.py:758
  25.6 9.0 %collective-permute-start.5 = (f32[12,16,128]{2,1,0:T(8,128)S(1)}, f32[12,16,128]{2,1,0:T(8,128)S(1)}, u32[]{:S(2)}, u32[]{:S(2)}) collective-permute-start(f32[12,16,128]{2,1,0:T(8,128)S(1)} %get-tuple-element.51), channel_id=1, source_target_pairs={{0,128},{32,160},{64,192},{96,224},{128,0},{160,32},{192,64},{224,... | collective-permute-start | bytes 294920 | tf_op jit(solution)/shard_map/ppermute | solution.py:758
  28.5 7.5 %collective-permute-start.6 = (f32[12,16,128]{2,1,0:T(8,128)S(1)}, f32[12,16,128]{2,1,0:T(8,128)S(1)}, u32[]{:S(2)}, u32[]{:S(2)}) collective-permute-start(f32[12,16,128]{2,1,0:T(8,128)S(1)} %get-tuple-element.52), channel_id=1, source_target_pairs={{0,160},{32,128},{64,224},{96,192},{128,32},{160,0},{192,96},{224,... | collective-permute-start | bytes 294920 | tf_op jit(solution)/shard_map/ppermute | solution.py:758
  31.2 7.3 %collective-permute-start.7 = (f32[12,16,128]{2,1,0:T(8,128)S(1)}, f32[12,16,128]{2,1,0:T(8,128)S(1)}, u32[]{:S(2)}, u32[]{:S(2)}) collective-permute-start(f32[12,16,128]{2,1,0:T(8,128)S(1)} %get-tuple-element.53), channel_id=1, source_target_pairs={{0,224},{32,192},{64,160},{96,128},{128,96},{160,64},{192,32},{224... | collective-permute-start | bytes 294920 | tf_op jit(solution)/shard_map/ppermute | solution.py:758
  32.2 6.2 %collective-permute-start.8 = (f32[12,16,128]{2,1,0:T(8,128)S(1)}, f32[12,16,128]{2,1,0:T(8,128)S(1)}, u32[]{:S(2)}, u32[]{:S(2)}) collective-permute-start(f32[12,16,128]{2,1,0:T(8,128)S(1)} %get-tuple-element.54), channel_id=1, source_target_pairs={{0,64},{32,96},{64,0},{96,32},{128,192},{160,224},{192,128},{224,1... | collective-permute-start | bytes 294920 | tf_op jit(solution)/shard_map/ppermute | solution.py:758
  32.8 7.0 %collective-permute-start.9 = (f32[12,16,128]{2,1,0:T(8,128)S(1)}, f32[12,16,128]{2,1,0:T(8,128)S(1)}, u32[]{:S(2)}, u32[]{:S(2)}) collective-permute-start(f32[12,16,128]{2,1,0:T(8,128)S(1)} %get-tuple-element.55), channel_id=1, source_target_pairs={{0,192},{32,224},{64,128},{96,160},{128,64},{160,96},{192,0},{224,... | collective-permute-start | bytes 294920 | tf_op jit(solution)/shard_map/ppermute | solution.py:758
  34.6 5.9 %collective-permute-start.10 = (f32[12,16,128]{2,1,0:T(8,128)S(1)}, f32[12,16,128]{2,1,0:T(8,128)S(1)}, u32[]{:S(2)}, u32[]{:S(2)}) collective-permute-start(f32[12,16,128]{2,1,0:T(8,128)S(1)} %get-tuple-element.56), channel_id=1, source_target_pairs={{0,96},{32,64},{64,32},{96,0},{128,224},{160,192},{192,160},{224,1... | collective-permute-start | bytes 294920 | tf_op jit(solution)/shard_map/ppermute | solution.py:758
  45.0 6.8 %collective-permute-start.16 = (f32[3,16,128]{2,1,0:T(8,128)S(1)}, f32[3,16,128]{2,1,0:T(8,128)S(1)}, u32[]{:S(2)}, u32[]{:S(2)}) collective-permute-start(f32[3,16,128]{2,1,0:T(8,128)S(1)} %get-tuple-element.71), channel_id=1, source_target_pairs={{0,16},{1,17},{2,18},{3,19},{4,20},{5,21},{6,22},{7,23},{8,24},{9,... | collective-permute-start | bytes 73736 | tf_op jit(solution)/shard_map/ppermute | solution.py:758
  46.2 5.5 %collective-permute-start.15 = (f32[3,16,128]{2,1,0:T(8,128)S(1)}, f32[3,16,128]{2,1,0:T(8,128)S(1)}, u32[]{:S(2)}, u32[]{:S(2)}) collective-permute-start(f32[3,16,128]{2,1,0:T(8,128)S(1)} %get-tuple-element.71), channel_id=1, source_target_pairs={{0,8},{1,9},{2,10},{3,11},{4,12},{5,13},{6,14},{7,15},{8,0},{9,1},... | collective-permute-start | bytes 73736 | tf_op jit(solution)/shard_map/ppermute | solution.py:758
  53.5 22.0 %collective-permute-start.17 = (f32[18,16,128]{2,1,0:T(8,128)S(1)}, f32[18,16,128]{2,1,0:T(8,128)S(1)}, u32[]{:S(2)}, u32[]{:S(2)}) collective-permute-start(f32[18,16,128]{2,1,0:T(8,128)S(1)} %get-tuple-element.75), channel_id=1, source_target_pairs={{0,128},{32,160},{64,192},{96,224},{128,0},{160,32},{192,64},{224,... | collective-permute-start | bytes 442376 | tf_op jit(solution)/shard_map/ppermute | solution.py:758
  54.8 20.7 %collective-permute-start.18 = (f32[18,16,128]{2,1,0:T(8,128)S(1)}, f32[18,16,128]{2,1,0:T(8,128)S(1)}, u32[]{:S(2)}, u32[]{:S(2)}) collective-permute-start(f32[18,16,128]{2,1,0:T(8,128)S(1)} %get-tuple-element.76), channel_id=1, source_target_pairs={{0,160},{32,128},{64,224},{96,192},{128,32},{160,0},{192,96},{224,... | collective-permute-start | bytes 442376 | tf_op jit(solution)/shard_map/ppermute | solution.py:758
  61.7 21.6 %all-to-all-start.1 = ((f32[256,1,128]{2,1,0:T(1,128)}), f32[256,1,128]{2,1,0:T(1,128)S(1)}, u32[]{:S(2)}, u32[]{:S(2)}) async-start(f32[256,1,128]{2,1,0:T(1,128)} %bitcast.7), calls=%async_computation.1 | async-start | bytes 262144 | tf_op jit(solution)/shard_map/all_to_all | solution.py:754
  70.7 6.9 %collective-permute-start.19 = (f32[18,16,128]{2,1,0:T(8,128)S(1)}, f32[18,16,128]{2,1,0:T(8,128)S(1)}, u32[]{:S(2)}, u32[]{:S(2)}) collective-permute-start(f32[18,16,128]{2,1,0:T(8,128)S(1)} %get-tuple-element.77), channel_id=1, source_target_pairs={{0,224},{32,192},{64,160},{96,128},{128,96},{160,64},{192,32},{224... | collective-permute-start | bytes 442376 | tf_op jit(solution)/shard_map/ppermute | solution.py:758
  73.6 6.1 %collective-permute-start.20 = (f32[18,16,128]{2,1,0:T(8,128)S(1)}, f32[18,16,128]{2,1,0:T(8,128)S(1)}, u32[]{:S(2)}, u32[]{:S(2)}) collective-permute-start(f32[18,16,128]{2,1,0:T(8,128)S(1)} %get-tuple-element.78), channel_id=1, source_target_pairs={{0,64},{32,96},{64,0},{96,32},{128,192},{160,224},{192,128},{224,1... | collective-permute-start | bytes 442376 | tf_op jit(solution)/shard_map/ppermute | solution.py:758
  73.6 9.1 %collective-permute-start.21 = (f32[18,16,128]{2,1,0:T(8,128)S(1)}, f32[18,16,128]{2,1,0:T(8,128)S(1)}, u32[]{:S(2)}, u32[]{:S(2)}) collective-permute-start(f32[18,16,128]{2,1,0:T(8,128)S(1)} %get-tuple-element.79), channel_id=1, source_target_pairs={{0,192},{32,224},{64,128},{96,160},{128,64},{160,96},{192,0},{224,... | collective-permute-start | bytes 442376 | tf_op jit(solution)/shard_map/ppermute | solution.py:758
  75.5 7.8 %collective-permute-start.22 = (f32[18,16,128]{2,1,0:T(8,128)S(1)}, f32[18,16,128]{2,1,0:T(8,128)S(1)}, u32[]{:S(2)}, u32[]{:S(2)}) collective-permute-start(f32[18,16,128]{2,1,0:T(8,128)S(1)} %get-tuple-element.80), channel_id=1, source_target_pairs={{0,96},{32,64},{64,32},{96,0},{128,224},{160,192},{192,160},{224,1... | collective-permute-start | bytes 442376 | tf_op jit(solution)/shard_map/ppermute | solution.py:758
  75.5 7.8 %collective-permute-start.23 = (f32[18,16,128]{2,1,0:T(8,128)S(1)}, f32[18,16,128]{2,1,0:T(8,128)S(1)}, u32[]{:S(2)}, u32[]{:S(2)}) collective-permute-start(f32[18,16,128]{2,1,0:T(8,128)S(1)} %get-tuple-element.81), channel_id=1, source_target_pairs={{0,32},{32,0},{64,96},{96,64},{128,160},{160,128},{192,224},{224,1... | collective-permute-start | bytes 442376 | tf_op jit(solution)/shard_map/ppermute | solution.py:758
  84.2 6.0 %collective-permute-start.24 = (f32[9,16,128]{2,1,0:T(8,128)S(1)}, f32[9,16,128]{2,1,0:T(8,128)S(1)}, u32[]{:S(2)}, u32[]{:S(2)}) collective-permute-start(f32[9,16,128]{2,1,0:T(8,128)S(1)} %get-tuple-element.83), channel_id=1, source_target_pairs={{0,128},{32,160},{64,192},{96,224},{128,0},{160,32},{192,64},{224,... | collective-permute-start | bytes 221192 | tf_op jit(solution)/shard_map/ppermute | solution.py:758
  85.4 7.1 %collective-permute-start.25 = (f32[9,16,128]{2,1,0:T(8,128)S(1)}, f32[9,16,128]{2,1,0:T(8,128)S(1)}, u32[]{:S(2)}, u32[]{:S(2)}) collective-permute-start(f32[9,16,128]{2,1,0:T(8,128)S(1)} %get-tuple-element.84), channel_id=1, source_target_pairs={{0,160},{32,128},{64,224},{96,192},{128,32},{160,0},{192,96},{224,... | collective-permute-start | bytes 221192 | tf_op jit(solution)/shard_map/ppermute | solution.py:758
  88.2 5.8 %collective-permute-start.26 = (f32[9,16,128]{2,1,0:T(8,128)S(1)}, f32[9,16,128]{2,1,0:T(8,128)S(1)}, u32[]{:S(2)}, u32[]{:S(2)}) collective-permute-start(f32[9,16,128]{2,1,0:T(8,128)S(1)} %get-tuple-element.85), channel_id=1, source_target_pairs={{0,224},{32,192},{64,160},{96,128},{128,96},{160,64},{192,32},{224... | collective-permute-start | bytes 221192 | tf_op jit(solution)/shard_map/ppermute | solution.py:758
  88.7 5.3 %collective-permute-start.27 = (f32[9,16,128]{2,1,0:T(8,128)S(1)}, f32[9,16,128]{2,1,0:T(8,128)S(1)}, u32[]{:S(2)}, u32[]{:S(2)}) collective-permute-start(f32[9,16,128]{2,1,0:T(8,128)S(1)} %get-tuple-element.86), channel_id=1, source_target_pairs={{0,64},{32,96},{64,0},{96,32},{128,192},{160,224},{192,128},{224,1... | collective-permute-start | bytes 221192 | tf_op jit(solution)/shard_map/ppermute | solution.py:758
  88.7 6.0 %collective-permute-start.28 = (f32[9,16,128]{2,1,0:T(8,128)S(1)}, f32[9,16,128]{2,1,0:T(8,128)S(1)}, u32[]{:S(2)}, u32[]{:S(2)}) collective-permute-start(f32[9,16,128]{2,1,0:T(8,128)S(1)} %get-tuple-element.87), channel_id=1, source_target_pairs={{0,192},{32,224},{64,128},{96,160},{128,64},{160,96},{192,0},{224,... | collective-permute-start | bytes 221192 | tf_op jit(solution)/shard_map/ppermute | solution.py:758
  90.3 5.4 %collective-permute-start.29 = (f32[9,16,128]{2,1,0:T(8,128)S(1)}, f32[9,16,128]{2,1,0:T(8,128)S(1)}, u32[]{:S(2)}, u32[]{:S(2)}) collective-permute-start(f32[9,16,128]{2,1,0:T(8,128)S(1)} %get-tuple-element.88), channel_id=1, source_target_pairs={{0,96},{32,64},{64,32},{96,0},{128,224},{160,192},{192,160},{224,1... | collective-permute-start | bytes 221192 | tf_op jit(solution)/shard_map/ppermute | solution.py:758
  (18 other events, 297.7 us)

commit v6 on v5

--- a/solution.py
+++ b/solution.py
@@ -28,7 +28,10 @@
 SLOT_TILES = SLOTS // LANES
 BLOCK = 9
 SHARE = BLOCK + SLOT_TILES
+LINE = ORDER - 1
+PAIRED = BLOCK + 2
 SCALARS = 5
+WIDTH = SCALARS * ROWS
 STEP_ORDER = [4, 5, 7, 2, 6, 3, 1]
 LEVEL_ORDER = [0, 2, 1, 3, 4]
 SPACING = 0.25
@@ -103,8 +106,8 @@
     return np.concatenate([first, second], axis=1).astype(np.float32), cross.astype(np.float32)
 
 
-def helmholtz_shift():
-    rows_global = lax.axis_index("mode") * ROWS + lax.broadcasted_iota(jnp.int32, (ROWS, LANES), 0)
+def helmholtz_shift(mode):
+    rows_global = mode * ROWS + lax.broadcasted_iota(jnp.int32, (ROWS, LANES), 0)
     wavenumber = jnp.right_shift(rows_global, 1).astype(F32)
     spanwise = wavenumber * (2.0 * math.pi / (PLANES * SPACING))
     spanwise = jnp.where(rows_global == 1, math.pi / SPACING, spanwise)
@@ -244,7 +247,20 @@
 
 
 def sent_place(index):
-    return index // BLOCK, index % BLOCK
+    if index < INNER:
+        return index // LINE, index % LINE
+    extra = index - INNER
+    block = min(extra // 2, MODES - 1)
+    row = extra - 2 * block
+    return block, row + LINE if row < 2 else row - 2
+
+
+def kept_place(index):
+    block, row = sent_place(index)
+    return block, row + 2
+
+
+EMPTY_PLACES = [(MODES - 1, row) for row in range(2, LINE)]
 
 
 def read_skeleton(load):
@@ -454,10 +470,11 @@
         copy.start()
         outs.append(copy)
 
-    width = ORDER - 1
     base = 2 * HIGH * ROWS
-    for index in range(TILES, MODES * BLOCK - INNER):
-        packed_ref[index] = jnp.zeros((ROWS, LANES), F32)
+    tail = list(range(TILES - 4)) + [TILES - 2, TILES - 1] + [None] * len(EMPTY_PLACES) + [TILES - 4, TILES - 3]
+    for position, index in enumerate(tail):
+        if index is None:
+            packed_ref[position] = jnp.zeros((ROWS, LANES), F32)
     ins[0].wait()
     edge_rows = edge_ref[...]
     one_hot_cycle(edge_rows, selectors_ref)
@@ -472,8 +489,8 @@
     send(inner_ref, inner_hbm)
     send(padded_ref, padded_hbm)
     ins[7].wait()
-    for line in range(width):
-        send(forcing_ref.at[pl.ds((line + 1) * SIDE + 1, width)], out_hbm.at[pl.ds(line * width, width)])
+    for line in range(LINE):
+        send(forcing_ref.at[pl.ds((line + 1) * SIDE + 1, LINE)], out_hbm.at[pl.ds(line * BLOCK, LINE)])
     high_rows = jnp.right_shift(edge_rows, 8)
     for slot in range(CYCLE):
         node = CYCLE_NODES[slot]
@@ -485,10 +502,12 @@
     skeleton = total[: HIGH * ROWS] + total[HIGH * ROWS : base]
 
     def store(index, value):
-        packed_ref[index] = value
+        packed_ref[tail.index(index)] = value
 
     write_skeleton(skeleton, store)
-    send(packed_ref, out_hbm.at[pl.ds(INNER, MODES * BLOCK - INNER)])
+    for line in range(LINE):
+        send(packed_ref.at[pl.ds(2 * line, 2)], out_hbm.at[pl.ds(line * BLOCK + LINE, 2)])
+    send(packed_ref.at[pl.ds(TILES - 4, BLOCK)], out_hbm.at[pl.ds(LINE * BLOCK, BLOCK)])
     selectors = slot_selectors(shared_rows)
     pairs = diagonal_slots(total[base:], shared_rows, selectors, padded_ref, skeleton_ref)
     send(skeleton_ref, skeleton_hbm)
@@ -535,6 +554,18 @@
         extra_ref[tile] = chosen[ROWS:]
 
 
+def column_kernel(inner_ref, o0, o1, o2, o3, o4, o5, o6, o7, out_ref):
+    mode = lax.axis_index("mode")
+    start = jnp.minimum(mode, LINE - 1) * LINE
+    for step, in_ref in enumerate([o0, o1, o2, o3, o4, o5, o6, o7]):
+        origin = jnp.bitwise_xor(mode, step)
+        shift = helmholtz_shift(origin)
+        for index in range(LINE):
+            laplace = inner_ref[0, pl.ds(start + index, 1), :]
+            mass = inner_ref[1, pl.ds(start + index, 1), :]
+            out_ref[index, place(origin), :] = in_ref[index] * (1.0 / (laplace + shift * mass))
+
+
 def first_kernel(
     i4, i5, i7, i2, i6, i3, i1, i0, extra_ref, lists_ref, edge_ref, metric_ref,
     inner_ref, diagonal_ref, penalty_ref, search_ref, inverse_ref, result_ref, source_ref, kept_ref, slots_ref,
@@ -546,7 +577,7 @@
         source_ref[jnp.bitwise_xor(mode, step)] = in_ref[:BLOCK]
     shared_rows = lists_ref[:SLOT_TILES, :]
     right_slots = slot_selectors(shared_rows)
-    shift = helmholtz_shift()
+    shift = helmholtz_shift(lax.axis_index("mode"))
     shift_ref[...] = shift
     edge_rows = edge_ref[...]
 
@@ -613,18 +644,15 @@
         search = search_ref[index]
         moved = value * inverse_ref[index] - search
         moved_ref[index] = moved
-        both_ref[block, row] = search
-        both_ref[block, BLOCK + row] = moved
+        both_ref[block, row] = moved
         crossed = crossed + value * moved
         sourced = sourced + source_ref[block, row] * moved
     for high in range(HIGH):
         for part in range(2):
-            block, row = sent_place(INNER + 2 * high + part)
+            block, row = kept_place(INNER + 2 * high + part)
             both_ref[block, row] = kept_ref[2, row_block(high), lane_block(part)]
-    for index in range(INNER + TILES, MODES * BLOCK):
-        block, row = sent_place(index)
+    for block, row in EMPTY_PLACES[2:]:
         both_ref[block, row] = jnp.zeros((ROWS, LANES), F32)
-        both_ref[block, BLOCK + row] = jnp.zeros((ROWS, LANES), F32)
     sums_ref[0] = crossed
     sums_ref[1] = sourced
 
@@ -646,7 +674,7 @@
     for high in range(HIGH):
         for part in range(2):
             block, row = sent_place(INNER + 2 * high + part)
-            both_ref[block, BLOCK + row] = change[row_block(high), lane_block(part)]
+            both_ref[block, row] = change[row_block(high), lane_block(part)]
     mode = lax.axis_index("mode")
     for step, out_ref in enumerate([o0, o1, o2, o3, o4, o5, o6, o7]):
         out_ref[...] = both_ref[jnp.bitwise_xor(mode, step)]
@@ -659,7 +687,7 @@
     moved_ref, change_ref, sums_ref, changed_sums_ref, edge_ref, metric_ref, penalty_ref, message_ref,
     cycle_ref, first_ref, energy_ref, shift_ref,
 ):
-    shift_ref[...] = helmholtz_shift()
+    shift_ref[...] = helmholtz_shift(lax.axis_index("mode"))
     change = change_ref[...]
 
     def store(slot, value):
@@ -675,11 +703,11 @@
         column = jnp.sum(value, axis=1, keepdims=True)
         spread = jnp.where(lanes == sublanes + index * ROWS, column, spread)
     message = jnp.sum(spread, axis=0, keepdims=True)
-    message_ref[...] = jnp.broadcast_to(message, message_ref.shape)
+    message_ref[...] = jnp.broadcast_to(message[:, :WIDTH], message_ref.shape)
 
 
 def combine_kernel(
-    matrix_ref, scalars_ref, i4, i5, i7, i2, i6, i3, i1, i0, o0, o1, o2, o3, o4, o5, o6, o7, block_ref
+    matrix_ref, scalars_ref, column_ref, i4, i5, i7, i2, i6, i3, i1, i0, o0, o1, o2, o3, o4, o5, o6, o7, block_ref
 ):
     mode = lax.axis_index("mode")
     sublanes = lax.broadcasted_iota(jnp.int32, (ROWS, LANES), 0)
@@ -687,6 +715,7 @@
     for step, in_ref in enumerate([i0, i1, i2, i3, i4, i5, i6, i7]):
         origin = jnp.bitwise_xor(mode, step)
         total = jnp.sum(scalars_ref[origin], axis=0, keepdims=True)
+        total = jnp.concatenate([total, jnp.zeros((1, LANES - WIDTH), F32)], axis=1)
         g00, g01, g11, h0, h1 = [
             jnp.sum(jnp.where(lanes == sublanes + index * ROWS, total, 0.0), axis=1, keepdims=True)
             for index in range(SCALARS)
@@ -696,7 +725,13 @@
         second = jnp.where(pivot > 0.0, (h1 - ratio * h0) / pivot, 0.0)
         first = h0 / g00 - ratio * second
         for index in range(BLOCK):
-            block_ref[index, place(origin), :] = first * in_ref[index] + second * in_ref[BLOCK + index]
+            if index < LINE:
+                search = column_ref[index, place(origin), :]
+                if index < 2:
+                    search = jnp.where(mode == MODES - 1, in_ref[index + 2], search)
+            else:
+                search = in_ref[index + 2]
+            block_ref[index, place(origin), :] = first * search + second * in_ref[index]
     matrix = relative_rows(matrix_ref, mode)
     for index in range(BLOCK):
         mixed = jnp.dot(matrix, block_ref[index], precision=HIGHEST, preferred_element_type=F32)
@@ -796,7 +831,7 @@
         + [pltpu.VMEM(part.shape, part.dtype) for part in packed_shapes[1:]]
         + [
             pltpu.VMEM((2, NODES, LANES), F32), pltpu.VMEM(((2 * HIGH + QUADS) * ROWS, CYCLE * LANES), BF16), right,
-            pltpu.SemaphoreType.DMA((len(operands),)), pltpu.SemaphoreType.DMA((ORDER + 5,)),
+            pltpu.SemaphoreType.DMA((len(operands),)), pltpu.SemaphoreType.DMA((2 * LINE + 6,)),
         ],
         *operands,
         in_specs=[hbm] * len(operands), out_specs=[hbm] * len(packed_shapes), limit=FIRST_LIMIT,
@@ -806,6 +841,7 @@
         transform_kernel, [shape(SHARE, ROWS, LANES)] * MODES + [shape(SLOT_TILES, 8, LANES)],
         [pltpu.VMEM((SLOT_TILES, PLANES, LANES), F32)], forward, gathered, *exchange(message), lists,
     )
+    column = call(column_kernel, shape(LINE, PLANES, LANES), [], inner, *mixed)
     inside = shape(INNER, ROWS, LANES)
     search, inverse, applied, source, kept, slots, sums = call(
         first_kernel,
@@ -816,24 +852,25 @@
         [left, right, cycle, first, energy, energy],
         *swap_steps(mixed), extra, lists, edge_rows, metric, inner, diagonal, penalties,
     )
-    pair = shape(MODES, 2 * BLOCK, ROWS, LANES)
+    pair = shape(MODES, PAIRED, ROWS, LANES)
     moved, moved_sums, filled = call(
         change_kernel, [inside, shape(2, ROWS, LANES), pair], [], search, inverse, applied, source, kept
     )
     change, changed_sums, both, *pairs = call(
         second_kernel,
-        [shape(*wide), shape(2, ROWS, LANES), pair] + [shape(2 * BLOCK, ROWS, LANES)] * MODES,
+        [shape(*wide), shape(2, ROWS, LANES), pair] + [shape(PAIRED, ROWS, LANES)] * MODES,
         [left_slots],
         kept, moved_sums, filled, *exchange(slots), lists,
         input_output_aliases={2: 2},
     )
     message = call(
-        energy_kernel, shape(MODES * ELEMS_AXIS, LANES), [cycle, first, energy, energy],
+        energy_kernel, shape(MODES * ELEMS_AXIS, WIDTH), [cycle, first, energy, energy],
         moved, change, sums, changed_sums, edge_rows, metric, penalties,
     )
-    scalars = swap_blocks(message, ("mode", "elem")).reshape(MODES, ELEMS_AXIS, LANES)
+    scalars = swap_blocks(message, ("mode", "elem")).reshape(MODES, ELEMS_AXIS, WIDTH)
     mixed = call(
-        combine_kernel, blocks, [pltpu.VMEM((BLOCK, PLANES, LANES), F32)], backward, scalars, *swap_steps(pairs)
+        combine_kernel, blocks, [pltpu.VMEM((BLOCK, PLANES, LANES), F32)], backward, scalars, column,
+        *swap_steps(pairs)
     )
     result = call(
         unpack_kernel, shape(NODES, ROWS, LANES),

time: 97.5 us -> 97.6 us (level)
    ppermute x31, waiting for transfers between devices: 17.7 us -> 15.1 us  [permute(): lax.ppermute(value, axis, [(i, i ^ flip) for i in range(lax.axis_size(axi...]
    all_to_all x2, waiting for transfers between devices: 0.01 us -> 2.33 us  [swap_blocks(): return lax.all_to_all(blocks, axis, split_axis=0, concat_axis=0, tiled=True)]
    pallas_call x8 -> x9, Pallas kernels: 14.6 us -> 14.7 us  [call(): pl.pallas_call(kernel, out_shape=out_shapes, scratch_shapes=scratch, comp...]
where the time goes in v6:
time: 97.6 us; the launch traced here: 97.4 us
  starting transfers between devices  64.8 us (66%)
  waiting for transfers between devices  17.4 us (18%)
  Pallas kernels  14.7 us (15%)
    ppermute x31, starting transfers between devices, permute(): lax.ppermute(value, axis, [(i, i ^ flip) for i in range(lax.axis_size(axi...  49.1 us
    all_to_all x2, starting transfers between devices, swap_blocks(): return lax.all_to_all(blocks, axis, split_axis=0, concat_axis=0, tiled=True)  15.8 us
    ppermute x31, waiting for transfers between devices, permute(): lax.ppermute(value, axis, [(i, i ^ flip) for i in range(lax.axis_size(axi...  15.1 us
    pallas_call x9, Pallas kernels, call(): pl.pallas_call(kernel, out_shape=out_shapes, scratch_shapes=scratch, comp...  14.7 us
    all_to_all x2, waiting for transfers between devices, swap_blocks(): return lax.all_to_all(blocks, axis, split_axis=0, concat_axis=0, tiled=True)  2.33 us
  transfers between devices with their start and end apart: 33, of which 16 were waited for; matrix products, arithmetic and copies ran while one was open for 0% of the time, Pallas kernels for 3%

profile of v6, /device:TPU:1, one launch (start us, length us, event | category | flops | bytes accessed | tf_op | source)
XLA Modules:
  0.0 97.4 jit_solution(11992666969082667644)
XLA Ops:
  0.0 4.2 %shard_map.100 = (f32[72,16,128]{2,1,0:T(8,128)}, f32[3,24,128]{2,1,0:T(8,128)}, f32[2,49,128]{2,1,0:T(8,128)}, f32[2,9,256]{2,1,0:T(8,128)}, f32[9,256]{1,0:T(8,128)}, /*index=5*/s32[8,128]{1,0:T(8,128)}) custom-call(f32[81,16,128]{2,1,0:T(8,128)} %bitcast.19, s32[32,128]{1,0:T(8,128)} %bitcast.15, s32[3,128]{1,0:T(4,128)} %bitcast.21, s32[3,128]{1,0:T(4,128)} %bitcast.22, ...), custom_call_target="tpu_custom_call" | custom-call | tf_op jit(solution)/shard_map/pallas_call | solution.py:775
  4.2 6.8 %all-to-all-start = ((f32[8,9,16,128]{3,2,1,0:T(8,128)}), f32[8,9,16,128]{3,2,1,0:T(8,128)S(1)}, u32[]{:S(2)}, u32[]{:S(2)}) async-start(f32[8,9,16,128]{3,2,1,0:T(8,128)} %bitcast.20), calls=%async_computation | async-start | bytes 1179648 | tf_op jit(solution)/shard_map/all_to_all | solution.py:789
  11.0 6.0 %collective-permute-start.4 = (f32[3,24,128]{2,1,0:T(8,128)S(1)}, f32[3,24,128]{2,1,0:T(8,128)S(1)}, u32[]{:S(2)}, u32[]{:S(2)}) collective-permute-start(f32[3,24,128]{2,1,0:T(8,128)S(1)} %copy-done.8), channel_id=1, source_target_pairs={{0,16},{1,17},{2,18},{3,19},{4,20},{5,21},{6,22},{7,23},{8,24},{9,... | collective-permute-start | bytes 110600 | tf_op jit(solution)/shard_map/ppermute | solution.py:793
  18.3 2.9 %collective-permute-start.2 = (f32[3,24,128]{2,1,0:T(8,128)S(1)}, f32[3,24,128]{2,1,0:T(8,128)S(1)}, u32[]{:S(2)}, u32[]{:S(2)}) collective-permute-start(f32[3,24,128]{2,1,0:T(8,128)S(1)} %copy-done.8), channel_id=1, source_target_pairs={{0,2},{1,3},{2,0},{3,1},{4,6},{5,7},{6,4},{7,5},{8,10},{9,11},{10,... | collective-permute-start | bytes 110600 | tf_op jit(solution)/shard_map/ppermute | solution.py:793
  25.6 3.0 %collective-permute-start.5 = (f32[12,16,128]{2,1,0:T(8,128)S(1)}, f32[12,16,128]{2,1,0:T(8,128)S(1)}, u32[]{:S(2)}, u32[]{:S(2)}) collective-permute-start(f32[12,16,128]{2,1,0:T(8,128)S(1)} %get-tuple-element.51.o4), channel_id=1, source_target_pairs={{0,128},{32,160},{64,192},{96,224},{128,0},{160,32},{192,64},{224,... | collective-permute-start | bytes 294920 | tf_op jit(solution)/shard_map/ppermute | solution.py:793
  28.6 2.6 %collective-permute-start.6 = (f32[12,16,128]{2,1,0:T(8,128)S(1)}, f32[12,16,128]{2,1,0:T(8,128)S(1)}, u32[]{:S(2)}, u32[]{:S(2)}) collective-permute-start(f32[12,16,128]{2,1,0:T(8,128)S(1)} %get-tuple-element.52.o5), channel_id=1, source_target_pairs={{0,160},{32,128},{64,224},{96,192},{128,32},{160,0},{192,96},{224,... | collective-permute-start | bytes 294920 | tf_op jit(solution)/shard_map/ppermute | solution.py:793
  32.9 1.8 %collective-permute-start.9 = (f32[12,16,128]{2,1,0:T(8,128)S(1)}, f32[12,16,128]{2,1,0:T(8,128)S(1)}, u32[]{:S(2)}, u32[]{:S(2)}) collective-permute-start(f32[12,16,128]{2,1,0:T(8,128)S(1)} %get-tuple-element.55.o6), channel_id=1, source_target_pairs={{0,192},{32,224},{64,128},{96,160},{128,64},{160,96},{192,0},{224,... | collective-permute-start | bytes 294920 | tf_op jit(solution)/shard_map/ppermute | solution.py:793
  34.6 1.5 %collective-permute-start.10 = (f32[12,16,128]{2,1,0:T(8,128)S(1)}, f32[12,16,128]{2,1,0:T(8,128)S(1)}, u32[]{:S(2)}, u32[]{:S(2)}) collective-permute-start(f32[12,16,128]{2,1,0:T(8,128)S(1)} %get-tuple-element.56.o3), channel_id=1, source_target_pairs={{0,96},{32,64},{64,32},{96,0},{128,224},{160,192},{192,160},{224,1... | collective-permute-start | bytes 294920 | tf_op jit(solution)/shard_map/ppermute | solution.py:793
  38.5 1.4 %collective-permute-done.9.i6 = f32[12,16,128]{2,1,0:T(8,128)S(1)} collective-permute-done((f32[12,16,128]{2,1,0:T(8,128)S(1)}, f32[12,16,128]{2,1,0:T(8,128)S(1)}, u32[]{:S(2)}, u32[]{:S(2)}) %collective-permute-start.9) | collective-permute-done | bytes 98336 | tf_op jit(solution)/shard_map/ppermute | solution.py:793
  40.6 4.4 %shard_map.102 = (f32[49,16,128]{2,1,0:T(8,128)S(1)}, f32[49,16,128]{2,1,0:T(8,128)S(1)}, f32[81,16,128]{2,1,0:T(8,128)S(1)}, f32[8,9,16,128]{3,2,1,0:T(8,128)S(...) custom-call(f32[12,16,128]{2,1,0:T(8,128)S(1)} %collective-permute-done.5.i4, ...), custom_call_target="tpu_custom_call" | custom-call | tf_op jit(solution)/shard_map/pallas_call | solution.py:775
  46.8 2.9 %collective-permute-start.14 = (f32[3,16,128]{2,1,0:T(8,128)S(1)}, f32[3,16,128]{2,1,0:T(8,128)S(1)}, u32[]{:S(2)}, u32[]{:S(2)}) collective-permute-start(f32[3,16,128]{2,1,0:T(8,128)S(1)} %get-tuple-element.71), channel_id=1, source_target_pairs={{0,2},{1,3},{2,0},{3,1},{4,6},{5,7},{6,4},{7,5},{8,10},{9,11},{10,... | collective-permute-start | bytes 73736 | tf_op jit(solution)/shard_map/ppermute | solution.py:793
  54.8 4.6 %collective-permute-start.18 = (f32[11,16,128]{2,1,0:T(8,128)S(1)}, f32[11,16,128]{2,1,0:T(8,128)S(1)}, u32[]{:S(2)}, u32[]{:S(2)}) collective-permute-start(f32[11,16,128]{2,1,0:T(8,128)S(1)} %get-tuple-element.76), channel_id=1, source_target_pairs={{0,160},{32,128},{64,224},{96,192},{128,32},{160,0},{192,96},{224,... | collective-permute-start | bytes 270344 | tf_op jit(solution)/shard_map/ppermute | solution.py:793
  59.5 2.3 %shard_map.105 = f32[256,80]{1,0:T(8,128)} custom-call(f32[49,16,128]{2,1,0:T(8,128)S(1)} %get-tuple-element.68.moved_ref, f32[144,256]{1,0:T(8,128)S(1)} %get-tuple-element.72.change_ref, f32[2,16,128]{2,1,0:T(8,128)S(1)} %get-tuple-element.73.sums_ref, f32[2,16,128]{2,1,0:T(8,128)S(1)} %get-tuple-element.74.changed_sums_ref, s32[32,128]{1,0:T(8,128)S(1)} %bitcast.17, ...), custom_call_target="tpu_custom_call" | custom-call | tf_op jit(solution)/shard_map/pallas_call | solution.py:775
  61.8 8.9 %all-to-all-start.1 = ((f32[256,1,80]{2,1,0:T(1,128)}), f32[256,1,80]{2,1,0:T(1,128)S(1)}, u32[]{:S(2)}, u32[]{:S(2)}) async-start(f32[256,1,80]{2,1,0:T(1,128)} %bitcast.7), calls=%async_computation.1 | async-start | bytes 262144 | tf_op jit(solution)/shard_map/all_to_all | solution.py:789
  70.7 2.9 %collective-permute-start.19 = (f32[11,16,128]{2,1,0:T(8,128)S(1)}, f32[11,16,128]{2,1,0:T(8,128)S(1)}, u32[]{:S(2)}, u32[]{:S(2)}) collective-permute-start(f32[11,16,128]{2,1,0:T(8,128)S(1)} %get-tuple-element.77), channel_id=1, source_target_pairs={{0,224},{32,192},{64,160},{96,128},{128,96},{160,64},{192,32},{224... | collective-permute-start | bytes 270344 | tf_op jit(solution)/shard_map/ppermute | solution.py:793
  73.7 1.9 %collective-permute-start.21 = (f32[11,16,128]{2,1,0:T(8,128)S(1)}, f32[11,16,128]{2,1,0:T(8,128)S(1)}, u32[]{:S(2)}, u32[]{:S(2)}) collective-permute-start(f32[11,16,128]{2,1,0:T(8,128)S(1)} %get-tuple-element.79), channel_id=1, source_target_pairs={{0,192},{32,224},{64,128},{96,160},{128,64},{160,96},{192,0},{224,... | collective-permute-start | bytes 270344 | tf_op jit(solution)/shard_map/ppermute | solution.py:793
  76.9 1.4 %collective-permute-done.20.i2 = f32[11,16,128]{2,1,0:T(8,128)S(1)} collective-permute-done((f32[11,16,128]{2,1,0:T(8,128)S(1)}, f32[11,16,128]{2,1,0:T(8,128)S(1)}, u32[]{:S(2)}, u32[]{:S(2)}) %collective-permute-start.20) | collective-permute-done | bytes 90144 | tf_op jit(solution)/shard_map/ppermute | solution.py:793
  78.4 1.7 %collective-permute-done.21.i6 = f32[11,16,128]{2,1,0:T(8,128)S(1)} collective-permute-done((f32[11,16,128]{2,1,0:T(8,128)S(1)}, f32[11,16,128]{2,1,0:T(8,128)S(1)}, u32[]{:S(2)}, u32[]{:S(2)}) %collective-permute-start.21) | collective-permute-done | bytes 90144 | tf_op jit(solution)/shard_map/ppermute | solution.py:793
  80.9 2.3 %all-to-all-done.1 = f32[256,1,80]{2,1,0:T(1,128)S(1)} async-done(((f32[256,1,80]{2,1,0:T(1,128)}), f32[256,1,80]{2,1,0:T(1,128)S(1)}, u32[]{:S(2)}, u32[]{:S(2)}) %all-to-all-start.1) | async-done | bytes 81952 | tf_op jit(solution)/shard_map/all_to_all | solution.py:789
  85.5 2.7 %collective-permute-start.25 = (f32[9,16,128]{2,1,0:T(8,128)S(1)}, f32[9,16,128]{2,1,0:T(8,128)S(1)}, u32[]{:S(2)}, u32[]{:S(2)}) collective-permute-start(f32[9,16,128]{2,1,0:T(8,128)S(1)} %get-tuple-element.84), channel_id=1, source_target_pairs={{0,160},{32,128},{64,224},{96,192},{128,32},{160,0},{192,96},{224,... | collective-permute-start | bytes 221192 | tf_op jit(solution)/shard_map/ppermute | solution.py:793
  88.5 1.6 %collective-permute-start.28 = (f32[9,16,128]{2,1,0:T(8,128)S(1)}, f32[9,16,128]{2,1,0:T(8,128)S(1)}, u32[]{:S(2)}, u32[]{:S(2)}) collective-permute-start(f32[9,16,128]{2,1,0:T(8,128)S(1)} %get-tuple-element.87), channel_id=1, source_target_pairs={{0,192},{32,224},{64,128},{96,160},{128,64},{160,96},{192,0},{224,... | collective-permute-start | bytes 221192 | tf_op jit(solution)/shard_map/ppermute | solution.py:793
  90.2 2.4 %collective-permute-start.29 = (f32[9,16,128]{2,1,0:T(8,128)S(1)}, f32[9,16,128]{2,1,0:T(8,128)S(1)}, u32[]{:S(2)}, u32[]{:S(2)}) collective-permute-start(f32[9,16,128]{2,1,0:T(8,128)S(1)} %get-tuple-element.88), channel_id=1, source_target_pairs={{0,96},{32,64},{64,32},{96,0},{128,224},{160,192},{192,160},{224,1... | collective-permute-start | bytes 221192 | tf_op jit(solution)/shard_map/ppermute | solution.py:793
  92.6 1.4 %collective-permute-done.26.i7 = f32[9,16,128]{2,1,0:T(8,128)S(1)} collective-permute-done((f32[9,16,128]{2,1,0:T(8,128)S(1)}, f32[9,16,128]{2,1,0:T(8,128)S(1)}, u32[]{:S(2)}, u32[]{:S(2)}) %collective-permute-start.26) | collective-permute-done | bytes 73760 | tf_op jit(solution)/shard_map/ppermute | solution.py:793
  95.7 1.5 %shard_map.108 = f32[81,16,128]{2,1,0:T(8,128)} custom-call(f32[9,16,128]{2,1,0:T(8,128)S(1)} %collective-permute-done.24.i4, f32[9,16,128]{2,1,0:T(8,128)S(1)} %collective-permute-done.25.i5, f32[9,16,128]{2,1,0:T(8,128)S(1)} %collective-permute-done.26.i7, f32[9,16,128]{2,1,0:T(8,128)S(1)} %collective-permute-done.27.i2, ...), custom_call_target="tpu_custom_call" | custom-call | tf_op jit(solution)/shard_map/pallas_call | solution.py:775
  (69 shorter events, 23.6 us)
Async XLA Ops:
  4.2 20.5 %all-to-all-start = ((f32[8,9,16,128]{3,2,1,0:T(8,128)}), f32[8,9,16,128]{3,2,1,0:T(8,128)S(1)}, u32[]{:S(2)}, u32[]{:S(2)}) async-start(f32[8,9,16,128]{3,2,1,0:T(8,128)} %bitcast.20), calls=%async_computation | async-start | bytes 1179648 | tf_op jit(solution)/shard_map/all_to_all | solution.py:789
  11.0 11.3 %collective-permute-start.4 = (f32[3,24,128]{2,1,0:T(8,128)S(1)}, f32[3,24,128]{2,1,0:T(8,128)S(1)}, u32[]{:S(2)}, u32[]{:S(2)}) collective-permute-start(f32[3,24,128]{2,1,0:T(8,128)S(1)} %copy-done.8), channel_id=1, source_target_pairs={{0,16},{1,17},{2,18},{3,19},{4,20},{5,21},{6,22},{7,23},{8,24},{9,... | collective-permute-start | bytes 110600 | tf_op jit(solution)/shard_map/ppermute | solution.py:793
  17.1 5.3 %collective-permute-start.3 = (f32[3,24,128]{2,1,0:T(8,128)S(1)}, f32[3,24,128]{2,1,0:T(8,128)S(1)}, u32[]{:S(2)}, u32[]{:S(2)}) collective-permute-start(f32[3,24,128]{2,1,0:T(8,128)S(1)} %copy-done.8), channel_id=1, source_target_pairs={{0,8},{1,9},{2,10},{3,11},{4,12},{5,13},{6,14},{7,15},{8,0},{9,1},... | collective-permute-start | bytes 110600 | tf_op jit(solution)/shard_map/ppermute | solution.py:793
  25.6 9.0 %collective-permute-start.5 = (f32[12,16,128]{2,1,0:T(8,128)S(1)}, f32[12,16,128]{2,1,0:T(8,128)S(1)}, u32[]{:S(2)}, u32[]{:S(2)}) collective-permute-start(f32[12,16,128]{2,1,0:T(8,128)S(1)} %get-tuple-element.51.o4), channel_id=1, source_target_pairs={{0,128},{32,160},{64,192},{96,224},{128,0},{160,32},{192,64},{224,... | collective-permute-start | bytes 294920 | tf_op jit(solution)/shard_map/ppermute | solution.py:793
  28.6 7.5 %collective-permute-start.6 = (f32[12,16,128]{2,1,0:T(8,128)S(1)}, f32[12,16,128]{2,1,0:T(8,128)S(1)}, u32[]{:S(2)}, u32[]{:S(2)}) collective-permute-start(f32[12,16,128]{2,1,0:T(8,128)S(1)} %get-tuple-element.52.o5), channel_id=1, source_target_pairs={{0,160},{32,128},{64,224},{96,192},{128,32},{160,0},{192,96},{224,... | collective-permute-start | bytes 294920 | tf_op jit(solution)/shard_map/ppermute | solution.py:793
  31.2 7.3 %collective-permute-start.7 = (f32[12,16,128]{2,1,0:T(8,128)S(1)}, f32[12,16,128]{2,1,0:T(8,128)S(1)}, u32[]{:S(2)}, u32[]{:S(2)}) collective-permute-start(f32[12,16,128]{2,1,0:T(8,128)S(1)} %get-tuple-element.53.o7), channel_id=1, source_target_pairs={{0,224},{32,192},{64,160},{96,128},{128,96},{160,64},{192,32},{224... | collective-permute-start | bytes 294920 | tf_op jit(solution)/shard_map/ppermute | solution.py:793
  32.3 6.2 %collective-permute-start.8 = (f32[12,16,128]{2,1,0:T(8,128)S(1)}, f32[12,16,128]{2,1,0:T(8,128)S(1)}, u32[]{:S(2)}, u32[]{:S(2)}) collective-permute-start(f32[12,16,128]{2,1,0:T(8,128)S(1)} %get-tuple-element.54.o2), channel_id=1, source_target_pairs={{0,64},{32,96},{64,0},{96,32},{128,192},{160,224},{192,128},{224,1... | collective-permute-start | bytes 294920 | tf_op jit(solution)/shard_map/ppermute | solution.py:793
  32.9 7.0 %collective-permute-start.9 = (f32[12,16,128]{2,1,0:T(8,128)S(1)}, f32[12,16,128]{2,1,0:T(8,128)S(1)}, u32[]{:S(2)}, u32[]{:S(2)}) collective-permute-start(f32[12,16,128]{2,1,0:T(8,128)S(1)} %get-tuple-element.55.o6), channel_id=1, source_target_pairs={{0,192},{32,224},{64,128},{96,160},{128,64},{160,96},{192,0},{224,... | collective-permute-start | bytes 294920 | tf_op jit(solution)/shard_map/ppermute | solution.py:793
  34.6 5.9 %collective-permute-start.10 = (f32[12,16,128]{2,1,0:T(8,128)S(1)}, f32[12,16,128]{2,1,0:T(8,128)S(1)}, u32[]{:S(2)}, u32[]{:S(2)}) collective-permute-start(f32[12,16,128]{2,1,0:T(8,128)S(1)} %get-tuple-element.56.o3), channel_id=1, source_target_pairs={{0,96},{32,64},{64,32},{96,0},{128,224},{160,192},{192,160},{224,1... | collective-permute-start | bytes 294920 | tf_op jit(solution)/shard_map/ppermute | solution.py:793
  45.1 6.8 %collective-permute-start.16 = (f32[3,16,128]{2,1,0:T(8,128)S(1)}, f32[3,16,128]{2,1,0:T(8,128)S(1)}, u32[]{:S(2)}, u32[]{:S(2)}) collective-permute-start(f32[3,16,128]{2,1,0:T(8,128)S(1)} %get-tuple-element.71), channel_id=1, source_target_pairs={{0,16},{1,17},{2,18},{3,19},{4,20},{5,21},{6,22},{7,23},{8,24},{9,... | collective-permute-start | bytes 73736 | tf_op jit(solution)/shard_map/ppermute | solution.py:793
  46.3 5.5 %collective-permute-start.15 = (f32[3,16,128]{2,1,0:T(8,128)S(1)}, f32[3,16,128]{2,1,0:T(8,128)S(1)}, u32[]{:S(2)}, u32[]{:S(2)}) collective-permute-start(f32[3,16,128]{2,1,0:T(8,128)S(1)} %get-tuple-element.71), channel_id=1, source_target_pairs={{0,8},{1,9},{2,10},{3,11},{4,12},{5,13},{6,14},{7,15},{8,0},{9,1},... | collective-permute-start | bytes 73736 | tf_op jit(solution)/shard_map/ppermute | solution.py:793
  53.5 22.1 %collective-permute-start.17 = (f32[11,16,128]{2,1,0:T(8,128)S(1)}, f32[11,16,128]{2,1,0:T(8,128)S(1)}, u32[]{:S(2)}, u32[]{:S(2)}) collective-permute-start(f32[11,16,128]{2,1,0:T(8,128)S(1)} %get-tuple-element.75), channel_id=1, source_target_pairs={{0,128},{32,160},{64,192},{96,224},{128,0},{160,32},{192,64},{224,... | collective-permute-start | bytes 270344 | tf_op jit(solution)/shard_map/ppermute | solution.py:793
  54.8 20.7 %collective-permute-start.18 = (f32[11,16,128]{2,1,0:T(8,128)S(1)}, f32[11,16,128]{2,1,0:T(8,128)S(1)}, u32[]{:S(2)}, u32[]{:S(2)}) collective-permute-start(f32[11,16,128]{2,1,0:T(8,128)S(1)} %get-tuple-element.76), channel_id=1, source_target_pairs={{0,160},{32,128},{64,224},{96,192},{128,32},{160,0},{192,96},{224,... | collective-permute-start | bytes 270344 | tf_op jit(solution)/shard_map/ppermute | solution.py:793
  61.8 21.5 %all-to-all-start.1 = ((f32[256,1,80]{2,1,0:T(1,128)}), f32[256,1,80]{2,1,0:T(1,128)S(1)}, u32[]{:S(2)}, u32[]{:S(2)}) async-start(f32[256,1,80]{2,1,0:T(1,128)} %bitcast.7), calls=%async_computation.1 | async-start | bytes 262144 | tf_op jit(solution)/shard_map/all_to_all | solution.py:789
  70.7 6.2 %collective-permute-start.19 = (f32[11,16,128]{2,1,0:T(8,128)S(1)}, f32[11,16,128]{2,1,0:T(8,128)S(1)}, u32[]{:S(2)}, u32[]{:S(2)}) collective-permute-start(f32[11,16,128]{2,1,0:T(8,128)S(1)} %get-tuple-element.77), channel_id=1, source_target_pairs={{0,224},{32,192},{64,160},{96,128},{128,96},{160,64},{192,32},{224... | collective-permute-start | bytes 270344 | tf_op jit(solution)/shard_map/ppermute | solution.py:793
  73.7 6.4 %collective-permute-start.21 = (f32[11,16,128]{2,1,0:T(8,128)S(1)}, f32[11,16,128]{2,1,0:T(8,128)S(1)}, u32[]{:S(2)}, u32[]{:S(2)}) collective-permute-start(f32[11,16,128]{2,1,0:T(8,128)S(1)} %get-tuple-element.79), channel_id=1, source_target_pairs={{0,192},{32,224},{64,128},{96,160},{128,64},{160,96},{192,0},{224,... | collective-permute-start | bytes 270344 | tf_op jit(solution)/shard_map/ppermute | solution.py:793
  75.5 5.4 %collective-permute-start.22 = (f32[11,16,128]{2,1,0:T(8,128)S(1)}, f32[11,16,128]{2,1,0:T(8,128)S(1)}, u32[]{:S(2)}, u32[]{:S(2)}) collective-permute-start(f32[11,16,128]{2,1,0:T(8,128)S(1)} %get-tuple-element.80), channel_id=1, source_target_pairs={{0,96},{32,64},{64,32},{96,0},{128,224},{160,192},{192,160},{224,1... | collective-permute-start | bytes 270344 | tf_op jit(solution)/shard_map/ppermute | solution.py:793
  75.6 5.4 %collective-permute-start.23 = (f32[11,16,128]{2,1,0:T(8,128)S(1)}, f32[11,16,128]{2,1,0:T(8,128)S(1)}, u32[]{:S(2)}, u32[]{:S(2)}) collective-permute-start(f32[11,16,128]{2,1,0:T(8,128)S(1)} %get-tuple-element.81), channel_id=1, source_target_pairs={{0,32},{32,0},{64,96},{96,64},{128,160},{160,128},{192,224},{224,1... | collective-permute-start | bytes 270344 | tf_op jit(solution)/shard_map/ppermute | solution.py:793
  84.2 6.0 %collective-permute-start.24 = (f32[9,16,128]{2,1,0:T(8,128)S(1)}, f32[9,16,128]{2,1,0:T(8,128)S(1)}, u32[]{:S(2)}, u32[]{:S(2)}) collective-permute-start(f32[9,16,128]{2,1,0:T(8,128)S(1)} %get-tuple-element.83), channel_id=1, source_target_pairs={{0,128},{32,160},{64,192},{96,224},{128,0},{160,32},{192,64},{224,... | collective-permute-start | bytes 221192 | tf_op jit(solution)/shard_map/ppermute | solution.py:793
  85.5 7.1 %collective-permute-start.25 = (f32[9,16,128]{2,1,0:T(8,128)S(1)}, f32[9,16,128]{2,1,0:T(8,128)S(1)}, u32[]{:S(2)}, u32[]{:S(2)}) collective-permute-start(f32[9,16,128]{2,1,0:T(8,128)S(1)} %get-tuple-element.84), channel_id=1, source_target_pairs={{0,160},{32,128},{64,224},{96,192},{128,32},{160,0},{192,96},{224,... | collective-permute-start | bytes 221192 | tf_op jit(solution)/shard_map/ppermute | solution.py:793
  88.2 5.8 %collective-permute-start.26 = (f32[9,16,128]{2,1,0:T(8,128)S(1)}, f32[9,16,128]{2,1,0:T(8,128)S(1)}, u32[]{:S(2)}, u32[]{:S(2)}) collective-permute-start(f32[9,16,128]{2,1,0:T(8,128)S(1)} %get-tuple-element.85), channel_id=1, source_target_pairs={{0,224},{32,192},{64,160},{96,128},{128,96},{160,64},{192,32},{224... | collective-permute-start | bytes 221192 | tf_op jit(solution)/shard_map/ppermute | solution.py:793
  88.2 5.8 %collective-permute-start.27 = (f32[9,16,128]{2,1,0:T(8,128)S(1)}, f32[9,16,128]{2,1,0:T(8,128)S(1)}, u32[]{:S(2)}, u32[]{:S(2)}) collective-permute-start(f32[9,16,128]{2,1,0:T(8,128)S(1)} %get-tuple-element.86), channel_id=1, source_target_pairs={{0,64},{32,96},{64,0},{96,32},{128,192},{160,224},{192,128},{224,1... | collective-permute-start | bytes 221192 | tf_op jit(solution)/shard_map/ppermute | solution.py:793
  88.5 6.1 %collective-permute-start.28 = (f32[9,16,128]{2,1,0:T(8,128)S(1)}, f32[9,16,128]{2,1,0:T(8,128)S(1)}, u32[]{:S(2)}, u32[]{:S(2)}) collective-permute-start(f32[9,16,128]{2,1,0:T(8,128)S(1)} %get-tuple-element.87), channel_id=1, source_target_pairs={{0,192},{32,224},{64,128},{96,160},{128,64},{160,96},{192,0},{224,... | collective-permute-start | bytes 221192 | tf_op jit(solution)/shard_map/ppermute | solution.py:793
  90.2 5.5 %collective-permute-start.29 = (f32[9,16,128]{2,1,0:T(8,128)S(1)}, f32[9,16,128]{2,1,0:T(8,128)S(1)}, u32[]{:S(2)}, u32[]{:S(2)}) collective-permute-start(f32[9,16,128]{2,1,0:T(8,128)S(1)} %get-tuple-element.88), channel_id=1, source_target_pairs={{0,96},{32,64},{64,32},{96,0},{128,224},{160,192},{192,160},{224,1... | collective-permute-start | bytes 221192 | tf_op jit(solution)/shard_map/ppermute | solution.py:793
  (18 other events, 166.9 us)

commit v7 on v6

--- a/solution.py
+++ b/solution.py
@@ -31,7 +31,6 @@
 LINE = ORDER - 1
 PAIRED = BLOCK + 2
 SCALARS = 5
-WIDTH = SCALARS * ROWS
 STEP_ORDER = [4, 5, 7, 2, 6, 3, 1]
 LEVEL_ORDER = [0, 2, 1, 3, 4]
 SPACING = 0.25
@@ -345,18 +344,18 @@
     return load
 
 
-def gradients(load, first_ref, metric_ref, visit):
+def gradients(load, first_ref, metric_ref, rows, visit):
     for j in range(SIDE):
         line = derivative_line([load(k * SIDE + j) for k in range(SIDE)], False)
         for i in range(SIDE):
-            first_ref[i * SIDE + j] = line[i]
+            first_ref[i * SIDE + j, rows, :] = line[i]
     for i in range(SIDE):
         line = derivative_line([load(i * SIDE + k) for k in range(SIDE)], False)
         seconds = []
         for j in range(SIDE):
             node = i * SIDE + j
             m0, m1, m2 = [metric_ref[node, c : c + 1, :] for c in range(3)]
-            g1, g2 = first_ref[node], line[j]
+            g1, g2 = first_ref[node, rows, :], line[j]
             p1 = m0 * g1 + m2 * g2
             p2 = m2 * g1 + m1 * g2
             visit(node, g1, g2, p1, p2)
@@ -365,16 +364,15 @@
 
 
 def apply_operator(inner_ref, cycle_ref, result_ref, first_ref, energy_ref, metric_ref, shift_ref):
-    @pl.loop(0, 2)
-    def half(part):
-        rows = pl.ds(pl.multiple_of(part * 8, 8), 8)
+    for part in range(2):
+        rows = slice(part * 8, part * 8 + 8)
         shift = shift_ref[rows, :]
         load = grid_load(inner_ref, cycle_ref, rows)
 
         def visit(node, g1, g2, p1, p2):
-            first_ref[node] = p1
-
-        for i, seconds in gradients(load, first_ref, metric_ref, visit):
+            first_ref[node, rows, :] = p1
+
+        for i, seconds in gradients(load, first_ref, metric_ref, rows, visit):
             line = derivative_line(seconds, True)
             for j in range(SIDE):
                 node = i * SIDE + j
@@ -382,7 +380,7 @@
                 result_ref[node, rows, :] = line[j] + mass * load(node)
         energy = jnp.zeros((8, LANES), F32)
         for j in range(SIDE):
-            line = derivative_line([first_ref[k * SIDE + j] for k in range(SIDE)], True)
+            line = derivative_line([first_ref[k * SIDE + j, rows, :] for k in range(SIDE)], True)
             for i in range(SIDE):
                 node = i * SIDE + j
                 value = result_ref[node, rows, :] + line[i]
@@ -392,9 +390,8 @@
 
 
 def apply_energy(inner_ref, cycle_ref, first_ref, energy_ref, metric_ref, shift_ref):
-    @pl.loop(0, 2)
-    def half(part):
-        rows = pl.ds(pl.multiple_of(part * 8, 8), 8)
+    for part in range(2):
+        rows = slice(part * 8, part * 8 + 8)
         shift = shift_ref[rows, :]
         load = grid_load(inner_ref, cycle_ref, rows)
         sums = [jnp.zeros((8, LANES), F32)]
@@ -404,7 +401,7 @@
             mass = shift * metric_ref[node, 3:4, :]
             sums[0] = sums[0] + (g1 * p1 + g2 * p2 + mass * value * value)
 
-        for i, seconds in gradients(load, first_ref, metric_ref, visit):
+        for i, seconds in gradients(load, first_ref, metric_ref, rows, visit):
             pass
         energy_ref[rows, :] = sums[0]
 
@@ -703,7 +700,7 @@
         column = jnp.sum(value, axis=1, keepdims=True)
         spread = jnp.where(lanes == sublanes + index * ROWS, column, spread)
     message = jnp.sum(spread, axis=0, keepdims=True)
-    message_ref[...] = jnp.broadcast_to(message[:, :WIDTH], message_ref.shape)
+    message_ref[...] = jnp.broadcast_to(message, message_ref.shape)
 
 
 def combine_kernel(
@@ -715,7 +712,6 @@
     for step, in_ref in enumerate([i0, i1, i2, i3, i4, i5, i6, i7]):
         origin = jnp.bitwise_xor(mode, step)
         total = jnp.sum(scalars_ref[origin], axis=0, keepdims=True)
-        total = jnp.concatenate([total, jnp.zeros((1, LANES - WIDTH), F32)], axis=1)
         g00, g01, g11, h0, h1 = [
             jnp.sum(jnp.where(lanes == sublanes + index * ROWS, total, 0.0), axis=1, keepdims=True)
             for index in range(SCALARS)
@@ -812,7 +808,7 @@
     right = pltpu.VMEM((LOW, CYCLE * LANES), BF16)
     left_slots = pltpu.VMEM((2 * HIGH * ROWS, SLOTS), BF16)
     cycle = pltpu.VMEM((CYCLE, ROWS, LANES), F32)
-    first = pltpu.VMEM((NODES, 8, LANES), F32)
+    first = pltpu.VMEM((NODES, ROWS, LANES), F32)
     energy = pltpu.VMEM((ROWS, LANES), F32)
     packing = pltpu.VMEM((MODES, BLOCK, ROWS, LANES), F32)
     wide = (HIGH * ROWS, LOW)
@@ -864,10 +860,10 @@
         input_output_aliases={2: 2},
     )
     message = call(
-        energy_kernel, shape(MODES * ELEMS_AXIS, WIDTH), [cycle, first, energy, energy],
+        energy_kernel, shape(MODES * ELEMS_AXIS, LANES), [cycle, first, energy, energy],
         moved, change, sums, changed_sums, edge_rows, metric, penalties,
     )
-    scalars = swap_blocks(message, ("mode", "elem")).reshape(MODES, ELEMS_AXIS, WIDTH)
+    scalars = swap_blocks(message, ("mode", "elem")).reshape(MODES, ELEMS_AXIS, LANES)
     mixed = call(
         combine_kernel, blocks, [pltpu.VMEM((BLOCK, PLANES, LANES), F32)], backward, scalars, column,
         *swap_steps(pairs)

time: 97.6 us -> 95.4 us (0.977)
  waiting for transfers between devices: 17.4 us -> 15.5 us
    all_to_all x2, starting transfers between devices: 15.8 us -> 18.4 us  [swap_blocks(): return lax.all_to_all(blocks, axis, split_axis=0, concat_axis=0, tiled=True)]
    ppermute x31, starting transfers between devices: 49.1 us -> 46.5 us  [permute(): lax.ppermute(value, axis, [(i, i ^ flip) for i in range(lax.axis_size(axi...]
    all_to_all x2, waiting for transfers between devices: 2.33 us -> 0.01 us  [swap_blocks(): return lax.all_to_all(blocks, axis, split_axis=0, concat_axis=0, tiled=True)]
  transfers between devices with their start and end apart: 33 -> 33, of which waited for: 16 -> 15; matrix products, arithmetic and copies ran while one was open for 0% -> 0% of each run, Pallas kernels for 3% -> 0%
where the time goes in v7:
time: 95.4 us; the launch traced here: 95.1 us
  starting transfers between devices  64.9 us (68%)
  waiting for transfers between devices  15.5 us (16%)
  Pallas kernels  14.3 us (15%)
    ppermute x31, starting transfers between devices, permute(): lax.ppermute(value, axis, [(i, i ^ flip) for i in range(lax.axis_size(axi...  46.5 us
    all_to_all x2, starting transfers between devices, swap_blocks(): return lax.all_to_all(blocks, axis, split_axis=0, concat_axis=0, tiled=True)  18.4 us
    ppermute x31, waiting for transfers between devices, permute(): lax.ppermute(value, axis, [(i, i ^ flip) for i in range(lax.axis_size(axi...  15.4 us
    pallas_call x9, Pallas kernels, call(): pl.pallas_call(kernel, out_shape=out_shapes, scratch_shapes=scratch, comp...  14.3 us
  transfers between devices with their start and end apart: 33, of which 15 were waited for; matrix products, arithmetic and copies ran while one was open for 0% of the time, Pallas kernels for 0%

profile of v7, /device:TPU:1, one launch (start us, length us, event | category | flops | bytes accessed | tf_op | source)
XLA Modules:
  0.0 95.1 jit_solution(2253081681458284832)
XLA Ops:
  0.0 4.2 %shard_map.100 = (f32[72,16,128]{2,1,0:T(8,128)}, f32[3,24,128]{2,1,0:T(8,128)}, f32[2,49,128]{2,1,0:T(8,128)}, f32[2,9,256]{2,1,0:T(8,128)}, f32[9,256]{1,0:T(8,128)}, /*index=5*/s32[8,128]{1,0:T(8,128)}) custom-call(f32[81,16,128]{2,1,0:T(8,128)} %bitcast.19, s32[32,128]{1,0:T(8,128)} %bitcast.15, s32[3,128]{1,0:T(4,128)} %bitcast.21, s32[3,128]{1,0:T(4,128)} %bitcast.22, ...), custom_call_target="tpu_custom_call" | custom-call | tf_op jit(solution)/shard_map/pallas_call | solution.py:771
  4.2 6.8 %all-to-all-start = ((f32[8,9,16,128]{3,2,1,0:T(8,128)}), f32[8,9,16,128]{3,2,1,0:T(8,128)S(1)}, u32[]{:S(2)}, u32[]{:S(2)}) async-start(f32[8,9,16,128]{3,2,1,0:T(8,128)} %bitcast.20), calls=%async_computation | async-start | bytes 1179648 | tf_op jit(solution)/shard_map/all_to_all | solution.py:785
  11.0 6.0 %collective-permute-start.4 = (f32[3,24,128]{2,1,0:T(8,128)S(1)}, f32[3,24,128]{2,1,0:T(8,128)S(1)}, u32[]{:S(2)}, u32[]{:S(2)}) collective-permute-start(f32[3,24,128]{2,1,0:T(8,128)S(1)} %copy-done.8), channel_id=1, source_target_pairs={{0,16},{1,17},{2,18},{3,19},{4,20},{5,21},{6,22},{7,23},{8,24},{9,... | collective-permute-start | bytes 110600 | tf_op jit(solution)/shard_map/ppermute | solution.py:789
  18.3 2.9 %collective-permute-start.2 = (f32[3,24,128]{2,1,0:T(8,128)S(1)}, f32[3,24,128]{2,1,0:T(8,128)S(1)}, u32[]{:S(2)}, u32[]{:S(2)}) collective-permute-start(f32[3,24,128]{2,1,0:T(8,128)S(1)} %copy-done.8), channel_id=1, source_target_pairs={{0,2},{1,3},{2,0},{3,1},{4,6},{5,7},{6,4},{7,5},{8,10},{9,11},{10,... | collective-permute-start | bytes 110600 | tf_op jit(solution)/shard_map/ppermute | solution.py:789
  22.6 1.4 %collective-permute-done.1.a2 = f32[3,24,128]{2,1,0:T(8,128)S(1)} collective-permute-done((f32[3,24,128]{2,1,0:T(8,128)S(1)}, f32[3,24,128]{2,1,0:T(8,128)S(1)}, u32[]{:S(2)}, u32[]{:S(2)}) %collective-permute-start.1) | collective-permute-done | bytes 36896 | tf_op jit(solution)/shard_map/ppermute | solution.py:789
  25.6 3.0 %collective-permute-start.5 = (f32[12,16,128]{2,1,0:T(8,128)S(1)}, f32[12,16,128]{2,1,0:T(8,128)S(1)}, u32[]{:S(2)}, u32[]{:S(2)}) collective-permute-start(f32[12,16,128]{2,1,0:T(8,128)S(1)} %get-tuple-element.51.o4), channel_id=1, source_target_pairs={{0,128},{32,160},{64,192},{96,224},{128,0},{160,32},{192,64},{224,... | collective-permute-start | bytes 294920 | tf_op jit(solution)/shard_map/ppermute | solution.py:789
  28.6 2.6 %collective-permute-start.6 = (f32[12,16,128]{2,1,0:T(8,128)S(1)}, f32[12,16,128]{2,1,0:T(8,128)S(1)}, u32[]{:S(2)}, u32[]{:S(2)}) collective-permute-start(f32[12,16,128]{2,1,0:T(8,128)S(1)} %get-tuple-element.52.o5), channel_id=1, source_target_pairs={{0,160},{32,128},{64,224},{96,192},{128,32},{160,0},{192,96},{224,... | collective-permute-start | bytes 294920 | tf_op jit(solution)/shard_map/ppermute | solution.py:789
  32.9 1.8 %collective-permute-start.9 = (f32[12,16,128]{2,1,0:T(8,128)S(1)}, f32[12,16,128]{2,1,0:T(8,128)S(1)}, u32[]{:S(2)}, u32[]{:S(2)}) collective-permute-start(f32[12,16,128]{2,1,0:T(8,128)S(1)} %get-tuple-element.55.o6), channel_id=1, source_target_pairs={{0,192},{32,224},{64,128},{96,160},{128,64},{160,96},{192,0},{224,... | collective-permute-start | bytes 294920 | tf_op jit(solution)/shard_map/ppermute | solution.py:789
  34.6 1.5 %collective-permute-start.10 = (f32[12,16,128]{2,1,0:T(8,128)S(1)}, f32[12,16,128]{2,1,0:T(8,128)S(1)}, u32[]{:S(2)}, u32[]{:S(2)}) collective-permute-start(f32[12,16,128]{2,1,0:T(8,128)S(1)} %get-tuple-element.56.o3), channel_id=1, source_target_pairs={{0,96},{32,64},{64,32},{96,0},{128,224},{160,192},{192,160},{224,1... | collective-permute-start | bytes 294920 | tf_op jit(solution)/shard_map/ppermute | solution.py:789
  38.5 1.4 %collective-permute-done.9.i6 = f32[12,16,128]{2,1,0:T(8,128)S(1)} collective-permute-done((f32[12,16,128]{2,1,0:T(8,128)S(1)}, f32[12,16,128]{2,1,0:T(8,128)S(1)}, u32[]{:S(2)}, u32[]{:S(2)}) %collective-permute-start.9) | collective-permute-done | bytes 98336 | tf_op jit(solution)/shard_map/ppermute | solution.py:789
  40.6 4.0 %shard_map.102 = (f32[49,16,128]{2,1,0:T(8,128)S(1)}, f32[49,16,128]{2,1,0:T(8,128)S(1)}, f32[81,16,128]{2,1,0:T(8,128)S(1)}, f32[8,9,16,128]{3,2,1,0:T(8,128)S(...) custom-call(f32[12,16,128]{2,1,0:T(8,128)S(1)} %collective-permute-done.5.i4, ...), custom_call_target="tpu_custom_call" | custom-call | tf_op jit(solution)/shard_map/pallas_call | solution.py:771
  46.4 2.9 %collective-permute-start.14 = (f32[3,16,128]{2,1,0:T(8,128)S(1)}, f32[3,16,128]{2,1,0:T(8,128)S(1)}, u32[]{:S(2)}, u32[]{:S(2)}) collective-permute-start(f32[3,16,128]{2,1,0:T(8,128)S(1)} %get-tuple-element.71), channel_id=1, source_target_pairs={{0,2},{1,3},{2,0},{3,1},{4,6},{5,7},{6,4},{7,5},{8,10},{9,11},{10,... | collective-permute-start | bytes 73736 | tf_op jit(solution)/shard_map/ppermute | solution.py:789
  53.1 2.3 %shard_map.105 = f32[256,128]{1,0:T(8,128)} custom-call(f32[49,16,128]{2,1,0:T(8,128)S(1)} %get-tuple-element.68.moved_ref, f32[144,256]{1,0:T(8,128)S(1)} %get-tuple-element.72.change_ref, f32[2,16,128]{2,1,0:T(8,128)S(1)} %get-tuple-element.73.sums_ref, f32[2,16,128]{2,1,0:T(8,128)S(1)} %get-tuple-element.74.changed_sums_ref, s32[32,128]{1,0:T(8,128)S(1)} %bitcast.17, ...), custom_call_target="tpu_custom_call" | custom-call | tf_op jit(solution)/shard_map/pallas_call | solution.py:771
  55.4 11.6 %all-to-all-start.1 = ((f32[256,1,128]{2,1,0:T(1,128)}), f32[256,1,128]{2,1,0:T(1,128)S(1)}, u32[]{:S(2)}, u32[]{:S(2)}) async-start(f32[256,1,128]{2,1,0:T(1,128)} %bitcast.7), calls=%async_computation.1 | async-start | bytes 262144 | tf_op jit(solution)/shard_map/all_to_all | solution.py:785
  67.0 3.0 %collective-permute-start.17 = (f32[11,16,128]{2,1,0:T(8,128)S(1)}, f32[11,16,128]{2,1,0:T(8,128)S(1)}, u32[]{:S(2)}, u32[]{:S(2)}) collective-permute-start(f32[11,16,128]{2,1,0:T(8,128)S(1)} %get-tuple-element.75), channel_id=1, source_target_pairs={{0,128},{32,160},{64,192},{96,224},{128,0},{160,32},{192,64},{224,... | collective-permute-start | bytes 270344 | tf_op jit(solution)/shard_map/ppermute | solution.py:789
  70.0 2.4 %collective-permute-start.18 = (f32[11,16,128]{2,1,0:T(8,128)S(1)}, f32[11,16,128]{2,1,0:T(8,128)S(1)}, u32[]{:S(2)}, u32[]{:S(2)}) collective-permute-start(f32[11,16,128]{2,1,0:T(8,128)S(1)} %get-tuple-element.76), channel_id=1, source_target_pairs={{0,160},{32,128},{64,224},{96,192},{128,32},{160,0},{192,96},{224,... | collective-permute-start | bytes 270344 | tf_op jit(solution)/shard_map/ppermute | solution.py:789
  73.8 3.0 %collective-permute-start.22 = (f32[11,16,128]{2,1,0:T(8,128)S(1)}, f32[11,16,128]{2,1,0:T(8,128)S(1)}, u32[]{:S(2)}, u32[]{:S(2)}) collective-permute-start(f32[11,16,128]{2,1,0:T(8,128)S(1)} %get-tuple-element.80), channel_id=1, source_target_pairs={{0,96},{32,64},{64,32},{96,0},{128,224},{160,192},{192,160},{224,1... | collective-permute-start | bytes 270344 | tf_op jit(solution)/shard_map/ppermute | solution.py:789
  78.1 1.5 %collective-permute-done.19.i7 = f32[11,16,128]{2,1,0:T(8,128)S(1)} collective-permute-done((f32[11,16,128]{2,1,0:T(8,128)S(1)}, f32[11,16,128]{2,1,0:T(8,128)S(1)}, u32[]{:S(2)}, u32[]{:S(2)}) %collective-permute-start.19) | collective-permute-done | bytes 90144 | tf_op jit(solution)/shard_map/ppermute | solution.py:789
  79.6 1.7 %collective-permute-done.21.i6 = f32[11,16,128]{2,1,0:T(8,128)S(1)} collective-permute-done((f32[11,16,128]{2,1,0:T(8,128)S(1)}, f32[11,16,128]{2,1,0:T(8,128)S(1)}, u32[]{:S(2)}, u32[]{:S(2)}) %collective-permute-start.21) | collective-permute-done | bytes 90144 | tf_op jit(solution)/shard_map/ppermute | solution.py:789
  82.2 1.4 %collective-permute-start.24 = (f32[9,16,128]{2,1,0:T(8,128)S(1)}, f32[9,16,128]{2,1,0:T(8,128)S(1)}, u32[]{:S(2)}, u32[]{:S(2)}) collective-permute-start(f32[9,16,128]{2,1,0:T(8,128)S(1)} %get-tuple-element.83), channel_id=1, source_target_pairs={{0,128},{32,160},{64,192},{96,224},{128,0},{160,32},{192,64},{224,... | collective-permute-start | bytes 221192 | tf_op jit(solution)/shard_map/ppermute | solution.py:789
  83.6 2.4 %collective-permute-start.25 = (f32[9,16,128]{2,1,0:T(8,128)S(1)}, f32[9,16,128]{2,1,0:T(8,128)S(1)}, u32[]{:S(2)}, u32[]{:S(2)}) collective-permute-start(f32[9,16,128]{2,1,0:T(8,128)S(1)} %get-tuple-element.84), channel_id=1, source_target_pairs={{0,160},{32,128},{64,224},{96,192},{128,32},{160,0},{192,96},{224,... | collective-permute-start | bytes 221192 | tf_op jit(solution)/shard_map/ppermute | solution.py:789
  86.7 1.6 %collective-permute-start.28 = (f32[9,16,128]{2,1,0:T(8,128)S(1)}, f32[9,16,128]{2,1,0:T(8,128)S(1)}, u32[]{:S(2)}, u32[]{:S(2)}) collective-permute-start(f32[9,16,128]{2,1,0:T(8,128)S(1)} %get-tuple-element.87), channel_id=1, source_target_pairs={{0,192},{32,224},{64,128},{96,160},{128,64},{160,96},{192,0},{224,... | collective-permute-start | bytes 221192 | tf_op jit(solution)/shard_map/ppermute | solution.py:789
  88.3 2.1 %collective-permute-start.29 = (f32[9,16,128]{2,1,0:T(8,128)S(1)}, f32[9,16,128]{2,1,0:T(8,128)S(1)}, u32[]{:S(2)}, u32[]{:S(2)}) collective-permute-start(f32[9,16,128]{2,1,0:T(8,128)S(1)} %get-tuple-element.88), channel_id=1, source_target_pairs={{0,96},{32,64},{64,32},{96,0},{128,224},{160,192},{192,160},{224,1... | collective-permute-start | bytes 221192 | tf_op jit(solution)/shard_map/ppermute | solution.py:789
  93.4 1.5 %shard_map.108 = f32[81,16,128]{2,1,0:T(8,128)} custom-call(f32[9,16,128]{2,1,0:T(8,128)S(1)} %collective-permute-done.24.i4, f32[9,16,128]{2,1,0:T(8,128)S(1)} %collective-permute-done.25.i5, f32[9,16,128]{2,1,0:T(8,128)S(1)} %collective-permute-done.26.i7, f32[9,16,128]{2,1,0:T(8,128)S(1)} %collective-permute-done.27.i2, ...), custom_call_target="tpu_custom_call" | custom-call | tf_op jit(solution)/shard_map/pallas_call | solution.py:771
  (69 shorter events, 21.9 us)
Async XLA Ops:
  4.2 20.5 %all-to-all-start = ((f32[8,9,16,128]{3,2,1,0:T(8,128)}), f32[8,9,16,128]{3,2,1,0:T(8,128)S(1)}, u32[]{:S(2)}, u32[]{:S(2)}) async-start(f32[8,9,16,128]{3,2,1,0:T(8,128)} %bitcast.20), calls=%async_computation | async-start | bytes 1179648 | tf_op jit(solution)/shard_map/all_to_all | solution.py:785
  11.0 11.3 %collective-permute-start.4 = (f32[3,24,128]{2,1,0:T(8,128)S(1)}, f32[3,24,128]{2,1,0:T(8,128)S(1)}, u32[]{:S(2)}, u32[]{:S(2)}) collective-permute-start(f32[3,24,128]{2,1,0:T(8,128)S(1)} %copy-done.8), channel_id=1, source_target_pairs={{0,16},{1,17},{2,18},{3,19},{4,20},{5,21},{6,22},{7,23},{8,24},{9,... | collective-permute-start | bytes 110600 | tf_op jit(solution)/shard_map/ppermute | solution.py:789
  17.1 5.3 %collective-permute-start.3 = (f32[3,24,128]{2,1,0:T(8,128)S(1)}, f32[3,24,128]{2,1,0:T(8,128)S(1)}, u32[]{:S(2)}, u32[]{:S(2)}) collective-permute-start(f32[3,24,128]{2,1,0:T(8,128)S(1)} %copy-done.8), channel_id=1, source_target_pairs={{0,8},{1,9},{2,10},{3,11},{4,12},{5,13},{6,14},{7,15},{8,0},{9,1},... | collective-permute-start | bytes 110600 | tf_op jit(solution)/shard_map/ppermute | solution.py:789
  25.6 9.0 %collective-permute-start.5 = (f32[12,16,128]{2,1,0:T(8,128)S(1)}, f32[12,16,128]{2,1,0:T(8,128)S(1)}, u32[]{:S(2)}, u32[]{:S(2)}) collective-permute-start(f32[12,16,128]{2,1,0:T(8,128)S(1)} %get-tuple-element.51.o4), channel_id=1, source_target_pairs={{0,128},{32,160},{64,192},{96,224},{128,0},{160,32},{192,64},{224,... | collective-permute-start | bytes 294920 | tf_op jit(solution)/shard_map/ppermute | solution.py:789
  28.6 7.5 %collective-permute-start.6 = (f32[12,16,128]{2,1,0:T(8,128)S(1)}, f32[12,16,128]{2,1,0:T(8,128)S(1)}, u32[]{:S(2)}, u32[]{:S(2)}) collective-permute-start(f32[12,16,128]{2,1,0:T(8,128)S(1)} %get-tuple-element.52.o5), channel_id=1, source_target_pairs={{0,160},{32,128},{64,224},{96,192},{128,32},{160,0},{192,96},{224,... | collective-permute-start | bytes 294920 | tf_op jit(solution)/shard_map/ppermute | solution.py:789
  31.2 7.3 %collective-permute-start.7 = (f32[12,16,128]{2,1,0:T(8,128)S(1)}, f32[12,16,128]{2,1,0:T(8,128)S(1)}, u32[]{:S(2)}, u32[]{:S(2)}) collective-permute-start(f32[12,16,128]{2,1,0:T(8,128)S(1)} %get-tuple-element.53.o7), channel_id=1, source_target_pairs={{0,224},{32,192},{64,160},{96,128},{128,96},{160,64},{192,32},{224... | collective-permute-start | bytes 294920 | tf_op jit(solution)/shard_map/ppermute | solution.py:789
  32.3 6.2 %collective-permute-start.8 = (f32[12,16,128]{2,1,0:T(8,128)S(1)}, f32[12,16,128]{2,1,0:T(8,128)S(1)}, u32[]{:S(2)}, u32[]{:S(2)}) collective-permute-start(f32[12,16,128]{2,1,0:T(8,128)S(1)} %get-tuple-element.54.o2), channel_id=1, source_target_pairs={{0,64},{32,96},{64,0},{96,32},{128,192},{160,224},{192,128},{224,1... | collective-permute-start | bytes 294920 | tf_op jit(solution)/shard_map/ppermute | solution.py:789
  32.9 7.0 %collective-permute-start.9 = (f32[12,16,128]{2,1,0:T(8,128)S(1)}, f32[12,16,128]{2,1,0:T(8,128)S(1)}, u32[]{:S(2)}, u32[]{:S(2)}) collective-permute-start(f32[12,16,128]{2,1,0:T(8,128)S(1)} %get-tuple-element.55.o6), channel_id=1, source_target_pairs={{0,192},{32,224},{64,128},{96,160},{128,64},{160,96},{192,0},{224,... | collective-permute-start | bytes 294920 | tf_op jit(solution)/shard_map/ppermute | solution.py:789
  34.6 5.9 %collective-permute-start.10 = (f32[12,16,128]{2,1,0:T(8,128)S(1)}, f32[12,16,128]{2,1,0:T(8,128)S(1)}, u32[]{:S(2)}, u32[]{:S(2)}) collective-permute-start(f32[12,16,128]{2,1,0:T(8,128)S(1)} %get-tuple-element.56.o3), channel_id=1, source_target_pairs={{0,96},{32,64},{64,32},{96,0},{128,224},{160,192},{192,160},{224,1... | collective-permute-start | bytes 294920 | tf_op jit(solution)/shard_map/ppermute | solution.py:789
  44.7 6.8 %collective-permute-start.16 = (f32[3,16,128]{2,1,0:T(8,128)S(1)}, f32[3,16,128]{2,1,0:T(8,128)S(1)}, u32[]{:S(2)}, u32[]{:S(2)}) collective-permute-start(f32[3,16,128]{2,1,0:T(8,128)S(1)} %get-tuple-element.71), channel_id=1, source_target_pairs={{0,16},{1,17},{2,18},{3,19},{4,20},{5,21},{6,22},{7,23},{8,24},{9,... | collective-permute-start | bytes 73736 | tf_op jit(solution)/shard_map/ppermute | solution.py:789
  45.9 5.5 %collective-permute-start.15 = (f32[3,16,128]{2,1,0:T(8,128)S(1)}, f32[3,16,128]{2,1,0:T(8,128)S(1)}, u32[]{:S(2)}, u32[]{:S(2)}) collective-permute-start(f32[3,16,128]{2,1,0:T(8,128)S(1)} %get-tuple-element.71), channel_id=1, source_target_pairs={{0,8},{1,9},{2,10},{3,11},{4,12},{5,13},{6,14},{7,15},{8,0},{9,1},... | collective-permute-start | bytes 73736 | tf_op jit(solution)/shard_map/ppermute | solution.py:789
  55.4 25.9 %all-to-all-start.1 = ((f32[256,1,128]{2,1,0:T(1,128)}), f32[256,1,128]{2,1,0:T(1,128)S(1)}, u32[]{:S(2)}, u32[]{:S(2)}) async-start(f32[256,1,128]{2,1,0:T(1,128)} %bitcast.7), calls=%async_computation.1 | async-start | bytes 262144 | tf_op jit(solution)/shard_map/all_to_all | solution.py:785
  67.0 6.8 %collective-permute-start.17 = (f32[11,16,128]{2,1,0:T(8,128)S(1)}, f32[11,16,128]{2,1,0:T(8,128)S(1)}, u32[]{:S(2)}, u32[]{:S(2)}) collective-permute-start(f32[11,16,128]{2,1,0:T(8,128)S(1)} %get-tuple-element.75), channel_id=1, source_target_pairs={{0,128},{32,160},{64,192},{96,224},{128,0},{160,32},{192,64},{224,... | collective-permute-start | bytes 270344 | tf_op jit(solution)/shard_map/ppermute | solution.py:789
  70.0 8.0 %collective-permute-start.18 = (f32[11,16,128]{2,1,0:T(8,128)S(1)}, f32[11,16,128]{2,1,0:T(8,128)S(1)}, u32[]{:S(2)}, u32[]{:S(2)}) collective-permute-start(f32[11,16,128]{2,1,0:T(8,128)S(1)} %get-tuple-element.76), channel_id=1, source_target_pairs={{0,160},{32,128},{64,224},{96,192},{128,32},{160,0},{192,96},{224,... | collective-permute-start | bytes 270344 | tf_op jit(solution)/shard_map/ppermute | solution.py:789
  72.4 7.2 %collective-permute-start.19 = (f32[11,16,128]{2,1,0:T(8,128)S(1)}, f32[11,16,128]{2,1,0:T(8,128)S(1)}, u32[]{:S(2)}, u32[]{:S(2)}) collective-permute-start(f32[11,16,128]{2,1,0:T(8,128)S(1)} %get-tuple-element.77), channel_id=1, source_target_pairs={{0,224},{32,192},{64,160},{96,128},{128,96},{160,64},{192,32},{224... | collective-permute-start | bytes 270344 | tf_op jit(solution)/shard_map/ppermute | solution.py:789
  72.9 6.7 %collective-permute-start.20 = (f32[11,16,128]{2,1,0:T(8,128)S(1)}, f32[11,16,128]{2,1,0:T(8,128)S(1)}, u32[]{:S(2)}, u32[]{:S(2)}) collective-permute-start(f32[11,16,128]{2,1,0:T(8,128)S(1)} %get-tuple-element.78), channel_id=1, source_target_pairs={{0,64},{32,96},{64,0},{96,32},{128,192},{160,224},{192,128},{224,1... | collective-permute-start | bytes 270344 | tf_op jit(solution)/shard_map/ppermute | solution.py:789
  72.9 8.4 %collective-permute-start.21 = (f32[11,16,128]{2,1,0:T(8,128)S(1)}, f32[11,16,128]{2,1,0:T(8,128)S(1)}, u32[]{:S(2)}, u32[]{:S(2)}) collective-permute-start(f32[11,16,128]{2,1,0:T(8,128)S(1)} %get-tuple-element.79), channel_id=1, source_target_pairs={{0,192},{32,224},{64,128},{96,160},{128,64},{160,96},{192,0},{224,... | collective-permute-start | bytes 270344 | tf_op jit(solution)/shard_map/ppermute | solution.py:789
  73.8 7.5 %collective-permute-start.22 = (f32[11,16,128]{2,1,0:T(8,128)S(1)}, f32[11,16,128]{2,1,0:T(8,128)S(1)}, u32[]{:S(2)}, u32[]{:S(2)}) collective-permute-start(f32[11,16,128]{2,1,0:T(8,128)S(1)} %get-tuple-element.80), channel_id=1, source_target_pairs={{0,96},{32,64},{64,32},{96,0},{128,224},{160,192},{192,160},{224,1... | collective-permute-start | bytes 270344 | tf_op jit(solution)/shard_map/ppermute | solution.py:789
  82.2 6.0 %collective-permute-start.24 = (f32[9,16,128]{2,1,0:T(8,128)S(1)}, f32[9,16,128]{2,1,0:T(8,128)S(1)}, u32[]{:S(2)}, u32[]{:S(2)}) collective-permute-start(f32[9,16,128]{2,1,0:T(8,128)S(1)} %get-tuple-element.83), channel_id=1, source_target_pairs={{0,128},{32,160},{64,192},{96,224},{128,0},{160,32},{192,64},{224,... | collective-permute-start | bytes 221192 | tf_op jit(solution)/shard_map/ppermute | solution.py:789
  83.6 6.7 %collective-permute-start.25 = (f32[9,16,128]{2,1,0:T(8,128)S(1)}, f32[9,16,128]{2,1,0:T(8,128)S(1)}, u32[]{:S(2)}, u32[]{:S(2)}) collective-permute-start(f32[9,16,128]{2,1,0:T(8,128)S(1)} %get-tuple-element.84), channel_id=1, source_target_pairs={{0,160},{32,128},{64,224},{96,192},{128,32},{160,0},{192,96},{224,... | collective-permute-start | bytes 221192 | tf_op jit(solution)/shard_map/ppermute | solution.py:789
  86.0 5.8 %collective-permute-start.26 = (f32[9,16,128]{2,1,0:T(8,128)S(1)}, f32[9,16,128]{2,1,0:T(8,128)S(1)}, u32[]{:S(2)}, u32[]{:S(2)}) collective-permute-start(f32[9,16,128]{2,1,0:T(8,128)S(1)} %get-tuple-element.85), channel_id=1, source_target_pairs={{0,224},{32,192},{64,160},{96,128},{128,96},{160,64},{192,32},{224... | collective-permute-start | bytes 221192 | tf_op jit(solution)/shard_map/ppermute | solution.py:789
  86.7 5.1 %collective-permute-start.27 = (f32[9,16,128]{2,1,0:T(8,128)S(1)}, f32[9,16,128]{2,1,0:T(8,128)S(1)}, u32[]{:S(2)}, u32[]{:S(2)}) collective-permute-start(f32[9,16,128]{2,1,0:T(8,128)S(1)} %get-tuple-element.86), channel_id=1, source_target_pairs={{0,64},{32,96},{64,0},{96,32},{128,192},{160,224},{192,128},{224,1... | collective-permute-start | bytes 221192 | tf_op jit(solution)/shard_map/ppermute | solution.py:789
  86.7 6.0 %collective-permute-start.28 = (f32[9,16,128]{2,1,0:T(8,128)S(1)}, f32[9,16,128]{2,1,0:T(8,128)S(1)}, u32[]{:S(2)}, u32[]{:S(2)}) collective-permute-start(f32[9,16,128]{2,1,0:T(8,128)S(1)} %get-tuple-element.87), channel_id=1, source_target_pairs={{0,192},{32,224},{64,128},{96,160},{128,64},{160,96},{192,0},{224,... | collective-permute-start | bytes 221192 | tf_op jit(solution)/shard_map/ppermute | solution.py:789
  88.3 5.2 %collective-permute-start.29 = (f32[9,16,128]{2,1,0:T(8,128)S(1)}, f32[9,16,128]{2,1,0:T(8,128)S(1)}, u32[]{:S(2)}, u32[]{:S(2)}) collective-permute-start(f32[9,16,128]{2,1,0:T(8,128)S(1)} %get-tuple-element.88), channel_id=1, source_target_pairs={{0,96},{32,64},{64,32},{96,0},{128,224},{160,192},{192,160},{224,1... | collective-permute-start | bytes 221192 | tf_op jit(solution)/shard_map/ppermute | solution.py:789
  (18 other events, 161.2 us)

commit v8 on v7

--- a/solution.py
+++ b/solution.py
@@ -31,7 +31,7 @@
 LINE = ORDER - 1
 PAIRED = BLOCK + 2
 SCALARS = 5
-STEP_ORDER = [4, 5, 7, 2, 6, 3, 1]
+STEP_ORDER = [4, 7, 5, 2, 6, 3, 1]
 LEVEL_ORDER = [0, 2, 1, 3, 4]
 SPACING = 0.25
 F32 = jnp.float32
@@ -564,7 +564,7 @@
 
 
 def first_kernel(
-    i4, i5, i7, i2, i6, i3, i1, i0, extra_ref, lists_ref, edge_ref, metric_ref,
+    i4, i7, i5, i2, i6, i3, i1, i0, extra_ref, lists_ref, edge_ref, metric_ref,
     inner_ref, diagonal_ref, penalty_ref, search_ref, inverse_ref, result_ref, source_ref, kept_ref, slots_ref,
     sums_ref, left_ref, right_ref, cycle_ref, first_ref, energy_ref, shift_ref,
 ):
@@ -704,7 +704,7 @@
 
 
 def combine_kernel(
-    matrix_ref, scalars_ref, column_ref, i4, i5, i7, i2, i6, i3, i1, i0, o0, o1, o2, o3, o4, o5, o6, o7, block_ref
+    matrix_ref, scalars_ref, column_ref, i4, i7, i5, i2, i6, i3, i1, i0, o0, o1, o2, o3, o4, o5, o6, o7, block_ref
 ):
     mode = lax.axis_index("mode")
     sublanes = lax.broadcasted_iota(jnp.int32, (ROWS, LANES), 0)
@@ -736,7 +736,7 @@
 
 
 def unpack_kernel(
-    i4, i5, i7, i2, i6, i3, i1, i0, edge_ref, out_hbm, packed_ref, out_ref, semaphores
+    i4, i7, i5, i2, i6, i3, i1, i0, edge_ref, out_hbm, packed_ref, out_ref, semaphores
 ):
     mode = lax.axis_index("mode")
     for step, in_ref in enumerate([i0, i1, i2, i3, i4, i5, i6, i7]):

time: 95.4 us -> 94.5 us (level)
  starting transfers between devices: 64.9 us -> 63.8 us
    ppermute x31, starting transfers between devices: 46.5 us -> 45.5 us  [permute(): lax.ppermute(value, axis, [(i, i ^ flip) for i in range(lax.axis_size(axi...]
where the time goes in v8:
time: 94.5 us; the launch traced here: 94.3 us
  starting transfers between devices  63.8 us (68%)
  waiting for transfers between devices  15.7 us (17%)
  Pallas kernels  14.3 us (15%)
    ppermute x31, starting transfers between devices, permute(): lax.ppermute(value, axis, [(i, i ^ flip) for i in range(lax.axis_size(axi...  45.5 us
    all_to_all x2, starting transfers between devices, swap_blocks(): return lax.all_to_all(blocks, axis, split_axis=0, concat_axis=0, tiled=True)  18.4 us
    ppermute x31, waiting for transfers between devices, permute(): lax.ppermute(value, axis, [(i, i ^ flip) for i in range(lax.axis_size(axi...  15.7 us
    pallas_call x9, Pallas kernels, call(): pl.pallas_call(kernel, out_shape=out_shapes, scratch_shapes=scratch, comp...  14.3 us
  transfers between devices with their start and end apart: 33, of which 15 were waited for; matrix products, arithmetic and copies ran while one was open for 0% of the time, Pallas kernels for 0%

profile of v8, /device:TPU:1, one launch (start us, length us, event | category | flops | bytes accessed | tf_op | source)
XLA Modules:
  0.0 94.3 jit_solution(3365055589376414887)
XLA Ops:
  0.0 4.2 %shard_map.100 = (f32[72,16,128]{2,1,0:T(8,128)}, f32[3,24,128]{2,1,0:T(8,128)}, f32[2,49,128]{2,1,0:T(8,128)}, f32[2,9,256]{2,1,0:T(8,128)}, f32[9,256]{1,0:T(8,128)}, /*index=5*/s32[8,128]{1,0:T(8,128)}) custom-call(f32[81,16,128]{2,1,0:T(8,128)} %bitcast.19, s32[32,128]{1,0:T(8,128)} %bitcast.15, s32[3,128]{1,0:T(4,128)} %bitcast.21, s32[3,128]{1,0:T(4,128)} %bitcast.22, ...), custom_call_target="tpu_custom_call" | custom-call | tf_op jit(solution)/shard_map/pallas_call | solution.py:771
  4.2 6.8 %all-to-all-start = ((f32[8,9,16,128]{3,2,1,0:T(8,128)}), f32[8,9,16,128]{3,2,1,0:T(8,128)S(1)}, u32[]{:S(2)}, u32[]{:S(2)}) async-start(f32[8,9,16,128]{3,2,1,0:T(8,128)} %bitcast.20), calls=%async_computation | async-start | bytes 1179648 | tf_op jit(solution)/shard_map/all_to_all | solution.py:785
  11.0 6.0 %collective-permute-start.4 = (f32[3,24,128]{2,1,0:T(8,128)S(1)}, f32[3,24,128]{2,1,0:T(8,128)S(1)}, u32[]{:S(2)}, u32[]{:S(2)}) collective-permute-start(f32[3,24,128]{2,1,0:T(8,128)S(1)} %copy-done.8), channel_id=1, source_target_pairs={{0,16},{1,17},{2,18},{3,19},{4,20},{5,21},{6,22},{7,23},{8,24},{9,... | collective-permute-start | bytes 110600 | tf_op jit(solution)/shard_map/ppermute | solution.py:789
  18.3 2.9 %collective-permute-start.2 = (f32[3,24,128]{2,1,0:T(8,128)S(1)}, f32[3,24,128]{2,1,0:T(8,128)S(1)}, u32[]{:S(2)}, u32[]{:S(2)}) collective-permute-start(f32[3,24,128]{2,1,0:T(8,128)S(1)} %copy-done.8), channel_id=1, source_target_pairs={{0,2},{1,3},{2,0},{3,1},{4,6},{5,7},{6,4},{7,5},{8,10},{9,11},{10,... | collective-permute-start | bytes 110600 | tf_op jit(solution)/shard_map/ppermute | solution.py:789
  22.6 1.4 %collective-permute-done.1.a2 = f32[3,24,128]{2,1,0:T(8,128)S(1)} collective-permute-done((f32[3,24,128]{2,1,0:T(8,128)S(1)}, f32[3,24,128]{2,1,0:T(8,128)S(1)}, u32[]{:S(2)}, u32[]{:S(2)}) %collective-permute-start.1) | collective-permute-done | bytes 36896 | tf_op jit(solution)/shard_map/ppermute | solution.py:789
  25.6 3.0 %collective-permute-start.5 = (f32[12,16,128]{2,1,0:T(8,128)S(1)}, f32[12,16,128]{2,1,0:T(8,128)S(1)}, u32[]{:S(2)}, u32[]{:S(2)}) collective-permute-start(f32[12,16,128]{2,1,0:T(8,128)S(1)} %get-tuple-element.51.o4), channel_id=1, source_target_pairs={{0,128},{32,160},{64,192},{96,224},{128,0},{160,32},{192,64},{224,... | collective-permute-start | bytes 294920 | tf_op jit(solution)/shard_map/ppermute | solution.py:789
  28.6 3.7 %collective-permute-start.6 = (f32[12,16,128]{2,1,0:T(8,128)S(1)}, f32[12,16,128]{2,1,0:T(8,128)S(1)}, u32[]{:S(2)}, u32[]{:S(2)}) collective-permute-start(f32[12,16,128]{2,1,0:T(8,128)S(1)} %get-tuple-element.52.o7), channel_id=1, source_target_pairs={{0,224},{32,192},{64,160},{96,128},{128,96},{160,64},{192,32},{224... | collective-permute-start | bytes 294920 | tf_op jit(solution)/shard_map/ppermute | solution.py:789
  32.9 1.8 %collective-permute-start.9 = (f32[12,16,128]{2,1,0:T(8,128)S(1)}, f32[12,16,128]{2,1,0:T(8,128)S(1)}, u32[]{:S(2)}, u32[]{:S(2)}) collective-permute-start(f32[12,16,128]{2,1,0:T(8,128)S(1)} %get-tuple-element.55.o6), channel_id=1, source_target_pairs={{0,192},{32,224},{64,128},{96,160},{128,64},{160,96},{192,0},{224,... | collective-permute-start | bytes 294920 | tf_op jit(solution)/shard_map/ppermute | solution.py:789
  35.8 1.7 %collective-permute-done.6.i7 = f32[12,16,128]{2,1,0:T(8,128)S(1)} collective-permute-done((f32[12,16,128]{2,1,0:T(8,128)S(1)}, f32[12,16,128]{2,1,0:T(8,128)S(1)}, u32[]{:S(2)}, u32[]{:S(2)}) %collective-permute-start.6) | collective-permute-done | bytes 98336 | tf_op jit(solution)/shard_map/ppermute | solution.py:789
  40.1 4.1 %shard_map.102 = (f32[49,16,128]{2,1,0:T(8,128)S(1)}, f32[49,16,128]{2,1,0:T(8,128)S(1)}, f32[81,16,128]{2,1,0:T(8,128)S(1)}, f32[8,9,16,128]{3,2,1,0:T(8,128)S(...) custom-call(f32[12,16,128]{2,1,0:T(8,128)S(1)} %collective-permute-done.5.i4, ...), custom_call_target="tpu_custom_call" | custom-call | tf_op jit(solution)/shard_map/pallas_call | solution.py:771
  44.2 1.2 %collective-permute-start.16 = (f32[3,16,128]{2,1,0:T(8,128)S(1)}, f32[3,16,128]{2,1,0:T(8,128)S(1)}, u32[]{:S(2)}, u32[]{:S(2)}) collective-permute-start(f32[3,16,128]{2,1,0:T(8,128)S(1)} %get-tuple-element.71), channel_id=1, source_target_pairs={{0,16},{1,17},{2,18},{3,19},{4,20},{5,21},{6,22},{7,23},{8,24},{9,... | collective-permute-start | bytes 73736 | tf_op jit(solution)/shard_map/ppermute | solution.py:789
  45.7 3.2 %collective-permute-start.14 = (f32[3,16,128]{2,1,0:T(8,128)S(1)}, f32[3,16,128]{2,1,0:T(8,128)S(1)}, u32[]{:S(2)}, u32[]{:S(2)}) collective-permute-start(f32[3,16,128]{2,1,0:T(8,128)S(1)} %get-tuple-element.71), channel_id=1, source_target_pairs={{0,2},{1,3},{2,0},{3,1},{4,6},{5,7},{6,4},{7,5},{8,10},{9,11},{10,... | collective-permute-start | bytes 73736 | tf_op jit(solution)/shard_map/ppermute | solution.py:789
  53.0 2.3 %shard_map.105 = f32[256,128]{1,0:T(8,128)} custom-call(f32[49,16,128]{2,1,0:T(8,128)S(1)} %get-tuple-element.68.moved_ref, f32[144,256]{1,0:T(8,128)S(1)} %get-tuple-element.72.change_ref, f32[2,16,128]{2,1,0:T(8,128)S(1)} %get-tuple-element.73.sums_ref, f32[2,16,128]{2,1,0:T(8,128)S(1)} %get-tuple-element.74.changed_sums_ref, s32[32,128]{1,0:T(8,128)S(1)} %bitcast.17, ...), custom_call_target="tpu_custom_call" | custom-call | tf_op jit(solution)/shard_map/pallas_call | solution.py:771
  55.3 11.5 %all-to-all-start.1 = ((f32[256,1,128]{2,1,0:T(1,128)}), f32[256,1,128]{2,1,0:T(1,128)S(1)}, u32[]{:S(2)}, u32[]{:S(2)}) async-start(f32[256,1,128]{2,1,0:T(1,128)} %bitcast.7), calls=%async_computation.1 | async-start | bytes 262144 | tf_op jit(solution)/shard_map/all_to_all | solution.py:785
  66.9 3.0 %collective-permute-start.17 = (f32[11,16,128]{2,1,0:T(8,128)S(1)}, f32[11,16,128]{2,1,0:T(8,128)S(1)}, u32[]{:S(2)}, u32[]{:S(2)}) collective-permute-start(f32[11,16,128]{2,1,0:T(8,128)S(1)} %get-tuple-element.75), channel_id=1, source_target_pairs={{0,128},{32,160},{64,192},{96,224},{128,0},{160,32},{192,64},{224,... | collective-permute-start | bytes 270344 | tf_op jit(solution)/shard_map/ppermute | solution.py:789
  69.9 1.4 %collective-permute-start.18 = (f32[11,16,128]{2,1,0:T(8,128)S(1)}, f32[11,16,128]{2,1,0:T(8,128)S(1)}, u32[]{:S(2)}, u32[]{:S(2)}) collective-permute-start(f32[11,16,128]{2,1,0:T(8,128)S(1)} %get-tuple-element.76), channel_id=1, source_target_pairs={{0,224},{32,192},{64,160},{96,128},{128,96},{160,64},{192,32},{224... | collective-permute-start | bytes 270344 | tf_op jit(solution)/shard_map/ppermute | solution.py:789
  74.3 1.7 %collective-permute-start.22 = (f32[11,16,128]{2,1,0:T(8,128)S(1)}, f32[11,16,128]{2,1,0:T(8,128)S(1)}, u32[]{:S(2)}, u32[]{:S(2)}) collective-permute-start(f32[11,16,128]{2,1,0:T(8,128)S(1)} %get-tuple-element.80), channel_id=1, source_target_pairs={{0,96},{32,64},{64,32},{96,0},{128,224},{160,192},{192,160},{224,1... | collective-permute-start | bytes 270344 | tf_op jit(solution)/shard_map/ppermute | solution.py:789
  76.0 3.3 %collective-permute-done.18.i7 = f32[11,16,128]{2,1,0:T(8,128)S(1)} collective-permute-done((f32[11,16,128]{2,1,0:T(8,128)S(1)}, f32[11,16,128]{2,1,0:T(8,128)S(1)}, u32[]{:S(2)}, u32[]{:S(2)}) %collective-permute-start.18) | collective-permute-done | bytes 90144 | tf_op jit(solution)/shard_map/ppermute | solution.py:789
  79.9 1.4 %collective-permute-done.21.i6 = f32[11,16,128]{2,1,0:T(8,128)S(1)} collective-permute-done((f32[11,16,128]{2,1,0:T(8,128)S(1)}, f32[11,16,128]{2,1,0:T(8,128)S(1)}, u32[]{:S(2)}, u32[]{:S(2)}) %collective-permute-start.21) | collective-permute-done | bytes 90144 | tf_op jit(solution)/shard_map/ppermute | solution.py:789
  83.4 1.9 %collective-permute-start.25 = (f32[9,16,128]{2,1,0:T(8,128)S(1)}, f32[9,16,128]{2,1,0:T(8,128)S(1)}, u32[]{:S(2)}, u32[]{:S(2)}) collective-permute-start(f32[9,16,128]{2,1,0:T(8,128)S(1)} %get-tuple-element.84), channel_id=1, source_target_pairs={{0,224},{32,192},{64,160},{96,128},{128,96},{160,64},{192,32},{224... | collective-permute-start | bytes 221192 | tf_op jit(solution)/shard_map/ppermute | solution.py:789
  86.9 1.3 %collective-permute-start.28 = (f32[9,16,128]{2,1,0:T(8,128)S(1)}, f32[9,16,128]{2,1,0:T(8,128)S(1)}, u32[]{:S(2)}, u32[]{:S(2)}) collective-permute-start(f32[9,16,128]{2,1,0:T(8,128)S(1)} %get-tuple-element.87), channel_id=1, source_target_pairs={{0,192},{32,224},{64,128},{96,160},{128,64},{160,96},{192,0},{224,... | collective-permute-start | bytes 221192 | tf_op jit(solution)/shard_map/ppermute | solution.py:789
  88.2 1.4 %collective-permute-start.29 = (f32[9,16,128]{2,1,0:T(8,128)S(1)}, f32[9,16,128]{2,1,0:T(8,128)S(1)}, u32[]{:S(2)}, u32[]{:S(2)}) collective-permute-start(f32[9,16,128]{2,1,0:T(8,128)S(1)} %get-tuple-element.88), channel_id=1, source_target_pairs={{0,96},{32,64},{64,32},{96,0},{128,224},{160,192},{192,160},{224,1... | collective-permute-start | bytes 221192 | tf_op jit(solution)/shard_map/ppermute | solution.py:789
  89.6 1.4 %collective-permute-done.25.i7 = f32[9,16,128]{2,1,0:T(8,128)S(1)} collective-permute-done((f32[9,16,128]{2,1,0:T(8,128)S(1)}, f32[9,16,128]{2,1,0:T(8,128)S(1)}, u32[]{:S(2)}, u32[]{:S(2)}) %collective-permute-start.25) | collective-permute-done | bytes 73760 | tf_op jit(solution)/shard_map/ppermute | solution.py:789
  92.6 1.5 %shard_map.108 = f32[81,16,128]{2,1,0:T(8,128)} custom-call(f32[9,16,128]{2,1,0:T(8,128)S(1)} %collective-permute-done.24.i4, f32[9,16,128]{2,1,0:T(8,128)S(1)} %collective-permute-done.25.i7, f32[9,16,128]{2,1,0:T(8,128)S(1)} %collective-permute-done.26.i5, f32[9,16,128]{2,1,0:T(8,128)S(1)} %collective-permute-done.27.i2, ...), custom_call_target="tpu_custom_call" | custom-call | tf_op jit(solution)/shard_map/pallas_call | solution.py:771
  (69 shorter events, 21.6 us)
Async XLA Ops:
  4.2 20.5 %all-to-all-start = ((f32[8,9,16,128]{3,2,1,0:T(8,128)}), f32[8,9,16,128]{3,2,1,0:T(8,128)S(1)}, u32[]{:S(2)}, u32[]{:S(2)}) async-start(f32[8,9,16,128]{3,2,1,0:T(8,128)} %bitcast.20), calls=%async_computation | async-start | bytes 1179648 | tf_op jit(solution)/shard_map/all_to_all | solution.py:785
  11.0 11.3 %collective-permute-start.4 = (f32[3,24,128]{2,1,0:T(8,128)S(1)}, f32[3,24,128]{2,1,0:T(8,128)S(1)}, u32[]{:S(2)}, u32[]{:S(2)}) collective-permute-start(f32[3,24,128]{2,1,0:T(8,128)S(1)} %copy-done.8), channel_id=1, source_target_pairs={{0,16},{1,17},{2,18},{3,19},{4,20},{5,21},{6,22},{7,23},{8,24},{9,... | collective-permute-start | bytes 110600 | tf_op jit(solution)/shard_map/ppermute | solution.py:789
  17.1 5.3 %collective-permute-start.3 = (f32[3,24,128]{2,1,0:T(8,128)S(1)}, f32[3,24,128]{2,1,0:T(8,128)S(1)}, u32[]{:S(2)}, u32[]{:S(2)}) collective-permute-start(f32[3,24,128]{2,1,0:T(8,128)S(1)} %copy-done.8), channel_id=1, source_target_pairs={{0,8},{1,9},{2,10},{3,11},{4,12},{5,13},{6,14},{7,15},{8,0},{9,1},... | collective-permute-start | bytes 110600 | tf_op jit(solution)/shard_map/ppermute | solution.py:789
  25.6 9.0 %collective-permute-start.5 = (f32[12,16,128]{2,1,0:T(8,128)S(1)}, f32[12,16,128]{2,1,0:T(8,128)S(1)}, u32[]{:S(2)}, u32[]{:S(2)}) collective-permute-start(f32[12,16,128]{2,1,0:T(8,128)S(1)} %get-tuple-element.51.o4), channel_id=1, source_target_pairs={{0,128},{32,160},{64,192},{96,224},{128,0},{160,32},{192,64},{224,... | collective-permute-start | bytes 294920 | tf_op jit(solution)/shard_map/ppermute | solution.py:789
  28.6 8.9 %collective-permute-start.6 = (f32[12,16,128]{2,1,0:T(8,128)S(1)}, f32[12,16,128]{2,1,0:T(8,128)S(1)}, u32[]{:S(2)}, u32[]{:S(2)}) collective-permute-start(f32[12,16,128]{2,1,0:T(8,128)S(1)} %get-tuple-element.52.o7), channel_id=1, source_target_pairs={{0,224},{32,192},{64,160},{96,128},{128,96},{160,64},{192,32},{224... | collective-permute-start | bytes 294920 | tf_op jit(solution)/shard_map/ppermute | solution.py:789
  32.3 6.3 %collective-permute-start.7 = (f32[12,16,128]{2,1,0:T(8,128)S(1)}, f32[12,16,128]{2,1,0:T(8,128)S(1)}, u32[]{:S(2)}, u32[]{:S(2)}) collective-permute-start(f32[12,16,128]{2,1,0:T(8,128)S(1)} %get-tuple-element.53.o5), channel_id=1, source_target_pairs={{0,160},{32,128},{64,224},{96,192},{128,32},{160,0},{192,96},{224,... | collective-permute-start | bytes 294920 | tf_op jit(solution)/shard_map/ppermute | solution.py:789
  32.3 6.3 %collective-permute-start.8 = (f32[12,16,128]{2,1,0:T(8,128)S(1)}, f32[12,16,128]{2,1,0:T(8,128)S(1)}, u32[]{:S(2)}, u32[]{:S(2)}) collective-permute-start(f32[12,16,128]{2,1,0:T(8,128)S(1)} %get-tuple-element.54.o2), channel_id=1, source_target_pairs={{0,64},{32,96},{64,0},{96,32},{128,192},{160,224},{192,128},{224,1... | collective-permute-start | bytes 294920 | tf_op jit(solution)/shard_map/ppermute | solution.py:789
  32.9 6.8 %collective-permute-start.9 = (f32[12,16,128]{2,1,0:T(8,128)S(1)}, f32[12,16,128]{2,1,0:T(8,128)S(1)}, u32[]{:S(2)}, u32[]{:S(2)}) collective-permute-start(f32[12,16,128]{2,1,0:T(8,128)S(1)} %get-tuple-element.55.o6), channel_id=1, source_target_pairs={{0,192},{32,224},{64,128},{96,160},{128,64},{160,96},{192,0},{224,... | collective-permute-start | bytes 294920 | tf_op jit(solution)/shard_map/ppermute | solution.py:789
  34.6 5.4 %collective-permute-start.10 = (f32[12,16,128]{2,1,0:T(8,128)S(1)}, f32[12,16,128]{2,1,0:T(8,128)S(1)}, u32[]{:S(2)}, u32[]{:S(2)}) collective-permute-start(f32[12,16,128]{2,1,0:T(8,128)S(1)} %get-tuple-element.56.o3), channel_id=1, source_target_pairs={{0,96},{32,64},{64,32},{96,0},{128,224},{160,192},{192,160},{224,1... | collective-permute-start | bytes 294920 | tf_op jit(solution)/shard_map/ppermute | solution.py:789
  44.2 6.7 %collective-permute-start.16 = (f32[3,16,128]{2,1,0:T(8,128)S(1)}, f32[3,16,128]{2,1,0:T(8,128)S(1)}, u32[]{:S(2)}, u32[]{:S(2)}) collective-permute-start(f32[3,16,128]{2,1,0:T(8,128)S(1)} %get-tuple-element.71), channel_id=1, source_target_pairs={{0,16},{1,17},{2,18},{3,19},{4,20},{5,21},{6,22},{7,23},{8,24},{9,... | collective-permute-start | bytes 73736 | tf_op jit(solution)/shard_map/ppermute | solution.py:789
  45.4 5.4 %collective-permute-start.15 = (f32[3,16,128]{2,1,0:T(8,128)S(1)}, f32[3,16,128]{2,1,0:T(8,128)S(1)}, u32[]{:S(2)}, u32[]{:S(2)}) collective-permute-start(f32[3,16,128]{2,1,0:T(8,128)S(1)} %get-tuple-element.71), channel_id=1, source_target_pairs={{0,8},{1,9},{2,10},{3,11},{4,12},{5,13},{6,14},{7,15},{8,0},{9,1},... | collective-permute-start | bytes 73736 | tf_op jit(solution)/shard_map/ppermute | solution.py:789
  45.7 5.2 %collective-permute-start.14 = (f32[3,16,128]{2,1,0:T(8,128)S(1)}, f32[3,16,128]{2,1,0:T(8,128)S(1)}, u32[]{:S(2)}, u32[]{:S(2)}) collective-permute-start(f32[3,16,128]{2,1,0:T(8,128)S(1)} %get-tuple-element.71), channel_id=1, source_target_pairs={{0,2},{1,3},{2,0},{3,1},{4,6},{5,7},{6,4},{7,5},{8,10},{9,11},{10,... | collective-permute-start | bytes 73736 | tf_op jit(solution)/shard_map/ppermute | solution.py:789
  55.3 26.0 %all-to-all-start.1 = ((f32[256,1,128]{2,1,0:T(1,128)}), f32[256,1,128]{2,1,0:T(1,128)S(1)}, u32[]{:S(2)}, u32[]{:S(2)}) async-start(f32[256,1,128]{2,1,0:T(1,128)} %bitcast.7), calls=%async_computation.1 | async-start | bytes 262144 | tf_op jit(solution)/shard_map/all_to_all | solution.py:785
  66.9 7.4 %collective-permute-start.17 = (f32[11,16,128]{2,1,0:T(8,128)S(1)}, f32[11,16,128]{2,1,0:T(8,128)S(1)}, u32[]{:S(2)}, u32[]{:S(2)}) collective-permute-start(f32[11,16,128]{2,1,0:T(8,128)S(1)} %get-tuple-element.75), channel_id=1, source_target_pairs={{0,128},{32,160},{64,192},{96,224},{128,0},{160,32},{192,64},{224,... | collective-permute-start | bytes 270344 | tf_op jit(solution)/shard_map/ppermute | solution.py:789
  69.9 9.5 %collective-permute-start.18 = (f32[11,16,128]{2,1,0:T(8,128)S(1)}, f32[11,16,128]{2,1,0:T(8,128)S(1)}, u32[]{:S(2)}, u32[]{:S(2)}) collective-permute-start(f32[11,16,128]{2,1,0:T(8,128)S(1)} %get-tuple-element.76), channel_id=1, source_target_pairs={{0,224},{32,192},{64,160},{96,128},{128,96},{160,64},{192,32},{224... | collective-permute-start | bytes 270344 | tf_op jit(solution)/shard_map/ppermute | solution.py:789
  71.3 8.6 %collective-permute-start.19 = (f32[11,16,128]{2,1,0:T(8,128)S(1)}, f32[11,16,128]{2,1,0:T(8,128)S(1)}, u32[]{:S(2)}, u32[]{:S(2)}) collective-permute-start(f32[11,16,128]{2,1,0:T(8,128)S(1)} %get-tuple-element.77), channel_id=1, source_target_pairs={{0,160},{32,128},{64,224},{96,192},{128,32},{160,0},{192,96},{224,... | collective-permute-start | bytes 270344 | tf_op jit(solution)/shard_map/ppermute | solution.py:789
  72.3 7.7 %collective-permute-start.20 = (f32[11,16,128]{2,1,0:T(8,128)S(1)}, f32[11,16,128]{2,1,0:T(8,128)S(1)}, u32[]{:S(2)}, u32[]{:S(2)}) collective-permute-start(f32[11,16,128]{2,1,0:T(8,128)S(1)} %get-tuple-element.78), channel_id=1, source_target_pairs={{0,64},{32,96},{64,0},{96,32},{128,192},{160,224},{192,128},{224,1... | collective-permute-start | bytes 270344 | tf_op jit(solution)/shard_map/ppermute | solution.py:789
  73.4 7.9 %collective-permute-start.21 = (f32[11,16,128]{2,1,0:T(8,128)S(1)}, f32[11,16,128]{2,1,0:T(8,128)S(1)}, u32[]{:S(2)}, u32[]{:S(2)}) collective-permute-start(f32[11,16,128]{2,1,0:T(8,128)S(1)} %get-tuple-element.79), channel_id=1, source_target_pairs={{0,192},{32,224},{64,128},{96,160},{128,64},{160,96},{192,0},{224,... | collective-permute-start | bytes 270344 | tf_op jit(solution)/shard_map/ppermute | solution.py:789
  74.3 7.0 %collective-permute-start.22 = (f32[11,16,128]{2,1,0:T(8,128)S(1)}, f32[11,16,128]{2,1,0:T(8,128)S(1)}, u32[]{:S(2)}, u32[]{:S(2)}) collective-permute-start(f32[11,16,128]{2,1,0:T(8,128)S(1)} %get-tuple-element.80), channel_id=1, source_target_pairs={{0,96},{32,64},{64,32},{96,0},{128,224},{160,192},{192,160},{224,1... | collective-permute-start | bytes 270344 | tf_op jit(solution)/shard_map/ppermute | solution.py:789
  82.2 6.0 %collective-permute-start.24 = (f32[9,16,128]{2,1,0:T(8,128)S(1)}, f32[9,16,128]{2,1,0:T(8,128)S(1)}, u32[]{:S(2)}, u32[]{:S(2)}) collective-permute-start(f32[9,16,128]{2,1,0:T(8,128)S(1)} %get-tuple-element.83), channel_id=1, source_target_pairs={{0,128},{32,160},{64,192},{96,224},{128,0},{160,32},{192,64},{224,... | collective-permute-start | bytes 221192 | tf_op jit(solution)/shard_map/ppermute | solution.py:789
  83.4 7.7 %collective-permute-start.25 = (f32[9,16,128]{2,1,0:T(8,128)S(1)}, f32[9,16,128]{2,1,0:T(8,128)S(1)}, u32[]{:S(2)}, u32[]{:S(2)}) collective-permute-start(f32[9,16,128]{2,1,0:T(8,128)S(1)} %get-tuple-element.84), channel_id=1, source_target_pairs={{0,224},{32,192},{64,160},{96,128},{128,96},{160,64},{192,32},{224... | collective-permute-start | bytes 221192 | tf_op jit(solution)/shard_map/ppermute | solution.py:789
  85.2 6.2 %collective-permute-start.26 = (f32[9,16,128]{2,1,0:T(8,128)S(1)}, f32[9,16,128]{2,1,0:T(8,128)S(1)}, u32[]{:S(2)}, u32[]{:S(2)}) collective-permute-start(f32[9,16,128]{2,1,0:T(8,128)S(1)} %get-tuple-element.85), channel_id=1, source_target_pairs={{0,160},{32,128},{64,224},{96,192},{128,32},{160,0},{192,96},{224,... | collective-permute-start | bytes 221192 | tf_op jit(solution)/shard_map/ppermute | solution.py:789
  86.0 5.5 %collective-permute-start.27 = (f32[9,16,128]{2,1,0:T(8,128)S(1)}, f32[9,16,128]{2,1,0:T(8,128)S(1)}, u32[]{:S(2)}, u32[]{:S(2)}) collective-permute-start(f32[9,16,128]{2,1,0:T(8,128)S(1)} %get-tuple-element.86), channel_id=1, source_target_pairs={{0,64},{32,96},{64,0},{96,32},{128,192},{160,224},{192,128},{224,1... | collective-permute-start | bytes 221192 | tf_op jit(solution)/shard_map/ppermute | solution.py:789
  86.9 4.9 %collective-permute-start.28 = (f32[9,16,128]{2,1,0:T(8,128)S(1)}, f32[9,16,128]{2,1,0:T(8,128)S(1)}, u32[]{:S(2)}, u32[]{:S(2)}) collective-permute-start(f32[9,16,128]{2,1,0:T(8,128)S(1)} %get-tuple-element.87), channel_id=1, source_target_pairs={{0,192},{32,224},{64,128},{96,160},{128,64},{160,96},{192,0},{224,... | collective-permute-start | bytes 221192 | tf_op jit(solution)/shard_map/ppermute | solution.py:789
  (18 other events, 151.9 us)
